TPU v7x, 32 devices: a whole 2x2x4 slice. The times are simulated.
32 devices in a mesh: rows: 8 (over z, x), cols: 4 (over y, core).
Axes of the slice: x: 2, y: 2, z: 4, core: 2. Of those that a mesh axis runs over, the one named last changes fastest.
Arguments:
- panel_u: bfloat16 [8, 16, 1024, 256], P('rows', 'cols'), may hold values from -2.5 to 2.5
- panel_v: bfloat16 [8, 16, 1024, 256], P('rows', 'cols'), may hold values from -0.1875 to 0.1875
- panel_rank: int32 [8, 16], P('rows', 'cols'), may hold values from 128 to 256
- pivot_u: bfloat16 [2, 16, 1024, 256], P(None, 'cols', 'rows'), may hold values from -2.5 to 2.5
- pivot_v: bfloat16 [2, 16, 1024, 256], P(None, 'cols', 'rows'), may hold values from -0.1875 to 0.1875
- pivot_rank: int32 [2, 16], P(None, 'cols'), may hold values from 128 to 256
- orig_u: bfloat16 [2, 8, 1024, 256], P(None, 'rows'), may hold values from -6 to 6
- orig_v: bfloat16 [2, 8, 1024, 256], P(None, 'rows'), may hold values from -0.375 to 0.375
- sampler: bfloat16 [1024, 256], replicated, may hold values from -6 to 6
Outputs:
- basis: float32 [2, 8, 1024, 256], P(None, 'rows', 'cols')
- coeff: float32 [2, 8, 1024, 256], P(None, 'rows', 'cols')
Inputs may be any that keep to these rules, and one draw needn't show every extreme that they name: `panel_rank`: rank of each panel tile; factor columns at and beyond it carry no weight. `pivot_rank`: rank of each pivot row tile; factor columns at and beyond it carry no weight.
All inputs are finite; a program needn't handle non-finite values.
Results may differ from a plain program's by a relative error of at most 0.012.
Values may be sent and summed in bfloat16 or wider, within the bound.
No kernel may reach another device: no remote copies, remote signals or barrier semaphores. Data moves between devices by JAX's collectives and lax.ppermute only.
A program may use at most 64 MiB of HBM per device.

v0:
```python
import functools
import math

import jax
import jax.numpy as jnp
import numpy as np
from jax import lax
from jax.experimental import pallas as pl
from jax.experimental.pallas import tpu as pltpu
from jax.sharding import PartitionSpec as P

F32 = jnp.float32
BF16 = jnp.bfloat16
BLOCK = 32
GROUP = 4
SUB = 8
RING_MOST = 16
MIB = 1 << 20


def dot(a, b):
    return lax.dot_general(a, b, (((1,), (0,)), ((), ())), preferred_element_type=F32)


def dot00(a, b):
    return lax.dot_general(a, b, (((0,), (0,)), ((), ())), preferred_element_type=F32)


def dot11(a, b):
    return lax.dot_general(a, b, (((1,), (1,)), ((), ())), preferred_element_type=F32)


def split3(x):
    high = x.astype(BF16)
    rest = x - high.astype(F32)
    mid = rest.astype(BF16)
    low = (rest - mid.astype(F32)).astype(BF16)
    return high, mid, low


def reciprocal(x):
    guess = pl.reciprocal(x, approx=True)
    guess = guess * (2.0 - x * guess)
    return guess * (2.0 - x * guess)


def eliminate(panel, first):
    rows, width = panel.shape
    lanes = 128
    tile = (SUB, lanes)
    lane = lax.broadcasted_iota(jnp.int32, tile, 1)
    sub = lax.broadcasted_iota(jnp.int32, tile, 0)
    high = rows // SUB
    halves = width // lanes
    part = [
        [panel[v * SUB : (v + 1) * SUB, h * lanes : (h + 1) * lanes] for h in range(halves)]
        for v in range(high)
    ]
    mine = first // lanes
    pivots = [jnp.ones(tile, F32) for _ in range(high)]
    for k in range(0, rows, GROUP):
        at = first % lanes + k
        top, low = k // SUB, k % SUB
        inside = (lane >= at) & (lane < at + GROUP)
        column = [
            [jnp.broadcast_to(part[v][mine][:, at + m : at + m + 1], tile) for v in range(top, high)]
            for m in range(GROUP)
        ]
        small = [
            [jnp.broadcast_to(column[b][0][low + a : low + a + 1, :], tile) for b in range(a + 1)]
            for a in range(GROUP)
        ]
        row = []
        for a in range(GROUP):
            row.append([jnp.broadcast_to(part[top][h][low + a : low + a + 1, :], tile) for h in range(halves)])
            row[a][mine] = jnp.where(inside, jnp.where(lane == at + a, 1.0, 0.0), row[a][mine])
        factor = []
        for m in range(GROUP):
            inverse = reciprocal(small[m][m])
            pivots[top] = jnp.where(sub == low + m, small[m][m], pivots[top])
            for a in range(m + 1, GROUP):
                ratio = small[a][m] * inverse
                for b in range(m + 1, a + 1):
                    small[a][b] = small[a][b] - ratio * small[b][m]
                row[a] = [x - ratio * y for x, y in zip(row[a], row[m])]
            factor.append([c * inverse for c in column[m]])
            for b in range(m + 1, GROUP):
                column[b] = [c - f * small[b][m] for c, f in zip(column[b], factor[m])]
        for v in range(top, high):
            for h in range(halves):
                old = part[v][h]
                value = jnp.where(inside, 0.0, old) if h == mine else old
                for m in range(GROUP):
                    value = value - factor[m][v - top] * row[m][h]
                if v == top:
                    if low > 0:
                        value = jnp.where(sub < low, old, value)
                    for m in range(GROUP):
                        value = jnp.where(sub == low + m, row[m][h], value)
                part[v][h] = value
    done = []
    for v in range(high):
        scale = lax.rsqrt(pivots[v])
        cells = []
        for h in range(halves):
            value = part[v][h] * scale
            if h == mine:
                start = first % lanes
                value = jnp.where((lane > start + v * SUB + sub) & (lane < start + rows), 0.0, value)
            cells.append(value)
        done.append(jnp.concatenate(cells, 1))
    return jnp.concatenate(done, 0)


def invert_blocks(work, begin, end):
    width = work.shape[0]
    lane = lax.broadcasted_iota(jnp.int32, (1, width), 1)
    for first in range(begin, end, BLOCK):
        last = first + BLOCK
        panel = eliminate(work[first:last, :], first)
        work[first:last, :] = panel
        if last < width:
            base = last // 128 * 128
            high, mid, low = split3(panel)
            left = jnp.concatenate([high, high, mid, mid, high, low], 0)[:, base:]
            right = jnp.concatenate([high, mid, high, mid, low, high], 0)
            update = dot00(left, right)[last - base :, :]
            inside = (lane >= first) & (lane < last)
            work[last:, :] = jnp.where(inside, 0.0, work[last:, :]) - update


def orthonormal_kernel(info, start, *refs):
    parts, (qt, basis, given, yt, work) = refs[:-5], refs[-5:]
    width, order = yt.shape
    core = info[0]
    total = start[...]
    for part in parts:
        total = total - part[...].astype(F32)
    yt[...] = total
    high, mid, low = split3(yt[...])
    cross = dot11(high, mid) + dot11(high, low)
    work[...] = dot11(high, high) + (cross + cross.T + dot11(mid, mid))
    invert_blocks(work, 0, width)
    row = lax.broadcasted_iota(jnp.int32, (width, width), 0)
    col = lax.broadcasted_iota(jnp.int32, (width, width), 1)
    m_high, m_low, _ = split3(jnp.where(col <= row, work[...], 0.0))
    high, mid, _ = split3(yt[...])
    product = dot(m_high, high) + (dot(m_high, mid) + dot(m_low, high))
    qt[...] = product.astype(BF16)
    yt[...] = product
    share = basis.shape[0]
    for out, index in ((basis, info[1]), (given, info[1] + 1 - 2 * core)):
        rows = yt[:, pl.ds(pl.multiple_of(index * share, 128), share)]
        out[...] = rows.T * math.sqrt(order)


def gather_kernel(places, blocks, info, panel_vt, sampler_t, *refs):
    new = len(places)
    u, v = refs[:new], refs[new : 2 * new]
    kept = refs[2 * new : -3]
    sampled, met, u_all = refs[-3:]
    pivots, priors, order, width = u_all.shape
    slab = order // blocks
    spans = [pl.ds(pl.multiple_of(info[2 + p] * slab, 128), slab) for p in places]
    drawn = jnp.concatenate([sampler_t[:, span] for span in spans], 1)
    for j in range(priors):
        left = jnp.concatenate([panel_vt[j, :, span] for span in spans], 1)
        for c in range(pivots):
            u_new = jnp.concatenate([block[c, j] for block in u], 0)
            v_new = jnp.concatenate([block[c, j] for block in v], 0)
            one, two = dot(drawn, u_new), dot(left, v_new)
            if kept:
                one, two = one + kept[0][c, j], two + kept[1][c, j]
            sampled[c, j] = one
            met[c, j] = two
            for n, p in enumerate(places):
                u_all[c, j, p * slab : (p + 1) * slab, :] = u_new[n * slab : (n + 1) * slab, :]


def update_kernel(own_column, info, panel_rank, pivot_rank, sampled, met, panel_u, cross, out):
    priors, width, _ = cross.shape
    column = info[0] if own_column else 1 - info[0]
    row = lax.broadcasted_iota(jnp.int32, (width, width), 0)
    col = lax.broadcasted_iota(jnp.int32, (width, width), 1)
    terms = []
    for j in range(priors):
        inside = (row < panel_rank[0, j]) & (col < pivot_rank[column, j])
        cross[j] = jnp.where(inside, met[column, j], 0.0).astype(BF16)
        terms.append(dot11(sampled[column, j].astype(BF16), cross[j]).astype(BF16))
    half = out.shape[1] // 2
    for at in (0, half):
        total = jnp.zeros((width, half), F32)
        for j in range(priors):
            total += dot11(terms[j], panel_u[j, at : at + half, :])
        out[:, at : at + half] = total.astype(out.dtype)


def project_kernel(blocks, own_column, info, qt, panel_u, cross, u_all, orig_u, orig_v, give, keep, own, work, u_buf, v_buf, sems):
    _, priors, order, width = u_all.shape
    slab = order // blocks
    pairs, share, _ = keep.shape
    core = info[0]
    column = core if own_column else 1 - core
    rows = pl.ds(pl.multiple_of(info[1] * share, 16), share)
    fetch_u = pltpu.make_async_copy(orig_u.at[column], u_buf, sems.at[0])
    fetch_v = pltpu.make_async_copy(orig_v.at[column, rows], v_buf, sems.at[1])
    fetch_u.start()
    fetch_v.start()
    mids = []
    for j in range(priors):
        inner = dot(qt[...], panel_u[j]).astype(BF16)
        mids.append(dot(inner, cross[j]).astype(BF16))
    some = max(1, blocks // 2)
    for begin in range(0, blocks, some):
        total = jnp.zeros((some * slab, width), F32)
        for j in range(priors):
            total += dot11(u_all[column, j, begin * slab : (begin + some) * slab, :], mids[j])
        for n in range(some):
            place = pl.ds(pl.multiple_of(info[2 + begin + n] * slab, SUB), slab)
            work[place, :] = total[n * slab : (n + 1) * slab, :]
    for a in range(pairs):
        for out, which in ((give, 1 - core), (keep, core)):
            place = pl.ds(pl.multiple_of((2 * a + which) * share, SUB), share)
            out[a] = work[place, :].astype(out.dtype)
    fetch_u.wait()
    fetch_v.wait()
    own[...] = dot11(v_buf[...], dot(qt[...], u_buf[...]).astype(BF16))


def turn_kernel(panel_v, sampler, panel_vt, sampler_t):
    sampler_t[...] = sampler[...].T
    for j in range(panel_v.shape[0]):
        panel_vt[j] = panel_v[j].T


def start_kernel(info, sampler_t, orig_u, orig_v, out):
    core = info[0]
    proj = dot(sampler_t[...], orig_v[core]).astype(BF16)
    out[...] = dot11(proj, orig_u[core])


def run(kernel, scalars, arrays, outs, scratch, limit, flops, name, aliases={}, apart=()):
    smem = pl.BlockSpec(memory_space=pltpu.SMEM)
    vmem = pl.BlockSpec(memory_space=pltpu.VMEM)
    shapes = [jax.ShapeDtypeStruct(*o) for o in outs]
    moved = sum(a.size * a.dtype.itemsize for a in list(arrays) + shapes)
    return pl.pallas_call(
        kernel,
        out_shape=shapes,
        in_specs=[smem] * len(scalars) + [vmem] * len(arrays) + [pl.BlockSpec(memory_space=pl.ANY)] * len(apart),
        out_specs=[vmem] * len(shapes),
        scratch_shapes=scratch,
        input_output_aliases=aliases,
        compiler_params=pltpu.CompilerParams(vmem_limit_bytes=limit * MIB),
        cost_estimate=pl.CostEstimate(flops=flops, bytes_accessed=moved, transcendentals=0),
        name=name,
    )(*scalars, *arrays, *apart)


def ring_order(count):
    if count % 2:
        return list(range(count))
    return list(range(0, count, 2)) + list(range(count - 1, 0, -2))


class Ring:
    def __init__(self, arrays, order, axis):
        count = len(order)
        self.count, self.axis, self.near = count, axis, (count - 1) // 2
        self.ahead = [(order[(p + 1) % count], order[p]) for p in range(count)]
        self.behind = [(order[p], order[(p + 1) % count]) for p in range(count)]
        self.found = [{0: a} for a in arrays]
        self.up, self.down = list(arrays), list(arrays)

    def step(self, number):
        for t in range(2):
            if number <= self.near or t == 0:
                self.up[t] = lax.ppermute(self.up[t], self.axis, self.ahead)
                self.found[t][number] = self.up[t]
            if number <= self.near or t == 1:
                self.down[t] = lax.ppermute(self.down[t], self.axis, self.behind)
                self.found[t][self.count - number] = self.down[t]

    def hold(self, value, t, number):
        if number > self.near:
            return value
        places = (number, self.count - number)
        value, *kept = lax.optimization_barrier((value, *(self.found[t][d] for d in places)))
        for d, block in zip(places, kept):
            self.found[t][d] = block
        return value

    def tie(self, value, number, which=(0, 1)):
        lists = [(self.up, t, number) for t in which if number <= self.near or t == 0]
        lists += [(self.down, t, self.count - number) for t in which if number <= self.near or t == 1]
        value, *held = lax.optimization_barrier((value, *(way[t] for way, t, _ in lists)))
        for (way, t, place), block in zip(lists, held):
            way[t] = self.found[t][place] = block
        return value

    def blocks(self, t):
        return [self.found[t][d] for d in range(self.count)]


def body(panel_u, panel_v, panel_rank, pivot_u, pivot_v, pivot_rank, orig_u, orig_v, sampler):
    order, width = panel_u.shape[2:]
    priors = panel_u.shape[1]
    pivots = pivot_u.shape[0]
    count = lax.axis_size("rows")
    cols = lax.axis_size("cols")
    pairs = cols // 2
    half, share = order // 2, order // cols
    me = lax.axis_index("cols")
    core, pair = me % 2, me // 2
    swap = [(i, i ^ 1) for i in range(cols)]

    ring = ring_order(count)
    place = np.argsort(np.array(ring))
    table = np.array([[ring[(place[r] + d) % count] for d in range(count)] for r in range(count)], np.int32)
    last = count // 2
    whole = count % 2 == 1 or last < 4 or count > RING_MOST
    if whole:
        table = np.zeros((count, 1), np.int32)
    sources = jnp.asarray(table)[lax.axis_index("rows")]
    info = jnp.concatenate([jnp.stack([core, me]).astype(jnp.int32), sources])

    panel_u, panel_v, orig_u, orig_v = panel_u[0], panel_v[0], orig_u[:, 0], orig_v[:, 0]
    square = 2 * width * width
    panel_vt, sampler_t = run(
        turn_kernel, [], [panel_v, sampler], [((priors, width, order), BF16), ((sampler.shape[1], order), BF16)], [], 12,
        10 * square * order, "turn"
    )
    (start,) = run(
        start_kernel, [info], [sampler_t, orig_u, orig_v], [((width, order), F32)], [], 12,
        2 * square * order, "start"
    )

    def shifted(x, shift):
        return lax.ppermute(x, "cols", [(i, (i + 2 * shift) % cols) for i in range(cols)])

    matrix = pltpu.VMEM((width, width), F32)
    tall = pltpu.VMEM((width, order), F32)

    def gathered(places, blocks, new_u, new_v, kept):
        new = len(places)
        shapes = [
            ((pivots, priors, width, width), F32), ((pivots, priors, width, width), F32),
            ((pivots, priors, order, width), BF16)
        ]
        first = 3 + 2 * new
        return run(
            functools.partial(gather_kernel, places, blocks), [info], [panel_vt, sampler_t, *new_u, *new_v, *kept],
            shapes, [], 28, 2 * pivots * priors * square * order * new // blocks, "gather",
            {first + n: n for n in range(len(kept))}
        )

    def updated(own_column, sampled, met):
        return run(
            functools.partial(update_kernel, own_column), [info, panel_rank, pivot_rank], [sampled, met, panel_u],
            [((priors, width, width), BF16), ((width, order), F32 if own_column else BF16)], [], 16,
            2 * priors * square * (order + width), "update"
        )

    def projected(own_column, blocks, qt, cross, u_all):
        return run(
            functools.partial(project_kernel, blocks, own_column), [info], [qt, panel_u, cross, u_all],
            [((pairs, share, width), BF16), ((pairs, share, width), F32), ((share, width), F32)],
            [
                pltpu.VMEM((order, width), F32), pltpu.VMEM((order, width), BF16), pltpu.VMEM((share, width), BF16),
                pltpu.SemaphoreType.DMA((2,))
            ],
            20, 3 * priors * square * (2 * order + width), "project", apart=[orig_u, orig_v]
        )

    def placed(mine, other):
        return jnp.where(core == 0, jnp.stack([mine, other]), jnp.stack([other, mine]))

    if whole:
        blocks = 1
        new_u, new_v = ([lax.all_gather(x, "rows", axis=2, tiled=True)] for x in (pivot_u, pivot_v))
        sampled, met, u_all = gathered([0], 1, new_u, new_v, [])
    else:
        blocks = count
        now, kept = Ring([pivot_u, pivot_v], ring, "rows"), []
        for number in range(1, last + 1):
            now.step(number)
            if 1 < number < last:
                kept[0] = now.tie(kept[0], number, (0,))
                if number == 2:
                    start = now.tie(start, number, (1,))
            places = sorted({number, count - number} | ({0} if number == 1 else set()))
            new_u, new_v = ([now.found[t][p] for p in places] for t in range(2))
            kept = list(gathered(places, count, new_u, new_v, kept))
        sampled, met, u_all = kept
    cross_other, give = updated(False, sampled, met)
    recv = lax.ppermute(give, "cols", swap)
    cross_own, keep = updated(True, sampled, met)
    sent = (keep + recv.astype(F32)).astype(BF16)
    parts = [keep, recv, *(shifted(sent, shift) for shift in range(1, pairs))]
    qt, rows, given = run(
        orthonormal_kernel, [info], [start, *parts],
        [((width, order), BF16), ((share, width), F32), ((share, width), F32)], [tall, matrix], 16,
        128 * square * order, "orthonormal"
    )
    qt_other = lax.ppermute(qt, "cols", swap)
    rows_other = lax.ppermute(given, "cols", swap)
    give_a, keep_a, own_a = projected(True, blocks, qt, cross_own, u_all)
    qt_other, give_a, keep_a, own_a = lax.optimization_barrier((qt_other, give_a, keep_a, own_a))
    give_b, keep_b, own_b = projected(False, blocks, qt_other, cross_other, u_all)
    results = []
    for keep, own, give in ((keep_b, own_b, give_a), (keep_a, own_a, give_b)):
        chip = keep + lax.ppermute(give, "cols", swap).astype(F32)
        total = own - lax.dynamic_index_in_dim(chip, pair, 0, False)
        for shift in range(1, pairs):
            sent = lax.dynamic_index_in_dim(chip, (pair + shift) % pairs, 0, False).astype(BF16)
            total = total - shifted(sent, shift).astype(F32)
        results.append(total)
    basis, coeff = placed(rows, rows_other), placed(results[1], results[0])
    return (basis[:, None], coeff[:, None])


def solution(mesh):
    placed = (
        P("rows", "cols", None, None),
        P("rows", "cols", None, None),
        P("rows", "cols"),
        P(None, "cols", "rows", None),
        P(None, "cols", "rows", None),
        P(None, "cols"),
        P(None, "rows", None, None),
        P(None, "rows", None, None),
        P(),
    )
    return jax.shard_map(
        body,
        mesh=mesh,
        in_specs=placed,
        out_specs=(P(None, "rows", "cols", None), P(None, "rows", "cols", None)),
        check_vma=False,
    )
```

profile of v0, /device:TPU:0, one launch (start us, length us, event | category | flops | bytes accessed | tf_op | source)
XLA Modules:
  0.0 139.8 jit_solution(5607086331992817530)
XLA Ops:
  0.6 3.0 %collective-permute-start.4 = (bf16[2,4,128,256]{3,2,1,0:T(8,128)(2,1)}, bf16[2,4,128,256]{3,2,1,0:T(8,128)(2,1)}, u32[]{:S(2)}, u32[]{:S(2)}) collective-permute-start(bf16[2,4,128,256]{3,2,1,0:T(8,128)(2,1)} %refs_0_.1), channel_id=1, source_target_pairs={{8,0},{16,8},{24,16},{28,24},{20,28},{12,20},{4,12},{0,4},{9,1},{1... | collective-permute-start | bytes 1572872 | tf_op jit(solution)/shard_map/ppermute | solution.py:278
  3.8 1.9 %collective-permute-start = (bf16[2,4,128,256]{3,2,1,0:T(8,128)(2,1)}, bf16[2,4,128,256]{3,2,1,0:T(8,128)(2,1)S(1)}, u32[]{:S(2)}, u32[]{:S(2)}) collective-permute-start(bf16[2,4,128,256]{3,2,1,0:T(8,128)(2,1)} %refs_3_.1), channel_id=1, source_target_pairs={{8,0},{16,8},{24,16},{28,24},{20,28},{12,20},{4,12},{0,4},{9,1},{1... | collective-permute-start | bytes 1572872 | tf_op jit(solution)/shard_map/ppermute | solution.py:278
  5.8 11.0 %collective-permute-done.4.refs_1_ = bf16[2,4,128,256]{3,2,1,0:T(8,128)(2,1)} collective-permute-done((bf16[2,4,128,256]{3,2,1,0:T(8,128)(2,1)}, bf16[2,4,128,256]{3,2,1,0:T(8,128)(2,1)}, u32[]{:S(2)}, u32[]{:S(2)}) %collective-permute-start.4) | collective-permute-done | bytes 524320 | tf_op jit(solution)/shard_map/ppermute | solution.py:278
  16.8 2.0 %collective-permute-start.6 = (bf16[2,4,128,256]{3,2,1,0:T(8,128)(2,1)}, bf16[2,4,128,256]{3,2,1,0:T(8,128)(2,1)S(1)}, u32[]{:S(2)}, u32[]{:S(2)}) collective-permute-start(bf16[2,4,128,256]{3,2,1,0:T(8,128)(2,1)} %collective-permute-done.4.refs_1_), channel_id=1, source_target_pairs={{8,0},{16,8},{24,16},{28,24},{20,28},{12,20},{4,12},{0,4},{9,1},{1... | collective-permute-start | bytes 1572872 | tf_op jit(solution)/shard_map/ppermute | solution.py:278
  18.9 9.0 %collective-permute-done.refs_4_ = bf16[2,4,128,256]{3,2,1,0:T(8,128)(2,1)S(1)} collective-permute-done((bf16[2,4,128,256]{3,2,1,0:T(8,128)(2,1)}, bf16[2,4,128,256]{3,2,1,0:T(8,128)(2,1)S(1)}, u32[]{:S(2)}, u32[]{:S(2)}) %collective-permute-start) | collective-permute-done | bytes 524320 | tf_op jit(solution)/shard_map/ppermute | solution.py:278
  27.9 2.0 %collective-permute-start.1 = (bf16[2,4,128,256]{3,2,1,0:T(8,128)(2,1)S(1)}, bf16[2,4,128,256]{3,2,1,0:T(8,128)(2,1)S(1)}, u32[]{:S(2)}, u32[]{:S(2)}) collective-permute-start(bf16[2,4,128,256]{3,2,1,0:T(8,128)(2,1)S(1)} %collective-permute-done.refs_4_), channel_id=1, source_target_pairs={{8,0},{16,8},{24,16},{28,24},{20,28},{12,20},{4,12},{0,4},{9,1},{1... | collective-permute-start | bytes 1572872 | tf_op jit(solution)/shard_map/ppermute | solution.py:278
  30.8 1.6 %copy-done.7 = bf16[1,4,1024,256]{3,2,1,0:T(8,128)(2,1)S(1)} copy-done((bf16[1,4,1024,256]{3,2,1,0:T(8,128)(2,1)S(1)}, bf16[1,4,1024,256]{3,2,1,0:T(8,128)(2,1)}, u32[]{:S(2)}) %copy-start.7) | copy-done | bytes 2097176
  36.3 2.5 %gather.4 = (f32[2,4,256,256]{3,2,1,0:T(8,128)S(1)}, f32[2,4,256,256]{3,2,1,0:T(8,128)S(1)}, bf16[2,4,1024,256]{3,2,1,0:T(8,128)(2,1)S(1)}) custom-call(s32[10]{0:T(128)S(1)} %pad_add_fusion.info, bf16[4,256,1024]{2,1,0:T(8,128)(2,1)S(1)} %get-tuple-element.44.panel_vt, bf16[256,1024]{1,0:T(8,128)(2,1)S(1)} %get-tuple-element.42.sampler_t, ...), custom_call_target="tpu_custom_call" | custom-call | flops 805306368 | bytes 14155776 | tf_op jit(solution)/shard_map/gather/pallas_call | solution.py:247
  39.1 2.0 %collective-permute-done.7.refs_1_ = bf16[2,4,128,256]{3,2,1,0:T(8,128)(2,1)S(1)} collective-permute-done((bf16[2,4,128,256]{3,2,1,0:T(8,128)(2,1)}, bf16[2,4,128,256]{3,2,1,0:T(8,128)(2,1)S(1)}, u32[]{:S(2)}, u32[]{:S(2)}) %collective-permute-start.7) | collective-permute-done | bytes 524320 | tf_op jit(solution)/shard_map/ppermute | solution.py:281
  41.1 1.6 %collective-permute-start.8 = (bf16[2,4,128,256]{3,2,1,0:T(8,128)(2,1)S(1)}, bf16[2,4,128,256]{3,2,1,0:T(8,128)(2,1)S(1)}, u32[]{:S(2)}, u32[]{:S(2)}) collective-permute-start(bf16[2,4,128,256]{3,2,1,0:T(8,128)(2,1)S(1)} %collective-permute-done.6.refs_0_), channel_id=1, source_target_pairs={{8,0},{16,8},{24,16},{28,24},{20,28},{12,20},{4,12},{0,4},{9,1},{1... | collective-permute-start | bytes 1572872 | tf_op jit(solution)/shard_map/ppermute | solution.py:278
  43.2 7.2 %collective-permute-done.1.refs_2_ = bf16[2,4,128,256]{3,2,1,0:T(8,128)(2,1)S(1)} collective-permute-done((bf16[2,4,128,256]{3,2,1,0:T(8,128)(2,1)S(1)}, bf16[2,4,128,256]{3,2,1,0:T(8,128)(2,1)S(1)}, u32[]{:S(2)}, u32[]{:S(2)}) %collective-permute-start.1) | collective-permute-done | bytes 524320 | tf_op jit(solution)/shard_map/ppermute | solution.py:278
  50.4 2.0 %collective-permute-done.3.refs_3_ = bf16[2,4,128,256]{3,2,1,0:T(8,128)(2,1)S(1)} collective-permute-done((bf16[2,4,128,256]{3,2,1,0:T(8,128)(2,1)S(1)}, bf16[2,4,128,256]{3,2,1,0:T(8,128)(2,1)S(1)}, u32[]{:S(2)}, u32[]{:S(2)}) %collective-permute-start.3) | collective-permute-done | bytes 524320 | tf_op jit(solution)/shard_map/ppermute | solution.py:281
  52.5 1.9 %collective-permute-start.13 = (bf16[2,4,128,256]{3,2,1,0:T(8,128)(2,1)S(1)}, bf16[2,4,128,256]{3,2,1,0:T(8,128)(2,1)S(1)}, u32[]{:S(2)}, u32[]{:S(2)}) collective-permute-start(bf16[2,4,128,256]{3,2,1,0:T(8,128)(2,1)S(1)} %collective-permute-done.1.refs_2_), channel_id=1, source_target_pairs={{8,0},{16,8},{24,16},{28,24},{20,28},{12,20},{4,12},{0,4},{9,1},{1... | collective-permute-start | bytes 1572872 | tf_op jit(solution)/shard_map/ppermute | solution.py:278
  54.4 1.6 %gather.5 = (f32[2,4,256,256]{3,2,1,0:T(8,128)S(1)}, f32[2,4,256,256]{3,2,1,0:T(8,128)S(1)}, bf16[2,4,1024,256]{3,2,1,0:T(8,128)(2,1)S(1)}) custom-call(s32[10]{0:T(128)S(1)} %pad_add_fusion.info, bf16[4,256,1024]{2,1,0:T(8,128)(2,1)S(1)} %get-tuple-element.44.panel_vt, ...), custom_call_target="tpu_custom_call", output_to_operand_aliasing={{0}: (7, {}), {1}: (8, {}), {2}: (9, {})} | custom-call | flops 536870912 | bytes 21495808 | tf_op jit(solution)/shard_map/gather/pallas_call | solution.py:247
  56.1 5.6 %collective-permute-done.8.refs_0_ = bf16[2,4,128,256]{3,2,1,0:T(8,128)(2,1)S(1)} collective-permute-done((bf16[2,4,128,256]{3,2,1,0:T(8,128)(2,1)S(1)}, bf16[2,4,128,256]{3,2,1,0:T(8,128)(2,1)S(1)}, u32[]{:S(2)}, u32[]{:S(2)}) %collective-permute-start.8) | collective-permute-done | bytes 524320 | tf_op jit(solution)/shard_map/ppermute | solution.py:278
  61.6 2.0 %collective-permute-done.9.refs_1_ = bf16[2,4,128,256]{3,2,1,0:T(8,128)(2,1)S(1)} collective-permute-done((bf16[2,4,128,256]{3,2,1,0:T(8,128)(2,1)S(1)}, bf16[2,4,128,256]{3,2,1,0:T(8,128)(2,1)S(1)}, u32[]{:S(2)}, u32[]{:S(2)}) %collective-permute-start.9) | collective-permute-done | bytes 524320 | tf_op jit(solution)/shard_map/ppermute | solution.py:281
  63.6 1.6 %collective-permute-start.10 = (bf16[2,4,128,256]{3,2,1,0:T(8,128)(2,1)S(1)}, bf16[2,4,128,256]{3,2,1,0:T(8,128)(2,1)S(1)}, u32[]{:S(2)}, u32[]{:S(2)}) collective-permute-start(bf16[2,4,128,256]{3,2,1,0:T(8,128)(2,1)S(1)} %collective-permute-done.8.refs_0_), channel_id=1, source_target_pairs={{8,0},{16,8},{24,16},{28,24},{20,28},{12,20},{4,12},{0,4},{9,1},{1... | collective-permute-start | bytes 1572872 | tf_op jit(solution)/shard_map/ppermute | solution.py:278
  65.2 8.2 %collective-permute-done.11.refs_3_ = bf16[2,4,128,256]{3,2,1,0:T(8,128)(2,1)S(1)} collective-permute-done((bf16[2,4,128,256]{3,2,1,0:T(8,128)(2,1)S(1)}, bf16[2,4,128,256]{3,2,1,0:T(8,128)(2,1)S(1)}, u32[]{:S(2)}, u32[]{:S(2)}) %collective-permute-start.11) | collective-permute-done | bytes 524320 | tf_op jit(solution)/shard_map/ppermute | solution.py:281
  73.8 1.6 %gather.6 = (f32[2,4,256,256]{3,2,1,0:T(8,128)S(1)}, f32[2,4,256,256]{3,2,1,0:T(8,128)S(1)}, bf16[2,4,1024,256]{3,2,1,0:T(8,128)(2,1)S(1)}) custom-call(s32[10]{0:T(128)S(1)} %pad_add_fusion.info, bf16[4,256,1024]{2,1,0:T(8,128)(2,1)S(1)} %get-tuple-element.44.panel_vt, ...), custom_call_target="tpu_custom_call", output_to_operand_aliasing={{0}: (7, {}), {1}: (8, {}), {2}: (9, {})} | custom-call | flops 536870912 | bytes 21495808 | tf_op jit(solution)/shard_map/gather/pallas_call | solution.py:247
  75.5 7.8 %collective-permute-done.10.refs_0_ = bf16[2,4,128,256]{3,2,1,0:T(8,128)(2,1)S(1)} collective-permute-done((bf16[2,4,128,256]{3,2,1,0:T(8,128)(2,1)S(1)}, bf16[2,4,128,256]{3,2,1,0:T(8,128)(2,1)S(1)}, u32[]{:S(2)}, u32[]{:S(2)}) %collective-permute-start.10) | collective-permute-done | bytes 524320 | tf_op jit(solution)/shard_map/ppermute | solution.py:278
  83.3 2.6 %collective-permute-done.12.refs_1_ = bf16[2,4,128,256]{3,2,1,0:T(8,128)(2,1)S(1)} collective-permute-done((bf16[2,4,128,256]{3,2,1,0:T(8,128)(2,1)S(1)}, bf16[2,4,128,256]{3,2,1,0:T(8,128)(2,1)S(1)}, u32[]{:S(2)}, u32[]{:S(2)}) %collective-permute-start.12) | collective-permute-done | bytes 524320 | tf_op jit(solution)/shard_map/ppermute | solution.py:281
  85.9 1.5 %gather.7 = (f32[2,4,256,256]{3,2,1,0:T(8,128)S(1)}, f32[2,4,256,256]{3,2,1,0:T(8,128)S(1)}, bf16[2,4,1024,256]{3,2,1,0:T(8,128)(2,1)S(1)}) custom-call(s32[10]{0:T(128)S(1)} %pad_add_fusion.info, bf16[4,256,1024]{2,1,0:T(8,128)(2,1)S(1)} %get-tuple-element.44.panel_vt, ...), custom_call_target="tpu_custom_call", output_to_operand_aliasing={{0}: (5, {}), {1}: (6, {}), {2}: (7, {})} | custom-call | flops 268435456 | bytes 20447232 | tf_op jit(solution)/shard_map/gather/pallas_call | solution.py:247
  87.5 1.5 %update.3 = (bf16[4,256,256]{2,1,0:T(8,128)(2,1)S(1)}, bf16[256,1024]{1,0:T(8,128)(2,1)S(1)}) custom-call(s32[10]{0:T(128)S(1)} %pad_add_fusion.info, s32[1,4]{1,0:T(1,128)S(1)} %copy-done.6, s32[2,4]{1,0:T(2,128)S(1)} %copy-done.5, f32[2,4,256,256]{3,2,1,0:T(8,128)S(1)} %get-tuple-element.62.sampled, f32[2,4,256,256]{3,2,1,0:T(8,128)S(1)} %get-tuple-element.63.met, ...), custom_call_target="tpu_custom_call" | custom-call | flops 1342177280 | bytes 7340032 | tf_op jit(solution)/shard_map/update/pallas_call | solution.py:247
  89.0 1.5 %update.2 = (bf16[4,256,256]{2,1,0:T(8,128)(2,1)S(1)}, f32[256,1024]{1,0:T(8,128)S(1)}) custom-call(s32[10]{0:T(128)S(1)} %pad_add_fusion.info, s32[1,4]{1,0:T(1,128)S(1)} %copy-done.6, s32[2,4]{1,0:T(2,128)S(1)} %copy-done.5, f32[2,4,256,256]{3,2,1,0:T(8,128)S(1)} %get-tuple-element.62.sampled, f32[2,4,256,256]{3,2,1,0:T(8,128)S(1)} %get-tuple-element.63.met, ...), custom_call_target="tpu_custom_call" | custom-call | flops 1342177280 | bytes 7864320 | tf_op jit(solution)/shard_map/update/pallas_call | solution.py:247
  91.1 1.6 %collective-permute-start.15 = (bf16[256,1024]{1,0:T(8,128)(2,1)S(1)}, bf16[256,1024]{1,0:T(8,128)(2,1)S(1)}, u32[]{:S(2)}, u32[]{:S(2)}) collective-permute-start(bf16[256,1024]{1,0:T(8,128)(2,1)S(1)} %add_convert_fusion), channel_id=1, source_target_pairs={{0,2},{1,3},{2,0},{3,1},{4,6},{5,7},{6,4},{7,5},{8,10},{9,11},{10,... | collective-permute-start | bytes 1572872 | tf_op jit(solution)/shard_map/ppermute | solution.py:339
  92.7 12.4 %collective-permute-done.15.refs_2_ = bf16[256,1024]{1,0:T(8,128)(2,1)S(1)} collective-permute-done((bf16[256,1024]{1,0:T(8,128)(2,1)S(1)}, bf16[256,1024]{1,0:T(8,128)(2,1)S(1)}, u32[]{:S(2)}, u32[]{:S(2)}) %collective-permute-start.15) | collective-permute-done | bytes 524320 | tf_op jit(solution)/shard_map/ppermute | solution.py:339
  105.1 15.0 %orthonormal.1 = (bf16[256,1024]{1,0:T(8,128)(2,1)S(1)}, f32[256,256]{1,0:T(8,128)S(1)}, f32[256,256]{1,0:T(8,128)S(1)}) custom-call(s32[10]{0:T(128)S(1)} %pad_add_fusion.info, f32[256,1024]{1,0:T(8,128)S(1)} %start.1, f32[256,1024]{1,0:T(8,128)S(1)} %get-tuple-element.64.refs_0_, bf16[256,1024]{1,0:T(8,128)(2,1)S(1)} %collective-permute-done.14.refs_1_, ...), custom_call_target="tpu_custom_call" | custom-call | flops 17179869184 | bytes 4194304 | tf_op jit(solution)/shard_map/orthonormal/pallas_call | solution.py:247
  120.7 4.2 %project.2 = (bf16[2,256,256]{2,1,0:T(8,128)(2,1)S(1)}, f32[2,256,256]{2,1,0:T(8,128)S(1)}, f32[256,256]{1,0:T(8,128)S(1)}) custom-call(s32[10]{0:T(128)S(1)} %pad_add_fusion.info, bf16[256,1024]{1,0:T(8,128)(2,1)S(1)} %get-tuple-element.68.qt, bf16[4,1024,256]{2,1,0:T(8,128)(2,1)S(1)} %bitcast.32, bf16[4,256,256]{2,1,0:T(8,128)(2,1)S(1)} %get-tuple-element.69.cross, ...), custom_call_target="tpu_custom_call" | custom-call | flops 3623878656 | bytes 8388608 | tf_op jit(solution)/shard_map/project/pallas_call | solution.py:247
  124.8 3.9 %project.3 = (bf16[2,256,256]{2,1,0:T(8,128)(2,1)S(1)}, f32[2,256,256]{2,1,0:T(8,128)S(1)}, f32[256,256]{1,0:T(8,128)S(1)}) custom-call(s32[10]{0:T(128)S(1)} %pad_add_fusion.info, bf16[256,1024]{1,0:T(8,128)(2,1)S(1)} %collective-permute-done.17.qt, bf16[4,1024,256]{2,1,0:T(8,128)(2,1)S(1)} %bitcast.33, bf16[4,256,256]{2,1,0:T(8,128)(2,1)S(1)} %get-tuple-element.77.cross, ...), custom_call_target="tpu_custom_call" | custom-call | flops 3623878656 | bytes 8388608 | tf_op jit(solution)/shard_map/project/pallas_call | solution.py:247
  130.5 1.6 %collective-permute-start.19 = (bf16[256,256]{1,0:T(8,128)(2,1)S(1)}, bf16[256,256]{1,0:T(8,128)(2,1)S(1)}, u32[]{:S(2)}, u32[]{:S(2)}) collective-permute-start(bf16[256,256]{1,0:T(8,128)(2,1)S(1)} %fusion.4), channel_id=1, source_target_pairs={{0,2},{1,3},{2,0},{3,1},{4,6},{5,7},{6,4},{7,5},{8,10},{9,11},{10,... | collective-permute-start | bytes 393224 | tf_op jit(solution)/shard_map/ppermute | solution.py:339
  133.1 3.8 %collective-permute-done.19 = bf16[256,256]{1,0:T(8,128)(2,1)S(1)} collective-permute-done((bf16[256,256]{1,0:T(8,128)(2,1)S(1)}, bf16[256,256]{1,0:T(8,128)(2,1)S(1)}, u32[]{:S(2)}, u32[]{:S(2)}) %collective-permute-start.19) | collective-permute-done | bytes 131104 | tf_op jit(solution)/shard_map/ppermute | solution.py:339
  136.9 2.0 %collective-permute-done.21 = bf16[256,256]{1,0:T(8,128)(2,1)S(1)} collective-permute-done((bf16[256,256]{1,0:T(8,128)(2,1)S(1)}, bf16[256,256]{1,0:T(8,128)(2,1)S(1)}, u32[]{:S(2)}, u32[]{:S(2)}) %collective-permute-start.21) | collective-permute-done | bytes 131104 | tf_op jit(solution)/shard_map/ppermute | solution.py:339
  (52 shorter events, 11.4 us)
Async XLA Ops:
  0.6 16.1 %collective-permute-start.4 = (bf16[2,4,128,256]{3,2,1,0:T(8,128)(2,1)}, bf16[2,4,128,256]{3,2,1,0:T(8,128)(2,1)}, u32[]{:S(2)}, u32[]{:S(2)}) collective-permute-start(bf16[2,4,128,256]{3,2,1,0:T(8,128)(2,1)} %refs_0_.1), channel_id=1, source_target_pairs={{8,0},{16,8},{24,16},{28,24},{20,28},{12,20},{4,12},{0,4},{9,1},{1... | collective-permute-start | bytes 1572872 | tf_op jit(solution)/shard_map/ppermute | solution.py:278
  3.6 15.2 %collective-permute-start.5 = (bf16[2,4,128,256]{3,2,1,0:T(8,128)(2,1)}, bf16[2,4,128,256]{3,2,1,0:T(8,128)(2,1)}, u32[]{:S(2)}, u32[]{:S(2)}) collective-permute-start(bf16[2,4,128,256]{3,2,1,0:T(8,128)(2,1)} %refs_0_.1), channel_id=1, source_target_pairs={{0,8},{8,16},{16,24},{24,28},{28,20},{20,12},{12,4},{4,0},{1,9},{9... | collective-permute-start | bytes 1572872 | tf_op jit(solution)/shard_map/ppermute | solution.py:281
  3.8 24.1 %collective-permute-start = (bf16[2,4,128,256]{3,2,1,0:T(8,128)(2,1)}, bf16[2,4,128,256]{3,2,1,0:T(8,128)(2,1)S(1)}, u32[]{:S(2)}, u32[]{:S(2)}) collective-permute-start(bf16[2,4,128,256]{3,2,1,0:T(8,128)(2,1)} %refs_3_.1), channel_id=1, source_target_pairs={{8,0},{16,8},{24,16},{28,24},{20,28},{12,20},{4,12},{0,4},{9,1},{1... | collective-permute-start | bytes 1572872 | tf_op jit(solution)/shard_map/ppermute | solution.py:278
  5.6 24.3 %collective-permute-start.2 = (bf16[2,4,128,256]{3,2,1,0:T(8,128)(2,1)}, bf16[2,4,128,256]{3,2,1,0:T(8,128)(2,1)S(1)}, u32[]{:S(2)}, u32[]{:S(2)}) collective-permute-start(bf16[2,4,128,256]{3,2,1,0:T(8,128)(2,1)} %refs_3_.1), channel_id=1, source_target_pairs={{0,8},{8,16},{16,24},{24,28},{28,20},{20,12},{12,4},{4,0},{1,9},{9... | collective-permute-start | bytes 1572872 | tf_op jit(solution)/shard_map/ppermute | solution.py:281
  16.8 22.4 %collective-permute-start.6 = (bf16[2,4,128,256]{3,2,1,0:T(8,128)(2,1)}, bf16[2,4,128,256]{3,2,1,0:T(8,128)(2,1)S(1)}, u32[]{:S(2)}, u32[]{:S(2)}) collective-permute-start(bf16[2,4,128,256]{3,2,1,0:T(8,128)(2,1)} %collective-permute-done.4.refs_1_), channel_id=1, source_target_pairs={{8,0},{16,8},{24,16},{28,24},{20,28},{12,20},{4,12},{0,4},{9,1},{1... | collective-permute-start | bytes 1572872 | tf_op jit(solution)/shard_map/ppermute | solution.py:278
  18.8 22.4 %collective-permute-start.7 = (bf16[2,4,128,256]{3,2,1,0:T(8,128)(2,1)}, bf16[2,4,128,256]{3,2,1,0:T(8,128)(2,1)S(1)}, u32[]{:S(2)}, u32[]{:S(2)}) collective-permute-start(bf16[2,4,128,256]{3,2,1,0:T(8,128)(2,1)} %collective-permute-done.5.refs_2_), channel_id=1, source_target_pairs={{0,8},{8,16},{16,24},{24,28},{28,20},{20,12},{12,4},{4,0},{1,9},{9... | collective-permute-start | bytes 1572872 | tf_op jit(solution)/shard_map/ppermute | solution.py:281
  27.9 22.5 %collective-permute-start.1 = (bf16[2,4,128,256]{3,2,1,0:T(8,128)(2,1)S(1)}, bf16[2,4,128,256]{3,2,1,0:T(8,128)(2,1)S(1)}, u32[]{:S(2)}, u32[]{:S(2)}) collective-permute-start(bf16[2,4,128,256]{3,2,1,0:T(8,128)(2,1)S(1)} %collective-permute-done.refs_4_), channel_id=1, source_target_pairs={{8,0},{16,8},{24,16},{28,24},{20,28},{12,20},{4,12},{0,4},{9,1},{1... | collective-permute-start | bytes 1572872 | tf_op jit(solution)/shard_map/ppermute | solution.py:278
  29.9 22.5 %collective-permute-start.3 = (bf16[2,4,128,256]{3,2,1,0:T(8,128)(2,1)S(1)}, bf16[2,4,128,256]{3,2,1,0:T(8,128)(2,1)S(1)}, u32[]{:S(2)}, u32[]{:S(2)}) collective-permute-start(bf16[2,4,128,256]{3,2,1,0:T(8,128)(2,1)S(1)} %collective-permute-done.2.refs_5_), channel_id=1, source_target_pairs={{0,8},{8,16},{16,24},{24,28},{28,20},{20,12},{12,4},{4,0},{1,9},{9... | collective-permute-start | bytes 1572872 | tf_op jit(solution)/shard_map/ppermute | solution.py:281
  30.8 1.6 %copy-start.7 = (bf16[1,4,1024,256]{3,2,1,0:T(8,128)(2,1)S(1)}, bf16[1,4,1024,256]{3,2,1,0:T(8,128)(2,1)}, u32[]{:S(2)}) copy-start(bf16[1,4,1024,256]{3,2,1,0:T(8,128)(2,1)} %param.11) | copy-start | bytes 6291460
  32.4 1.0 copy-start.8
  33.4 1.2 copy-start.1
  33.4 1.5 %copy-start.2 = (bf16[2,1,1024,256]{3,2,1,0:T(8,128)(2,1)S(1)}, bf16[2,1,1024,256]{3,2,1,0:T(8,128)(2,1)}, u32[]{:S(2)}) copy-start(bf16[2,1,1024,256]{3,2,1,0:T(8,128)(2,1)} %param.17) | copy-start | bytes 3145732
  34.2 2.0 %copy-start.3 = (bf16[2,4,128,256]{3,2,1,0:T(8,128)(2,1)S(1)}, bf16[2,4,128,256]{3,2,1,0:T(8,128)(2,1)}, u32[]{:S(2)}) copy-start(bf16[2,4,128,256]{3,2,1,0:T(8,128)(2,1)} %refs_0_.1) | copy-start | bytes 1572868
  34.2 2.0 %copy-start.4 = (bf16[2,4,128,256]{3,2,1,0:T(8,128)(2,1)S(1)}, bf16[2,4,128,256]{3,2,1,0:T(8,128)(2,1)}, u32[]{:S(2)}) copy-start(bf16[2,4,128,256]{3,2,1,0:T(8,128)(2,1)} %refs_3_.1) | copy-start | bytes 1572868
  41.1 20.5 %collective-permute-start.8 = (bf16[2,4,128,256]{3,2,1,0:T(8,128)(2,1)S(1)}, bf16[2,4,128,256]{3,2,1,0:T(8,128)(2,1)S(1)}, u32[]{:S(2)}, u32[]{:S(2)}) collective-permute-start(bf16[2,4,128,256]{3,2,1,0:T(8,128)(2,1)S(1)} %collective-permute-done.6.refs_0_), channel_id=1, source_target_pairs={{8,0},{16,8},{24,16},{28,24},{20,28},{12,20},{4,12},{0,4},{9,1},{1... | collective-permute-start | bytes 1572872 | tf_op jit(solution)/shard_map/ppermute | solution.py:278
  42.7 20.9 %collective-permute-start.9 = (bf16[2,4,128,256]{3,2,1,0:T(8,128)(2,1)S(1)}, bf16[2,4,128,256]{3,2,1,0:T(8,128)(2,1)S(1)}, u32[]{:S(2)}, u32[]{:S(2)}) collective-permute-start(bf16[2,4,128,256]{3,2,1,0:T(8,128)(2,1)S(1)} %collective-permute-done.7.refs_1_), channel_id=1, source_target_pairs={{0,8},{8,16},{16,24},{24,28},{28,20},{20,12},{12,4},{4,0},{1,9},{9... | collective-permute-start | bytes 1572872 | tf_op jit(solution)/shard_map/ppermute | solution.py:281
  52.4 21.0 %collective-permute-start.11 = (bf16[2,4,128,256]{3,2,1,0:T(8,128)(2,1)S(1)}, bf16[2,4,128,256]{3,2,1,0:T(8,128)(2,1)S(1)}, u32[]{:S(2)}, u32[]{:S(2)}) collective-permute-start(bf16[2,4,128,256]{3,2,1,0:T(8,128)(2,1)S(1)} %collective-permute-done.3.refs_3_), channel_id=1, source_target_pairs={{0,8},{8,16},{16,24},{24,28},{28,20},{20,12},{12,4},{4,0},{1,9},{9... | collective-permute-start | bytes 1572872 | tf_op jit(solution)/shard_map/ppermute | solution.py:281
  52.5 21.3 %collective-permute-start.13 = (bf16[2,4,128,256]{3,2,1,0:T(8,128)(2,1)S(1)}, bf16[2,4,128,256]{3,2,1,0:T(8,128)(2,1)S(1)}, u32[]{:S(2)}, u32[]{:S(2)}) collective-permute-start(bf16[2,4,128,256]{3,2,1,0:T(8,128)(2,1)S(1)} %collective-permute-done.1.refs_2_), channel_id=1, source_target_pairs={{8,0},{16,8},{24,16},{28,24},{20,28},{12,20},{4,12},{0,4},{9,1},{1... | collective-permute-start | bytes 1572872 | tf_op jit(solution)/shard_map/ppermute | solution.py:278
  63.6 19.6 %collective-permute-start.10 = (bf16[2,4,128,256]{3,2,1,0:T(8,128)(2,1)S(1)}, bf16[2,4,128,256]{3,2,1,0:T(8,128)(2,1)S(1)}, u32[]{:S(2)}, u32[]{:S(2)}) collective-permute-start(bf16[2,4,128,256]{3,2,1,0:T(8,128)(2,1)S(1)} %collective-permute-done.8.refs_0_), channel_id=1, source_target_pairs={{8,0},{16,8},{24,16},{28,24},{20,28},{12,20},{4,12},{0,4},{9,1},{1... | collective-permute-start | bytes 1572872 | tf_op jit(solution)/shard_map/ppermute | solution.py:278
  73.4 12.5 %collective-permute-start.12 = (bf16[2,4,128,256]{3,2,1,0:T(8,128)(2,1)S(1)}, bf16[2,4,128,256]{3,2,1,0:T(8,128)(2,1)S(1)}, u32[]{:S(2)}, u32[]{:S(2)}) collective-permute-start(bf16[2,4,128,256]{3,2,1,0:T(8,128)(2,1)S(1)} %collective-permute-done.11.refs_3_), channel_id=1, source_target_pairs={{0,8},{8,16},{16,24},{24,28},{28,20},{20,12},{12,4},{4,0},{1,9},{9... | collective-permute-start | bytes 1572872 | tf_op jit(solution)/shard_map/ppermute | solution.py:281
  85.9 1.6 %copy-start = (bf16[1,4,1024,256]{3,2,1,0:T(8,128)(2,1)S(1)}, bf16[1,4,1024,256]{3,2,1,0:T(8,128)(2,1)}, u32[]{:S(2)}) copy-start(bf16[1,4,1024,256]{3,2,1,0:T(8,128)(2,1)} %param.10) | copy-start | bytes 6291460
  85.9 1.6 %copy-start.5 = (s32[2,4]{1,0:T(2,128)S(1)}, s32[2,4]{1,0:T(2,128)}, u32[]{:S(2)}) copy-start(s32[2,4]{1,0:T(2,128)} %pivot_rank.3) | copy-start | bytes 100
  85.9 1.6 %copy-start.6 = (s32[1,4]{1,0:T(1,128)S(1)}, s32[1,4]{1,0:T(1,128)}, u32[]{:S(2)}) copy-start(s32[1,4]{1,0:T(1,128)} %panel_rank.3) | copy-start | bytes 52
  88.9 2.0 %collective-permute-start.14 = (bf16[256,1024]{1,0:T(8,128)(2,1)S(1)}, bf16[256,1024]{1,0:T(8,128)(2,1)S(1)}, u32[]{:S(2)}, u32[]{:S(2)}) collective-permute-start(bf16[256,1024]{1,0:T(8,128)(2,1)S(1)} %get-tuple-element.65), channel_id=1, source_target_pairs={{0,1},{1,0},{2,3},{3,2},{4,5},{5,4},{6,7},{7,6},{8,9},{9,8},{10,11... | collective-permute-start | bytes 1572872 | tf_op jit(solution)/shard_map/ppermute | solution.py:396
  91.1 14.0 %collective-permute-start.15 = (bf16[256,1024]{1,0:T(8,128)(2,1)S(1)}, bf16[256,1024]{1,0:T(8,128)(2,1)S(1)}, u32[]{:S(2)}, u32[]{:S(2)}) collective-permute-start(bf16[256,1024]{1,0:T(8,128)(2,1)S(1)} %add_convert_fusion), channel_id=1, source_target_pairs={{0,2},{1,3},{2,0},{3,1},{4,6},{5,7},{6,4},{7,5},{8,10},{9,11},{10,... | collective-permute-start | bytes 1572872 | tf_op jit(solution)/shard_map/ppermute | solution.py:339
  120.1 4.7 %collective-permute-start.17 = (bf16[256,1024]{1,0:T(8,128)(2,1)S(1)}, bf16[256,1024]{1,0:T(8,128)(2,1)S(1)}, u32[]{:S(2)}, u32[]{:S(2)}) collective-permute-start(bf16[256,1024]{1,0:T(8,128)(2,1)S(1)} %get-tuple-element.68.qt), channel_id=1, source_target_pairs={{0,1},{1,0},{2,3},{3,2},{4,5},{5,4},{6,7},{7,6},{8,9},{9,8},{10,11... | collective-permute-start | bytes 1572872 | tf_op jit(solution)/shard_map/ppermute | solution.py:405
  120.2 8.8 %collective-permute-start.16 = (f32[256,256]{1,0:T(8,128)S(1)}, f32[256,256]{1,0:T(8,128)S(1)}, u32[]{:S(2)}, u32[]{:S(2)}) collective-permute-start(f32[256,256]{1,0:T(8,128)S(1)} %get-tuple-element.67), channel_id=1, source_target_pairs={{0,1},{1,0},{2,3},{3,2},{4,5},{5,4},{6,7},{7,6},{8,9},{9,8},{10,11... | collective-permute-start | bytes 786440 | tf_op jit(solution)/shard_map/ppermute | solution.py:406
  128.8 1.6 %collective-permute-start.18 = (bf16[2,256,256]{2,1,0:T(8,128)(2,1)S(1)}, bf16[2,256,256]{2,1,0:T(8,128)(2,1)S(1)}, u32[]{:S(2)}, u32[]{:S(2)}) collective-permute-start(bf16[2,256,256]{2,1,0:T(8,128)(2,1)S(1)} %get-tuple-element.78), channel_id=1, source_target_pairs={{0,1},{1,0},{2,3},{3,2},{4,5},{5,4},{6,7},{7,6},{8,9},{9,8},{10,11... | collective-permute-start | bytes 786440 | tf_op jit(solution)/shard_map/ppermute | solution.py:412
  129.8 2.3 %collective-permute-start.20 = (bf16[2,256,256]{2,1,0:T(8,128)(2,1)S(1)}, bf16[2,256,256]{2,1,0:T(8,128)(2,1)S(1)}, u32[]{:S(2)}, u32[]{:S(2)}) collective-permute-start(bf16[2,256,256]{2,1,0:T(8,128)(2,1)S(1)} %get-tuple-element.81), channel_id=1, source_target_pairs={{0,1},{1,0},{2,3},{3,2},{4,5},{5,4},{6,7},{7,6},{8,9},{9,8},{10,11... | collective-permute-start | bytes 786440 | tf_op jit(solution)/shard_map/ppermute | solution.py:412
  130.5 6.4 %collective-permute-start.19 = (bf16[256,256]{1,0:T(8,128)(2,1)S(1)}, bf16[256,256]{1,0:T(8,128)(2,1)S(1)}, u32[]{:S(2)}, u32[]{:S(2)}) collective-permute-start(bf16[256,256]{1,0:T(8,128)(2,1)S(1)} %fusion.4), channel_id=1, source_target_pairs={{0,2},{1,3},{2,0},{3,1},{4,6},{5,7},{6,4},{7,5},{8,10},{9,11},{10,... | collective-permute-start | bytes 393224 | tf_op jit(solution)/shard_map/ppermute | solution.py:339
  132.2 6.7 %collective-permute-start.21 = (bf16[256,256]{1,0:T(8,128)(2,1)S(1)}, bf16[256,256]{1,0:T(8,128)(2,1)S(1)}, u32[]{:S(2)}, u32[]{:S(2)}) collective-permute-start(bf16[256,256]{1,0:T(8,128)(2,1)S(1)} %fusion.5), channel_id=1, source_target_pairs={{0,2},{1,3},{2,0},{3,1},{4,6},{5,7},{6,4},{7,5},{8,10},{9,11},{10,... | collective-permute-start | bytes 393224 | tf_op jit(solution)/shard_map/ppermute | solution.py:339
where the time goes:
time: 140 us
  waiting for transfers between devices  76.6 us (55%)
  Pallas kernels  35.3 us (25%)
  starting transfers between devices  20.7 us (15%)
  local copies, waits for them, and re-layouts  4.18 us (3%)
  other arithmetic  2.08 us (1%)
    ppermute x7, waiting for transfers between devices, step(): self.up[t] = lax.ppermute(self.up[t], self.axis, self.ahead)  40.9 us
    pallas_call x11, Pallas kernels, run(): pl.pallas_call(kernel, out_shape=shapes, in_specs=[smem] * len(scalars) +...  35.3 us
    ppermute x3, waiting for transfers between devices, shifted(): lax.ppermute(x, 'cols', [(i, (i + 2 * shift) % cols) for i in range(cols)])  18.2 us
    ppermute x7, waiting for transfers between devices, step(): self.down[t] = lax.ppermute(self.down[t], self.axis, self.behind)  16.9 us
    ppermute x7, starting transfers between devices, step(): self.up[t] = lax.ppermute(self.up[t], self.axis, self.ahead)  13.9 us
    ppermute x3, starting transfers between devices, shifted(): lax.ppermute(x, 'cols', [(i, (i + 2 * shift) % cols) for i in range(cols)])  4.07 us
    unnamed x18, local copies, waits for them, and re-layouts  3.44 us
  transfers between devices with their start and end apart: 22, of which 16 were waited for; matrix products, arithmetic and copies ran while one was open for 1% of the time, Pallas kernels for 12%

commit v1 on v0

--- a/solution.py
+++ b/solution.py
@@ -12,7 +12,6 @@
 F32 = jnp.float32
 BF16 = jnp.bfloat16
 BLOCK = 32
-GROUP = 4
 SUB = 8
 RING_MOST = 16
 MIB = 1 << 20
@@ -36,12 +35,6 @@
     mid = rest.astype(BF16)
     low = (rest - mid.astype(F32)).astype(BF16)
     return high, mid, low
-
-
-def reciprocal(x):
-    guess = pl.reciprocal(x, approx=True)
-    guess = guess * (2.0 - x * guess)
-    return guess * (2.0 - x * guess)
 
 
 def eliminate(panel, first):
@@ -56,56 +49,54 @@
         [panel[v * SUB : (v + 1) * SUB, h * lanes : (h + 1) * lanes] for h in range(halves)]
         for v in range(high)
     ]
-    mine = first // lanes
-    pivots = [jnp.ones(tile, F32) for _ in range(high)]
-    for k in range(0, rows, GROUP):
-        at = first % lanes + k
-        top, low = k // SUB, k % SUB
-        inside = (lane >= at) & (lane < at + GROUP)
+    mine, start = first // lanes, first % lanes
+    scales = []
+    for top in range(high):
+        at = start + top * SUB
+        inside = (lane >= at) & (lane < at + SUB)
         column = [
             [jnp.broadcast_to(part[v][mine][:, at + m : at + m + 1], tile) for v in range(top, high)]
-            for m in range(GROUP)
+            for m in range(SUB)
         ]
         small = [
-            [jnp.broadcast_to(column[b][0][low + a : low + a + 1, :], tile) for b in range(a + 1)]
-            for a in range(GROUP)
+            [jnp.broadcast_to(column[b][0][a : a + 1, :], tile) for b in range(a + 1)] for a in range(SUB)
         ]
         row = []
-        for a in range(GROUP):
-            row.append([jnp.broadcast_to(part[top][h][low + a : low + a + 1, :], tile) for h in range(halves)])
+        for a in range(SUB):
+            row.append([jnp.broadcast_to(part[top][h][a : a + 1, :], tile) for h in range(halves)])
             row[a][mine] = jnp.where(inside, jnp.where(lane == at + a, 1.0, 0.0), row[a][mine])
+        pivots = small[0][0]
         factor = []
-        for m in range(GROUP):
-            inverse = reciprocal(small[m][m])
-            pivots[top] = jnp.where(sub == low + m, small[m][m], pivots[top])
-            for a in range(m + 1, GROUP):
+        for m in range(SUB):
+            inverse = pl.reciprocal(small[m][m], approx=True)
+            if m:
+                pivots = jnp.where(sub == m, small[m][m], pivots)
+            for a in range(m + 1, SUB):
                 ratio = small[a][m] * inverse
                 for b in range(m + 1, a + 1):
                     small[a][b] = small[a][b] - ratio * small[b][m]
                 row[a] = [x - ratio * y for x, y in zip(row[a], row[m])]
-            factor.append([c * inverse for c in column[m]])
-            for b in range(m + 1, GROUP):
-                column[b] = [c - f * small[b][m] for c, f in zip(column[b], factor[m])]
-        for v in range(top, high):
+            factor.append([c * inverse for c in column[m][1:]])
+            for b in range(m + 1, SUB):
+                column[b][1:] = [c - f * small[b][m] for c, f in zip(column[b][1:], factor[m])]
+        for v in range(top + 1, high):
             for h in range(halves):
-                old = part[v][h]
-                value = jnp.where(inside, 0.0, old) if h == mine else old
-                for m in range(GROUP):
-                    value = value - factor[m][v - top] * row[m][h]
-                if v == top:
-                    if low > 0:
-                        value = jnp.where(sub < low, old, value)
-                    for m in range(GROUP):
-                        value = jnp.where(sub == low + m, row[m][h], value)
+                value = jnp.where(inside, 0.0, part[v][h]) if h == mine else part[v][h]
+                for m in range(SUB):
+                    value = value - factor[m][v - top - 1] * row[m][h]
                 part[v][h] = value
+        for h in range(halves):
+            value = row[0][h]
+            for m in range(1, SUB):
+                value = jnp.where(sub == m, row[m][h], value)
+            part[top][h] = value
+        scales.append(lax.rsqrt(pivots))
     done = []
     for v in range(high):
-        scale = lax.rsqrt(pivots[v])
         cells = []
         for h in range(halves):
-            value = part[v][h] * scale
+            value = part[v][h] * scales[v]
             if h == mine:
-                start = first % lanes
                 value = jnp.where((lane > start + v * SUB + sub) & (lane < start + rows), 0.0, value)
             cells.append(value)
         done.append(jnp.concatenate(cells, 1))
@@ -177,16 +168,23 @@
                 u_all[c, j, p * slab : (p + 1) * slab, :] = u_new[n * slab : (n + 1) * slab, :]
 
 
-def update_kernel(own_column, info, panel_rank, pivot_rank, sampled, met, panel_u, cross, out):
+def update_kernel(own_column, places, blocks, info, panel_rank, pivot_rank, sampled, met, panel_u, panel_vt, sampler_t, *refs):
+    cross, out = refs[-2:]
     priors, width, _ = cross.shape
+    slab = panel_vt.shape[2] // blocks
     column = info[0] if own_column else 1 - info[0]
     row = lax.broadcasted_iota(jnp.int32, (width, width), 0)
     col = lax.broadcasted_iota(jnp.int32, (width, width), 1)
     terms = []
     for j in range(priors):
+        one, two = sampled[column, j], met[column, j]
+        for n, place in enumerate(places):
+            span = pl.ds(pl.multiple_of(info[2 + place] * slab, 128), slab)
+            one += dot(sampler_t[:, span], refs[n][column, j])
+            two += dot(panel_vt[j, :, span], refs[len(places) + n][column, j])
         inside = (row < panel_rank[0, j]) & (col < pivot_rank[column, j])
-        cross[j] = jnp.where(inside, met[column, j], 0.0).astype(BF16)
-        terms.append(dot11(sampled[column, j].astype(BF16), cross[j]).astype(BF16))
+        cross[j] = jnp.where(inside, two, 0.0).astype(BF16)
+        terms.append(dot11(one.astype(BF16), cross[j]).astype(BF16))
     half = out.shape[1] // 2
     for at in (0, half):
         total = jnp.zeros((width, half), F32)
@@ -195,26 +193,28 @@
         out[:, at : at + half] = total.astype(out.dtype)
 
 
-def project_kernel(blocks, own_column, info, qt, panel_u, cross, u_all, orig_u, orig_v, give, keep, own, work, u_buf, v_buf, sems):
+def project_kernel(places, blocks, own_column, info, qt, panel_u, cross, u_all, *refs):
+    give, keep, work = refs[-3:]
     _, priors, order, width = u_all.shape
     slab = order // blocks
     pairs, share, _ = keep.shape
     core = info[0]
     column = core if own_column else 1 - core
-    rows = pl.ds(pl.multiple_of(info[1] * share, 16), share)
-    fetch_u = pltpu.make_async_copy(orig_u.at[column], u_buf, sems.at[0])
-    fetch_v = pltpu.make_async_copy(orig_v.at[column, rows], v_buf, sems.at[1])
-    fetch_u.start()
-    fetch_v.start()
     mids = []
     for j in range(priors):
         inner = dot(qt[...], panel_u[j]).astype(BF16)
         mids.append(dot(inner, cross[j]).astype(BF16))
+
+    def rows_of(j, b):
+        if b in places:
+            return refs[places.index(b)][column, j]
+        return u_all[column, j, b * slab : (b + 1) * slab, :]
+
     some = max(1, blocks // 2)
     for begin in range(0, blocks, some):
         total = jnp.zeros((some * slab, width), F32)
         for j in range(priors):
-            total += dot11(u_all[column, j, begin * slab : (begin + some) * slab, :], mids[j])
+            total += dot11(jnp.concatenate([rows_of(j, begin + n) for n in range(some)], 0), mids[j])
         for n in range(some):
             place = pl.ds(pl.multiple_of(info[2 + begin + n] * slab, SUB), slab)
             work[place, :] = total[n * slab : (n + 1) * slab, :]
@@ -222,9 +222,43 @@
         for out, which in ((give, 1 - core), (keep, core)):
             place = pl.ds(pl.multiple_of((2 * a + which) * share, SUB), share)
             out[a] = work[place, :].astype(out.dtype)
-    fetch_u.wait()
-    fetch_v.wait()
-    own[...] = dot11(v_buf[...], dot(qt[...], u_buf[...]).astype(BF16))
+
+
+def own_kernel(info, qt, qt_other, orig_u, orig_v, out, u_buf, v_buf, sems):
+    share = out.shape[1]
+    rows = pl.ds(pl.multiple_of(info[1] * share, 16), share)
+    copies = []
+    for n, column in enumerate((1 - info[0], info[0])):
+        copies.append(pltpu.make_async_copy(orig_u.at[column], u_buf.at[n], sems.at[2 * n]))
+        copies.append(pltpu.make_async_copy(orig_v.at[column, rows], v_buf.at[n], sems.at[2 * n + 1]))
+    for copy in copies:
+        copy.start()
+    for n, q in enumerate((qt_other, qt)):
+        copies[2 * n].wait()
+        copies[2 * n + 1].wait()
+        out[n] = dot11(v_buf[n], dot(q[...], u_buf[n]).astype(BF16))
+
+
+def halve_kernel(info, keep_b, keep_a, give_a, give_b, kept, *sent):
+    pair = info[1] // 2
+    pairs = keep_a.shape[0]
+    for n, (keep, recv) in enumerate(((keep_b, give_a), (keep_a, give_b))):
+        for shift in range(pairs):
+            a = lax.rem(pair + shift, pairs)
+            total = keep[a] + recv[a].astype(F32)
+            if shift:
+                sent[shift - 1][n] = total.astype(BF16)
+            else:
+                kept[n] = total
+
+
+def close_kernel(info, own, kept, *refs):
+    out = refs[-1]
+    for n, column in enumerate((1 - info[0], info[0])):
+        total = own[n] - kept[n]
+        for recv in refs[:-1]:
+            total = total - recv[n].astype(F32)
+        out[column] = total
 
 
 def turn_kernel(panel_v, sampler, panel_vt, sampler_t):
@@ -356,29 +390,27 @@
 
     def updated(own_column, sampled, met):
         return run(
-            functools.partial(update_kernel, own_column), [info, panel_rank, pivot_rank], [sampled, met, panel_u],
-            [((priors, width, width), BF16), ((width, order), F32 if own_column else BF16)], [], 16,
+            functools.partial(update_kernel, own_column, places, blocks), [info, panel_rank, pivot_rank],
+            [sampled, met, panel_u, panel_vt, sampler_t, *new_u, *new_v],
+            [((priors, width, width), BF16), ((width, order), F32 if own_column else BF16)], [], 20,
             2 * priors * square * (order + width), "update"
         )
 
-    def projected(own_column, blocks, qt, cross, u_all):
+    def projected(own_column, qt, cross):
         return run(
-            functools.partial(project_kernel, blocks, own_column), [info], [qt, panel_u, cross, u_all],
-            [((pairs, share, width), BF16), ((pairs, share, width), F32), ((share, width), F32)],
-            [
-                pltpu.VMEM((order, width), F32), pltpu.VMEM((order, width), BF16), pltpu.VMEM((share, width), BF16),
-                pltpu.SemaphoreType.DMA((2,))
-            ],
-            20, 3 * priors * square * (2 * order + width), "project", apart=[orig_u, orig_v]
+            functools.partial(project_kernel, places, blocks, own_column), [info], [qt, panel_u, cross, u_all, *new_u],
+            [((pairs, share, width), BF16), ((pairs, share, width), F32)], [pltpu.VMEM((order, width), F32)],
+            20, 3 * priors * square * (2 * order + width), "project"
         )
 
     def placed(mine, other):
         return jnp.where(core == 0, jnp.stack([mine, other]), jnp.stack([other, mine]))
 
     if whole:
-        blocks = 1
+        blocks, places = 1, []
         new_u, new_v = ([lax.all_gather(x, "rows", axis=2, tiled=True)] for x in (pivot_u, pivot_v))
         sampled, met, u_all = gathered([0], 1, new_u, new_v, [])
+        new_u, new_v = [], []
     else:
         blocks = count
         now, kept = Ring([pivot_u, pivot_v], ring, "rows"), []
@@ -390,7 +422,8 @@
                     start = now.tie(start, number, (1,))
             places = sorted({number, count - number} | ({0} if number == 1 else set()))
             new_u, new_v = ([now.found[t][p] for p in places] for t in range(2))
-            kept = list(gathered(places, count, new_u, new_v, kept))
+            if number < last:
+                kept = list(gathered(places, count, new_u, new_v, kept))
         sampled, met, u_all = kept
     cross_other, give = updated(False, sampled, met)
     recv = lax.ppermute(give, "cols", swap)
@@ -404,18 +437,23 @@
     )
     qt_other = lax.ppermute(qt, "cols", swap)
     rows_other = lax.ppermute(given, "cols", swap)
-    give_a, keep_a, own_a = projected(True, blocks, qt, cross_own, u_all)
-    qt_other, give_a, keep_a, own_a = lax.optimization_barrier((qt_other, give_a, keep_a, own_a))
-    give_b, keep_b, own_b = projected(False, blocks, qt_other, cross_other, u_all)
-    results = []
-    for keep, own, give in ((keep_b, own_b, give_a), (keep_a, own_a, give_b)):
-        chip = keep + lax.ppermute(give, "cols", swap).astype(F32)
-        total = own - lax.dynamic_index_in_dim(chip, pair, 0, False)
-        for shift in range(1, pairs):
-            sent = lax.dynamic_index_in_dim(chip, (pair + shift) % pairs, 0, False).astype(BF16)
-            total = total - shifted(sent, shift).astype(F32)
-        results.append(total)
-    basis, coeff = placed(rows, rows_other), placed(results[1], results[0])
+    give_a, keep_a = projected(True, qt, cross_own)
+    qt_other, give_a, keep_a = lax.optimization_barrier((qt_other, give_a, keep_a))
+    give_b, keep_b = projected(False, qt_other, cross_other)
+    give_a, give_b = lax.ppermute(give_a, "cols", swap), lax.ppermute(give_b, "cols", swap)
+    both = (pivots, share, width)
+    kept, *sent = run(
+        halve_kernel, [info], [keep_b, keep_a, give_a, give_b], [(both, F32)] + [(both, BF16)] * (pairs - 1), [], 8,
+        square, "halve"
+    )
+    recv = [shifted(each, shift) for shift, each in enumerate(sent, 1)]
+    (own,) = run(
+        own_kernel, [info], [qt, qt_other], [(both, F32)],
+        [pltpu.VMEM((pivots, order, width), BF16), pltpu.VMEM((pivots, share, width), BF16), pltpu.SemaphoreType.DMA((4,))],
+        12, 4 * square * order, "own", apart=[orig_u, orig_v]
+    )
+    (coeff,) = run(close_kernel, [info], [own, kept, *recv], [(both, F32)], [], 8, square, "close")
+    basis = placed(rows, rows_other)
     return (basis[:, None], coeff[:, None])
 
 

time: 140 us -> 137 us (0.979)
  waiting for transfers between devices: 76.6 us -> 73.7 us
    ppermute x3 -> x2, waiting for transfers between devices: 18.2 us -> 15.9 us  [shifted(): lax.ppermute(x, 'cols', [(i, (i + 2 * shift) % cols) for i in range(cols)])]
    ppermute x3 -> x2, starting transfers between devices: 4.07 us -> 3.09 us  [shifted(): lax.ppermute(x, 'cols', [(i, (i + 2 * shift) % cols) for i in range(cols)])]
    unnamed x18 -> x22, local copies, waits for them, and re-layouts: 3.44 us -> 4.19 us
    pallas_call x11 -> x13, Pallas kernels: 35.3 us -> 35.4 us  [run(): pl.pallas_call(kernel, out_shape=shapes, in_specs=[smem] * len(scalars) +...]
  transfers between devices with their start and end apart: 22 -> 21, of which waited for: 16 -> 13; matrix products, arithmetic and copies ran while one was open for 1% -> 2% of each run, Pallas kernels for 12% -> 15%
where the time goes in v1:
time: 137 us
  waiting for transfers between devices  73.7 us (54%)
  Pallas kernels  35.4 us (26%)
  starting transfers between devices  19.7 us (14%)
  local copies, waits for them, and re-layouts  4.88 us (4%)
  other arithmetic  2.12 us (2%)
    ppermute x7, waiting for transfers between devices, step(): self.up[t] = lax.ppermute(self.up[t], self.axis, self.ahead)  39.7 us
    pallas_call x13, Pallas kernels, run(): pl.pallas_call(kernel, out_shape=shapes, in_specs=[smem] * len(scalars) +...  35.4 us
    ppermute x7, waiting for transfers between devices, step(): self.down[t] = lax.ppermute(self.down[t], self.axis, self.behind)  17 us
    ppermute x2, waiting for transfers between devices, shifted(): lax.ppermute(x, 'cols', [(i, (i + 2 * shift) % cols) for i in range(cols)])  15.9 us
    ppermute x7, starting transfers between devices, step(): self.up[t] = lax.ppermute(self.up[t], self.axis, self.ahead)  13.9 us
    unnamed x22, local copies, waits for them, and re-layouts  4.19 us
    ppermute x2, starting transfers between devices, shifted(): lax.ppermute(x, 'cols', [(i, (i + 2 * shift) % cols) for i in range(cols)])  3.09 us
  transfers between devices with their start and end apart: 21, of which 13 were waited for; matrix products, arithmetic and copies ran while one was open for 2% of the time, Pallas kernels for 15%

profile of v1, /device:TPU:0, one launch (start us, length us, event | category | flops | bytes accessed | tf_op | source)
XLA Modules:
  0.0 136.7 jit_solution(1004772648229013703)
XLA Ops:
  0.6 3.0 %collective-permute-start.4 = (bf16[2,4,128,256]{3,2,1,0:T(8,128)(2,1)}, bf16[2,4,128,256]{3,2,1,0:T(8,128)(2,1)}, u32[]{:S(2)}, u32[]{:S(2)}) collective-permute-start(bf16[2,4,128,256]{3,2,1,0:T(8,128)(2,1)} %refs_0_.1), channel_id=1, source_target_pairs={{8,0},{16,8},{24,16},{28,24},{20,28},{12,20},{4,12},{0,4},{9,1},{1... | collective-permute-start | bytes 1572872 | tf_op jit(solution)/shard_map/ppermute | solution.py:312
  3.8 1.9 %collective-permute-start = (bf16[2,4,128,256]{3,2,1,0:T(8,128)(2,1)}, bf16[2,4,128,256]{3,2,1,0:T(8,128)(2,1)}, u32[]{:S(2)}, u32[]{:S(2)}) collective-permute-start(bf16[2,4,128,256]{3,2,1,0:T(8,128)(2,1)} %refs_3_.1), channel_id=1, source_target_pairs={{8,0},{16,8},{24,16},{28,24},{20,28},{12,20},{4,12},{0,4},{9,1},{1... | collective-permute-start | bytes 1572872 | tf_op jit(solution)/shard_map/ppermute | solution.py:312
  5.8 11.0 %collective-permute-done.4.refs_1_ = bf16[2,4,128,256]{3,2,1,0:T(8,128)(2,1)} collective-permute-done((bf16[2,4,128,256]{3,2,1,0:T(8,128)(2,1)}, bf16[2,4,128,256]{3,2,1,0:T(8,128)(2,1)}, u32[]{:S(2)}, u32[]{:S(2)}) %collective-permute-start.4) | collective-permute-done | bytes 524320 | tf_op jit(solution)/shard_map/ppermute | solution.py:312
  16.8 2.0 %collective-permute-start.6 = (bf16[2,4,128,256]{3,2,1,0:T(8,128)(2,1)}, bf16[2,4,128,256]{3,2,1,0:T(8,128)(2,1)S(1)}, u32[]{:S(2)}, u32[]{:S(2)}) collective-permute-start(bf16[2,4,128,256]{3,2,1,0:T(8,128)(2,1)} %collective-permute-done.4.refs_1_), channel_id=1, source_target_pairs={{8,0},{16,8},{24,16},{28,24},{20,28},{12,20},{4,12},{0,4},{9,1},{1... | collective-permute-start | bytes 1572872 | tf_op jit(solution)/shard_map/ppermute | solution.py:312
  18.9 9.1 %collective-permute-done.refs_4_ = bf16[2,4,128,256]{3,2,1,0:T(8,128)(2,1)} collective-permute-done((bf16[2,4,128,256]{3,2,1,0:T(8,128)(2,1)}, bf16[2,4,128,256]{3,2,1,0:T(8,128)(2,1)}, u32[]{:S(2)}, u32[]{:S(2)}) %collective-permute-start) | collective-permute-done | bytes 524320 | tf_op jit(solution)/shard_map/ppermute | solution.py:312
  28.0 2.0 %collective-permute-start.1 = (bf16[2,4,128,256]{3,2,1,0:T(8,128)(2,1)}, bf16[2,4,128,256]{3,2,1,0:T(8,128)(2,1)S(1)}, u32[]{:S(2)}, u32[]{:S(2)}) collective-permute-start(bf16[2,4,128,256]{3,2,1,0:T(8,128)(2,1)} %collective-permute-done.refs_4_), channel_id=1, source_target_pairs={{8,0},{16,8},{24,16},{28,24},{20,28},{12,20},{4,12},{0,4},{9,1},{1... | collective-permute-start | bytes 1572872 | tf_op jit(solution)/shard_map/ppermute | solution.py:312
  30.9 1.6 %copy-done.9 = bf16[1,4,1024,256]{3,2,1,0:T(8,128)(2,1)S(1)} copy-done((bf16[1,4,1024,256]{3,2,1,0:T(8,128)(2,1)S(1)}, bf16[1,4,1024,256]{3,2,1,0:T(8,128)(2,1)}, u32[]{:S(2)}) %copy-start.9) | copy-done | bytes 2097176
  36.4 2.8 %gather.3 = (f32[2,4,256,256]{3,2,1,0:T(8,128)S(1)}, f32[2,4,256,256]{3,2,1,0:T(8,128)S(1)}, bf16[2,4,1024,256]{3,2,1,0:T(8,128)(2,1)S(1)}) custom-call(s32[10]{0:T(128)S(1)} %pad_add_fusion.info, bf16[4,256,1024]{2,1,0:T(8,128)(2,1)S(1)} %get-tuple-element.40.panel_vt, bf16[256,1024]{1,0:T(8,128)(2,1)S(1)} %get-tuple-element.38.sampler_t, ...), custom_call_target="tpu_custom_call" | custom-call | flops 805306368 | bytes 14155776 | tf_op jit(solution)/shard_map/gather/pallas_call | solution.py:281
  39.2 2.0 %collective-permute-done.7.refs_1_ = bf16[2,4,128,256]{3,2,1,0:T(8,128)(2,1)} collective-permute-done((bf16[2,4,128,256]{3,2,1,0:T(8,128)(2,1)}, bf16[2,4,128,256]{3,2,1,0:T(8,128)(2,1)}, u32[]{:S(2)}, u32[]{:S(2)}) %collective-permute-start.7) | collective-permute-done | bytes 524320 | tf_op jit(solution)/shard_map/ppermute | solution.py:315
  41.3 1.6 %collective-permute-start.8 = (bf16[2,4,128,256]{3,2,1,0:T(8,128)(2,1)S(1)}, bf16[2,4,128,256]{3,2,1,0:T(8,128)(2,1)S(1)}, u32[]{:S(2)}, u32[]{:S(2)}) collective-permute-start(bf16[2,4,128,256]{3,2,1,0:T(8,128)(2,1)S(1)} %collective-permute-done.6.refs_0_), channel_id=1, source_target_pairs={{8,0},{16,8},{24,16},{28,24},{20,28},{12,20},{4,12},{0,4},{9,1},{1... | collective-permute-start | bytes 1572872 | tf_op jit(solution)/shard_map/ppermute | solution.py:312
  43.3 7.1 %collective-permute-done.1.refs_2_ = bf16[2,4,128,256]{3,2,1,0:T(8,128)(2,1)S(1)} collective-permute-done((bf16[2,4,128,256]{3,2,1,0:T(8,128)(2,1)}, bf16[2,4,128,256]{3,2,1,0:T(8,128)(2,1)S(1)}, u32[]{:S(2)}, u32[]{:S(2)}) %collective-permute-start.1) | collective-permute-done | bytes 524320 | tf_op jit(solution)/shard_map/ppermute | solution.py:312
  50.4 2.1 %collective-permute-done.3.refs_3_ = bf16[2,4,128,256]{3,2,1,0:T(8,128)(2,1)} collective-permute-done((bf16[2,4,128,256]{3,2,1,0:T(8,128)(2,1)}, bf16[2,4,128,256]{3,2,1,0:T(8,128)(2,1)}, u32[]{:S(2)}, u32[]{:S(2)}) %collective-permute-start.3) | collective-permute-done | bytes 524320 | tf_op jit(solution)/shard_map/ppermute | solution.py:315
  52.6 1.9 %collective-permute-start.10 = (bf16[2,4,128,256]{3,2,1,0:T(8,128)(2,1)S(1)}, bf16[2,4,128,256]{3,2,1,0:T(8,128)(2,1)S(1)}, u32[]{:S(2)}, u32[]{:S(2)}) collective-permute-start(bf16[2,4,128,256]{3,2,1,0:T(8,128)(2,1)S(1)} %collective-permute-done.1.refs_2_), channel_id=1, source_target_pairs={{8,0},{16,8},{24,16},{28,24},{20,28},{12,20},{4,12},{0,4},{9,1},{1... | collective-permute-start | bytes 1572872 | tf_op jit(solution)/shard_map/ppermute | solution.py:312
  54.5 2.3 %gather.4 = (f32[2,4,256,256]{3,2,1,0:T(8,128)S(1)}, f32[2,4,256,256]{3,2,1,0:T(8,128)S(1)}, bf16[2,4,1024,256]{3,2,1,0:T(8,128)(2,1)S(1)}) custom-call(s32[10]{0:T(128)S(1)} %pad_add_fusion.info, bf16[4,256,1024]{2,1,0:T(8,128)(2,1)S(1)} %get-tuple-element.40.panel_vt, ...), custom_call_target="tpu_custom_call", output_to_operand_aliasing={{0}: (7, {}), {1}: (8, {}), {2}: (9, {})} | custom-call | flops 536870912 | bytes 21495808 | tf_op jit(solution)/shard_map/gather/pallas_call | solution.py:281
  56.8 4.8 %collective-permute-done.8.refs_0_ = bf16[2,4,128,256]{3,2,1,0:T(8,128)(2,1)S(1)} collective-permute-done((bf16[2,4,128,256]{3,2,1,0:T(8,128)(2,1)S(1)}, bf16[2,4,128,256]{3,2,1,0:T(8,128)(2,1)S(1)}, u32[]{:S(2)}, u32[]{:S(2)}) %collective-permute-start.8) | collective-permute-done | bytes 524320 | tf_op jit(solution)/shard_map/ppermute | solution.py:312
  61.6 2.0 %collective-permute-done.9.refs_1_ = bf16[2,4,128,256]{3,2,1,0:T(8,128)(2,1)S(1)} collective-permute-done((bf16[2,4,128,256]{3,2,1,0:T(8,128)(2,1)}, bf16[2,4,128,256]{3,2,1,0:T(8,128)(2,1)S(1)}, u32[]{:S(2)}, u32[]{:S(2)}) %collective-permute-start.9) | collective-permute-done | bytes 524320 | tf_op jit(solution)/shard_map/ppermute | solution.py:315
  63.6 1.6 %collective-permute-start.12 = (bf16[2,4,128,256]{3,2,1,0:T(8,128)(2,1)S(1)}, bf16[2,4,128,256]{3,2,1,0:T(8,128)(2,1)S(1)}, u32[]{:S(2)}, u32[]{:S(2)}) collective-permute-start(bf16[2,4,128,256]{3,2,1,0:T(8,128)(2,1)S(1)} %collective-permute-done.8.refs_0_), channel_id=1, source_target_pairs={{8,0},{16,8},{24,16},{28,24},{20,28},{12,20},{4,12},{0,4},{9,1},{1... | collective-permute-start | bytes 1572872 | tf_op jit(solution)/shard_map/ppermute | solution.py:312
  65.2 8.2 %collective-permute-done.11.refs_3_ = bf16[2,4,128,256]{3,2,1,0:T(8,128)(2,1)S(1)} collective-permute-done((bf16[2,4,128,256]{3,2,1,0:T(8,128)(2,1)}, bf16[2,4,128,256]{3,2,1,0:T(8,128)(2,1)S(1)}, u32[]{:S(2)}, u32[]{:S(2)}) %collective-permute-start.11) | collective-permute-done | bytes 524320 | tf_op jit(solution)/shard_map/ppermute | solution.py:315
  73.8 1.6 %gather.5 = (f32[2,4,256,256]{3,2,1,0:T(8,128)S(1)}, f32[2,4,256,256]{3,2,1,0:T(8,128)S(1)}, bf16[2,4,1024,256]{3,2,1,0:T(8,128)(2,1)S(1)}) custom-call(s32[10]{0:T(128)S(1)} %pad_add_fusion.info, bf16[4,256,1024]{2,1,0:T(8,128)(2,1)S(1)} %get-tuple-element.40.panel_vt, ...), custom_call_target="tpu_custom_call", output_to_operand_aliasing={{0}: (7, {}), {1}: (8, {}), {2}: (9, {})} | custom-call | flops 536870912 | bytes 21495808 | tf_op jit(solution)/shard_map/gather/pallas_call | solution.py:281
  75.5 7.8 %collective-permute-done.12.refs_0_ = bf16[2,4,128,256]{3,2,1,0:T(8,128)(2,1)S(1)} collective-permute-done((bf16[2,4,128,256]{3,2,1,0:T(8,128)(2,1)S(1)}, bf16[2,4,128,256]{3,2,1,0:T(8,128)(2,1)S(1)}, u32[]{:S(2)}, u32[]{:S(2)}) %collective-permute-start.12) | collective-permute-done | bytes 524320 | tf_op jit(solution)/shard_map/ppermute | solution.py:312
  83.3 2.6 %collective-permute-done.13.refs_1_ = bf16[2,4,128,256]{3,2,1,0:T(8,128)(2,1)S(1)} collective-permute-done((bf16[2,4,128,256]{3,2,1,0:T(8,128)(2,1)S(1)}, bf16[2,4,128,256]{3,2,1,0:T(8,128)(2,1)S(1)}, u32[]{:S(2)}, u32[]{:S(2)}) %collective-permute-start.13) | collective-permute-done | bytes 524320 | tf_op jit(solution)/shard_map/ppermute | solution.py:315
  85.9 2.3 %update.3 = (bf16[4,256,256]{2,1,0:T(8,128)(2,1)S(1)}, bf16[256,1024]{1,0:T(8,128)(2,1)S(1)}) custom-call(s32[10]{0:T(128)S(1)} %pad_add_fusion.info, s32[1,4]{1,0:T(1,128)S(1)} %copy-done.8, s32[2,4]{1,0:T(2,128)S(1)} %copy-done.7, f32[2,4,256,256]{3,2,1,0:T(8,128)S(1)} %get-tuple-element.55.sampled, f32[2,4,256,256]{3,2,1,0:T(8,128)S(1)} %get-tuple-element.56.met, ...), custom_call_target="tpu_custom_call" | custom-call | flops 1342177280 | bytes 11010048 | tf_op jit(solution)/shard_map/update/pallas_call | solution.py:281
  88.3 2.3 %update.2 = (bf16[4,256,256]{2,1,0:T(8,128)(2,1)S(1)}, f32[256,1024]{1,0:T(8,128)S(1)}) custom-call(s32[10]{0:T(128)S(1)} %pad_add_fusion.info, s32[1,4]{1,0:T(1,128)S(1)} %copy-done.8, s32[2,4]{1,0:T(2,128)S(1)} %copy-done.7, f32[2,4,256,256]{3,2,1,0:T(8,128)S(1)} %get-tuple-element.55.sampled, f32[2,4,256,256]{3,2,1,0:T(8,128)S(1)} %get-tuple-element.56.met, ...), custom_call_target="tpu_custom_call" | custom-call | flops 1342177280 | bytes 11534336 | tf_op jit(solution)/shard_map/update/pallas_call | solution.py:281
  90.8 1.6 %collective-permute-start.15 = (bf16[256,1024]{1,0:T(8,128)(2,1)S(1)}, bf16[256,1024]{1,0:T(8,128)(2,1)S(1)}, u32[]{:S(2)}, u32[]{:S(2)}) collective-permute-start(bf16[256,1024]{1,0:T(8,128)(2,1)S(1)} %add_convert_fusion), channel_id=1, source_target_pairs={{0,2},{1,3},{2,0},{3,1},{4,6},{5,7},{6,4},{7,5},{8,10},{9,11},{10,... | collective-permute-start | bytes 1572872 | tf_op jit(solution)/shard_map/ppermute | solution.py:373
  92.4 12.8 %collective-permute-done.15.refs_2_ = bf16[256,1024]{1,0:T(8,128)(2,1)S(1)} collective-permute-done((bf16[256,1024]{1,0:T(8,128)(2,1)S(1)}, bf16[256,1024]{1,0:T(8,128)(2,1)S(1)}, u32[]{:S(2)}, u32[]{:S(2)}) %collective-permute-start.15) | collective-permute-done | bytes 524320 | tf_op jit(solution)/shard_map/ppermute | solution.py:373
  105.2 10.7 %orthonormal.1 = (bf16[256,1024]{1,0:T(8,128)(2,1)S(1)}, f32[256,256]{1,0:T(8,128)S(1)}, f32[256,256]{1,0:T(8,128)}) custom-call(s32[10]{0:T(128)S(1)} %pad_add_fusion.info, f32[256,1024]{1,0:T(8,128)S(1)} %start.1, f32[256,1024]{1,0:T(8,128)S(1)} %get-tuple-element.57.refs_0_, bf16[256,1024]{1,0:T(8,128)(2,1)S(1)} %collective-permute-done.14.refs_1_, ...), custom_call_target="tpu_custom_call" | custom-call | flops 17179869184 | bytes 4194304 | tf_op jit(solution)/shard_map/orthonormal/pallas_call | solution.py:281
  115.9 2.9 %project.2 = (bf16[2,256,256]{2,1,0:T(8,128)(2,1)S(1)}, f32[2,256,256]{2,1,0:T(8,128)S(1)}) custom-call(s32[10]{0:T(128)S(1)} %pad_add_fusion.info, bf16[256,1024]{1,0:T(8,128)(2,1)S(1)} %get-tuple-element.61.qt, bf16[4,1024,256]{2,1,0:T(8,128)(2,1)S(1)} %bitcast.15, bf16[4,256,256]{2,1,0:T(8,128)(2,1)S(1)} %get-tuple-element.62.cross, ...), custom_call_target="tpu_custom_call" | custom-call | flops 3623878656 | bytes 8650752 | tf_op jit(solution)/shard_map/project/pallas_call | solution.py:281
  119.3 3.1 %project.3 = (bf16[2,256,256]{2,1,0:T(8,128)(2,1)S(1)}, f32[2,256,256]{2,1,0:T(8,128)S(1)}) custom-call(s32[10]{0:T(128)S(1)} %pad_add_fusion.info, bf16[256,1024]{1,0:T(8,128)(2,1)S(1)} %collective-permute-done.17.qt_other.qt, bf16[4,1024,256]{2,1,0:T(8,128)(2,1)S(1)} %bitcast.16, bf16[4,256,256]{2,1,0:T(8,128)(2,1)S(1)} %get-tuple-element.67.cross, ...), custom_call_target="tpu_custom_call" | custom-call | flops 3623878656 | bytes 8650752 | tf_op jit(solution)/shard_map/project/pallas_call | solution.py:281
  127.7 1.9 %maximum_select_fusion = f32[2,1,256,256]{3,2,1,0:T(8,128)} fusion(f32[1,1,256,256]{3,2,1,0:T(8,128)} %bitcast.8, f32[1,1,256,256]{3,2,1,0:T(8,128)S(1)} %bitcast.21, pred[]{:T(512)S(6)} %eq.5), kind=kLoop, calls=%fused_computation.1 | loop fusion | flops 393216 | bytes 1048577 | tf_op jit(solution)/shard_map/jit(_where)/select_n | solution.py:407
  129.5 2.2 %own.1 = f32[2,256,256]{2,1,0:T(8,128)S(1)} custom-call(s32[10]{0:T(128)S(1)} %pad_add_fusion.info, bf16[256,1024]{1,0:T(8,128)(2,1)S(1)} %get-tuple-element.61.qt, bf16[256,1024]{1,0:T(8,128)(2,1)S(1)} %collective-permute-done.17.qt_other.qt, bf16[2,1024,256]{2,1,0:T(8,128)(2,1)S(1)} %bitcast.18, bf16[2,1024,256]{2,1,0:T(8,128)(2,1)S(1)} %bitcast.20), custom_call_target="tpu_custom_call" | custom-call | flops 536870912 | bytes 1572864 | tf_op jit(solution)/shard_map/own/pallas_call | solution.py:281
  131.8 3.1 %collective-permute-done.20.refs_0_ = bf16[2,256,256]{2,1,0:T(8,128)(2,1)} collective-permute-done((bf16[2,256,256]{2,1,0:T(8,128)(2,1)}, bf16[2,256,256]{2,1,0:T(8,128)(2,1)}, u32[]{:S(2)}, u32[]{:S(2)}) %collective-permute-start.20) | collective-permute-done | bytes 262176 | tf_op jit(solution)/shard_map/ppermute | solution.py:373
  134.8 1.8 %close.1 = f32[2,256,256]{2,1,0:T(8,128)} custom-call(s32[10]{0:T(128)S(1)} %pad_add_fusion.info, f32[2,256,256]{2,1,0:T(8,128)S(1)} %own.1, f32[2,256,256]{2,1,0:T(8,128)S(1)} %copy-done.6, bf16[2,256,256]{2,1,0:T(8,128)(2,1)} %collective-permute-done.20.refs_0_), custom_call_target="tpu_custom_call" | custom-call | flops 131072 | bytes 1835008 | tf_op jit(solution)/shard_map/close/pallas_call | solution.py:281
  (49 shorter events, 12.3 us)
Async XLA Ops:
  0.6 16.1 %collective-permute-start.4 = (bf16[2,4,128,256]{3,2,1,0:T(8,128)(2,1)}, bf16[2,4,128,256]{3,2,1,0:T(8,128)(2,1)}, u32[]{:S(2)}, u32[]{:S(2)}) collective-permute-start(bf16[2,4,128,256]{3,2,1,0:T(8,128)(2,1)} %refs_0_.1), channel_id=1, source_target_pairs={{8,0},{16,8},{24,16},{28,24},{20,28},{12,20},{4,12},{0,4},{9,1},{1... | collective-permute-start | bytes 1572872 | tf_op jit(solution)/shard_map/ppermute | solution.py:312
  3.6 15.2 %collective-permute-start.5 = (bf16[2,4,128,256]{3,2,1,0:T(8,128)(2,1)}, bf16[2,4,128,256]{3,2,1,0:T(8,128)(2,1)}, u32[]{:S(2)}, u32[]{:S(2)}) collective-permute-start(bf16[2,4,128,256]{3,2,1,0:T(8,128)(2,1)} %refs_0_.1), channel_id=1, source_target_pairs={{0,8},{8,16},{16,24},{24,28},{28,20},{20,12},{12,4},{4,0},{1,9},{9... | collective-permute-start | bytes 1572872 | tf_op jit(solution)/shard_map/ppermute | solution.py:315
  3.8 24.2 %collective-permute-start = (bf16[2,4,128,256]{3,2,1,0:T(8,128)(2,1)}, bf16[2,4,128,256]{3,2,1,0:T(8,128)(2,1)}, u32[]{:S(2)}, u32[]{:S(2)}) collective-permute-start(bf16[2,4,128,256]{3,2,1,0:T(8,128)(2,1)} %refs_3_.1), channel_id=1, source_target_pairs={{8,0},{16,8},{24,16},{28,24},{20,28},{12,20},{4,12},{0,4},{9,1},{1... | collective-permute-start | bytes 1572872 | tf_op jit(solution)/shard_map/ppermute | solution.py:312
  5.6 24.4 %collective-permute-start.2 = (bf16[2,4,128,256]{3,2,1,0:T(8,128)(2,1)}, bf16[2,4,128,256]{3,2,1,0:T(8,128)(2,1)}, u32[]{:S(2)}, u32[]{:S(2)}) collective-permute-start(bf16[2,4,128,256]{3,2,1,0:T(8,128)(2,1)} %refs_3_.1), channel_id=1, source_target_pairs={{0,8},{8,16},{16,24},{24,28},{28,20},{20,12},{12,4},{4,0},{1,9},{9... | collective-permute-start | bytes 1572872 | tf_op jit(solution)/shard_map/ppermute | solution.py:315
  16.8 22.4 %collective-permute-start.6 = (bf16[2,4,128,256]{3,2,1,0:T(8,128)(2,1)}, bf16[2,4,128,256]{3,2,1,0:T(8,128)(2,1)S(1)}, u32[]{:S(2)}, u32[]{:S(2)}) collective-permute-start(bf16[2,4,128,256]{3,2,1,0:T(8,128)(2,1)} %collective-permute-done.4.refs_1_), channel_id=1, source_target_pairs={{8,0},{16,8},{24,16},{28,24},{20,28},{12,20},{4,12},{0,4},{9,1},{1... | collective-permute-start | bytes 1572872 | tf_op jit(solution)/shard_map/ppermute | solution.py:312
  18.8 22.5 %collective-permute-start.7 = (bf16[2,4,128,256]{3,2,1,0:T(8,128)(2,1)}, bf16[2,4,128,256]{3,2,1,0:T(8,128)(2,1)}, u32[]{:S(2)}, u32[]{:S(2)}) collective-permute-start(bf16[2,4,128,256]{3,2,1,0:T(8,128)(2,1)} %collective-permute-done.5.refs_2_), channel_id=1, source_target_pairs={{0,8},{8,16},{16,24},{24,28},{28,20},{20,12},{12,4},{4,0},{1,9},{9... | collective-permute-start | bytes 1572872 | tf_op jit(solution)/shard_map/ppermute | solution.py:315
  28.0 22.4 %collective-permute-start.1 = (bf16[2,4,128,256]{3,2,1,0:T(8,128)(2,1)}, bf16[2,4,128,256]{3,2,1,0:T(8,128)(2,1)S(1)}, u32[]{:S(2)}, u32[]{:S(2)}) collective-permute-start(bf16[2,4,128,256]{3,2,1,0:T(8,128)(2,1)} %collective-permute-done.refs_4_), channel_id=1, source_target_pairs={{8,0},{16,8},{24,16},{28,24},{20,28},{12,20},{4,12},{0,4},{9,1},{1... | collective-permute-start | bytes 1572872 | tf_op jit(solution)/shard_map/ppermute | solution.py:312
  30.0 22.5 %collective-permute-start.3 = (bf16[2,4,128,256]{3,2,1,0:T(8,128)(2,1)}, bf16[2,4,128,256]{3,2,1,0:T(8,128)(2,1)}, u32[]{:S(2)}, u32[]{:S(2)}) collective-permute-start(bf16[2,4,128,256]{3,2,1,0:T(8,128)(2,1)} %collective-permute-done.2.refs_5_), channel_id=1, source_target_pairs={{0,8},{8,16},{16,24},{24,28},{28,20},{20,12},{12,4},{4,0},{1,9},{9... | collective-permute-start | bytes 1572872 | tf_op jit(solution)/shard_map/ppermute | solution.py:315
  30.9 1.6 %copy-start.9 = (bf16[1,4,1024,256]{3,2,1,0:T(8,128)(2,1)S(1)}, bf16[1,4,1024,256]{3,2,1,0:T(8,128)(2,1)}, u32[]{:S(2)}) copy-start(bf16[1,4,1024,256]{3,2,1,0:T(8,128)(2,1)} %param.11) | copy-start | bytes 6291460
  32.5 1.0 copy-start.10
  33.5 1.2 copy-start.1
  33.5 1.5 %copy-start.2 = (bf16[2,1,1024,256]{3,2,1,0:T(8,128)(2,1)S(1)}, bf16[2,1,1024,256]{3,2,1,0:T(8,128)(2,1)}, u32[]{:S(2)}) copy-start(bf16[2,1,1024,256]{3,2,1,0:T(8,128)(2,1)} %param.17) | copy-start | bytes 3145732
  34.3 2.0 %copy-start.3 = (bf16[2,4,128,256]{3,2,1,0:T(8,128)(2,1)S(1)}, bf16[2,4,128,256]{3,2,1,0:T(8,128)(2,1)}, u32[]{:S(2)}) copy-start(bf16[2,4,128,256]{3,2,1,0:T(8,128)(2,1)} %refs_0_.1) | copy-start | bytes 1572868
  34.3 2.0 %copy-start.4 = (bf16[2,4,128,256]{3,2,1,0:T(8,128)(2,1)S(1)}, bf16[2,4,128,256]{3,2,1,0:T(8,128)(2,1)}, u32[]{:S(2)}) copy-start(bf16[2,4,128,256]{3,2,1,0:T(8,128)(2,1)} %refs_3_.1) | copy-start | bytes 1572868
  41.3 20.4 %collective-permute-start.8 = (bf16[2,4,128,256]{3,2,1,0:T(8,128)(2,1)S(1)}, bf16[2,4,128,256]{3,2,1,0:T(8,128)(2,1)S(1)}, u32[]{:S(2)}, u32[]{:S(2)}) collective-permute-start(bf16[2,4,128,256]{3,2,1,0:T(8,128)(2,1)S(1)} %collective-permute-done.6.refs_0_), channel_id=1, source_target_pairs={{8,0},{16,8},{24,16},{28,24},{20,28},{12,20},{4,12},{0,4},{9,1},{1... | collective-permute-start | bytes 1572872 | tf_op jit(solution)/shard_map/ppermute | solution.py:312
  42.8 20.8 %collective-permute-start.9 = (bf16[2,4,128,256]{3,2,1,0:T(8,128)(2,1)}, bf16[2,4,128,256]{3,2,1,0:T(8,128)(2,1)S(1)}, u32[]{:S(2)}, u32[]{:S(2)}) collective-permute-start(bf16[2,4,128,256]{3,2,1,0:T(8,128)(2,1)} %collective-permute-done.7.refs_1_), channel_id=1, source_target_pairs={{0,8},{8,16},{16,24},{24,28},{28,20},{20,12},{12,4},{4,0},{1,9},{9... | collective-permute-start | bytes 1572872 | tf_op jit(solution)/shard_map/ppermute | solution.py:315
  52.5 20.9 %collective-permute-start.11 = (bf16[2,4,128,256]{3,2,1,0:T(8,128)(2,1)}, bf16[2,4,128,256]{3,2,1,0:T(8,128)(2,1)S(1)}, u32[]{:S(2)}, u32[]{:S(2)}) collective-permute-start(bf16[2,4,128,256]{3,2,1,0:T(8,128)(2,1)} %collective-permute-done.3.refs_3_), channel_id=1, source_target_pairs={{0,8},{8,16},{16,24},{24,28},{28,20},{20,12},{12,4},{4,0},{1,9},{9... | collective-permute-start | bytes 1572872 | tf_op jit(solution)/shard_map/ppermute | solution.py:315
  52.6 21.2 %collective-permute-start.10 = (bf16[2,4,128,256]{3,2,1,0:T(8,128)(2,1)S(1)}, bf16[2,4,128,256]{3,2,1,0:T(8,128)(2,1)S(1)}, u32[]{:S(2)}, u32[]{:S(2)}) collective-permute-start(bf16[2,4,128,256]{3,2,1,0:T(8,128)(2,1)S(1)} %collective-permute-done.1.refs_2_), channel_id=1, source_target_pairs={{8,0},{16,8},{24,16},{28,24},{20,28},{12,20},{4,12},{0,4},{9,1},{1... | collective-permute-start | bytes 1572872 | tf_op jit(solution)/shard_map/ppermute | solution.py:312
  63.6 19.6 %collective-permute-start.12 = (bf16[2,4,128,256]{3,2,1,0:T(8,128)(2,1)S(1)}, bf16[2,4,128,256]{3,2,1,0:T(8,128)(2,1)S(1)}, u32[]{:S(2)}, u32[]{:S(2)}) collective-permute-start(bf16[2,4,128,256]{3,2,1,0:T(8,128)(2,1)S(1)} %collective-permute-done.8.refs_0_), channel_id=1, source_target_pairs={{8,0},{16,8},{24,16},{28,24},{20,28},{12,20},{4,12},{0,4},{9,1},{1... | collective-permute-start | bytes 1572872 | tf_op jit(solution)/shard_map/ppermute | solution.py:312
  73.4 12.5 %collective-permute-start.13 = (bf16[2,4,128,256]{3,2,1,0:T(8,128)(2,1)S(1)}, bf16[2,4,128,256]{3,2,1,0:T(8,128)(2,1)S(1)}, u32[]{:S(2)}, u32[]{:S(2)}) collective-permute-start(bf16[2,4,128,256]{3,2,1,0:T(8,128)(2,1)S(1)} %collective-permute-done.11.refs_3_), channel_id=1, source_target_pairs={{0,8},{8,16},{16,24},{24,28},{28,20},{20,12},{12,4},{4,0},{1,9},{9... | collective-permute-start | bytes 1572872 | tf_op jit(solution)/shard_map/ppermute | solution.py:315
  73.8 12.0 %copy-start = (bf16[1,4,1024,256]{3,2,1,0:T(8,128)(2,1)S(1)}, bf16[1,4,1024,256]{3,2,1,0:T(8,128)(2,1)}, u32[]{:S(2)}) copy-start(bf16[1,4,1024,256]{3,2,1,0:T(8,128)(2,1)} %param.10) | copy-start | bytes 6291460
  73.8 12.0 %copy-start.7 = (s32[2,4]{1,0:T(2,128)S(1)}, s32[2,4]{1,0:T(2,128)}, u32[]{:S(2)}) copy-start(s32[2,4]{1,0:T(2,128)} %pivot_rank.3) | copy-start | bytes 100
  73.8 12.0 %copy-start.8 = (s32[1,4]{1,0:T(1,128)S(1)}, s32[1,4]{1,0:T(1,128)}, u32[]{:S(2)}) copy-start(s32[1,4]{1,0:T(1,128)} %panel_rank.3) | copy-start | bytes 52
  88.2 2.4 %collective-permute-start.14 = (bf16[256,1024]{1,0:T(8,128)(2,1)S(1)}, bf16[256,1024]{1,0:T(8,128)(2,1)S(1)}, u32[]{:S(2)}, u32[]{:S(2)}) collective-permute-start(bf16[256,1024]{1,0:T(8,128)(2,1)S(1)} %get-tuple-element.58), channel_id=1, source_target_pairs={{0,1},{1,0},{2,3},{3,2},{4,5},{5,4},{6,7},{7,6},{8,9},{9,8},{10,11... | collective-permute-start | bytes 1572872 | tf_op jit(solution)/shard_map/ppermute | solution.py:429
  90.8 14.4 %collective-permute-start.15 = (bf16[256,1024]{1,0:T(8,128)(2,1)S(1)}, bf16[256,1024]{1,0:T(8,128)(2,1)S(1)}, u32[]{:S(2)}, u32[]{:S(2)}) collective-permute-start(bf16[256,1024]{1,0:T(8,128)(2,1)S(1)} %add_convert_fusion), channel_id=1, source_target_pairs={{0,2},{1,3},{2,0},{3,1},{4,6},{5,7},{6,4},{7,5},{8,10},{9,11},{10,... | collective-permute-start | bytes 1572872 | tf_op jit(solution)/shard_map/ppermute | solution.py:373
  115.9 2.9 %collective-permute-start.17 = (bf16[256,1024]{1,0:T(8,128)(2,1)S(1)}, bf16[256,1024]{1,0:T(8,128)(2,1)S(1)}, u32[]{:S(2)}, u32[]{:S(2)}) collective-permute-start(bf16[256,1024]{1,0:T(8,128)(2,1)S(1)} %get-tuple-element.61.qt), channel_id=1, source_target_pairs={{0,1},{1,0},{2,3},{3,2},{4,5},{5,4},{6,7},{7,6},{8,9},{9,8},{10,11... | collective-permute-start | bytes 1572872 | tf_op jit(solution)/shard_map/ppermute | solution.py:438
  118.8 4.3 %collective-permute-start.18 = (bf16[2,256,256]{2,1,0:T(8,128)(2,1)S(1)}, bf16[2,256,256]{2,1,0:T(8,128)(2,1)S(1)}, u32[]{:S(2)}, u32[]{:S(2)}) collective-permute-start(bf16[2,256,256]{2,1,0:T(8,128)(2,1)S(1)} %get-tuple-element.70), channel_id=1, source_target_pairs={{0,1},{1,0},{2,3},{3,2},{4,5},{5,4},{6,7},{7,6},{8,9},{9,8},{10,11... | collective-permute-start | bytes 786440 | tf_op jit(solution)/shard_map/ppermute | solution.py:443
  122.4 1.6 %collective-permute-start.19 = (bf16[2,256,256]{2,1,0:T(8,128)(2,1)S(1)}, bf16[2,256,256]{2,1,0:T(8,128)(2,1)S(1)}, u32[]{:S(2)}, u32[]{:S(2)}) collective-permute-start(bf16[2,256,256]{2,1,0:T(8,128)(2,1)S(1)} %get-tuple-element.71), channel_id=1, source_target_pairs={{0,1},{1,0},{2,3},{3,2},{4,5},{5,4},{6,7},{7,6},{8,9},{9,8},{10,11... | collective-permute-start | bytes 786440 | tf_op jit(solution)/shard_map/ppermute | solution.py:443
  122.5 5.1 %collective-permute-start.16 = (f32[256,256]{1,0:T(8,128)}, f32[256,256]{1,0:T(8,128)}, u32[]{:S(2)}, u32[]{:S(2)}) collective-permute-start(f32[256,256]{1,0:T(8,128)} %get-tuple-element.60), channel_id=1, source_target_pairs={{0,1},{1,0},{2,3},{3,2},{4,5},{5,4},{6,7},{7,6},{8,9},{9,8},{10,11... | collective-permute-start | bytes 786440 | tf_op jit(solution)/shard_map/ppermute | solution.py:439
  125.4 0.8 copy-start.5
  126.2 8.7 %collective-permute-start.20 = (bf16[2,256,256]{2,1,0:T(8,128)(2,1)}, bf16[2,256,256]{2,1,0:T(8,128)(2,1)}, u32[]{:S(2)}, u32[]{:S(2)}) collective-permute-start(bf16[2,256,256]{2,1,0:T(8,128)(2,1)} %get-tuple-element.73), channel_id=1, source_target_pairs={{0,2},{1,3},{2,0},{3,1},{4,6},{5,7},{6,4},{7,5},{8,10},{9,11},{10,... | collective-permute-start | bytes 786440 | tf_op jit(solution)/shard_map/ppermute | solution.py:373
  129.5 5.3 %copy-start.6 = (f32[2,256,256]{2,1,0:T(8,128)S(1)}, f32[2,256,256]{2,1,0:T(8,128)}, u32[]{:S(2)}) copy-start(f32[2,256,256]{2,1,0:T(8,128)} %copy-done.5) | copy-start | bytes 1572868

commit v2 on v1

--- a/solution.py
+++ b/solution.py
@@ -168,8 +168,20 @@
                 u_all[c, j, p * slab : (p + 1) * slab, :] = u_new[n * slab : (n + 1) * slab, :]
 
 
-def update_kernel(own_column, places, blocks, info, panel_rank, pivot_rank, sampled, met, panel_u, panel_vt, sampler_t, *refs):
-    cross, out = refs[-2:]
+def sampled_kernel(places, blocks, info, sampled, sampler_t, *refs):
+    late, out = refs[:-1], refs[-1]
+    slab = sampler_t.shape[1] // blocks
+    for c in range(out.shape[0]):
+        for j in range(out.shape[1]):
+            total = sampled[c, j]
+            for place in places:
+                span = pl.ds(pl.multiple_of(info[2 + place] * slab, 128), slab)
+                total += dot(sampler_t[:, span], late[c][j])
+            out[c, j] = total.astype(BF16)
+
+
+def update_kernel(own_column, places, blocks, info, panel_rank, pivot_rank, sampled, met, panel_u, panel_vt, *refs):
+    late, (cross, out) = refs[:-2], refs[-2:]
     priors, width, _ = cross.shape
     slab = panel_vt.shape[2] // blocks
     column = info[0] if own_column else 1 - info[0]
@@ -177,14 +189,13 @@
     col = lax.broadcasted_iota(jnp.int32, (width, width), 1)
     terms = []
     for j in range(priors):
-        one, two = sampled[column, j], met[column, j]
-        for n, place in enumerate(places):
+        two = met[column, j]
+        for place in places:
             span = pl.ds(pl.multiple_of(info[2 + place] * slab, 128), slab)
-            one += dot(sampler_t[:, span], refs[n][column, j])
-            two += dot(panel_vt[j, :, span], refs[len(places) + n][column, j])
+            two += dot(panel_vt[j, :, span], jnp.where(column == 0, late[0][j], late[1][j]))
         inside = (row < panel_rank[0, j]) & (col < pivot_rank[column, j])
         cross[j] = jnp.where(inside, two, 0.0).astype(BF16)
-        terms.append(dot11(one.astype(BF16), cross[j]).astype(BF16))
+        terms.append(dot11(sampled[column, j], cross[j]).astype(BF16))
     half = out.shape[1] // 2
     for at in (0, half):
         total = jnp.zeros((width, half), F32)
@@ -207,7 +218,7 @@
 
     def rows_of(j, b):
         if b in places:
-            return refs[places.index(b)][column, j]
+            return jnp.where(column == 0, refs[0][j], refs[1][j])
         return u_all[column, j, b * slab : (b + 1) * slab, :]
 
     some = max(1, blocks // 2)
@@ -239,26 +250,12 @@
         out[n] = dot11(v_buf[n], dot(q[...], u_buf[n]).astype(BF16))
 
 
-def halve_kernel(info, keep_b, keep_a, give_a, give_b, kept, *sent):
-    pair = info[1] // 2
+def halve_kernel(info, keep_b, keep_a, give_a, give_b, *sent):
     pairs = keep_a.shape[0]
-    for n, (keep, recv) in enumerate(((keep_b, give_a), (keep_a, give_b))):
-        for shift in range(pairs):
-            a = lax.rem(pair + shift, pairs)
-            total = keep[a] + recv[a].astype(F32)
-            if shift:
-                sent[shift - 1][n] = total.astype(BF16)
-            else:
-                kept[n] = total
-
-
-def close_kernel(info, own, kept, *refs):
-    out = refs[-1]
-    for n, column in enumerate((1 - info[0], info[0])):
-        total = own[n] - kept[n]
-        for recv in refs[:-1]:
-            total = total - recv[n].astype(F32)
-        out[column] = total
+    for shift in range(1, pairs):
+        a = lax.rem(info[1] // 2 + shift, pairs)
+        for n, (keep, recv) in enumerate(((keep_b, give_a), (keep_a, give_b))):
+            sent[shift - 1][n] = (keep[a] + recv[a].astype(F32)).astype(BF16)
 
 
 def turn_kernel(panel_v, sampler, panel_vt, sampler_t):
@@ -308,21 +305,15 @@
 
     def step(self, number):
         for t in range(2):
-            if number <= self.near or t == 0:
-                self.up[t] = lax.ppermute(self.up[t], self.axis, self.ahead)
-                self.found[t][number] = self.up[t]
-            if number <= self.near or t == 1:
-                self.down[t] = lax.ppermute(self.down[t], self.axis, self.behind)
-                self.found[t][self.count - number] = self.down[t]
-
-    def hold(self, value, t, number):
-        if number > self.near:
-            return value
-        places = (number, self.count - number)
-        value, *kept = lax.optimization_barrier((value, *(self.found[t][d] for d in places)))
-        for d, block in zip(places, kept):
-            self.found[t][d] = block
-        return value
+            found = self.found[t]
+            if number <= self.near:
+                self.up[t] = found[number] = lax.ppermute(self.up[t], self.axis, self.ahead)
+                self.down[t] = found[self.count - number] = lax.ppermute(self.down[t], self.axis, self.behind)
+            else:
+                found[number] = [
+                    lax.ppermute(self.up[t][0], self.axis, self.ahead),
+                    lax.ppermute(self.down[t][1], self.axis, self.behind),
+                ]
 
     def tie(self, value, number, which=(0, 1)):
         lists = [(self.up, t, number) for t in which if number <= self.near or t == 0]
@@ -331,9 +322,6 @@
         for (way, t, place), block in zip(lists, held):
             way[t] = self.found[t][place] = block
         return value
-
-    def blocks(self, t):
-        return [self.found[t][d] for d in range(self.count)]
 
 
 def body(panel_u, panel_v, panel_rank, pivot_u, pivot_v, pivot_rank, orig_u, orig_v, sampler):
@@ -391,14 +379,14 @@
     def updated(own_column, sampled, met):
         return run(
             functools.partial(update_kernel, own_column, places, blocks), [info, panel_rank, pivot_rank],
-            [sampled, met, panel_u, panel_vt, sampler_t, *new_u, *new_v],
+            [sampled, met, panel_u, panel_vt, *late_v],
             [((priors, width, width), BF16), ((width, order), F32 if own_column else BF16)], [], 20,
             2 * priors * square * (order + width), "update"
         )
 
     def projected(own_column, qt, cross):
         return run(
-            functools.partial(project_kernel, places, blocks, own_column), [info], [qt, panel_u, cross, u_all, *new_u],
+            functools.partial(project_kernel, places, blocks, own_column), [info], [qt, panel_u, cross, u_all, *late_u],
             [((pairs, share, width), BF16), ((pairs, share, width), F32)], [pltpu.VMEM((order, width), F32)],
             20, 3 * priors * square * (2 * order + width), "project"
         )
@@ -410,7 +398,7 @@
         blocks, places = 1, []
         new_u, new_v = ([lax.all_gather(x, "rows", axis=2, tiled=True)] for x in (pivot_u, pivot_v))
         sampled, met, u_all = gathered([0], 1, new_u, new_v, [])
-        new_u, new_v = [], []
+        late_u, late_v = [], []
     else:
         blocks = count
         now, kept = Ring([pivot_u, pivot_v], ring, "rows"), []
@@ -420,11 +408,18 @@
                 kept[0] = now.tie(kept[0], number, (0,))
                 if number == 2:
                     start = now.tie(start, number, (1,))
-            places = sorted({number, count - number} | ({0} if number == 1 else set()))
-            new_u, new_v = ([now.found[t][p] for p in places] for t in range(2))
-            if number < last:
+            if number == last:
+                places = [last]
+                late_u, late_v = now.found[0][last], now.found[1][last]
+            else:
+                places = sorted({number, count - number} | ({0} if number == 1 else set()))
+                new_u, new_v = ([now.found[t][p] for p in places] for t in range(2))
                 kept = list(gathered(places, count, new_u, new_v, kept))
         sampled, met, u_all = kept
+    (sampled,) = run(
+        functools.partial(sampled_kernel, places, blocks), [info], [sampled, sampler_t, *late_u],
+        [((pivots, priors, width, width), BF16)], [], 12, square * order, "sampled"
+    )
     cross_other, give = updated(False, sampled, met)
     recv = lax.ppermute(give, "cols", swap)
     cross_own, keep = updated(True, sampled, met)
@@ -441,18 +436,24 @@
     qt_other, give_a, keep_a = lax.optimization_barrier((qt_other, give_a, keep_a))
     give_b, keep_b = projected(False, qt_other, cross_other)
     give_a, give_b = lax.ppermute(give_a, "cols", swap), lax.ppermute(give_b, "cols", swap)
-    both = (pivots, share, width)
-    kept, *sent = run(
-        halve_kernel, [info], [keep_b, keep_a, give_a, give_b], [(both, F32)] + [(both, BF16)] * (pairs - 1), [], 8,
+
+    sent = run(
+        halve_kernel, [info], [keep_b, keep_a, give_a, give_b], [((pivots, share, width), BF16)] * (pairs - 1), [], 8,
         square, "halve"
     )
     recv = [shifted(each, shift) for shift, each in enumerate(sent, 1)]
     (own,) = run(
-        own_kernel, [info], [qt, qt_other], [(both, F32)],
+        own_kernel, [info], [qt, qt_other], [((pivots, share, width), F32)],
         [pltpu.VMEM((pivots, order, width), BF16), pltpu.VMEM((pivots, share, width), BF16), pltpu.SemaphoreType.DMA((4,))],
         12, 4 * square * order, "own", apart=[orig_u, orig_v]
     )
-    (coeff,) = run(close_kernel, [info], [own, kept, *recv], [(both, F32)], [], 8, square, "close")
+    other, mine = (
+        own[n] - (lax.dynamic_index_in_dim(keep, pair, 0, False) + lax.dynamic_index_in_dim(part, pair, 0, False).astype(F32))
+        for n, (keep, part) in enumerate(((keep_b, give_a), (keep_a, give_b)))
+    )
+    coeff = lax.optimization_barrier(placed(mine, other))
+    for each in recv:
+        coeff = coeff - jnp.where(core == 0, each[::-1], each).astype(F32)
     basis = placed(rows, rows_other)
     return (basis[:, None], coeff[:, None])
 

time: 137 us -> 139 us (1.015)
  starting transfers between devices: 19.7 us -> 22.2 us
  other arithmetic: 2.12 us -> 4.19 us
  waiting for transfers between devices: 73.7 us -> 71.8 us
  Pallas kernels: 35.4 us -> 33.9 us
    ppermute x14 -> x16, waiting for transfers between devices: 56.8 us -> 53.3 us  [the longest x6 40.5 us: step(): self.up[t] = found[number] = lax.ppermute(self.up[t], self.axis, self.ahead)]
    ppermute x14 -> x16, starting transfers between devices: 15.4 us -> 17.9 us  [the longest x6 12 us: step(): self.up[t] = found[number] = lax.ppermute(self.up[t], self.axis, self.ahead)]
    ppermute x2, waiting for transfers between devices: 15.9 us -> 18.3 us  [shifted(): lax.ppermute(x, 'cols', [(i, (i + 2 * shift) % cols) for i in range(cols)])]
    pallas_call x13, Pallas kernels: 35.4 us -> 33.9 us  [run(): pl.pallas_call(kernel, out_shape=shapes, in_specs=[smem] * len(scalars) +...]
    unnamed x22 -> x28, local copies, waits for them, and re-layouts: 4.19 us -> 5.46 us
  transfers between devices with their start and end apart: 21 -> 23, of which waited for: 13 -> 16; matrix products, arithmetic and copies ran while one was open for 2% -> 3% of each run, Pallas kernels for 15% -> 15%
where the time goes in v2:
time: 139 us
  waiting for transfers between devices  71.8 us (52%)
  Pallas kernels  33.9 us (24%)
  starting transfers between devices  22.2 us (16%)
  local copies, waits for them, and re-layouts  6.23 us (4%)
  other arithmetic  4.19 us (3%)
    ppermute x6, waiting for transfers between devices, step(): self.up[t] = found[number] = lax.ppermute(self.up[t], self.axis, self.ahead)  40.5 us
    pallas_call x13, Pallas kernels, run(): pl.pallas_call(kernel, out_shape=shapes, in_specs=[smem] * len(scalars) +...  33.9 us
    ppermute x2, waiting for transfers between devices, shifted(): lax.ppermute(x, 'cols', [(i, (i + 2 * shift) % cols) for i in range(cols)])  18.3 us
    ppermute x6, starting transfers between devices, step(): self.up[t] = found[number] = lax.ppermute(self.up[t], self.axis, self.ahead)  12 us
    ppermute x6, waiting for transfers between devices, step(): lax.ppermute(self.down[t], self.axis, self.behind)  6.1 us
    unnamed x28, local copies, waits for them, and re-layouts  5.46 us
    ppermute x2, starting transfers between devices, step(): lax.ppermute(self.up[t][0], self.axis, self.ahead)  3.65 us
    ppermute x2, waiting for transfers between devices, step(): lax.ppermute(self.down[t][1], self.axis, self.behind)  3.38 us
  transfers between devices with their start and end apart: 23, of which 16 were waited for; matrix products, arithmetic and copies ran while one was open for 3% of the time, Pallas kernels for 15%

profile of v2, /device:TPU:0, one launch (start us, length us, event | category | flops | bytes accessed | tf_op | source)
XLA Modules:
  0.0 139.1 jit_solution(3481995940102542003)
XLA Ops:
  0.6 3.0 %collective-permute-start.4 = (bf16[2,4,128,256]{3,2,1,0:T(8,128)(2,1)}, bf16[2,4,128,256]{3,2,1,0:T(8,128)(2,1)}, u32[]{:S(2)}, u32[]{:S(2)}) collective-permute-start(bf16[2,4,128,256]{3,2,1,0:T(8,128)(2,1)} %refs_0_.1), channel_id=1, source_target_pairs={{8,0},{16,8},{24,16},{28,24},{20,28},{12,20},{4,12},{0,4},{9,1},{1... | collective-permute-start | bytes 1572872 | tf_op jit(solution)/shard_map/ppermute | solution.py:310
  3.8 1.9 %collective-permute-start = (bf16[2,4,128,256]{3,2,1,0:T(8,128)(2,1)}, bf16[2,4,128,256]{3,2,1,0:T(8,128)(2,1)}, u32[]{:S(2)}, u32[]{:S(2)}) collective-permute-start(bf16[2,4,128,256]{3,2,1,0:T(8,128)(2,1)} %refs_3_.1), channel_id=1, source_target_pairs={{8,0},{16,8},{24,16},{28,24},{20,28},{12,20},{4,12},{0,4},{9,1},{1... | collective-permute-start | bytes 1572872 | tf_op jit(solution)/shard_map/ppermute | solution.py:310
  5.8 11.0 %collective-permute-done.4.refs_1_ = bf16[2,4,128,256]{3,2,1,0:T(8,128)(2,1)} collective-permute-done((bf16[2,4,128,256]{3,2,1,0:T(8,128)(2,1)}, bf16[2,4,128,256]{3,2,1,0:T(8,128)(2,1)}, u32[]{:S(2)}, u32[]{:S(2)}) %collective-permute-start.4) | collective-permute-done | bytes 524320 | tf_op jit(solution)/shard_map/ppermute | solution.py:310
  16.8 2.0 %collective-permute-start.6 = (bf16[2,4,128,256]{3,2,1,0:T(8,128)(2,1)}, bf16[2,4,128,256]{3,2,1,0:T(8,128)(2,1)S(1)}, u32[]{:S(2)}, u32[]{:S(2)}) collective-permute-start(bf16[2,4,128,256]{3,2,1,0:T(8,128)(2,1)} %collective-permute-done.4.refs_1_), channel_id=1, source_target_pairs={{8,0},{16,8},{24,16},{28,24},{20,28},{12,20},{4,12},{0,4},{9,1},{1... | collective-permute-start | bytes 1572872 | tf_op jit(solution)/shard_map/ppermute | solution.py:310
  19.7 1.6 %copy-done.12 = bf16[1,4,1024,256]{3,2,1,0:T(8,128)(2,1)S(1)} copy-done((bf16[1,4,1024,256]{3,2,1,0:T(8,128)(2,1)S(1)}, bf16[1,4,1024,256]{3,2,1,0:T(8,128)(2,1)}, u32[]{:S(2)}) %copy-start.12) | copy-done | bytes 2097176
  23.1 4.9 %collective-permute-done.refs_4_ = bf16[2,4,128,256]{3,2,1,0:T(8,128)(2,1)} collective-permute-done((bf16[2,4,128,256]{3,2,1,0:T(8,128)(2,1)}, bf16[2,4,128,256]{3,2,1,0:T(8,128)(2,1)}, u32[]{:S(2)}, u32[]{:S(2)}) %collective-permute-start) | collective-permute-done | bytes 524320 | tf_op jit(solution)/shard_map/ppermute | solution.py:310
  28.0 2.0 %collective-permute-start.1 = (bf16[2,4,128,256]{3,2,1,0:T(8,128)(2,1)}, bf16[2,4,128,256]{3,2,1,0:T(8,128)(2,1)S(1)}, u32[]{:S(2)}, u32[]{:S(2)}) collective-permute-start(bf16[2,4,128,256]{3,2,1,0:T(8,128)(2,1)} %collective-permute-done.refs_4_), channel_id=1, source_target_pairs={{8,0},{16,8},{24,16},{28,24},{20,28},{12,20},{4,12},{0,4},{9,1},{1... | collective-permute-start | bytes 1572872 | tf_op jit(solution)/shard_map/ppermute | solution.py:310
  30.1 2.9 %gather.3 = (f32[2,4,256,256]{3,2,1,0:T(8,128)S(1)}, f32[2,4,256,256]{3,2,1,0:T(8,128)S(1)}, bf16[2,4,1024,256]{3,2,1,0:T(8,128)(2,1)S(1)}) custom-call(s32[10]{0:T(128)S(1)} %pad_add_fusion.info, bf16[4,256,1024]{2,1,0:T(8,128)(2,1)S(1)} %get-tuple-element.38.panel_vt, bf16[256,1024]{1,0:T(8,128)(2,1)S(1)} %get-tuple-element.36.sampler_t, ...), custom_call_target="tpu_custom_call" | custom-call | flops 805306368 | bytes 14155776 | tf_op jit(solution)/shard_map/gather/pallas_call | solution.py:278
  33.1 6.0 %collective-permute-done.6.refs_0_ = bf16[2,4,128,256]{3,2,1,0:T(8,128)(2,1)S(1)} collective-permute-done((bf16[2,4,128,256]{3,2,1,0:T(8,128)(2,1)}, bf16[2,4,128,256]{3,2,1,0:T(8,128)(2,1)S(1)}, u32[]{:S(2)}, u32[]{:S(2)}) %collective-permute-start.6) | collective-permute-done | bytes 524320 | tf_op jit(solution)/shard_map/ppermute | solution.py:310
  39.1 2.0 %collective-permute-done.7.refs_1_ = bf16[2,4,128,256]{3,2,1,0:T(8,128)(2,1)S(1)} collective-permute-done((bf16[2,4,128,256]{3,2,1,0:T(8,128)(2,1)}, bf16[2,4,128,256]{3,2,1,0:T(8,128)(2,1)S(1)}, u32[]{:S(2)}, u32[]{:S(2)}) %collective-permute-start.7) | collective-permute-done | bytes 524320 | tf_op jit(solution)/shard_map/ppermute | solution.py:311
  44.5 5.9 %collective-permute-done.1.refs_2_ = bf16[2,4,128,256]{3,2,1,0:T(8,128)(2,1)S(1)} collective-permute-done((bf16[2,4,128,256]{3,2,1,0:T(8,128)(2,1)}, bf16[2,4,128,256]{3,2,1,0:T(8,128)(2,1)S(1)}, u32[]{:S(2)}, u32[]{:S(2)}) %collective-permute-start.1) | collective-permute-done | bytes 524320 | tf_op jit(solution)/shard_map/ppermute | solution.py:310
  50.4 2.0 %collective-permute-done.3.refs_3_ = bf16[2,4,128,256]{3,2,1,0:T(8,128)(2,1)S(1)} collective-permute-done((bf16[2,4,128,256]{3,2,1,0:T(8,128)(2,1)}, bf16[2,4,128,256]{3,2,1,0:T(8,128)(2,1)S(1)}, u32[]{:S(2)}, u32[]{:S(2)}) %collective-permute-start.3) | collective-permute-done | bytes 524320 | tf_op jit(solution)/shard_map/ppermute | solution.py:311
  54.4 1.6 %gather.4 = (f32[2,4,256,256]{3,2,1,0:T(8,128)S(1)}, f32[2,4,256,256]{3,2,1,0:T(8,128)S(1)}, bf16[2,4,1024,256]{3,2,1,0:T(8,128)(2,1)S(1)}) custom-call(s32[10]{0:T(128)S(1)} %pad_add_fusion.info, bf16[4,256,1024]{2,1,0:T(8,128)(2,1)S(1)} %get-tuple-element.38.panel_vt, ...), custom_call_target="tpu_custom_call", output_to_operand_aliasing={{0}: (7, {}), {1}: (8, {}), {2}: (9, {})} | custom-call | flops 536870912 | bytes 21495808 | tf_op jit(solution)/shard_map/gather/pallas_call | solution.py:278
  56.0 5.6 %collective-permute-done.8.refs_0_ = bf16[2,4,128,256]{3,2,1,0:T(8,128)(2,1)S(1)} collective-permute-done((bf16[2,4,128,256]{3,2,1,0:T(8,128)(2,1)S(1)}, bf16[2,4,128,256]{3,2,1,0:T(8,128)(2,1)S(1)}, u32[]{:S(2)}, u32[]{:S(2)}) %collective-permute-start.8) | collective-permute-done | bytes 524320 | tf_op jit(solution)/shard_map/ppermute | solution.py:310
  61.6 2.0 %collective-permute-done.9.refs_1_ = bf16[2,4,128,256]{3,2,1,0:T(8,128)(2,1)S(1)} collective-permute-done((bf16[2,4,128,256]{3,2,1,0:T(8,128)(2,1)S(1)}, bf16[2,4,128,256]{3,2,1,0:T(8,128)(2,1)S(1)}, u32[]{:S(2)}, u32[]{:S(2)}) %collective-permute-start.9) | collective-permute-done | bytes 524320 | tf_op jit(solution)/shard_map/ppermute | solution.py:311
  63.6 1.6 %collective-permute-start.12 = (bf16[4,128,256]{2,1,0:T(8,128)(2,1)S(1)}, bf16[4,128,256]{2,1,0:T(8,128)(2,1)S(1)}, u32[]{:S(2)}, u32[]{:S(2)}) collective-permute-start(bf16[4,128,256]{2,1,0:T(8,128)(2,1)S(1)} %slice_bitcast_fusion.3), channel_id=1, source_target_pairs={{8,0},{16,8},{24,16},{28,24},{20,28},{12,20},{4,12},{0,4},{9,1},{1... | collective-permute-start | bytes 786440 | tf_op jit(solution)/shard_map/ppermute | solution.py:314
  65.8 7.1 %collective-permute-done.10.refs_2_ = bf16[2,4,128,256]{3,2,1,0:T(8,128)(2,1)S(1)} collective-permute-done((bf16[2,4,128,256]{3,2,1,0:T(8,128)(2,1)S(1)}, bf16[2,4,128,256]{3,2,1,0:T(8,128)(2,1)S(1)}, u32[]{:S(2)}, u32[]{:S(2)}) %collective-permute-start.10) | collective-permute-done | bytes 524320 | tf_op jit(solution)/shard_map/ppermute | solution.py:310
  72.9 2.0 %collective-permute-start.14 = (bf16[4,128,256]{2,1,0:T(8,128)(2,1)S(1)}, bf16[4,128,256]{2,1,0:T(8,128)(2,1)S(1)}, u32[]{:S(2)}, u32[]{:S(2)}) collective-permute-start(bf16[4,128,256]{2,1,0:T(8,128)(2,1)S(1)} %slice_bitcast_fusion.1), channel_id=1, source_target_pairs={{8,0},{16,8},{24,16},{28,24},{20,28},{12,20},{4,12},{0,4},{9,1},{1... | collective-permute-start | bytes 786440 | tf_op jit(solution)/shard_map/ppermute | solution.py:314
  75.3 1.6 %gather.5 = (f32[2,4,256,256]{3,2,1,0:T(8,128)S(1)}, f32[2,4,256,256]{3,2,1,0:T(8,128)S(1)}, bf16[2,4,1024,256]{3,2,1,0:T(8,128)(2,1)S(1)}) custom-call(s32[10]{0:T(128)S(1)} %pad_add_fusion.info, bf16[4,256,1024]{2,1,0:T(8,128)(2,1)S(1)} %get-tuple-element.38.panel_vt, ...), custom_call_target="tpu_custom_call", output_to_operand_aliasing={{0}: (7, {}), {1}: (8, {}), {2}: (9, {})} | custom-call | flops 536870912 | bytes 21495808 | tf_op jit(solution)/shard_map/gather/pallas_call | solution.py:278
  78.5 2.0 %collective-permute-done.13.refs_1_ = bf16[4,128,256]{2,1,0:T(8,128)(2,1)S(1)} collective-permute-done((bf16[4,128,256]{2,1,0:T(8,128)(2,1)S(1)}, bf16[4,128,256]{2,1,0:T(8,128)(2,1)S(1)}, u32[]{:S(2)}, u32[]{:S(2)}) %collective-permute-start.13) | collective-permute-done | bytes 262176 | tf_op jit(solution)/shard_map/ppermute | solution.py:315
  81.5 1.8 %collective-permute-done.14.refs_0_ = bf16[4,128,256]{2,1,0:T(8,128)(2,1)S(1)} collective-permute-done((bf16[4,128,256]{2,1,0:T(8,128)(2,1)S(1)}, bf16[4,128,256]{2,1,0:T(8,128)(2,1)S(1)}, u32[]{:S(2)}, u32[]{:S(2)}) %collective-permute-start.14) | collective-permute-done | bytes 262176 | tf_op jit(solution)/shard_map/ppermute | solution.py:314
  84.6 1.7 %update.3 = (bf16[4,256,256]{2,1,0:T(8,128)(2,1)S(1)}, bf16[256,1024]{1,0:T(8,128)(2,1)S(1)}) custom-call(s32[10]{0:T(128)S(1)} %pad_add_fusion.info, s32[1,4]{1,0:T(1,128)S(1)} %copy-done.11, s32[2,4]{1,0:T(2,128)S(1)} %copy-done.10, bf16[2,4,256,256]{3,2,1,0:T(8,128)(2,1)S(1)} %sampled.1, f32[2,4,256,256]{3,2,1,0:T(8,128)S(1)} %get-tuple-element.54.met, ...), custom_call_target="tpu_custom_call" | custom-call | flops 1342177280 | bytes 8912896 | tf_op jit(solution)/shard_map/update/pallas_call | solution.py:278
  86.4 1.7 %update.2 = (bf16[4,256,256]{2,1,0:T(8,128)(2,1)S(1)}, f32[256,1024]{1,0:T(8,128)S(1)}) custom-call(s32[10]{0:T(128)S(1)} %pad_add_fusion.info, s32[1,4]{1,0:T(1,128)S(1)} %copy-done.11, s32[2,4]{1,0:T(2,128)S(1)} %copy-done.10, bf16[2,4,256,256]{3,2,1,0:T(8,128)(2,1)S(1)} %sampled.1, f32[2,4,256,256]{3,2,1,0:T(8,128)S(1)} %get-tuple-element.54.met, ...), custom_call_target="tpu_custom_call" | custom-call | flops 1342177280 | bytes 9437184 | tf_op jit(solution)/shard_map/update/pallas_call | solution.py:278
  88.5 1.6 %collective-permute-start.17 = (bf16[256,1024]{1,0:T(8,128)(2,1)S(1)}, bf16[256,1024]{1,0:T(8,128)(2,1)S(1)}, u32[]{:S(2)}, u32[]{:S(2)}) collective-permute-start(bf16[256,1024]{1,0:T(8,128)(2,1)S(1)} %add_convert_fusion), channel_id=1, source_target_pairs={{0,2},{1,3},{2,0},{3,1},{4,6},{5,7},{6,4},{7,5},{8,10},{9,11},{10,... | collective-permute-start | bytes 1572872 | tf_op jit(solution)/shard_map/ppermute | solution.py:361
  90.0 12.6 %collective-permute-done.17.refs_2_ = bf16[256,1024]{1,0:T(8,128)(2,1)S(1)} collective-permute-done((bf16[256,1024]{1,0:T(8,128)(2,1)S(1)}, bf16[256,1024]{1,0:T(8,128)(2,1)S(1)}, u32[]{:S(2)}, u32[]{:S(2)}) %collective-permute-start.17) | collective-permute-done | bytes 524320 | tf_op jit(solution)/shard_map/ppermute | solution.py:361
  102.7 10.7 %orthonormal.1 = (bf16[256,1024]{1,0:T(8,128)(2,1)S(1)}, f32[256,256]{1,0:T(8,128)S(1)}, f32[256,256]{1,0:T(8,128)}) custom-call(s32[10]{0:T(128)S(1)} %pad_add_fusion.info, f32[256,1024]{1,0:T(8,128)S(1)} %start.1, f32[256,1024]{1,0:T(8,128)S(1)} %get-tuple-element.55.refs_0_, bf16[256,1024]{1,0:T(8,128)(2,1)S(1)} %collective-permute-done.16.refs_1_, ...), custom_call_target="tpu_custom_call" | custom-call | flops 17179869184 | bytes 4194304 | tf_op jit(solution)/shard_map/orthonormal/pallas_call | solution.py:278
  114.5 3.6 %project.2 = (bf16[2,256,256]{2,1,0:T(8,128)(2,1)}, f32[2,256,256]{2,1,0:T(8,128)S(1)}) custom-call(s32[10]{0:T(128)S(1)} %pad_add_fusion.info, bf16[256,1024]{1,0:T(8,128)(2,1)S(1)} %get-tuple-element.59.qt, bf16[4,1024,256]{2,1,0:T(8,128)(2,1)S(1)} %bitcast.24, bf16[4,256,256]{2,1,0:T(8,128)(2,1)S(1)} %get-tuple-element.60.cross, ...), custom_call_target="tpu_custom_call" | custom-call | flops 3623878656 | bytes 8650752 | tf_op jit(solution)/shard_map/project/pallas_call | solution.py:278
  118.2 3.8 %project.3 = (bf16[2,256,256]{2,1,0:T(8,128)(2,1)}, f32[2,256,256]{2,1,0:T(8,128)S(1)}) custom-call(s32[10]{0:T(128)S(1)} %pad_add_fusion.info, bf16[256,1024]{1,0:T(8,128)(2,1)S(1)} %collective-permute-done.19.qt_other.qt, bf16[4,1024,256]{2,1,0:T(8,128)(2,1)S(1)} %bitcast.25, bf16[4,256,256]{2,1,0:T(8,128)(2,1)S(1)} %get-tuple-element.66.cross, ...), custom_call_target="tpu_custom_call" | custom-call | flops 3623878656 | bytes 8650752 | tf_op jit(solution)/shard_map/project/pallas_call | solution.py:278
  122.5 2.1 %maximum_select_fusion = f32[2,1,256,256]{3,2,1,0:T(8,128)} fusion(f32[1,1,256,256]{3,2,1,0:T(8,128)} %bitcast.12, f32[1,1,256,256]{3,2,1,0:T(8,128)} %bitcast.30, pred[]{:T(512)S(6)} %eq.4), kind=kLoop, calls=%fused_computation.1 | loop fusion | flops 393216 | bytes 1048577 | tf_op jit(solution)/shard_map/jit(_where)/select_n | solution.py:395
  126.7 2.2 %own.1 = f32[2,256,256]{2,1,0:T(8,128)S(1)} custom-call(s32[10]{0:T(128)S(1)} %pad_add_fusion.info, bf16[256,1024]{1,0:T(8,128)(2,1)S(1)} %copy-done.6, bf16[256,1024]{1,0:T(8,128)(2,1)S(1)} %copy-done.8, bf16[2,1024,256]{2,1,0:T(8,128)(2,1)S(1)} %bitcast.27, bf16[2,1024,256]{2,1,0:T(8,128)(2,1)S(1)} %bitcast.29), custom_call_target="tpu_custom_call" | custom-call | flops 536870912 | bytes 1572864 | tf_op jit(solution)/shard_map/own/pallas_call | solution.py:278
  129.9 1.6 %collective-permute-start.22 = (bf16[2,256,256]{2,1,0:T(8,128)(2,1)S(1)}, bf16[2,256,256]{2,1,0:T(8,128)(2,1)S(1)}, u32[]{:S(2)}, u32[]{:S(2)}) collective-permute-start(bf16[2,256,256]{2,1,0:T(8,128)(2,1)S(1)} %halve.1), channel_id=1, source_target_pairs={{0,2},{1,3},{2,0},{3,1},{4,6},{5,7},{6,4},{7,5},{8,10},{9,11},{10,... | collective-permute-start | bytes 786440 | tf_op jit(solution)/shard_map/ppermute | solution.py:361
  132.6 5.6 %collective-permute-done.22 = bf16[2,256,256]{2,1,0:T(8,128)(2,1)S(1)} collective-permute-done((bf16[2,256,256]{2,1,0:T(8,128)(2,1)S(1)}, bf16[2,256,256]{2,1,0:T(8,128)(2,1)S(1)}, u32[]{:S(2)}, u32[]{:S(2)}) %collective-permute-start.22) | collective-permute-done | bytes 262176 | tf_op jit(solution)/shard_map/ppermute | solution.py:361
  (66 shorter events, 20.6 us)
Async XLA Ops:
  0.6 16.1 %collective-permute-start.4 = (bf16[2,4,128,256]{3,2,1,0:T(8,128)(2,1)}, bf16[2,4,128,256]{3,2,1,0:T(8,128)(2,1)}, u32[]{:S(2)}, u32[]{:S(2)}) collective-permute-start(bf16[2,4,128,256]{3,2,1,0:T(8,128)(2,1)} %refs_0_.1), channel_id=1, source_target_pairs={{8,0},{16,8},{24,16},{28,24},{20,28},{12,20},{4,12},{0,4},{9,1},{1... | collective-permute-start | bytes 1572872 | tf_op jit(solution)/shard_map/ppermute | solution.py:310
  3.6 15.2 %collective-permute-start.5 = (bf16[2,4,128,256]{3,2,1,0:T(8,128)(2,1)}, bf16[2,4,128,256]{3,2,1,0:T(8,128)(2,1)}, u32[]{:S(2)}, u32[]{:S(2)}) collective-permute-start(bf16[2,4,128,256]{3,2,1,0:T(8,128)(2,1)} %refs_0_.1), channel_id=1, source_target_pairs={{0,8},{8,16},{16,24},{24,28},{28,20},{20,12},{12,4},{4,0},{1,9},{9... | collective-permute-start | bytes 1572872 | tf_op jit(solution)/shard_map/ppermute | solution.py:311
  3.8 24.2 %collective-permute-start = (bf16[2,4,128,256]{3,2,1,0:T(8,128)(2,1)}, bf16[2,4,128,256]{3,2,1,0:T(8,128)(2,1)}, u32[]{:S(2)}, u32[]{:S(2)}) collective-permute-start(bf16[2,4,128,256]{3,2,1,0:T(8,128)(2,1)} %refs_3_.1), channel_id=1, source_target_pairs={{8,0},{16,8},{24,16},{28,24},{20,28},{12,20},{4,12},{0,4},{9,1},{1... | collective-permute-start | bytes 1572872 | tf_op jit(solution)/shard_map/ppermute | solution.py:310
  5.6 24.4 %collective-permute-start.2 = (bf16[2,4,128,256]{3,2,1,0:T(8,128)(2,1)}, bf16[2,4,128,256]{3,2,1,0:T(8,128)(2,1)}, u32[]{:S(2)}, u32[]{:S(2)}) collective-permute-start(bf16[2,4,128,256]{3,2,1,0:T(8,128)(2,1)} %refs_3_.1), channel_id=1, source_target_pairs={{0,8},{8,16},{16,24},{24,28},{28,20},{20,12},{12,4},{4,0},{1,9},{9... | collective-permute-start | bytes 1572872 | tf_op jit(solution)/shard_map/ppermute | solution.py:311
  16.8 22.4 %collective-permute-start.6 = (bf16[2,4,128,256]{3,2,1,0:T(8,128)(2,1)}, bf16[2,4,128,256]{3,2,1,0:T(8,128)(2,1)S(1)}, u32[]{:S(2)}, u32[]{:S(2)}) collective-permute-start(bf16[2,4,128,256]{3,2,1,0:T(8,128)(2,1)} %collective-permute-done.4.refs_1_), channel_id=1, source_target_pairs={{8,0},{16,8},{24,16},{28,24},{20,28},{12,20},{4,12},{0,4},{9,1},{1... | collective-permute-start | bytes 1572872 | tf_op jit(solution)/shard_map/ppermute | solution.py:310
  18.8 22.4 %collective-permute-start.7 = (bf16[2,4,128,256]{3,2,1,0:T(8,128)(2,1)}, bf16[2,4,128,256]{3,2,1,0:T(8,128)(2,1)S(1)}, u32[]{:S(2)}, u32[]{:S(2)}) collective-permute-start(bf16[2,4,128,256]{3,2,1,0:T(8,128)(2,1)} %collective-permute-done.5.refs_2_), channel_id=1, source_target_pairs={{0,8},{8,16},{16,24},{24,28},{28,20},{20,12},{12,4},{4,0},{1,9},{9... | collective-permute-start | bytes 1572872 | tf_op jit(solution)/shard_map/ppermute | solution.py:311
  22.3 7.8 %copy-start.3 = (bf16[2,4,128,256]{3,2,1,0:T(8,128)(2,1)S(1)}, bf16[2,4,128,256]{3,2,1,0:T(8,128)(2,1)}, u32[]{:S(2)}) copy-start(bf16[2,4,128,256]{3,2,1,0:T(8,128)(2,1)} %refs_0_.1) | copy-start | bytes 1572868
  22.3 7.8 %copy-start.4 = (bf16[2,4,128,256]{3,2,1,0:T(8,128)(2,1)S(1)}, bf16[2,4,128,256]{3,2,1,0:T(8,128)(2,1)}, u32[]{:S(2)}) copy-start(bf16[2,4,128,256]{3,2,1,0:T(8,128)(2,1)} %refs_3_.1) | copy-start | bytes 1572868
  28.0 22.4 %collective-permute-start.1 = (bf16[2,4,128,256]{3,2,1,0:T(8,128)(2,1)}, bf16[2,4,128,256]{3,2,1,0:T(8,128)(2,1)S(1)}, u32[]{:S(2)}, u32[]{:S(2)}) collective-permute-start(bf16[2,4,128,256]{3,2,1,0:T(8,128)(2,1)} %collective-permute-done.refs_4_), channel_id=1, source_target_pairs={{8,0},{16,8},{24,16},{28,24},{20,28},{12,20},{4,12},{0,4},{9,1},{1... | collective-permute-start | bytes 1572872 | tf_op jit(solution)/shard_map/ppermute | solution.py:310
  30.0 22.4 %collective-permute-start.3 = (bf16[2,4,128,256]{3,2,1,0:T(8,128)(2,1)}, bf16[2,4,128,256]{3,2,1,0:T(8,128)(2,1)S(1)}, u32[]{:S(2)}, u32[]{:S(2)}) collective-permute-start(bf16[2,4,128,256]{3,2,1,0:T(8,128)(2,1)} %collective-permute-done.2.refs_5_), channel_id=1, source_target_pairs={{0,8},{8,16},{16,24},{24,28},{28,20},{20,12},{12,4},{4,0},{1,9},{9... | collective-permute-start | bytes 1572872 | tf_op jit(solution)/shard_map/ppermute | solution.py:311
  30.1 13.0 %copy-start.1 = (bf16[2,1,1024,256]{3,2,1,0:T(8,128)(2,1)S(1)}, bf16[2,1,1024,256]{3,2,1,0:T(8,128)(2,1)}, u32[]{:S(2)}) copy-start(bf16[2,1,1024,256]{3,2,1,0:T(8,128)(2,1)} %param.16) | copy-start | bytes 3145732
  30.1 13.0 %copy-start.2 = (bf16[2,1,1024,256]{3,2,1,0:T(8,128)(2,1)S(1)}, bf16[2,1,1024,256]{3,2,1,0:T(8,128)(2,1)}, u32[]{:S(2)}) copy-start(bf16[2,1,1024,256]{3,2,1,0:T(8,128)(2,1)} %param.17) | copy-start | bytes 3145732
  41.1 20.5 %collective-permute-start.8 = (bf16[2,4,128,256]{3,2,1,0:T(8,128)(2,1)S(1)}, bf16[2,4,128,256]{3,2,1,0:T(8,128)(2,1)S(1)}, u32[]{:S(2)}, u32[]{:S(2)}) collective-permute-start(bf16[2,4,128,256]{3,2,1,0:T(8,128)(2,1)S(1)} %collective-permute-done.6.refs_0_), channel_id=1, source_target_pairs={{8,0},{16,8},{24,16},{28,24},{20,28},{12,20},{4,12},{0,4},{9,1},{1... | collective-permute-start | bytes 1572872 | tf_op jit(solution)/shard_map/ppermute | solution.py:310
  42.7 20.9 %collective-permute-start.9 = (bf16[2,4,128,256]{3,2,1,0:T(8,128)(2,1)S(1)}, bf16[2,4,128,256]{3,2,1,0:T(8,128)(2,1)S(1)}, u32[]{:S(2)}, u32[]{:S(2)}) collective-permute-start(bf16[2,4,128,256]{3,2,1,0:T(8,128)(2,1)S(1)} %collective-permute-done.7.refs_1_), channel_id=1, source_target_pairs={{0,8},{8,16},{16,24},{24,28},{28,20},{20,12},{12,4},{4,0},{1,9},{9... | collective-permute-start | bytes 1572872 | tf_op jit(solution)/shard_map/ppermute | solution.py:311
  52.4 20.5 %collective-permute-start.10 = (bf16[2,4,128,256]{3,2,1,0:T(8,128)(2,1)S(1)}, bf16[2,4,128,256]{3,2,1,0:T(8,128)(2,1)S(1)}, u32[]{:S(2)}, u32[]{:S(2)}) collective-permute-start(bf16[2,4,128,256]{3,2,1,0:T(8,128)(2,1)S(1)} %collective-permute-done.1.refs_2_), channel_id=1, source_target_pairs={{8,0},{16,8},{24,16},{28,24},{20,28},{12,20},{4,12},{0,4},{9,1},{1... | collective-permute-start | bytes 1572872 | tf_op jit(solution)/shard_map/ppermute | solution.py:310
  54.0 20.9 %collective-permute-start.11 = (bf16[2,4,128,256]{3,2,1,0:T(8,128)(2,1)S(1)}, bf16[2,4,128,256]{3,2,1,0:T(8,128)(2,1)S(1)}, u32[]{:S(2)}, u32[]{:S(2)}) collective-permute-start(bf16[2,4,128,256]{3,2,1,0:T(8,128)(2,1)S(1)} %collective-permute-done.3.refs_3_), channel_id=1, source_target_pairs={{0,8},{8,16},{16,24},{24,28},{28,20},{20,12},{12,4},{4,0},{1,9},{9... | collective-permute-start | bytes 1572872 | tf_op jit(solution)/shard_map/ppermute | solution.py:311
  63.6 14.8 %collective-permute-start.12 = (bf16[4,128,256]{2,1,0:T(8,128)(2,1)S(1)}, bf16[4,128,256]{2,1,0:T(8,128)(2,1)S(1)}, u32[]{:S(2)}, u32[]{:S(2)}) collective-permute-start(bf16[4,128,256]{2,1,0:T(8,128)(2,1)S(1)} %slice_bitcast_fusion.3), channel_id=1, source_target_pairs={{8,0},{16,8},{24,16},{28,24},{20,28},{12,20},{4,12},{0,4},{9,1},{1... | collective-permute-start | bytes 786440 | tf_op jit(solution)/shard_map/ppermute | solution.py:314
  65.3 15.2 %collective-permute-start.13 = (bf16[4,128,256]{2,1,0:T(8,128)(2,1)S(1)}, bf16[4,128,256]{2,1,0:T(8,128)(2,1)S(1)}, u32[]{:S(2)}, u32[]{:S(2)}) collective-permute-start(bf16[4,128,256]{2,1,0:T(8,128)(2,1)S(1)} %slice_bitcast_fusion.2), channel_id=1, source_target_pairs={{0,8},{8,16},{16,24},{24,28},{28,20},{20,12},{12,4},{4,0},{1,9},{9... | collective-permute-start | bytes 786440 | tf_op jit(solution)/shard_map/ppermute | solution.py:315
  72.9 10.4 %collective-permute-start.14 = (bf16[4,128,256]{2,1,0:T(8,128)(2,1)S(1)}, bf16[4,128,256]{2,1,0:T(8,128)(2,1)S(1)}, u32[]{:S(2)}, u32[]{:S(2)}) collective-permute-start(bf16[4,128,256]{2,1,0:T(8,128)(2,1)S(1)} %slice_bitcast_fusion.1), channel_id=1, source_target_pairs={{8,0},{16,8},{24,16},{28,24},{20,28},{12,20},{4,12},{0,4},{9,1},{1... | collective-permute-start | bytes 786440 | tf_op jit(solution)/shard_map/ppermute | solution.py:314
  74.9 9.7 %collective-permute-start.15 = (bf16[4,128,256]{2,1,0:T(8,128)(2,1)S(1)}, bf16[4,128,256]{2,1,0:T(8,128)(2,1)S(1)}, u32[]{:S(2)}, u32[]{:S(2)}) collective-permute-start(bf16[4,128,256]{2,1,0:T(8,128)(2,1)S(1)} %slice_bitcast_fusion), channel_id=1, source_target_pairs={{0,8},{8,16},{16,24},{24,28},{28,20},{20,12},{12,4},{4,0},{1,9},{9... | collective-permute-start | bytes 786440 | tf_op jit(solution)/shard_map/ppermute | solution.py:315
  80.5 4.2 %copy-start = (bf16[1,4,1024,256]{3,2,1,0:T(8,128)(2,1)S(1)}, bf16[1,4,1024,256]{3,2,1,0:T(8,128)(2,1)}, u32[]{:S(2)}) copy-start(bf16[1,4,1024,256]{3,2,1,0:T(8,128)(2,1)} %param.10) | copy-start | bytes 6291460
  80.5 4.2 %copy-start.10 = (s32[2,4]{1,0:T(2,128)S(1)}, s32[2,4]{1,0:T(2,128)}, u32[]{:S(2)}) copy-start(s32[2,4]{1,0:T(2,128)} %pivot_rank.3) | copy-start | bytes 100
  80.5 4.2 %copy-start.11 = (s32[1,4]{1,0:T(1,128)S(1)}, s32[1,4]{1,0:T(1,128)}, u32[]{:S(2)}) copy-start(s32[1,4]{1,0:T(1,128)} %panel_rank.3) | copy-start | bytes 52
  86.3 2.0 %collective-permute-start.16 = (bf16[256,1024]{1,0:T(8,128)(2,1)S(1)}, bf16[256,1024]{1,0:T(8,128)(2,1)S(1)}, u32[]{:S(2)}, u32[]{:S(2)}) collective-permute-start(bf16[256,1024]{1,0:T(8,128)(2,1)S(1)} %get-tuple-element.56), channel_id=1, source_target_pairs={{0,1},{1,0},{2,3},{3,2},{4,5},{5,4},{6,7},{7,6},{8,9},{9,8},{10,11... | collective-permute-start | bytes 1572872 | tf_op jit(solution)/shard_map/ppermute | solution.py:424
  88.5 14.2 %collective-permute-start.17 = (bf16[256,1024]{1,0:T(8,128)(2,1)S(1)}, bf16[256,1024]{1,0:T(8,128)(2,1)S(1)}, u32[]{:S(2)}, u32[]{:S(2)}) collective-permute-start(bf16[256,1024]{1,0:T(8,128)(2,1)S(1)} %add_convert_fusion), channel_id=1, source_target_pairs={{0,2},{1,3},{2,0},{3,1},{4,6},{5,7},{6,4},{7,5},{8,10},{9,11},{10,... | collective-permute-start | bytes 1572872 | tf_op jit(solution)/shard_map/ppermute | solution.py:361
  114.0 4.1 %copy-start.5 = (bf16[256,1024]{1,0:T(8,128)(2,1)}, bf16[256,1024]{1,0:T(8,128)(2,1)S(1)}, u32[]{:S(2)}) copy-start(bf16[256,1024]{1,0:T(8,128)(2,1)S(1)} %get-tuple-element.59.qt) | copy-start | bytes 1572868
  114.0 4.1 %collective-permute-start.19 = (bf16[256,1024]{1,0:T(8,128)(2,1)S(1)}, bf16[256,1024]{1,0:T(8,128)(2,1)S(1)}, u32[]{:S(2)}, u32[]{:S(2)}) collective-permute-start(bf16[256,1024]{1,0:T(8,128)(2,1)S(1)} %get-tuple-element.59.qt), channel_id=1, source_target_pairs={{0,1},{1,0},{2,3},{3,2},{4,5},{5,4},{6,7},{7,6},{8,9},{9,8},{10,11... | collective-permute-start | bytes 1572872 | tf_op jit(solution)/shard_map/ppermute | solution.py:433
  114.0 8.5 %collective-permute-start.18 = (f32[256,256]{1,0:T(8,128)}, f32[256,256]{1,0:T(8,128)}, u32[]{:S(2)}, u32[]{:S(2)}) collective-permute-start(f32[256,256]{1,0:T(8,128)} %get-tuple-element.58), channel_id=1, source_target_pairs={{0,1},{1,0},{2,3},{3,2},{4,5},{5,4},{6,7},{7,6},{8,9},{9,8},{10,11... | collective-permute-start | bytes 786440 | tf_op jit(solution)/shard_map/ppermute | solution.py:434
  118.2 3.8 %copy-start.7 = (bf16[256,1024]{1,0:T(8,128)(2,1)}, bf16[256,1024]{1,0:T(8,128)(2,1)S(1)}, u32[]{:S(2)}) copy-start(bf16[256,1024]{1,0:T(8,128)(2,1)S(1)} %collective-permute-done.19.qt_other.qt) | copy-start | bytes 1572868
  122.0 6.9 %collective-permute-start.20 = (bf16[2,256,256]{2,1,0:T(8,128)(2,1)}, bf16[2,256,256]{2,1,0:T(8,128)(2,1)S(1)}, u32[]{:S(2)}, u32[]{:S(2)}) collective-permute-start(bf16[2,256,256]{2,1,0:T(8,128)(2,1)} %get-tuple-element.67), channel_id=1, source_target_pairs={{0,1},{1,0},{2,3},{3,2},{4,5},{5,4},{6,7},{7,6},{8,9},{9,8},{10,11... | collective-permute-start | bytes 786440 | tf_op jit(solution)/shard_map/ppermute | solution.py:438
  122.0 6.9 %collective-permute-start.21 = (bf16[2,256,256]{2,1,0:T(8,128)(2,1)}, bf16[2,256,256]{2,1,0:T(8,128)(2,1)}, u32[]{:S(2)}, u32[]{:S(2)}) collective-permute-start(bf16[2,256,256]{2,1,0:T(8,128)(2,1)} %get-tuple-element.69), channel_id=1, source_target_pairs={{0,1},{1,0},{2,3},{3,2},{4,5},{5,4},{6,7},{7,6},{8,9},{9,8},{10,11... | collective-permute-start | bytes 786440 | tf_op jit(solution)/shard_map/ppermute | solution.py:438
  129.9 8.3 %collective-permute-start.22 = (bf16[2,256,256]{2,1,0:T(8,128)(2,1)S(1)}, bf16[2,256,256]{2,1,0:T(8,128)(2,1)S(1)}, u32[]{:S(2)}, u32[]{:S(2)}) collective-permute-start(bf16[2,256,256]{2,1,0:T(8,128)(2,1)S(1)} %halve.1), channel_id=1, source_target_pairs={{0,2},{1,3},{2,0},{3,1},{4,6},{5,7},{6,4},{7,5},{8,10},{9,11},{10,... | collective-permute-start | bytes 786440 | tf_op jit(solution)/shard_map/ppermute | solution.py:361
  (5 other events, 5.4 us)

commit v3 on v2

--- a/solution.py
+++ b/solution.py
@@ -169,7 +169,7 @@
 
 
 def sampled_kernel(places, blocks, info, sampled, sampler_t, *refs):
-    late, out = refs[:-1], refs[-1]
+    late, (out, u_all) = refs[: len(refs) - 3], refs[-2:]
     slab = sampler_t.shape[1] // blocks
     for c in range(out.shape[0]):
         for j in range(out.shape[1]):
@@ -177,6 +177,7 @@
             for place in places:
                 span = pl.ds(pl.multiple_of(info[2 + place] * slab, 128), slab)
                 total += dot(sampler_t[:, span], late[c][j])
+                u_all[c, j, place * slab : (place + 1) * slab, :] = late[c][j]
             out[c, j] = total.astype(BF16)
 
 
@@ -204,8 +205,7 @@
         out[:, at : at + half] = total.astype(out.dtype)
 
 
-def project_kernel(places, blocks, own_column, info, qt, panel_u, cross, u_all, *refs):
-    give, keep, work = refs[-3:]
+def project_kernel(blocks, own_column, info, qt, panel_u, cross, u_all, give, keep, work):
     _, priors, order, width = u_all.shape
     slab = order // blocks
     pairs, share, _ = keep.shape
@@ -215,17 +215,11 @@
     for j in range(priors):
         inner = dot(qt[...], panel_u[j]).astype(BF16)
         mids.append(dot(inner, cross[j]).astype(BF16))
-
-    def rows_of(j, b):
-        if b in places:
-            return jnp.where(column == 0, refs[0][j], refs[1][j])
-        return u_all[column, j, b * slab : (b + 1) * slab, :]
-
     some = max(1, blocks // 2)
     for begin in range(0, blocks, some):
         total = jnp.zeros((some * slab, width), F32)
         for j in range(priors):
-            total += dot11(jnp.concatenate([rows_of(j, begin + n) for n in range(some)], 0), mids[j])
+            total += dot11(u_all[column, j, begin * slab : (begin + some) * slab, :], mids[j])
         for n in range(some):
             place = pl.ds(pl.multiple_of(info[2 + begin + n] * slab, SUB), slab)
             work[place, :] = total[n * slab : (n + 1) * slab, :]
@@ -235,19 +229,22 @@
             out[a] = work[place, :].astype(out.dtype)
 
 
-def own_kernel(info, qt, qt_other, orig_u, orig_v, out, u_buf, v_buf, sems):
+def own_kernel(info, qt, qt_other, keep_b, keep_a, give_a, give_b, orig_u, orig_v, out, u_buf, v_buf, sems):
     share = out.shape[1]
+    pair = info[1] // 2
     rows = pl.ds(pl.multiple_of(info[1] * share, 16), share)
+    work = ((1 - info[0], qt_other, keep_b, give_a), (info[0], qt, keep_a, give_b))
     copies = []
-    for n, column in enumerate((1 - info[0], info[0])):
+    for n, (column, *_) in enumerate(work):
         copies.append(pltpu.make_async_copy(orig_u.at[column], u_buf.at[n], sems.at[2 * n]))
         copies.append(pltpu.make_async_copy(orig_v.at[column, rows], v_buf.at[n], sems.at[2 * n + 1]))
     for copy in copies:
         copy.start()
-    for n, q in enumerate((qt_other, qt)):
+    for n, (column, q, keep, recv) in enumerate(work):
         copies[2 * n].wait()
         copies[2 * n + 1].wait()
-        out[n] = dot11(v_buf[n], dot(q[...], u_buf[n]).astype(BF16))
+        total = dot11(v_buf[n], dot(q[...], u_buf[n]).astype(BF16))
+        out[column] = total - (keep[pair] + recv[pair].astype(F32))
 
 
 def halve_kernel(info, keep_b, keep_a, give_a, give_b, *sent):
@@ -386,7 +383,7 @@
 
     def projected(own_column, qt, cross):
         return run(
-            functools.partial(project_kernel, places, blocks, own_column), [info], [qt, panel_u, cross, u_all, *late_u],
+            functools.partial(project_kernel, blocks, own_column), [info], [qt, panel_u, cross, u_all],
             [((pairs, share, width), BF16), ((pairs, share, width), F32)], [pltpu.VMEM((order, width), F32)],
             20, 3 * priors * square * (2 * order + width), "project"
         )
@@ -416,9 +413,10 @@
                 new_u, new_v = ([now.found[t][p] for p in places] for t in range(2))
                 kept = list(gathered(places, count, new_u, new_v, kept))
         sampled, met, u_all = kept
-    (sampled,) = run(
-        functools.partial(sampled_kernel, places, blocks), [info], [sampled, sampler_t, *late_u],
-        [((pivots, priors, width, width), BF16)], [], 12, square * order, "sampled"
+    sampled, u_all = run(
+        functools.partial(sampled_kernel, places, blocks), [info], [sampled, sampler_t, *late_u, u_all],
+        [((pivots, priors, width, width), BF16), ((pivots, priors, order, width), BF16)], [], 16, square * order,
+        "sampled", {3 + len(late_u): 1}
     )
     cross_other, give = updated(False, sampled, met)
     recv = lax.ppermute(give, "cols", swap)
@@ -441,17 +439,13 @@
         halve_kernel, [info], [keep_b, keep_a, give_a, give_b], [((pivots, share, width), BF16)] * (pairs - 1), [], 8,
         square, "halve"
     )
+    rows, qt, *sent = lax.optimization_barrier((rows, qt, *sent))
     recv = [shifted(each, shift) for shift, each in enumerate(sent, 1)]
-    (own,) = run(
-        own_kernel, [info], [qt, qt_other], [((pivots, share, width), F32)],
+    (coeff,) = run(
+        own_kernel, [info], [qt, qt_other, keep_b, keep_a, give_a, give_b], [((pivots, share, width), F32)],
         [pltpu.VMEM((pivots, order, width), BF16), pltpu.VMEM((pivots, share, width), BF16), pltpu.SemaphoreType.DMA((4,))],
         12, 4 * square * order, "own", apart=[orig_u, orig_v]
     )
-    other, mine = (
-        own[n] - (lax.dynamic_index_in_dim(keep, pair, 0, False) + lax.dynamic_index_in_dim(part, pair, 0, False).astype(F32))
-        for n, (keep, part) in enumerate(((keep_b, give_a), (keep_a, give_b)))
-    )
-    coeff = lax.optimization_barrier(placed(mine, other))
     for each in recv:
         coeff = coeff - jnp.where(core == 0, each[::-1], each).astype(F32)
     basis = placed(rows, rows_other)

time: 139 us -> 135 us (0.971)
  waiting for transfers between devices: 71.8 us -> 67.1 us
  local copies, waits for them, and re-layouts: 6.23 us -> 7.92 us
    ppermute x2, waiting for transfers between devices: 18.3 us -> 12.6 us  [shifted(): lax.ppermute(x, 'cols', [(i, (i + 2 * shift) % cols) for i in range(cols)])]
    unnamed x28 -> x34, local copies, waits for them, and re-layouts: 5.46 us -> 7.15 us
  transfers between devices with their start and end apart: 23 -> 23, of which waited for: 16 -> 16; matrix products, arithmetic and copies ran while one was open for 3% -> 2% of each run, Pallas kernels for 15% -> 15%
where the time goes in v3:
time: 135 us
  waiting for transfers between devices  67.1 us (50%)
  Pallas kernels  32.8 us (24%)
  starting transfers between devices  22.2 us (16%)
  local copies, waits for them, and re-layouts  7.92 us (6%)
  other arithmetic  4.02 us (3%)
    ppermute x6, waiting for transfers between devices, step(): self.up[t] = found[number] = lax.ppermute(self.up[t], self.axis, self.ahead)  40.4 us
    pallas_call x13, Pallas kernels, run(): pl.pallas_call(kernel, out_shape=shapes, in_specs=[smem] * len(scalars) +...  32.8 us
    ppermute x2, waiting for transfers between devices, shifted(): lax.ppermute(x, 'cols', [(i, (i + 2 * shift) % cols) for i in range(cols)])  12.6 us
    ppermute x6, starting transfers between devices, step(): self.up[t] = found[number] = lax.ppermute(self.up[t], self.axis, self.ahead)  12 us
    unnamed x34, local copies, waits for them, and re-layouts  7.15 us
    ppermute x6, waiting for transfers between devices, step(): lax.ppermute(self.down[t], self.axis, self.behind)  6.1 us
    ppermute x2, starting transfers between devices, step(): lax.ppermute(self.up[t][0], self.axis, self.ahead)  3.65 us
    ppermute x2, waiting for transfers between devices, step(): lax.ppermute(self.down[t][1], self.axis, self.behind)  3.38 us
  transfers between devices with their start and end apart: 23, of which 16 were waited for; matrix products, arithmetic and copies ran while one was open for 2% of the time, Pallas kernels for 15%

profile of v3, /device:TPU:0, one launch (start us, length us, event | category | flops | bytes accessed | tf_op | source)
XLA Modules:
  0.0 134.9 jit_solution(4336983341221069498)
XLA Ops:
  0.6 3.0 %collective-permute-start.4 = (bf16[2,4,128,256]{3,2,1,0:T(8,128)(2,1)}, bf16[2,4,128,256]{3,2,1,0:T(8,128)(2,1)}, u32[]{:S(2)}, u32[]{:S(2)}) collective-permute-start(bf16[2,4,128,256]{3,2,1,0:T(8,128)(2,1)} %refs_0_.1), channel_id=1, source_target_pairs={{8,0},{16,8},{24,16},{28,24},{20,28},{12,20},{4,12},{0,4},{9,1},{1... | collective-permute-start | bytes 1572872 | tf_op jit(solution)/shard_map/ppermute | solution.py:307
  3.8 1.9 %collective-permute-start = (bf16[2,4,128,256]{3,2,1,0:T(8,128)(2,1)}, bf16[2,4,128,256]{3,2,1,0:T(8,128)(2,1)}, u32[]{:S(2)}, u32[]{:S(2)}) collective-permute-start(bf16[2,4,128,256]{3,2,1,0:T(8,128)(2,1)} %refs_3_.1), channel_id=1, source_target_pairs={{8,0},{16,8},{24,16},{28,24},{20,28},{12,20},{4,12},{0,4},{9,1},{1... | collective-permute-start | bytes 1572872 | tf_op jit(solution)/shard_map/ppermute | solution.py:307
  5.8 11.0 %collective-permute-done.4.refs_1_ = bf16[2,4,128,256]{3,2,1,0:T(8,128)(2,1)} collective-permute-done((bf16[2,4,128,256]{3,2,1,0:T(8,128)(2,1)}, bf16[2,4,128,256]{3,2,1,0:T(8,128)(2,1)}, u32[]{:S(2)}, u32[]{:S(2)}) %collective-permute-start.4) | collective-permute-done | bytes 524320 | tf_op jit(solution)/shard_map/ppermute | solution.py:307
  16.8 2.0 %collective-permute-start.6 = (bf16[2,4,128,256]{3,2,1,0:T(8,128)(2,1)}, bf16[2,4,128,256]{3,2,1,0:T(8,128)(2,1)S(1)}, u32[]{:S(2)}, u32[]{:S(2)}) collective-permute-start(bf16[2,4,128,256]{3,2,1,0:T(8,128)(2,1)} %collective-permute-done.4.refs_1_), channel_id=1, source_target_pairs={{8,0},{16,8},{24,16},{28,24},{20,28},{12,20},{4,12},{0,4},{9,1},{1... | collective-permute-start | bytes 1572872 | tf_op jit(solution)/shard_map/ppermute | solution.py:307
  19.7 1.6 %copy-done.15 = bf16[1,4,1024,256]{3,2,1,0:T(8,128)(2,1)S(1)} copy-done((bf16[1,4,1024,256]{3,2,1,0:T(8,128)(2,1)S(1)}, bf16[1,4,1024,256]{3,2,1,0:T(8,128)(2,1)}, u32[]{:S(2)}) %copy-start.15) | copy-done | bytes 2097176
  23.1 4.9 %collective-permute-done.refs_4_ = bf16[2,4,128,256]{3,2,1,0:T(8,128)(2,1)} collective-permute-done((bf16[2,4,128,256]{3,2,1,0:T(8,128)(2,1)}, bf16[2,4,128,256]{3,2,1,0:T(8,128)(2,1)}, u32[]{:S(2)}, u32[]{:S(2)}) %collective-permute-start) | collective-permute-done | bytes 524320 | tf_op jit(solution)/shard_map/ppermute | solution.py:307
  28.0 2.0 %collective-permute-start.1 = (bf16[2,4,128,256]{3,2,1,0:T(8,128)(2,1)}, bf16[2,4,128,256]{3,2,1,0:T(8,128)(2,1)S(1)}, u32[]{:S(2)}, u32[]{:S(2)}) collective-permute-start(bf16[2,4,128,256]{3,2,1,0:T(8,128)(2,1)} %collective-permute-done.refs_4_), channel_id=1, source_target_pairs={{8,0},{16,8},{24,16},{28,24},{20,28},{12,20},{4,12},{0,4},{9,1},{1... | collective-permute-start | bytes 1572872 | tf_op jit(solution)/shard_map/ppermute | solution.py:307
  30.1 3.0 %gather.3 = (f32[2,4,256,256]{3,2,1,0:T(8,128)S(1)}, f32[2,4,256,256]{3,2,1,0:T(8,128)S(1)}, bf16[2,4,1024,256]{3,2,1,0:T(8,128)(2,1)S(1)}) custom-call(s32[10]{0:T(128)S(1)} %pad_add_fusion.info, bf16[4,256,1024]{2,1,0:T(8,128)(2,1)S(1)} %get-tuple-element.43.panel_vt, bf16[256,1024]{1,0:T(8,128)(2,1)S(1)} %get-tuple-element.41.sampler_t, ...), custom_call_target="tpu_custom_call" | custom-call | flops 805306368 | bytes 14155776 | tf_op jit(solution)/shard_map/gather/pallas_call | solution.py:275
  33.1 6.0 %collective-permute-done.6.refs_0_ = bf16[2,4,128,256]{3,2,1,0:T(8,128)(2,1)S(1)} collective-permute-done((bf16[2,4,128,256]{3,2,1,0:T(8,128)(2,1)}, bf16[2,4,128,256]{3,2,1,0:T(8,128)(2,1)S(1)}, u32[]{:S(2)}, u32[]{:S(2)}) %collective-permute-start.6) | collective-permute-done | bytes 524320 | tf_op jit(solution)/shard_map/ppermute | solution.py:307
  39.1 2.0 %collective-permute-done.7.refs_1_ = bf16[2,4,128,256]{3,2,1,0:T(8,128)(2,1)S(1)} collective-permute-done((bf16[2,4,128,256]{3,2,1,0:T(8,128)(2,1)}, bf16[2,4,128,256]{3,2,1,0:T(8,128)(2,1)S(1)}, u32[]{:S(2)}, u32[]{:S(2)}) %collective-permute-start.7) | collective-permute-done | bytes 524320 | tf_op jit(solution)/shard_map/ppermute | solution.py:308
  41.1 1.6 %collective-permute-start.8 = (bf16[2,4,128,256]{3,2,1,0:T(8,128)(2,1)S(1)}, bf16[2,4,128,256]{3,2,1,0:T(8,128)(2,1)S(1)}, u32[]{:S(2)}, u32[]{:S(2)}) collective-permute-start(bf16[2,4,128,256]{3,2,1,0:T(8,128)(2,1)S(1)} %collective-permute-done.6.refs_0_), channel_id=1, source_target_pairs={{8,0},{16,8},{24,16},{28,24},{20,28},{12,20},{4,12},{0,4},{9,1},{1... | collective-permute-start | bytes 1572872 | tf_op jit(solution)/shard_map/ppermute | solution.py:307
  44.5 5.9 %collective-permute-done.1.refs_2_ = bf16[2,4,128,256]{3,2,1,0:T(8,128)(2,1)S(1)} collective-permute-done((bf16[2,4,128,256]{3,2,1,0:T(8,128)(2,1)}, bf16[2,4,128,256]{3,2,1,0:T(8,128)(2,1)S(1)}, u32[]{:S(2)}, u32[]{:S(2)}) %collective-permute-start.1) | collective-permute-done | bytes 524320 | tf_op jit(solution)/shard_map/ppermute | solution.py:307
  50.4 2.0 %collective-permute-done.3.refs_3_ = bf16[2,4,128,256]{3,2,1,0:T(8,128)(2,1)S(1)} collective-permute-done((bf16[2,4,128,256]{3,2,1,0:T(8,128)(2,1)}, bf16[2,4,128,256]{3,2,1,0:T(8,128)(2,1)S(1)}, u32[]{:S(2)}, u32[]{:S(2)}) %collective-permute-start.3) | collective-permute-done | bytes 524320 | tf_op jit(solution)/shard_map/ppermute | solution.py:308
  54.4 1.6 %gather.4 = (f32[2,4,256,256]{3,2,1,0:T(8,128)S(1)}, f32[2,4,256,256]{3,2,1,0:T(8,128)S(1)}, bf16[2,4,1024,256]{3,2,1,0:T(8,128)(2,1)S(1)}) custom-call(s32[10]{0:T(128)S(1)} %pad_add_fusion.info, bf16[4,256,1024]{2,1,0:T(8,128)(2,1)S(1)} %get-tuple-element.43.panel_vt, ...), custom_call_target="tpu_custom_call", output_to_operand_aliasing={{0}: (7, {}), {1}: (8, {}), {2}: (9, {})} | custom-call | flops 536870912 | bytes 21495808 | tf_op jit(solution)/shard_map/gather/pallas_call | solution.py:275
  56.1 5.5 %collective-permute-done.8.refs_0_ = bf16[2,4,128,256]{3,2,1,0:T(8,128)(2,1)S(1)} collective-permute-done((bf16[2,4,128,256]{3,2,1,0:T(8,128)(2,1)S(1)}, bf16[2,4,128,256]{3,2,1,0:T(8,128)(2,1)S(1)}, u32[]{:S(2)}, u32[]{:S(2)}) %collective-permute-start.8) | collective-permute-done | bytes 524320 | tf_op jit(solution)/shard_map/ppermute | solution.py:307
  61.6 2.0 %collective-permute-done.9.refs_1_ = bf16[2,4,128,256]{3,2,1,0:T(8,128)(2,1)S(1)} collective-permute-done((bf16[2,4,128,256]{3,2,1,0:T(8,128)(2,1)S(1)}, bf16[2,4,128,256]{3,2,1,0:T(8,128)(2,1)S(1)}, u32[]{:S(2)}, u32[]{:S(2)}) %collective-permute-start.9) | collective-permute-done | bytes 524320 | tf_op jit(solution)/shard_map/ppermute | solution.py:308
  63.6 1.6 %collective-permute-start.12 = (bf16[4,128,256]{2,1,0:T(8,128)(2,1)S(1)}, bf16[4,128,256]{2,1,0:T(8,128)(2,1)S(1)}, u32[]{:S(2)}, u32[]{:S(2)}) collective-permute-start(bf16[4,128,256]{2,1,0:T(8,128)(2,1)S(1)} %slice_bitcast_fusion.3), channel_id=1, source_target_pairs={{8,0},{16,8},{24,16},{28,24},{20,28},{12,20},{4,12},{0,4},{9,1},{1... | collective-permute-start | bytes 786440 | tf_op jit(solution)/shard_map/ppermute | solution.py:311
  65.8 7.1 %collective-permute-done.10.refs_2_ = bf16[2,4,128,256]{3,2,1,0:T(8,128)(2,1)S(1)} collective-permute-done((bf16[2,4,128,256]{3,2,1,0:T(8,128)(2,1)S(1)}, bf16[2,4,128,256]{3,2,1,0:T(8,128)(2,1)S(1)}, u32[]{:S(2)}, u32[]{:S(2)}) %collective-permute-start.10) | collective-permute-done | bytes 524320 | tf_op jit(solution)/shard_map/ppermute | solution.py:307
  72.9 2.0 %collective-permute-start.14 = (bf16[4,128,256]{2,1,0:T(8,128)(2,1)S(1)}, bf16[4,128,256]{2,1,0:T(8,128)(2,1)S(1)}, u32[]{:S(2)}, u32[]{:S(2)}) collective-permute-start(bf16[4,128,256]{2,1,0:T(8,128)(2,1)S(1)} %slice_bitcast_fusion.1), channel_id=1, source_target_pairs={{8,0},{16,8},{24,16},{28,24},{20,28},{12,20},{4,12},{0,4},{9,1},{1... | collective-permute-start | bytes 786440 | tf_op jit(solution)/shard_map/ppermute | solution.py:311
  75.3 1.6 %gather.5 = (f32[2,4,256,256]{3,2,1,0:T(8,128)S(1)}, f32[2,4,256,256]{3,2,1,0:T(8,128)S(1)}, bf16[2,4,1024,256]{3,2,1,0:T(8,128)(2,1)S(1)}) custom-call(s32[10]{0:T(128)S(1)} %pad_add_fusion.info, bf16[4,256,1024]{2,1,0:T(8,128)(2,1)S(1)} %get-tuple-element.43.panel_vt, ...), custom_call_target="tpu_custom_call", output_to_operand_aliasing={{0}: (7, {}), {1}: (8, {}), {2}: (9, {})} | custom-call | flops 536870912 | bytes 21495808 | tf_op jit(solution)/shard_map/gather/pallas_call | solution.py:275
  78.5 2.0 %collective-permute-done.13.refs_1_ = bf16[4,128,256]{2,1,0:T(8,128)(2,1)S(1)} collective-permute-done((bf16[4,128,256]{2,1,0:T(8,128)(2,1)S(1)}, bf16[4,128,256]{2,1,0:T(8,128)(2,1)S(1)}, u32[]{:S(2)}, u32[]{:S(2)}) %collective-permute-start.13) | collective-permute-done | bytes 262176 | tf_op jit(solution)/shard_map/ppermute | solution.py:312
  81.5 1.8 %collective-permute-done.14.refs_0_ = bf16[4,128,256]{2,1,0:T(8,128)(2,1)S(1)} collective-permute-done((bf16[4,128,256]{2,1,0:T(8,128)(2,1)S(1)}, bf16[4,128,256]{2,1,0:T(8,128)(2,1)S(1)}, u32[]{:S(2)}, u32[]{:S(2)}) %collective-permute-start.14) | collective-permute-done | bytes 262176 | tf_op jit(solution)/shard_map/ppermute | solution.py:311
  84.6 1.7 %update.3 = (bf16[4,256,256]{2,1,0:T(8,128)(2,1)S(1)}, bf16[256,1024]{1,0:T(8,128)(2,1)S(1)}) custom-call(s32[10]{0:T(128)S(1)} %pad_add_fusion.info, s32[1,4]{1,0:T(1,128)S(1)} %copy-done.14, s32[2,4]{1,0:T(2,128)S(1)} %copy-done.13, bf16[2,4,256,256]{3,2,1,0:T(8,128)(2,1)S(1)} %get-tuple-element.60.sampled, f32[2,4,256,256]{3,2,1,0:T(8,128)S(1)} %get-tuple-element.61.met, ...), custom_call_target="tpu_custom_call" | custom-call | flops 1342177280 | bytes 8912896 | tf_op jit(solution)/shard_map/update/pallas_call | solution.py:275
  86.4 1.7 %update.2 = (bf16[4,256,256]{2,1,0:T(8,128)(2,1)S(1)}, f32[256,1024]{1,0:T(8,128)S(1)}) custom-call(s32[10]{0:T(128)S(1)} %pad_add_fusion.info, s32[1,4]{1,0:T(1,128)S(1)} %copy-done.14, s32[2,4]{1,0:T(2,128)S(1)} %copy-done.13, bf16[2,4,256,256]{3,2,1,0:T(8,128)(2,1)S(1)} %get-tuple-element.60.sampled, f32[2,4,256,256]{3,2,1,0:T(8,128)S(1)} %get-tuple-element.61.met, ...), custom_call_target="tpu_custom_call" | custom-call | flops 1342177280 | bytes 9437184 | tf_op jit(solution)/shard_map/update/pallas_call | solution.py:275
  88.5 1.6 %collective-permute-start.17 = (bf16[256,1024]{1,0:T(8,128)(2,1)S(1)}, bf16[256,1024]{1,0:T(8,128)(2,1)S(1)}, u32[]{:S(2)}, u32[]{:S(2)}) collective-permute-start(bf16[256,1024]{1,0:T(8,128)(2,1)S(1)} %add_convert_fusion), channel_id=1, source_target_pairs={{0,2},{1,3},{2,0},{3,1},{4,6},{5,7},{6,4},{7,5},{8,10},{9,11},{10,... | collective-permute-start | bytes 1572872 | tf_op jit(solution)/shard_map/ppermute | solution.py:358
  90.1 12.6 %collective-permute-done.17.refs_2_ = bf16[256,1024]{1,0:T(8,128)(2,1)S(1)} collective-permute-done((bf16[256,1024]{1,0:T(8,128)(2,1)S(1)}, bf16[256,1024]{1,0:T(8,128)(2,1)S(1)}, u32[]{:S(2)}, u32[]{:S(2)}) %collective-permute-start.17) | collective-permute-done | bytes 524320 | tf_op jit(solution)/shard_map/ppermute | solution.py:358
  102.7 10.7 %orthonormal.1 = (bf16[256,1024]{1,0:T(8,128)(2,1)S(1)}, f32[256,256]{1,0:T(8,128)S(1)}, f32[256,256]{1,0:T(8,128)}) custom-call(s32[10]{0:T(128)S(1)} %pad_add_fusion.info, f32[256,1024]{1,0:T(8,128)S(1)} %start.1, f32[256,1024]{1,0:T(8,128)S(1)} %get-tuple-element.62.refs_0_, bf16[256,1024]{1,0:T(8,128)(2,1)S(1)} %collective-permute-done.16.refs_1_, ...), custom_call_target="tpu_custom_call" | custom-call | flops 17179869184 | bytes 4194304 | tf_op jit(solution)/shard_map/orthonormal/pallas_call | solution.py:275
  114.1 2.9 %project.2 = (bf16[2,256,256]{2,1,0:T(8,128)(2,1)S(1)}, f32[2,256,256]{2,1,0:T(8,128)S(1)}) custom-call(s32[10]{0:T(128)S(1)} %pad_add_fusion.info, bf16[256,1024]{1,0:T(8,128)(2,1)S(1)} %get-tuple-element.78.qt, bf16[4,1024,256]{2,1,0:T(8,128)(2,1)S(1)} %bitcast.24, bf16[4,256,256]{2,1,0:T(8,128)(2,1)S(1)} %get-tuple-element.66.cross, ...), custom_call_target="tpu_custom_call" | custom-call | flops 3623878656 | bytes 8126464 | tf_op jit(solution)/shard_map/project/pallas_call | solution.py:275
  117.6 3.1 %project.3 = (bf16[2,256,256]{2,1,0:T(8,128)(2,1)S(1)}, f32[2,256,256]{2,1,0:T(8,128)S(1)}) custom-call(s32[10]{0:T(128)S(1)} %pad_add_fusion.info, bf16[256,1024]{1,0:T(8,128)(2,1)S(1)} %collective-permute-done.18.qt.qt_other, bf16[4,1024,256]{2,1,0:T(8,128)(2,1)S(1)} %bitcast.25, bf16[4,256,256]{2,1,0:T(8,128)(2,1)S(1)} %get-tuple-element.71.cross, ...), custom_call_target="tpu_custom_call" | custom-call | flops 3623878656 | bytes 8126464 | tf_op jit(solution)/shard_map/project/pallas_call | solution.py:275
  128.9 2.2 %own.1 = f32[2,256,256]{2,1,0:T(8,128)S(1)} custom-call(s32[10]{0:T(128)S(1)} %pad_add_fusion.info, bf16[256,1024]{1,0:T(8,128)(2,1)S(1)} %copy-done.8, bf16[256,1024]{1,0:T(8,128)(2,1)S(1)} %copy-done.10, f32[2,256,256]{2,1,0:T(8,128)S(1)} %get-tuple-element.72.keep_b, f32[2,256,256]{2,1,0:T(8,128)S(1)} %get-tuple-element.73.keep_a, ...), custom_call_target="tpu_custom_call" | custom-call | flops 536870912 | bytes 3145728 | tf_op jit(solution)/shard_map/own/pallas_call | solution.py:275
  131.1 1.9 %maximum_select_fusion = f32[2,1,256,256]{3,2,1,0:T(8,128)} fusion(f32[1,1,256,256]{3,2,1,0:T(8,128)} %bitcast.12, f32[1,1,256,256]{3,2,1,0:T(8,128)S(1)} %bitcast.30, pred[]{:T(512)S(6)} %eq.6), kind=kLoop, calls=%fused_computation.1 | loop fusion | flops 393216 | bytes 1048577 | tf_op jit(solution)/shard_map/jit(_where)/select_n | solution.py:392
  133.0 1.9 %subtract_bitcast_fusion = f32[2,1,256,256]{3,2,1,0:T(8,128)} fusion(f32[2,256,256]{2,1,0:T(8,128)S(1)} %own.1, bf16[2,256,256]{2,1,0:T(8,128)(2,1)} %collective-permute-done.22, pred[]{:T(512)S(6)} %eq.6), kind=kLoop, calls=%fused_computation.2 | loop fusion | flops 393216 | bytes 1310721
  (70 shorter events, 21.7 us)
Async XLA Ops:
  0.6 16.1 %collective-permute-start.4 = (bf16[2,4,128,256]{3,2,1,0:T(8,128)(2,1)}, bf16[2,4,128,256]{3,2,1,0:T(8,128)(2,1)}, u32[]{:S(2)}, u32[]{:S(2)}) collective-permute-start(bf16[2,4,128,256]{3,2,1,0:T(8,128)(2,1)} %refs_0_.1), channel_id=1, source_target_pairs={{8,0},{16,8},{24,16},{28,24},{20,28},{12,20},{4,12},{0,4},{9,1},{1... | collective-permute-start | bytes 1572872 | tf_op jit(solution)/shard_map/ppermute | solution.py:307
  3.6 15.2 %collective-permute-start.5 = (bf16[2,4,128,256]{3,2,1,0:T(8,128)(2,1)}, bf16[2,4,128,256]{3,2,1,0:T(8,128)(2,1)}, u32[]{:S(2)}, u32[]{:S(2)}) collective-permute-start(bf16[2,4,128,256]{3,2,1,0:T(8,128)(2,1)} %refs_0_.1), channel_id=1, source_target_pairs={{0,8},{8,16},{16,24},{24,28},{28,20},{20,12},{12,4},{4,0},{1,9},{9... | collective-permute-start | bytes 1572872 | tf_op jit(solution)/shard_map/ppermute | solution.py:308
  3.8 24.2 %collective-permute-start = (bf16[2,4,128,256]{3,2,1,0:T(8,128)(2,1)}, bf16[2,4,128,256]{3,2,1,0:T(8,128)(2,1)}, u32[]{:S(2)}, u32[]{:S(2)}) collective-permute-start(bf16[2,4,128,256]{3,2,1,0:T(8,128)(2,1)} %refs_3_.1), channel_id=1, source_target_pairs={{8,0},{16,8},{24,16},{28,24},{20,28},{12,20},{4,12},{0,4},{9,1},{1... | collective-permute-start | bytes 1572872 | tf_op jit(solution)/shard_map/ppermute | solution.py:307
  5.6 24.4 %collective-permute-start.2 = (bf16[2,4,128,256]{3,2,1,0:T(8,128)(2,1)}, bf16[2,4,128,256]{3,2,1,0:T(8,128)(2,1)}, u32[]{:S(2)}, u32[]{:S(2)}) collective-permute-start(bf16[2,4,128,256]{3,2,1,0:T(8,128)(2,1)} %refs_3_.1), channel_id=1, source_target_pairs={{0,8},{8,16},{16,24},{24,28},{28,20},{20,12},{12,4},{4,0},{1,9},{9... | collective-permute-start | bytes 1572872 | tf_op jit(solution)/shard_map/ppermute | solution.py:308
  16.8 22.4 %collective-permute-start.6 = (bf16[2,4,128,256]{3,2,1,0:T(8,128)(2,1)}, bf16[2,4,128,256]{3,2,1,0:T(8,128)(2,1)S(1)}, u32[]{:S(2)}, u32[]{:S(2)}) collective-permute-start(bf16[2,4,128,256]{3,2,1,0:T(8,128)(2,1)} %collective-permute-done.4.refs_1_), channel_id=1, source_target_pairs={{8,0},{16,8},{24,16},{28,24},{20,28},{12,20},{4,12},{0,4},{9,1},{1... | collective-permute-start | bytes 1572872 | tf_op jit(solution)/shard_map/ppermute | solution.py:307
  18.8 22.4 %collective-permute-start.7 = (bf16[2,4,128,256]{3,2,1,0:T(8,128)(2,1)}, bf16[2,4,128,256]{3,2,1,0:T(8,128)(2,1)S(1)}, u32[]{:S(2)}, u32[]{:S(2)}) collective-permute-start(bf16[2,4,128,256]{3,2,1,0:T(8,128)(2,1)} %collective-permute-done.5.refs_2_), channel_id=1, source_target_pairs={{0,8},{8,16},{16,24},{24,28},{28,20},{20,12},{12,4},{4,0},{1,9},{9... | collective-permute-start | bytes 1572872 | tf_op jit(solution)/shard_map/ppermute | solution.py:308
  22.3 7.8 %copy-start.5 = (bf16[2,4,128,256]{3,2,1,0:T(8,128)(2,1)S(1)}, bf16[2,4,128,256]{3,2,1,0:T(8,128)(2,1)}, u32[]{:S(2)}) copy-start(bf16[2,4,128,256]{3,2,1,0:T(8,128)(2,1)} %refs_0_.1) | copy-start | bytes 1572868
  22.3 7.8 %copy-start.6 = (bf16[2,4,128,256]{3,2,1,0:T(8,128)(2,1)S(1)}, bf16[2,4,128,256]{3,2,1,0:T(8,128)(2,1)}, u32[]{:S(2)}) copy-start(bf16[2,4,128,256]{3,2,1,0:T(8,128)(2,1)} %refs_3_.1) | copy-start | bytes 1572868
  28.0 22.4 %collective-permute-start.1 = (bf16[2,4,128,256]{3,2,1,0:T(8,128)(2,1)}, bf16[2,4,128,256]{3,2,1,0:T(8,128)(2,1)S(1)}, u32[]{:S(2)}, u32[]{:S(2)}) collective-permute-start(bf16[2,4,128,256]{3,2,1,0:T(8,128)(2,1)} %collective-permute-done.refs_4_), channel_id=1, source_target_pairs={{8,0},{16,8},{24,16},{28,24},{20,28},{12,20},{4,12},{0,4},{9,1},{1... | collective-permute-start | bytes 1572872 | tf_op jit(solution)/shard_map/ppermute | solution.py:307
  30.0 22.4 %collective-permute-start.3 = (bf16[2,4,128,256]{3,2,1,0:T(8,128)(2,1)}, bf16[2,4,128,256]{3,2,1,0:T(8,128)(2,1)S(1)}, u32[]{:S(2)}, u32[]{:S(2)}) collective-permute-start(bf16[2,4,128,256]{3,2,1,0:T(8,128)(2,1)} %collective-permute-done.2.refs_5_), channel_id=1, source_target_pairs={{0,8},{8,16},{16,24},{24,28},{28,20},{20,12},{12,4},{4,0},{1,9},{9... | collective-permute-start | bytes 1572872 | tf_op jit(solution)/shard_map/ppermute | solution.py:308
  30.1 13.0 %copy-start.1 = (bf16[2,1,1024,256]{3,2,1,0:T(8,128)(2,1)S(1)}, bf16[2,1,1024,256]{3,2,1,0:T(8,128)(2,1)}, u32[]{:S(2)}) copy-start(bf16[2,1,1024,256]{3,2,1,0:T(8,128)(2,1)} %param.16) | copy-start | bytes 3145732
  30.1 13.0 %copy-start.2 = (bf16[2,1,1024,256]{3,2,1,0:T(8,128)(2,1)S(1)}, bf16[2,1,1024,256]{3,2,1,0:T(8,128)(2,1)}, u32[]{:S(2)}) copy-start(bf16[2,1,1024,256]{3,2,1,0:T(8,128)(2,1)} %param.17) | copy-start | bytes 3145732
  41.1 20.5 %collective-permute-start.8 = (bf16[2,4,128,256]{3,2,1,0:T(8,128)(2,1)S(1)}, bf16[2,4,128,256]{3,2,1,0:T(8,128)(2,1)S(1)}, u32[]{:S(2)}, u32[]{:S(2)}) collective-permute-start(bf16[2,4,128,256]{3,2,1,0:T(8,128)(2,1)S(1)} %collective-permute-done.6.refs_0_), channel_id=1, source_target_pairs={{8,0},{16,8},{24,16},{28,24},{20,28},{12,20},{4,12},{0,4},{9,1},{1... | collective-permute-start | bytes 1572872 | tf_op jit(solution)/shard_map/ppermute | solution.py:307
  42.7 20.9 %collective-permute-start.9 = (bf16[2,4,128,256]{3,2,1,0:T(8,128)(2,1)S(1)}, bf16[2,4,128,256]{3,2,1,0:T(8,128)(2,1)S(1)}, u32[]{:S(2)}, u32[]{:S(2)}) collective-permute-start(bf16[2,4,128,256]{3,2,1,0:T(8,128)(2,1)S(1)} %collective-permute-done.7.refs_1_), channel_id=1, source_target_pairs={{0,8},{8,16},{16,24},{24,28},{28,20},{20,12},{12,4},{4,0},{1,9},{9... | collective-permute-start | bytes 1572872 | tf_op jit(solution)/shard_map/ppermute | solution.py:308
  52.4 20.5 %collective-permute-start.10 = (bf16[2,4,128,256]{3,2,1,0:T(8,128)(2,1)S(1)}, bf16[2,4,128,256]{3,2,1,0:T(8,128)(2,1)S(1)}, u32[]{:S(2)}, u32[]{:S(2)}) collective-permute-start(bf16[2,4,128,256]{3,2,1,0:T(8,128)(2,1)S(1)} %collective-permute-done.1.refs_2_), channel_id=1, source_target_pairs={{8,0},{16,8},{24,16},{28,24},{20,28},{12,20},{4,12},{0,4},{9,1},{1... | collective-permute-start | bytes 1572872 | tf_op jit(solution)/shard_map/ppermute | solution.py:307
  54.0 20.9 %collective-permute-start.11 = (bf16[2,4,128,256]{3,2,1,0:T(8,128)(2,1)S(1)}, bf16[2,4,128,256]{3,2,1,0:T(8,128)(2,1)S(1)}, u32[]{:S(2)}, u32[]{:S(2)}) collective-permute-start(bf16[2,4,128,256]{3,2,1,0:T(8,128)(2,1)S(1)} %collective-permute-done.3.refs_3_), channel_id=1, source_target_pairs={{0,8},{8,16},{16,24},{24,28},{28,20},{20,12},{12,4},{4,0},{1,9},{9... | collective-permute-start | bytes 1572872 | tf_op jit(solution)/shard_map/ppermute | solution.py:308
  63.6 14.8 %collective-permute-start.12 = (bf16[4,128,256]{2,1,0:T(8,128)(2,1)S(1)}, bf16[4,128,256]{2,1,0:T(8,128)(2,1)S(1)}, u32[]{:S(2)}, u32[]{:S(2)}) collective-permute-start(bf16[4,128,256]{2,1,0:T(8,128)(2,1)S(1)} %slice_bitcast_fusion.3), channel_id=1, source_target_pairs={{8,0},{16,8},{24,16},{28,24},{20,28},{12,20},{4,12},{0,4},{9,1},{1... | collective-permute-start | bytes 786440 | tf_op jit(solution)/shard_map/ppermute | solution.py:311
  65.3 15.2 %collective-permute-start.13 = (bf16[4,128,256]{2,1,0:T(8,128)(2,1)S(1)}, bf16[4,128,256]{2,1,0:T(8,128)(2,1)S(1)}, u32[]{:S(2)}, u32[]{:S(2)}) collective-permute-start(bf16[4,128,256]{2,1,0:T(8,128)(2,1)S(1)} %slice_bitcast_fusion.2), channel_id=1, source_target_pairs={{0,8},{8,16},{16,24},{24,28},{28,20},{20,12},{12,4},{4,0},{1,9},{9... | collective-permute-start | bytes 786440 | tf_op jit(solution)/shard_map/ppermute | solution.py:312
  72.9 10.4 %collective-permute-start.14 = (bf16[4,128,256]{2,1,0:T(8,128)(2,1)S(1)}, bf16[4,128,256]{2,1,0:T(8,128)(2,1)S(1)}, u32[]{:S(2)}, u32[]{:S(2)}) collective-permute-start(bf16[4,128,256]{2,1,0:T(8,128)(2,1)S(1)} %slice_bitcast_fusion.1), channel_id=1, source_target_pairs={{8,0},{16,8},{24,16},{28,24},{20,28},{12,20},{4,12},{0,4},{9,1},{1... | collective-permute-start | bytes 786440 | tf_op jit(solution)/shard_map/ppermute | solution.py:311
  74.9 9.7 %collective-permute-start.15 = (bf16[4,128,256]{2,1,0:T(8,128)(2,1)S(1)}, bf16[4,128,256]{2,1,0:T(8,128)(2,1)S(1)}, u32[]{:S(2)}, u32[]{:S(2)}) collective-permute-start(bf16[4,128,256]{2,1,0:T(8,128)(2,1)S(1)} %slice_bitcast_fusion), channel_id=1, source_target_pairs={{0,8},{8,16},{16,24},{24,28},{28,20},{20,12},{12,4},{4,0},{1,9},{9... | collective-permute-start | bytes 786440 | tf_op jit(solution)/shard_map/ppermute | solution.py:312
  80.5 4.2 %copy-start = (bf16[1,4,1024,256]{3,2,1,0:T(8,128)(2,1)S(1)}, bf16[1,4,1024,256]{3,2,1,0:T(8,128)(2,1)}, u32[]{:S(2)}) copy-start(bf16[1,4,1024,256]{3,2,1,0:T(8,128)(2,1)} %param.10) | copy-start | bytes 6291460
  80.5 4.2 %copy-start.13 = (s32[2,4]{1,0:T(2,128)S(1)}, s32[2,4]{1,0:T(2,128)}, u32[]{:S(2)}) copy-start(s32[2,4]{1,0:T(2,128)} %pivot_rank.3) | copy-start | bytes 100
  80.5 4.2 %copy-start.14 = (s32[1,4]{1,0:T(1,128)S(1)}, s32[1,4]{1,0:T(1,128)}, u32[]{:S(2)}) copy-start(s32[1,4]{1,0:T(1,128)} %panel_rank.3) | copy-start | bytes 52
  86.3 2.0 %collective-permute-start.16 = (bf16[256,1024]{1,0:T(8,128)(2,1)S(1)}, bf16[256,1024]{1,0:T(8,128)(2,1)S(1)}, u32[]{:S(2)}, u32[]{:S(2)}) collective-permute-start(bf16[256,1024]{1,0:T(8,128)(2,1)S(1)} %get-tuple-element.63), channel_id=1, source_target_pairs={{0,1},{1,0},{2,3},{3,2},{4,5},{5,4},{6,7},{7,6},{8,9},{9,8},{10,11... | collective-permute-start | bytes 1572872 | tf_op jit(solution)/shard_map/ppermute | solution.py:422
  88.5 14.2 %collective-permute-start.17 = (bf16[256,1024]{1,0:T(8,128)(2,1)S(1)}, bf16[256,1024]{1,0:T(8,128)(2,1)S(1)}, u32[]{:S(2)}, u32[]{:S(2)}) collective-permute-start(bf16[256,1024]{1,0:T(8,128)(2,1)S(1)} %add_convert_fusion), channel_id=1, source_target_pairs={{0,2},{1,3},{2,0},{3,1},{4,6},{5,7},{6,4},{7,5},{8,10},{9,11},{10,... | collective-permute-start | bytes 1572872 | tf_op jit(solution)/shard_map/ppermute | solution.py:358
  114.0 2.9 %copy-start.7 = (bf16[256,1024]{1,0:T(8,128)(2,1)}, bf16[256,1024]{1,0:T(8,128)(2,1)S(1)}, u32[]{:S(2)}) copy-start(bf16[256,1024]{1,0:T(8,128)(2,1)S(1)} %get-tuple-element.78.qt) | copy-start | bytes 1572868
  114.1 2.9 %collective-permute-start.18 = (bf16[256,1024]{1,0:T(8,128)(2,1)S(1)}, bf16[256,1024]{1,0:T(8,128)(2,1)S(1)}, u32[]{:S(2)}, u32[]{:S(2)}) collective-permute-start(bf16[256,1024]{1,0:T(8,128)(2,1)S(1)} %get-tuple-element.78.qt), channel_id=1, source_target_pairs={{0,1},{1,0},{2,3},{3,2},{4,5},{5,4},{6,7},{7,6},{8,9},{9,8},{10,11... | collective-permute-start | bytes 1572872 | tf_op jit(solution)/shard_map/ppermute | solution.py:431
  117.0 3.7 %copy-start.9 = (bf16[256,1024]{1,0:T(8,128)(2,1)}, bf16[256,1024]{1,0:T(8,128)(2,1)S(1)}, u32[]{:S(2)}) copy-start(bf16[256,1024]{1,0:T(8,128)(2,1)S(1)} %collective-permute-done.18.qt.qt_other) | copy-start | bytes 1572868
  117.0 4.3 %collective-permute-start.19 = (bf16[2,256,256]{2,1,0:T(8,128)(2,1)S(1)}, bf16[2,256,256]{2,1,0:T(8,128)(2,1)S(1)}, u32[]{:S(2)}, u32[]{:S(2)}) collective-permute-start(bf16[2,256,256]{2,1,0:T(8,128)(2,1)S(1)} %get-tuple-element.74), channel_id=1, source_target_pairs={{0,1},{1,0},{2,3},{3,2},{4,5},{5,4},{6,7},{7,6},{8,9},{9,8},{10,11... | collective-permute-start | bytes 786440 | tf_op jit(solution)/shard_map/ppermute | solution.py:436
  120.7 1.6 %collective-permute-start.20 = (bf16[2,256,256]{2,1,0:T(8,128)(2,1)S(1)}, bf16[2,256,256]{2,1,0:T(8,128)(2,1)S(1)}, u32[]{:S(2)}, u32[]{:S(2)}) collective-permute-start(bf16[2,256,256]{2,1,0:T(8,128)(2,1)S(1)} %get-tuple-element.75), channel_id=1, source_target_pairs={{0,1},{1,0},{2,3},{3,2},{4,5},{5,4},{6,7},{7,6},{8,9},{9,8},{10,11... | collective-permute-start | bytes 786440 | tf_op jit(solution)/shard_map/ppermute | solution.py:436
  120.8 10.3 %collective-permute-start.21 = (f32[256,256]{1,0:T(8,128)}, f32[256,256]{1,0:T(8,128)}, u32[]{:S(2)}, u32[]{:S(2)}) collective-permute-start(f32[256,256]{1,0:T(8,128)} %get-tuple-element.77), channel_id=1, source_target_pairs={{0,1},{1,0},{2,3},{3,2},{4,5},{5,4},{6,7},{7,6},{8,9},{9,8},{10,11... | collective-permute-start | bytes 786440 | tf_op jit(solution)/shard_map/ppermute | solution.py:432
  124.3 8.7 %collective-permute-start.22 = (bf16[2,256,256]{2,1,0:T(8,128)(2,1)}, bf16[2,256,256]{2,1,0:T(8,128)(2,1)}, u32[]{:S(2)}, u32[]{:S(2)}) collective-permute-start(bf16[2,256,256]{2,1,0:T(8,128)(2,1)} %halve.1), channel_id=1, source_target_pairs={{0,2},{1,3},{2,0},{3,1},{4,6},{5,7},{6,4},{7,5},{8,10},{9,11},{10,... | collective-permute-start | bytes 786440 | tf_op jit(solution)/shard_map/ppermute | solution.py:358
  (8 other events, 9.4 us)

commit v4 on v3

--- a/solution.py
+++ b/solution.py
@@ -121,7 +121,7 @@
 
 
 def orthonormal_kernel(info, start, *refs):
-    parts, (qt, basis, given, yt, work) = refs[:-5], refs[-5:]
+    parts, (qt, given, basis, yt, work, rows, sem) = refs[:-7], refs[-7:]
     width, order = yt.shape
     core = info[0]
     total = start[...]
@@ -137,12 +137,24 @@
     m_high, m_low, _ = split3(jnp.where(col <= row, work[...], 0.0))
     high, mid, _ = split3(yt[...])
     product = dot(m_high, high) + (dot(m_high, mid) + dot(m_low, high))
+    yt[...] = product
+    share = given.shape[0]
+
+    def rows_at(index):
+        return yt[:, pl.ds(pl.multiple_of(index * share, 128), share)].T * math.sqrt(order)
+
+    rows[...] = rows_at(info[1])
+    copy = pltpu.make_async_copy(rows, basis.at[core], sem.at[0])
+    copy.start()
+    given[...] = rows_at(info[1] + 1 - 2 * core)
     qt[...] = product.astype(BF16)
-    yt[...] = product
-    share = basis.shape[0]
-    for out, index in ((basis, info[1]), (given, info[1] + 1 - 2 * core)):
-        rows = yt[:, pl.ds(pl.multiple_of(index * share, 128), share)]
-        out[...] = rows.T * math.sqrt(order)
+    copy.wait()
+
+
+def place_kernel(info, given, basis, out, sem):
+    copy = pltpu.make_async_copy(given, out.at[1 - info[0]], sem.at[0])
+    copy.start()
+    copy.wait()
 
 
 def gather_kernel(places, blocks, info, panel_vt, sampler_t, *refs):
@@ -205,12 +217,14 @@
         out[:, at : at + half] = total.astype(out.dtype)
 
 
-def project_kernel(blocks, own_column, info, qt, panel_u, cross, u_all, give, keep, work):
+def project_kernel(blocks, own_column, info, qt, panel_u, cross, u_all, orig_u, give, keep, left, work, u_buf, sem):
     _, priors, order, width = u_all.shape
     slab = order // blocks
     pairs, share, _ = keep.shape
     core = info[0]
     column = core if own_column else 1 - core
+    copy = pltpu.make_async_copy(orig_u.at[column], u_buf, sem.at[0])
+    copy.start()
     mids = []
     for j in range(priors):
         inner = dot(qt[...], panel_u[j]).astype(BF16)
@@ -227,32 +241,31 @@
         for out, which in ((give, 1 - core), (keep, core)):
             place = pl.ds(pl.multiple_of((2 * a + which) * share, SUB), share)
             out[a] = work[place, :].astype(out.dtype)
-
-
-def own_kernel(info, qt, qt_other, keep_b, keep_a, give_a, give_b, orig_u, orig_v, out, u_buf, v_buf, sems):
-    share = out.shape[1]
-    pair = info[1] // 2
-    rows = pl.ds(pl.multiple_of(info[1] * share, 16), share)
-    work = ((1 - info[0], qt_other, keep_b, give_a), (info[0], qt, keep_a, give_b))
-    copies = []
-    for n, (column, *_) in enumerate(work):
-        copies.append(pltpu.make_async_copy(orig_u.at[column], u_buf.at[n], sems.at[2 * n]))
-        copies.append(pltpu.make_async_copy(orig_v.at[column, rows], v_buf.at[n], sems.at[2 * n + 1]))
-    for copy in copies:
-        copy.start()
-    for n, (column, q, keep, recv) in enumerate(work):
-        copies[2 * n].wait()
-        copies[2 * n + 1].wait()
-        total = dot11(v_buf[n], dot(q[...], u_buf[n]).astype(BF16))
-        out[column] = total - (keep[pair] + recv[pair].astype(F32))
+    copy.wait()
+    left[...] = dot(qt[...], u_buf[...]).astype(BF16)
 
 
 def halve_kernel(info, keep_b, keep_a, give_a, give_b, *sent):
     pairs = keep_a.shape[0]
     for shift in range(1, pairs):
         a = lax.rem(info[1] // 2 + shift, pairs)
-        for n, (keep, recv) in enumerate(((keep_b, give_a), (keep_a, give_b))):
-            sent[shift - 1][n] = (keep[a] + recv[a].astype(F32)).astype(BF16)
+        for column, keep, recv in ((1 - info[0], keep_b, give_a), (info[0], keep_a, give_b)):
+            sent[shift - 1][column] = (keep[a] + recv[a].astype(F32)).astype(BF16)
+
+
+def own_kernel(info, left_b, left_a, keep_b, keep_a, give_a, give_b, orig_v, out, v_buf, sems):
+    share = out.shape[1]
+    pair = info[1] // 2
+    rows = pl.ds(pl.multiple_of(info[1] * share, 16), share)
+    work = ((1 - info[0], left_b, keep_b, give_a), (info[0], left_a, keep_a, give_b))
+    copies = [
+        pltpu.make_async_copy(orig_v.at[column, rows], v_buf.at[n], sems.at[n]) for n, (column, *_) in enumerate(work)
+    ]
+    for copy in copies:
+        copy.start()
+    for n, (column, left, keep, recv) in enumerate(work):
+        copies[n].wait()
+        out[column] = dot11(v_buf[n], left[...]) - (keep[pair] + recv[pair].astype(F32))
 
 
 def turn_kernel(panel_v, sampler, panel_vt, sampler_t):
@@ -267,7 +280,7 @@
     out[...] = dot11(proj, orig_u[core])
 
 
-def run(kernel, scalars, arrays, outs, scratch, limit, flops, name, aliases={}, apart=()):
+def run(kernel, scalars, arrays, outs, scratch, limit, flops, name, aliases={}, apart=(), away=0):
     smem = pl.BlockSpec(memory_space=pltpu.SMEM)
     vmem = pl.BlockSpec(memory_space=pltpu.VMEM)
     shapes = [jax.ShapeDtypeStruct(*o) for o in outs]
@@ -276,7 +289,7 @@
         kernel,
         out_shape=shapes,
         in_specs=[smem] * len(scalars) + [vmem] * len(arrays) + [pl.BlockSpec(memory_space=pl.ANY)] * len(apart),
-        out_specs=[vmem] * len(shapes),
+        out_specs=[vmem] * (len(shapes) - away) + [pl.BlockSpec(memory_space=pl.ANY)] * away,
         scratch_shapes=scratch,
         input_output_aliases=aliases,
         compiler_params=pltpu.CompilerParams(vmem_limit_bytes=limit * MIB),
@@ -384,12 +397,10 @@
     def projected(own_column, qt, cross):
         return run(
             functools.partial(project_kernel, blocks, own_column), [info], [qt, panel_u, cross, u_all],
-            [((pairs, share, width), BF16), ((pairs, share, width), F32)], [pltpu.VMEM((order, width), F32)],
-            20, 3 * priors * square * (2 * order + width), "project"
+            [((pairs, share, width), BF16), ((pairs, share, width), F32), ((width, width), BF16)],
+            [pltpu.VMEM((order, width), F32), pltpu.VMEM((order, width), BF16), pltpu.SemaphoreType.DMA((1,))],
+            20, 3 * priors * square * (2 * order + width), "project", apart=[orig_u]
         )
-
-    def placed(mine, other):
-        return jnp.where(core == 0, jnp.stack([mine, other]), jnp.stack([other, mine]))
 
     if whole:
         blocks, places = 1, []
@@ -423,32 +434,33 @@
     cross_own, keep = updated(True, sampled, met)
     sent = (keep + recv.astype(F32)).astype(BF16)
     parts = [keep, recv, *(shifted(sent, shift) for shift in range(1, pairs))]
-    qt, rows, given = run(
+    qt, given, basis = run(
         orthonormal_kernel, [info], [start, *parts],
-        [((width, order), BF16), ((share, width), F32), ((share, width), F32)], [tall, matrix], 16,
-        128 * square * order, "orthonormal"
+        [((width, order), BF16), ((share, width), F32), ((pivots, share, width), F32)],
+        [tall, matrix, pltpu.VMEM((share, width), F32), pltpu.SemaphoreType.DMA((1,))], 16,
+        128 * square * order, "orthonormal", away=1
     )
     qt_other = lax.ppermute(qt, "cols", swap)
-    rows_other = lax.ppermute(given, "cols", swap)
-    give_a, keep_a = projected(True, qt, cross_own)
+    give_a, keep_a, left_a = projected(True, qt, cross_own)
     qt_other, give_a, keep_a = lax.optimization_barrier((qt_other, give_a, keep_a))
-    give_b, keep_b = projected(False, qt_other, cross_other)
+    give_b, keep_b, left_b = projected(False, qt_other, cross_other)
     give_a, give_b = lax.ppermute(give_a, "cols", swap), lax.ppermute(give_b, "cols", swap)
-
     sent = run(
         halve_kernel, [info], [keep_b, keep_a, give_a, give_b], [((pivots, share, width), BF16)] * (pairs - 1), [], 8,
         square, "halve"
     )
-    rows, qt, *sent = lax.optimization_barrier((rows, qt, *sent))
+    left_b, *sent = lax.optimization_barrier((left_b, *sent))
     recv = [shifted(each, shift) for shift, each in enumerate(sent, 1)]
     (coeff,) = run(
-        own_kernel, [info], [qt, qt_other, keep_b, keep_a, give_a, give_b], [((pivots, share, width), F32)],
-        [pltpu.VMEM((pivots, order, width), BF16), pltpu.VMEM((pivots, share, width), BF16), pltpu.SemaphoreType.DMA((4,))],
-        12, 4 * square * order, "own", apart=[orig_u, orig_v]
+        own_kernel, [info], [left_b, left_a, keep_b, keep_a, give_a, give_b], [((pivots, share, width), F32)],
+        [pltpu.VMEM((pivots, share, width), BF16), pltpu.SemaphoreType.DMA((2,))], 8, square * width, "own", apart=[orig_v]
+    )
+    (basis,) = run(
+        place_kernel, [info], [lax.ppermute(given, "cols", swap)], [((pivots, share, width), F32)],
+        [pltpu.SemaphoreType.DMA((1,))], 4, 1, "place", {2: 0}, [basis], 1
     )
     for each in recv:
-        coeff = coeff - jnp.where(core == 0, each[::-1], each).astype(F32)
-    basis = placed(rows, rows_other)
+        coeff = coeff - each.astype(F32)
     return (basis[:, None], coeff[:, None])
 
 

time: 135 us -> 133 us (0.985)
  waiting for transfers between devices: 67.1 us -> 72.4 us
  local copies, waits for them, and re-layouts: 7.92 us -> 3.42 us
  other arithmetic: 4.02 us -> 1.08 us
    unnamed x34 -> x18, local copies, waits for them, and re-layouts: 7.15 us -> 2.66 us
    ppermute x2, waiting for transfers between devices: 12.6 us -> 16.8 us  [shifted(): lax.ppermute(x, 'cols', [(i, (i + 2 * shift) % cols) for i in range(cols)])]
    select_n x1 -> x0, other arithmetic: 1.88 us -> none  [placed(): jnp.where(core == 0, jnp.stack([mine, other]), jnp.stack([other, mine]))]
    pallas_call x13 -> x14, Pallas kernels: 32.8 us -> 32.3 us  [run(): pl.pallas_call(kernel, out_shape=shapes, in_specs=[smem] * len(scalars) +...]
  transfers between devices with their start and end apart: 23 -> 23, of which waited for: 16 -> 17; matrix products, arithmetic and copies ran while one was open for 2% -> 1% of each run, Pallas kernels for 15% -> 15%
where the time goes in v4:
time: 133 us; the launch traced here: 132 us
  waiting for transfers between devices  72.4 us (54%)
  Pallas kernels  32.3 us (24%)
  starting transfers between devices  22.3 us (17%)
  local copies, waits for them, and re-layouts  3.42 us (3%)
    ppermute x6, waiting for transfers between devices, step(): self.up[t] = found[number] = lax.ppermute(self.up[t], self.axis, self.ahead)  41.6 us
    pallas_call x14, Pallas kernels, run(): pl.pallas_call(kernel, out_shape=shapes, in_specs=[smem] * len(scalars) +...  32.3 us
    ppermute x2, waiting for transfers between devices, shifted(): lax.ppermute(x, 'cols', [(i, (i + 2 * shift) % cols) for i in range(cols)])  16.8 us
    ppermute x6, starting transfers between devices, step(): self.up[t] = found[number] = lax.ppermute(self.up[t], self.axis, self.ahead)  12 us
    ppermute x6, waiting for transfers between devices, step(): lax.ppermute(self.down[t], self.axis, self.behind)  6.11 us
    ppermute x2, starting transfers between devices, step(): lax.ppermute(self.up[t][0], self.axis, self.ahead)  3.65 us
    ppermute x2, waiting for transfers between devices, step(): lax.ppermute(self.down[t][1], self.axis, self.behind)  3.38 us
    ppermute x2, waiting for transfers between devices, step(): lax.ppermute(self.up[t][0], self.axis, self.ahead)  3.36 us
  transfers between devices with their start and end apart: 23, of which 17 were waited for; matrix products, arithmetic and copies ran while one was open for 1% of the time, Pallas kernels for 15%

profile of v4, /device:TPU:0, one launch (start us, length us, event | category | flops | bytes accessed | tf_op | source)
XLA Modules:
  0.0 132.4 jit_solution(13570377977650725739)
XLA Ops:
  0.6 3.0 %collective-permute-start.4 = (bf16[2,4,128,256]{3,2,1,0:T(8,128)(2,1)}, bf16[2,4,128,256]{3,2,1,0:T(8,128)(2,1)S(1)}, u32[]{:S(2)}, u32[]{:S(2)}) collective-permute-start(bf16[2,4,128,256]{3,2,1,0:T(8,128)(2,1)} %refs_0_.1), channel_id=1, source_target_pairs={{8,0},{16,8},{24,16},{28,24},{20,28},{12,20},{4,12},{0,4},{9,1},{1... | collective-permute-start | bytes 1572872 | tf_op jit(solution)/shard_map/ppermute | solution.py:320
  3.8 1.9 %collective-permute-start = (bf16[2,4,128,256]{3,2,1,0:T(8,128)(2,1)}, bf16[2,4,128,256]{3,2,1,0:T(8,128)(2,1)S(1)}, u32[]{:S(2)}, u32[]{:S(2)}) collective-permute-start(bf16[2,4,128,256]{3,2,1,0:T(8,128)(2,1)} %refs_3_.1), channel_id=1, source_target_pairs={{8,0},{16,8},{24,16},{28,24},{20,28},{12,20},{4,12},{0,4},{9,1},{1... | collective-permute-start | bytes 1572872 | tf_op jit(solution)/shard_map/ppermute | solution.py:320
  5.8 10.9 %collective-permute-done.4.refs_1_ = bf16[2,4,128,256]{3,2,1,0:T(8,128)(2,1)S(1)} collective-permute-done((bf16[2,4,128,256]{3,2,1,0:T(8,128)(2,1)}, bf16[2,4,128,256]{3,2,1,0:T(8,128)(2,1)S(1)}, u32[]{:S(2)}, u32[]{:S(2)}) %collective-permute-start.4) | collective-permute-done | bytes 524320 | tf_op jit(solution)/shard_map/ppermute | solution.py:320
  16.7 2.0 %collective-permute-start.6 = (bf16[2,4,128,256]{3,2,1,0:T(8,128)(2,1)S(1)}, bf16[2,4,128,256]{3,2,1,0:T(8,128)(2,1)S(1)}, u32[]{:S(2)}, u32[]{:S(2)}) collective-permute-start(bf16[2,4,128,256]{3,2,1,0:T(8,128)(2,1)S(1)} %collective-permute-done.4.refs_1_), channel_id=1, source_target_pairs={{8,0},{16,8},{24,16},{28,24},{20,28},{12,20},{4,12},{0,4},{9,1},{1... | collective-permute-start | bytes 1572872 | tf_op jit(solution)/shard_map/ppermute | solution.py:320
  19.6 1.6 %copy-done.7 = bf16[1,4,1024,256]{3,2,1,0:T(8,128)(2,1)S(1)} copy-done((bf16[1,4,1024,256]{3,2,1,0:T(8,128)(2,1)S(1)}, bf16[1,4,1024,256]{3,2,1,0:T(8,128)(2,1)}, u32[]{:S(2)}) %copy-start.7) | copy-done | bytes 2097176
  23.0 4.9 %collective-permute-done.refs_4_ = bf16[2,4,128,256]{3,2,1,0:T(8,128)(2,1)S(1)} collective-permute-done((bf16[2,4,128,256]{3,2,1,0:T(8,128)(2,1)}, bf16[2,4,128,256]{3,2,1,0:T(8,128)(2,1)S(1)}, u32[]{:S(2)}, u32[]{:S(2)}) %collective-permute-start) | collective-permute-done | bytes 524320 | tf_op jit(solution)/shard_map/ppermute | solution.py:320
  27.9 2.0 %collective-permute-start.1 = (bf16[2,4,128,256]{3,2,1,0:T(8,128)(2,1)S(1)}, bf16[2,4,128,256]{3,2,1,0:T(8,128)(2,1)S(1)}, u32[]{:S(2)}, u32[]{:S(2)}) collective-permute-start(bf16[2,4,128,256]{3,2,1,0:T(8,128)(2,1)S(1)} %collective-permute-done.refs_4_), channel_id=1, source_target_pairs={{8,0},{16,8},{24,16},{28,24},{20,28},{12,20},{4,12},{0,4},{9,1},{1... | collective-permute-start | bytes 1572872 | tf_op jit(solution)/shard_map/ppermute | solution.py:320
  30.0 1.8 %gather.3 = (f32[2,4,256,256]{3,2,1,0:T(8,128)S(1)}, f32[2,4,256,256]{3,2,1,0:T(8,128)S(1)}, bf16[2,4,1024,256]{3,2,1,0:T(8,128)(2,1)S(1)}) custom-call(s32[10]{0:T(128)S(1)} %pad_add_fusion.info, bf16[4,256,1024]{2,1,0:T(8,128)(2,1)S(1)} %get-tuple-element.44.panel_vt, bf16[256,1024]{1,0:T(8,128)(2,1)S(1)} %get-tuple-element.42.sampler_t, ...), custom_call_target="tpu_custom_call" | custom-call | flops 805306368 | bytes 14155776 | tf_op jit(solution)/shard_map/gather/pallas_call | solution.py:288
  31.9 7.3 %collective-permute-done.6.refs_0_ = bf16[2,4,128,256]{3,2,1,0:T(8,128)(2,1)S(1)} collective-permute-done((bf16[2,4,128,256]{3,2,1,0:T(8,128)(2,1)S(1)}, bf16[2,4,128,256]{3,2,1,0:T(8,128)(2,1)S(1)}, u32[]{:S(2)}, u32[]{:S(2)}) %collective-permute-start.6) | collective-permute-done | bytes 524320 | tf_op jit(solution)/shard_map/ppermute | solution.py:320
  39.1 2.0 %collective-permute-done.7.refs_1_ = bf16[2,4,128,256]{3,2,1,0:T(8,128)(2,1)S(1)} collective-permute-done((bf16[2,4,128,256]{3,2,1,0:T(8,128)(2,1)S(1)}, bf16[2,4,128,256]{3,2,1,0:T(8,128)(2,1)S(1)}, u32[]{:S(2)}, u32[]{:S(2)}) %collective-permute-start.7) | collective-permute-done | bytes 524320 | tf_op jit(solution)/shard_map/ppermute | solution.py:321
  41.1 1.6 %collective-permute-start.8 = (bf16[2,4,128,256]{3,2,1,0:T(8,128)(2,1)S(1)}, bf16[2,4,128,256]{3,2,1,0:T(8,128)(2,1)S(1)}, u32[]{:S(2)}, u32[]{:S(2)}) collective-permute-start(bf16[2,4,128,256]{3,2,1,0:T(8,128)(2,1)S(1)} %collective-permute-done.6.refs_0_), channel_id=1, source_target_pairs={{8,0},{16,8},{24,16},{28,24},{20,28},{12,20},{4,12},{0,4},{9,1},{1... | collective-permute-start | bytes 1572872 | tf_op jit(solution)/shard_map/ppermute | solution.py:320
  44.5 5.9 %collective-permute-done.1.refs_2_ = bf16[2,4,128,256]{3,2,1,0:T(8,128)(2,1)S(1)} collective-permute-done((bf16[2,4,128,256]{3,2,1,0:T(8,128)(2,1)S(1)}, bf16[2,4,128,256]{3,2,1,0:T(8,128)(2,1)S(1)}, u32[]{:S(2)}, u32[]{:S(2)}) %collective-permute-start.1) | collective-permute-done | bytes 524320 | tf_op jit(solution)/shard_map/ppermute | solution.py:320
  50.4 2.0 %collective-permute-done.3.refs_3_ = bf16[2,4,128,256]{3,2,1,0:T(8,128)(2,1)S(1)} collective-permute-done((bf16[2,4,128,256]{3,2,1,0:T(8,128)(2,1)S(1)}, bf16[2,4,128,256]{3,2,1,0:T(8,128)(2,1)S(1)}, u32[]{:S(2)}, u32[]{:S(2)}) %collective-permute-start.3) | collective-permute-done | bytes 524320 | tf_op jit(solution)/shard_map/ppermute | solution.py:321
  52.4 1.6 %collective-permute-start.10 = (bf16[2,4,128,256]{3,2,1,0:T(8,128)(2,1)S(1)}, bf16[2,4,128,256]{3,2,1,0:T(8,128)(2,1)S(1)}, u32[]{:S(2)}, u32[]{:S(2)}) collective-permute-start(bf16[2,4,128,256]{3,2,1,0:T(8,128)(2,1)S(1)} %collective-permute-done.1.refs_2_), channel_id=1, source_target_pairs={{8,0},{16,8},{24,16},{28,24},{20,28},{12,20},{4,12},{0,4},{9,1},{1... | collective-permute-start | bytes 1572872 | tf_op jit(solution)/shard_map/ppermute | solution.py:320
  54.4 1.6 %gather.4 = (f32[2,4,256,256]{3,2,1,0:T(8,128)S(1)}, f32[2,4,256,256]{3,2,1,0:T(8,128)S(1)}, bf16[2,4,1024,256]{3,2,1,0:T(8,128)(2,1)S(1)}) custom-call(s32[10]{0:T(128)S(1)} %pad_add_fusion.info, bf16[4,256,1024]{2,1,0:T(8,128)(2,1)S(1)} %get-tuple-element.44.panel_vt, ...), custom_call_target="tpu_custom_call", output_to_operand_aliasing={{0}: (7, {}), {1}: (8, {}), {2}: (9, {})} | custom-call | flops 536870912 | bytes 21495808 | tf_op jit(solution)/shard_map/gather/pallas_call | solution.py:288
  56.1 5.5 %collective-permute-done.8.refs_0_ = bf16[2,4,128,256]{3,2,1,0:T(8,128)(2,1)S(1)} collective-permute-done((bf16[2,4,128,256]{3,2,1,0:T(8,128)(2,1)S(1)}, bf16[2,4,128,256]{3,2,1,0:T(8,128)(2,1)S(1)}, u32[]{:S(2)}, u32[]{:S(2)}) %collective-permute-start.8) | collective-permute-done | bytes 524320 | tf_op jit(solution)/shard_map/ppermute | solution.py:320
  61.6 2.0 %collective-permute-done.9.refs_1_ = bf16[2,4,128,256]{3,2,1,0:T(8,128)(2,1)S(1)} collective-permute-done((bf16[2,4,128,256]{3,2,1,0:T(8,128)(2,1)S(1)}, bf16[2,4,128,256]{3,2,1,0:T(8,128)(2,1)S(1)}, u32[]{:S(2)}, u32[]{:S(2)}) %collective-permute-start.9) | collective-permute-done | bytes 524320 | tf_op jit(solution)/shard_map/ppermute | solution.py:321
  63.6 1.6 %collective-permute-start.12 = (bf16[4,128,256]{2,1,0:T(8,128)(2,1)S(1)}, bf16[4,128,256]{2,1,0:T(8,128)(2,1)S(1)}, u32[]{:S(2)}, u32[]{:S(2)}) collective-permute-start(bf16[4,128,256]{2,1,0:T(8,128)(2,1)S(1)} %slice_bitcast_fusion.3), channel_id=1, source_target_pairs={{8,0},{16,8},{24,16},{28,24},{20,28},{12,20},{4,12},{0,4},{9,1},{1... | collective-permute-start | bytes 786440 | tf_op jit(solution)/shard_map/ppermute | solution.py:324
  65.8 7.1 %collective-permute-done.10.refs_2_ = bf16[2,4,128,256]{3,2,1,0:T(8,128)(2,1)S(1)} collective-permute-done((bf16[2,4,128,256]{3,2,1,0:T(8,128)(2,1)S(1)}, bf16[2,4,128,256]{3,2,1,0:T(8,128)(2,1)S(1)}, u32[]{:S(2)}, u32[]{:S(2)}) %collective-permute-start.10) | collective-permute-done | bytes 524320 | tf_op jit(solution)/shard_map/ppermute | solution.py:320
  72.9 2.0 %collective-permute-start.14 = (bf16[4,128,256]{2,1,0:T(8,128)(2,1)S(1)}, bf16[4,128,256]{2,1,0:T(8,128)(2,1)S(1)}, u32[]{:S(2)}, u32[]{:S(2)}) collective-permute-start(bf16[4,128,256]{2,1,0:T(8,128)(2,1)S(1)} %slice_bitcast_fusion.1), channel_id=1, source_target_pairs={{8,0},{16,8},{24,16},{28,24},{20,28},{12,20},{4,12},{0,4},{9,1},{1... | collective-permute-start | bytes 786440 | tf_op jit(solution)/shard_map/ppermute | solution.py:324
  75.3 1.6 %gather.5 = (f32[2,4,256,256]{3,2,1,0:T(8,128)S(1)}, f32[2,4,256,256]{3,2,1,0:T(8,128)S(1)}, bf16[2,4,1024,256]{3,2,1,0:T(8,128)(2,1)S(1)}) custom-call(s32[10]{0:T(128)S(1)} %pad_add_fusion.info, bf16[4,256,1024]{2,1,0:T(8,128)(2,1)S(1)} %get-tuple-element.44.panel_vt, ...), custom_call_target="tpu_custom_call", output_to_operand_aliasing={{0}: (7, {}), {1}: (8, {}), {2}: (9, {})} | custom-call | flops 536870912 | bytes 21495808 | tf_op jit(solution)/shard_map/gather/pallas_call | solution.py:288
  78.5 2.0 %collective-permute-done.13.refs_1_ = bf16[4,128,256]{2,1,0:T(8,128)(2,1)S(1)} collective-permute-done((bf16[4,128,256]{2,1,0:T(8,128)(2,1)S(1)}, bf16[4,128,256]{2,1,0:T(8,128)(2,1)S(1)}, u32[]{:S(2)}, u32[]{:S(2)}) %collective-permute-start.13) | collective-permute-done | bytes 262176 | tf_op jit(solution)/shard_map/ppermute | solution.py:325
  81.5 1.8 %collective-permute-done.14.refs_0_ = bf16[4,128,256]{2,1,0:T(8,128)(2,1)S(1)} collective-permute-done((bf16[4,128,256]{2,1,0:T(8,128)(2,1)S(1)}, bf16[4,128,256]{2,1,0:T(8,128)(2,1)S(1)}, u32[]{:S(2)}, u32[]{:S(2)}) %collective-permute-start.14) | collective-permute-done | bytes 262176 | tf_op jit(solution)/shard_map/ppermute | solution.py:324
  84.6 1.7 %update.3 = (bf16[4,256,256]{2,1,0:T(8,128)(2,1)S(1)}, bf16[256,1024]{1,0:T(8,128)(2,1)S(1)}) custom-call(s32[10]{0:T(128)S(1)} %pad_add_fusion.info, s32[1,4]{1,0:T(1,128)S(1)} %copy-done.6, s32[2,4]{1,0:T(2,128)S(1)} %copy-done.5, bf16[2,4,256,256]{3,2,1,0:T(8,128)(2,1)S(1)} %get-tuple-element.61.sampled, f32[2,4,256,256]{3,2,1,0:T(8,128)S(1)} %get-tuple-element.62.met, ...), custom_call_target="tpu_custom_call" | custom-call | flops 1342177280 | bytes 8912896 | tf_op jit(solution)/shard_map/update/pallas_call | solution.py:288
  86.4 1.7 %update.2 = (bf16[4,256,256]{2,1,0:T(8,128)(2,1)S(1)}, f32[256,1024]{1,0:T(8,128)S(1)}) custom-call(s32[10]{0:T(128)S(1)} %pad_add_fusion.info, s32[1,4]{1,0:T(1,128)S(1)} %copy-done.6, s32[2,4]{1,0:T(2,128)S(1)} %copy-done.5, bf16[2,4,256,256]{3,2,1,0:T(8,128)(2,1)S(1)} %get-tuple-element.61.sampled, f32[2,4,256,256]{3,2,1,0:T(8,128)S(1)} %get-tuple-element.62.met, ...), custom_call_target="tpu_custom_call" | custom-call | flops 1342177280 | bytes 9437184 | tf_op jit(solution)/shard_map/update/pallas_call | solution.py:288
  88.5 1.6 %collective-permute-start.17 = (bf16[256,1024]{1,0:T(8,128)(2,1)S(1)}, bf16[256,1024]{1,0:T(8,128)(2,1)S(1)}, u32[]{:S(2)}, u32[]{:S(2)}) collective-permute-start(bf16[256,1024]{1,0:T(8,128)(2,1)S(1)} %add_convert_fusion), channel_id=1, source_target_pairs={{0,2},{1,3},{2,0},{3,1},{4,6},{5,7},{6,4},{7,5},{8,10},{9,11},{10,... | collective-permute-start | bytes 1572872 | tf_op jit(solution)/shard_map/ppermute | solution.py:371
  90.1 12.6 %collective-permute-done.17.refs_2_ = bf16[256,1024]{1,0:T(8,128)(2,1)S(1)} collective-permute-done((bf16[256,1024]{1,0:T(8,128)(2,1)S(1)}, bf16[256,1024]{1,0:T(8,128)(2,1)S(1)}, u32[]{:S(2)}, u32[]{:S(2)}) %collective-permute-start.17) | collective-permute-done | bytes 524320 | tf_op jit(solution)/shard_map/ppermute | solution.py:371
  102.7 10.6 %orthonormal.1 = (bf16[256,1024]{1,0:T(8,128)(2,1)S(1)}, f32[256,256]{1,0:T(8,128)S(1)}, f32[2,256,256]{2,1,0:T(8,128)}) custom-call(s32[10]{0:T(128)S(1)} %pad_add_fusion.info, f32[256,1024]{1,0:T(8,128)S(1)} %start.1, f32[256,1024]{1,0:T(8,128)S(1)} %get-tuple-element.63.refs_0_, bf16[256,1024]{1,0:T(8,128)(2,1)S(1)} %collective-permute-done.16.refs_1_, ...), custom_call_target="tpu_custom_call" | custom-call | flops 17179869184 | bytes 4456448 | tf_op jit(solution)/shard_map/orthonormal/pallas_call | solution.py:288
  113.4 3.6 %project.2 = (bf16[2,256,256]{2,1,0:T(8,128)(2,1)S(1)}, f32[2,256,256]{2,1,0:T(8,128)S(1)}, bf16[256,256]{1,0:T(8,128)(2,1)S(1)}) custom-call(s32[10]{0:T(128)S(1)} %pad_add_fusion.info, bf16[256,1024]{1,0:T(8,128)(2,1)S(1)} %get-tuple-element.67.qt, bf16[4,1024,256]{2,1,0:T(8,128)(2,1)S(1)} %bitcast.25, bf16[4,256,256]{2,1,0:T(8,128)(2,1)S(1)} %get-tuple-element.68.cross, ...), custom_call_target="tpu_custom_call" | custom-call | flops 3623878656 | bytes 8257536 | tf_op jit(solution)/shard_map/project/pallas_call | solution.py:288
  117.5 3.4 %project.3 = (bf16[2,256,256]{2,1,0:T(8,128)(2,1)S(1)}, f32[2,256,256]{2,1,0:T(8,128)S(1)}, bf16[256,256]{1,0:T(8,128)(2,1)S(1)}) custom-call(s32[10]{0:T(128)S(1)} %pad_add_fusion.info, bf16[256,1024]{1,0:T(8,128)(2,1)S(1)} %collective-permute-done.19.qt, bf16[4,1024,256]{2,1,0:T(8,128)(2,1)S(1)} %bitcast.26, ...), custom_call_target="tpu_custom_call" | custom-call | flops 3623878656 | bytes 8257536 | tf_op jit(solution)/shard_map/project/pallas_call | solution.py:288
  123.1 1.6 %collective-permute-start.22 = (bf16[2,256,256]{2,1,0:T(8,128)(2,1)S(1)}, bf16[2,256,256]{2,1,0:T(8,128)(2,1)S(1)}, u32[]{:S(2)}, u32[]{:S(2)}) collective-permute-start(bf16[2,256,256]{2,1,0:T(8,128)(2,1)S(1)} %halve.1), channel_id=1, source_target_pairs={{0,2},{1,3},{2,0},{3,1},{4,6},{5,7},{6,4},{7,5},{8,10},{9,11},{10,... | collective-permute-start | bytes 786440 | tf_op jit(solution)/shard_map/ppermute | solution.py:371
  127.4 4.1 %collective-permute-done.22 = bf16[2,256,256]{2,1,0:T(8,128)(2,1)S(1)} collective-permute-done((bf16[2,256,256]{2,1,0:T(8,128)(2,1)S(1)}, bf16[2,256,256]{2,1,0:T(8,128)(2,1)S(1)}, u32[]{:S(2)}, u32[]{:S(2)}) %collective-permute-start.22) | collective-permute-done | bytes 262176 | tf_op jit(solution)/shard_map/ppermute | solution.py:371
  (54 shorter events, 17.0 us)
Async XLA Ops:
  0.6 16.0 %collective-permute-start.4 = (bf16[2,4,128,256]{3,2,1,0:T(8,128)(2,1)}, bf16[2,4,128,256]{3,2,1,0:T(8,128)(2,1)S(1)}, u32[]{:S(2)}, u32[]{:S(2)}) collective-permute-start(bf16[2,4,128,256]{3,2,1,0:T(8,128)(2,1)} %refs_0_.1), channel_id=1, source_target_pairs={{8,0},{16,8},{24,16},{28,24},{20,28},{12,20},{4,12},{0,4},{9,1},{1... | collective-permute-start | bytes 1572872 | tf_op jit(solution)/shard_map/ppermute | solution.py:320
  3.6 15.1 %collective-permute-start.5 = (bf16[2,4,128,256]{3,2,1,0:T(8,128)(2,1)}, bf16[2,4,128,256]{3,2,1,0:T(8,128)(2,1)S(1)}, u32[]{:S(2)}, u32[]{:S(2)}) collective-permute-start(bf16[2,4,128,256]{3,2,1,0:T(8,128)(2,1)} %refs_0_.1), channel_id=1, source_target_pairs={{0,8},{8,16},{16,24},{24,28},{28,20},{20,12},{12,4},{4,0},{1,9},{9... | collective-permute-start | bytes 1572872 | tf_op jit(solution)/shard_map/ppermute | solution.py:321
  3.8 24.1 %collective-permute-start = (bf16[2,4,128,256]{3,2,1,0:T(8,128)(2,1)}, bf16[2,4,128,256]{3,2,1,0:T(8,128)(2,1)S(1)}, u32[]{:S(2)}, u32[]{:S(2)}) collective-permute-start(bf16[2,4,128,256]{3,2,1,0:T(8,128)(2,1)} %refs_3_.1), channel_id=1, source_target_pairs={{8,0},{16,8},{24,16},{28,24},{20,28},{12,20},{4,12},{0,4},{9,1},{1... | collective-permute-start | bytes 1572872 | tf_op jit(solution)/shard_map/ppermute | solution.py:320
  5.6 24.3 %collective-permute-start.2 = (bf16[2,4,128,256]{3,2,1,0:T(8,128)(2,1)}, bf16[2,4,128,256]{3,2,1,0:T(8,128)(2,1)S(1)}, u32[]{:S(2)}, u32[]{:S(2)}) collective-permute-start(bf16[2,4,128,256]{3,2,1,0:T(8,128)(2,1)} %refs_3_.1), channel_id=1, source_target_pairs={{0,8},{8,16},{16,24},{24,28},{28,20},{20,12},{12,4},{4,0},{1,9},{9... | collective-permute-start | bytes 1572872 | tf_op jit(solution)/shard_map/ppermute | solution.py:321
  16.7 22.5 %collective-permute-start.6 = (bf16[2,4,128,256]{3,2,1,0:T(8,128)(2,1)S(1)}, bf16[2,4,128,256]{3,2,1,0:T(8,128)(2,1)S(1)}, u32[]{:S(2)}, u32[]{:S(2)}) collective-permute-start(bf16[2,4,128,256]{3,2,1,0:T(8,128)(2,1)S(1)} %collective-permute-done.4.refs_1_), channel_id=1, source_target_pairs={{8,0},{16,8},{24,16},{28,24},{20,28},{12,20},{4,12},{0,4},{9,1},{1... | collective-permute-start | bytes 1572872 | tf_op jit(solution)/shard_map/ppermute | solution.py:320
  18.7 22.5 %collective-permute-start.7 = (bf16[2,4,128,256]{3,2,1,0:T(8,128)(2,1)S(1)}, bf16[2,4,128,256]{3,2,1,0:T(8,128)(2,1)S(1)}, u32[]{:S(2)}, u32[]{:S(2)}) collective-permute-start(bf16[2,4,128,256]{3,2,1,0:T(8,128)(2,1)S(1)} %collective-permute-done.5.refs_2_), channel_id=1, source_target_pairs={{0,8},{8,16},{16,24},{24,28},{28,20},{20,12},{12,4},{4,0},{1,9},{9... | collective-permute-start | bytes 1572872 | tf_op jit(solution)/shard_map/ppermute | solution.py:321
  19.6 1.6 %copy-start.7 = (bf16[1,4,1024,256]{3,2,1,0:T(8,128)(2,1)S(1)}, bf16[1,4,1024,256]{3,2,1,0:T(8,128)(2,1)}, u32[]{:S(2)}) copy-start(bf16[1,4,1024,256]{3,2,1,0:T(8,128)(2,1)} %param.11) | copy-start | bytes 6291460
  21.2 1.0 copy-start.8
  22.2 7.8 %copy-start.3 = (bf16[2,4,128,256]{3,2,1,0:T(8,128)(2,1)S(1)}, bf16[2,4,128,256]{3,2,1,0:T(8,128)(2,1)}, u32[]{:S(2)}) copy-start(bf16[2,4,128,256]{3,2,1,0:T(8,128)(2,1)} %refs_0_.1) | copy-start | bytes 1572868
  22.2 7.8 %copy-start.4 = (bf16[2,4,128,256]{3,2,1,0:T(8,128)(2,1)S(1)}, bf16[2,4,128,256]{3,2,1,0:T(8,128)(2,1)}, u32[]{:S(2)}) copy-start(bf16[2,4,128,256]{3,2,1,0:T(8,128)(2,1)} %refs_3_.1) | copy-start | bytes 1572868
  27.9 22.5 %collective-permute-start.1 = (bf16[2,4,128,256]{3,2,1,0:T(8,128)(2,1)S(1)}, bf16[2,4,128,256]{3,2,1,0:T(8,128)(2,1)S(1)}, u32[]{:S(2)}, u32[]{:S(2)}) collective-permute-start(bf16[2,4,128,256]{3,2,1,0:T(8,128)(2,1)S(1)} %collective-permute-done.refs_4_), channel_id=1, source_target_pairs={{8,0},{16,8},{24,16},{28,24},{20,28},{12,20},{4,12},{0,4},{9,1},{1... | collective-permute-start | bytes 1572872 | tf_op jit(solution)/shard_map/ppermute | solution.py:320
  29.9 22.5 %collective-permute-start.3 = (bf16[2,4,128,256]{3,2,1,0:T(8,128)(2,1)S(1)}, bf16[2,4,128,256]{3,2,1,0:T(8,128)(2,1)S(1)}, u32[]{:S(2)}, u32[]{:S(2)}) collective-permute-start(bf16[2,4,128,256]{3,2,1,0:T(8,128)(2,1)S(1)} %collective-permute-done.2.refs_5_), channel_id=1, source_target_pairs={{0,8},{8,16},{16,24},{24,28},{28,20},{20,12},{12,4},{4,0},{1,9},{9... | collective-permute-start | bytes 1572872 | tf_op jit(solution)/shard_map/ppermute | solution.py:321
  30.0 13.1 %copy-start.1 = (bf16[2,1,1024,256]{3,2,1,0:T(8,128)(2,1)S(1)}, bf16[2,1,1024,256]{3,2,1,0:T(8,128)(2,1)}, u32[]{:S(2)}) copy-start(bf16[2,1,1024,256]{3,2,1,0:T(8,128)(2,1)} %param.17) | copy-start | bytes 3145732
  30.0 13.1 %copy-start.2 = (bf16[2,1,1024,256]{3,2,1,0:T(8,128)(2,1)S(1)}, bf16[2,1,1024,256]{3,2,1,0:T(8,128)(2,1)}, u32[]{:S(2)}) copy-start(bf16[2,1,1024,256]{3,2,1,0:T(8,128)(2,1)} %param.16) | copy-start | bytes 3145732
  41.1 20.5 %collective-permute-start.8 = (bf16[2,4,128,256]{3,2,1,0:T(8,128)(2,1)S(1)}, bf16[2,4,128,256]{3,2,1,0:T(8,128)(2,1)S(1)}, u32[]{:S(2)}, u32[]{:S(2)}) collective-permute-start(bf16[2,4,128,256]{3,2,1,0:T(8,128)(2,1)S(1)} %collective-permute-done.6.refs_0_), channel_id=1, source_target_pairs={{8,0},{16,8},{24,16},{28,24},{20,28},{12,20},{4,12},{0,4},{9,1},{1... | collective-permute-start | bytes 1572872 | tf_op jit(solution)/shard_map/ppermute | solution.py:320
  42.7 20.9 %collective-permute-start.9 = (bf16[2,4,128,256]{3,2,1,0:T(8,128)(2,1)S(1)}, bf16[2,4,128,256]{3,2,1,0:T(8,128)(2,1)S(1)}, u32[]{:S(2)}, u32[]{:S(2)}) collective-permute-start(bf16[2,4,128,256]{3,2,1,0:T(8,128)(2,1)S(1)} %collective-permute-done.7.refs_1_), channel_id=1, source_target_pairs={{0,8},{8,16},{16,24},{24,28},{28,20},{20,12},{12,4},{4,0},{1,9},{9... | collective-permute-start | bytes 1572872 | tf_op jit(solution)/shard_map/ppermute | solution.py:321
  52.4 20.5 %collective-permute-start.10 = (bf16[2,4,128,256]{3,2,1,0:T(8,128)(2,1)S(1)}, bf16[2,4,128,256]{3,2,1,0:T(8,128)(2,1)S(1)}, u32[]{:S(2)}, u32[]{:S(2)}) collective-permute-start(bf16[2,4,128,256]{3,2,1,0:T(8,128)(2,1)S(1)} %collective-permute-done.1.refs_2_), channel_id=1, source_target_pairs={{8,0},{16,8},{24,16},{28,24},{20,28},{12,20},{4,12},{0,4},{9,1},{1... | collective-permute-start | bytes 1572872 | tf_op jit(solution)/shard_map/ppermute | solution.py:320
  54.0 20.9 %collective-permute-start.11 = (bf16[2,4,128,256]{3,2,1,0:T(8,128)(2,1)S(1)}, bf16[2,4,128,256]{3,2,1,0:T(8,128)(2,1)S(1)}, u32[]{:S(2)}, u32[]{:S(2)}) collective-permute-start(bf16[2,4,128,256]{3,2,1,0:T(8,128)(2,1)S(1)} %collective-permute-done.3.refs_3_), channel_id=1, source_target_pairs={{0,8},{8,16},{16,24},{24,28},{28,20},{20,12},{12,4},{4,0},{1,9},{9... | collective-permute-start | bytes 1572872 | tf_op jit(solution)/shard_map/ppermute | solution.py:321
  63.6 14.8 %collective-permute-start.12 = (bf16[4,128,256]{2,1,0:T(8,128)(2,1)S(1)}, bf16[4,128,256]{2,1,0:T(8,128)(2,1)S(1)}, u32[]{:S(2)}, u32[]{:S(2)}) collective-permute-start(bf16[4,128,256]{2,1,0:T(8,128)(2,1)S(1)} %slice_bitcast_fusion.3), channel_id=1, source_target_pairs={{8,0},{16,8},{24,16},{28,24},{20,28},{12,20},{4,12},{0,4},{9,1},{1... | collective-permute-start | bytes 786440 | tf_op jit(solution)/shard_map/ppermute | solution.py:324
  65.3 15.2 %collective-permute-start.13 = (bf16[4,128,256]{2,1,0:T(8,128)(2,1)S(1)}, bf16[4,128,256]{2,1,0:T(8,128)(2,1)S(1)}, u32[]{:S(2)}, u32[]{:S(2)}) collective-permute-start(bf16[4,128,256]{2,1,0:T(8,128)(2,1)S(1)} %slice_bitcast_fusion.2), channel_id=1, source_target_pairs={{0,8},{8,16},{16,24},{24,28},{28,20},{20,12},{12,4},{4,0},{1,9},{9... | collective-permute-start | bytes 786440 | tf_op jit(solution)/shard_map/ppermute | solution.py:325
  72.9 10.4 %collective-permute-start.14 = (bf16[4,128,256]{2,1,0:T(8,128)(2,1)S(1)}, bf16[4,128,256]{2,1,0:T(8,128)(2,1)S(1)}, u32[]{:S(2)}, u32[]{:S(2)}) collective-permute-start(bf16[4,128,256]{2,1,0:T(8,128)(2,1)S(1)} %slice_bitcast_fusion.1), channel_id=1, source_target_pairs={{8,0},{16,8},{24,16},{28,24},{20,28},{12,20},{4,12},{0,4},{9,1},{1... | collective-permute-start | bytes 786440 | tf_op jit(solution)/shard_map/ppermute | solution.py:324
  74.9 9.7 %collective-permute-start.15 = (bf16[4,128,256]{2,1,0:T(8,128)(2,1)S(1)}, bf16[4,128,256]{2,1,0:T(8,128)(2,1)S(1)}, u32[]{:S(2)}, u32[]{:S(2)}) collective-permute-start(bf16[4,128,256]{2,1,0:T(8,128)(2,1)S(1)} %slice_bitcast_fusion), channel_id=1, source_target_pairs={{0,8},{8,16},{16,24},{24,28},{28,20},{20,12},{12,4},{4,0},{1,9},{9... | collective-permute-start | bytes 786440 | tf_op jit(solution)/shard_map/ppermute | solution.py:325
  80.5 4.2 %copy-start = (bf16[1,4,1024,256]{3,2,1,0:T(8,128)(2,1)S(1)}, bf16[1,4,1024,256]{3,2,1,0:T(8,128)(2,1)}, u32[]{:S(2)}) copy-start(bf16[1,4,1024,256]{3,2,1,0:T(8,128)(2,1)} %param.10) | copy-start | bytes 6291460
  80.5 4.2 %copy-start.5 = (s32[2,4]{1,0:T(2,128)S(1)}, s32[2,4]{1,0:T(2,128)}, u32[]{:S(2)}) copy-start(s32[2,4]{1,0:T(2,128)} %pivot_rank.3) | copy-start | bytes 100
  80.5 4.2 %copy-start.6 = (s32[1,4]{1,0:T(1,128)S(1)}, s32[1,4]{1,0:T(1,128)}, u32[]{:S(2)}) copy-start(s32[1,4]{1,0:T(1,128)} %panel_rank.3) | copy-start | bytes 52
  86.3 2.0 %collective-permute-start.16 = (bf16[256,1024]{1,0:T(8,128)(2,1)S(1)}, bf16[256,1024]{1,0:T(8,128)(2,1)S(1)}, u32[]{:S(2)}, u32[]{:S(2)}) collective-permute-start(bf16[256,1024]{1,0:T(8,128)(2,1)S(1)} %get-tuple-element.64), channel_id=1, source_target_pairs={{0,1},{1,0},{2,3},{3,2},{4,5},{5,4},{6,7},{7,6},{8,9},{9,8},{10,11... | collective-permute-start | bytes 1572872 | tf_op jit(solution)/shard_map/ppermute | solution.py:433
  88.5 14.2 %collective-permute-start.17 = (bf16[256,1024]{1,0:T(8,128)(2,1)S(1)}, bf16[256,1024]{1,0:T(8,128)(2,1)S(1)}, u32[]{:S(2)}, u32[]{:S(2)}) collective-permute-start(bf16[256,1024]{1,0:T(8,128)(2,1)S(1)} %add_convert_fusion), channel_id=1, source_target_pairs={{0,2},{1,3},{2,0},{3,1},{4,6},{5,7},{6,4},{7,5},{8,10},{9,11},{10,... | collective-permute-start | bytes 1572872 | tf_op jit(solution)/shard_map/ppermute | solution.py:371
  113.3 3.7 %collective-permute-start.19 = (bf16[256,1024]{1,0:T(8,128)(2,1)S(1)}, bf16[256,1024]{1,0:T(8,128)(2,1)S(1)}, u32[]{:S(2)}, u32[]{:S(2)}) collective-permute-start(bf16[256,1024]{1,0:T(8,128)(2,1)S(1)} %get-tuple-element.67.qt), channel_id=1, source_target_pairs={{0,1},{1,0},{2,3},{3,2},{4,5},{5,4},{6,7},{7,6},{8,9},{9,8},{10,11... | collective-permute-start | bytes 1572872 | tf_op jit(solution)/shard_map/ppermute | solution.py:443
  117.0 4.5 %collective-permute-start.20 = (bf16[2,256,256]{2,1,0:T(8,128)(2,1)S(1)}, bf16[2,256,256]{2,1,0:T(8,128)(2,1)S(1)}, u32[]{:S(2)}, u32[]{:S(2)}) collective-permute-start(bf16[2,256,256]{2,1,0:T(8,128)(2,1)S(1)} %get-tuple-element.77), channel_id=1, source_target_pairs={{0,1},{1,0},{2,3},{3,2},{4,5},{5,4},{6,7},{7,6},{8,9},{9,8},{10,11... | collective-permute-start | bytes 786440 | tf_op jit(solution)/shard_map/ppermute | solution.py:447
  120.9 1.6 %collective-permute-start.21 = (bf16[2,256,256]{2,1,0:T(8,128)(2,1)S(1)}, bf16[2,256,256]{2,1,0:T(8,128)(2,1)S(1)}, u32[]{:S(2)}, u32[]{:S(2)}) collective-permute-start(bf16[2,256,256]{2,1,0:T(8,128)(2,1)S(1)} %get-tuple-element.78), channel_id=1, source_target_pairs={{0,1},{1,0},{2,3},{3,2},{4,5},{5,4},{6,7},{7,6},{8,9},{9,8},{10,11... | collective-permute-start | bytes 786440 | tf_op jit(solution)/shard_map/ppermute | solution.py:447
  121.0 3.7 %collective-permute-start.18 = (f32[256,256]{1,0:T(8,128)S(1)}, f32[256,256]{1,0:T(8,128)S(1)}, u32[]{:S(2)}, u32[]{:S(2)}) collective-permute-start(f32[256,256]{1,0:T(8,128)S(1)} %get-tuple-element.65), channel_id=1, source_target_pairs={{0,1},{1,0},{2,3},{3,2},{4,5},{5,4},{6,7},{7,6},{8,9},{9,8},{10,11... | collective-permute-start | bytes 786440 | tf_op jit(solution)/shard_map/ppermute | solution.py:459
  123.1 8.4 %collective-permute-start.22 = (bf16[2,256,256]{2,1,0:T(8,128)(2,1)S(1)}, bf16[2,256,256]{2,1,0:T(8,128)(2,1)S(1)}, u32[]{:S(2)}, u32[]{:S(2)}) collective-permute-start(bf16[2,256,256]{2,1,0:T(8,128)(2,1)S(1)} %halve.1), channel_id=1, source_target_pairs={{0,2},{1,3},{2,0},{3,1},{4,6},{5,7},{6,4},{7,5},{8,10},{9,11},{10,... | collective-permute-start | bytes 786440 | tf_op jit(solution)/shard_map/ppermute | solution.py:371

commit v5 on v4

--- a/solution.py
+++ b/solution.py
@@ -120,14 +120,17 @@
             work[last:, :] = jnp.where(inside, 0.0, work[last:, :]) - update
 
 
-def orthonormal_kernel(info, start, *refs):
+def orthonormal_kernel(sums, info, start, *refs):
     parts, (qt, given, basis, yt, work, rows, sem) = refs[:-7], refs[-7:]
     width, order = yt.shape
     core = info[0]
-    total = start[...]
-    for part in parts:
-        total = total - part[...].astype(F32)
-    yt[...] = total
+    for c in range(len(parts) // sums):
+        @pl.when(core == c)
+        def _():
+            total = start[...]
+            for part in parts[c * sums : (c + 1) * sums]:
+                total = total - part[...].astype(F32)
+            yt[...] = total
     high, mid, low = split3(yt[...])
     cross = dot11(high, mid) + dot11(high, low)
     work[...] = dot11(high, high) + (cross + cross.T + dot11(mid, mid))
@@ -180,41 +183,30 @@
                 u_all[c, j, p * slab : (p + 1) * slab, :] = u_new[n * slab : (n + 1) * slab, :]
 
 
-def sampled_kernel(places, blocks, info, sampled, sampler_t, *refs):
-    late, (out, u_all) = refs[: len(refs) - 3], refs[-2:]
-    slab = sampler_t.shape[1] // blocks
-    for c in range(out.shape[0]):
-        for j in range(out.shape[1]):
-            total = sampled[c, j]
-            for place in places:
-                span = pl.ds(pl.multiple_of(info[2 + place] * slab, 128), slab)
-                total += dot(sampler_t[:, span], late[c][j])
-                u_all[c, j, place * slab : (place + 1) * slab, :] = late[c][j]
-            out[c, j] = total.astype(BF16)
-
-
-def update_kernel(own_column, places, blocks, info, panel_rank, pivot_rank, sampled, met, panel_u, panel_vt, *refs):
-    late, (cross, out) = refs[:-2], refs[-2:]
-    priors, width, _ = cross.shape
+def update_kernel(c, place, blocks, info, panel_rank, pivot_rank, sampled, met, panel_u, panel_vt, sampler_t, u_all, *refs):
+    cross, u_out, give, keep = refs[-4:]
+    _, priors, width, _ = cross.shape
     slab = panel_vt.shape[2] // blocks
-    column = info[0] if own_column else 1 - info[0]
     row = lax.broadcasted_iota(jnp.int32, (width, width), 0)
     col = lax.broadcasted_iota(jnp.int32, (width, width), 1)
     terms = []
     for j in range(priors):
-        two = met[column, j]
-        for place in places:
+        one, two = sampled[c, j], met[c, j]
+        if place is not None:
             span = pl.ds(pl.multiple_of(info[2 + place] * slab, 128), slab)
-            two += dot(panel_vt[j, :, span], jnp.where(column == 0, late[0][j], late[1][j]))
-        inside = (row < panel_rank[0, j]) & (col < pivot_rank[column, j])
-        cross[j] = jnp.where(inside, two, 0.0).astype(BF16)
-        terms.append(dot11(sampled[column, j], cross[j]).astype(BF16))
-    half = out.shape[1] // 2
+            one += dot(sampler_t[:, span], refs[0][j])
+            two += dot(panel_vt[j, :, span], refs[1][j])
+            u_out[c, j, place * slab : (place + 1) * slab, :] = refs[0][j]
+        inside = (row < panel_rank[0, j]) & (col < pivot_rank[c, j])
+        cross[c, j] = jnp.where(inside, two, 0.0).astype(BF16)
+        terms.append(dot11(one.astype(BF16), cross[c, j]).astype(BF16))
+    half = keep.shape[1] // 2
     for at in (0, half):
         total = jnp.zeros((width, half), F32)
         for j in range(priors):
             total += dot11(terms[j], panel_u[j, at : at + half, :])
-        out[:, at : at + half] = total.astype(out.dtype)
+        keep[:, at : at + half] = total
+        give[:, at : at + half] = total.astype(BF16)
 
 
 def project_kernel(blocks, own_column, info, qt, panel_u, cross, u_all, orig_u, give, keep, left, work, u_buf, sem):
@@ -228,7 +220,7 @@
     mids = []
     for j in range(priors):
         inner = dot(qt[...], panel_u[j]).astype(BF16)
-        mids.append(dot(inner, cross[j]).astype(BF16))
+        mids.append(dot(inner, cross[column, j]).astype(BF16))
     some = max(1, blocks // 2)
     for begin in range(0, blocks, some):
         total = jnp.zeros((some * slab, width), F32)
@@ -320,10 +312,8 @@
                 self.up[t] = found[number] = lax.ppermute(self.up[t], self.axis, self.ahead)
                 self.down[t] = found[self.count - number] = lax.ppermute(self.down[t], self.axis, self.behind)
             else:
-                found[number] = [
-                    lax.ppermute(self.up[t][0], self.axis, self.ahead),
-                    lax.ppermute(self.down[t][1], self.axis, self.behind),
-                ]
+                way, pairs = (self.down, self.behind) if t else (self.up, self.ahead)
+                found[number] = [lax.ppermute(way[t][c], self.axis, pairs) for c in range(way[t].shape[0])]
 
     def tie(self, value, number, which=(0, 1)):
         lists = [(self.up, t, number) for t in which if number <= self.near or t == 0]
@@ -367,8 +357,10 @@
         2 * square * order, "start"
     )
 
-    def shifted(x, shift):
-        return lax.ppermute(x, "cols", [(i, (i + 2 * shift) % cols) for i in range(cols)])
+    def shifted(x, shift, core_of=None):
+        return lax.ppermute(
+            x, "cols", [(i, (i + 2 * shift) % cols) for i in range(cols) if core_of is None or i % 2 == core_of]
+        )
 
     matrix = pltpu.VMEM((width, width), F32)
     tall = pltpu.VMEM((width, order), F32)
@@ -386,15 +378,22 @@
             {first + n: n for n in range(len(kept))}
         )
 
-    def updated(own_column, sampled, met):
+    def updated(c, u_all, late, cross):
+        fixed = 3
+        arrays = [sampled, met, panel_u, panel_vt, sampler_t, u_all, *late, *cross]
+        aliases = {fixed + 5: 1}
+        if cross:
+            aliases[fixed + len(arrays) - 1] = 0
         return run(
-            functools.partial(update_kernel, own_column, places, blocks), [info, panel_rank, pivot_rank],
-            [sampled, met, panel_u, panel_vt, *late_v],
-            [((priors, width, width), BF16), ((width, order), F32 if own_column else BF16)], [], 20,
-            2 * priors * square * (order + width), "update"
+            functools.partial(update_kernel, c, place, blocks), [info, panel_rank, pivot_rank], arrays,
+            [
+                ((pivots, priors, width, width), BF16), ((pivots, priors, order, width), BF16), ((width, order), BF16),
+                ((width, order), F32)
+            ],
+            [], 24, 2 * priors * square * (order + width), "update", aliases
         )
 
-    def projected(own_column, qt, cross):
+    def projected(own_column, qt):
         return run(
             functools.partial(project_kernel, blocks, own_column), [info], [qt, panel_u, cross, u_all],
             [((pairs, share, width), BF16), ((pairs, share, width), F32), ((width, width), BF16)],
@@ -403,10 +402,10 @@
         )
 
     if whole:
-        blocks, places = 1, []
+        blocks, place = 1, None
         new_u, new_v = ([lax.all_gather(x, "rows", axis=2, tiled=True)] for x in (pivot_u, pivot_v))
         sampled, met, u_all = gathered([0], 1, new_u, new_v, [])
-        late_u, late_v = [], []
+        late = [[] for _ in range(pivots)]
     else:
         blocks = count
         now, kept = Ring([pivot_u, pivot_v], ring, "rows"), []
@@ -417,33 +416,30 @@
                 if number == 2:
                     start = now.tie(start, number, (1,))
             if number == last:
-                places = [last]
-                late_u, late_v = now.found[0][last], now.found[1][last]
+                place = last
+                late = list(zip(now.found[0][last], now.found[1][last]))
             else:
                 places = sorted({number, count - number} | ({0} if number == 1 else set()))
                 new_u, new_v = ([now.found[t][p] for p in places] for t in range(2))
                 kept = list(gathered(places, count, new_u, new_v, kept))
         sampled, met, u_all = kept
-    sampled, u_all = run(
-        functools.partial(sampled_kernel, places, blocks), [info], [sampled, sampler_t, *late_u, u_all],
-        [((pivots, priors, width, width), BF16), ((pivots, priors, order, width), BF16)], [], 16, square * order,
-        "sampled", {3 + len(late_u): 1}
-    )
-    cross_other, give = updated(False, sampled, met)
-    recv = lax.ppermute(give, "cols", swap)
-    cross_own, keep = updated(True, sampled, met)
-    sent = (keep + recv.astype(F32)).astype(BF16)
-    parts = [keep, recv, *(shifted(sent, shift) for shift in range(1, pairs))]
+    cross, parts = [], []
+    for c in range(pivots):
+        *cross, u_all, give, keep = updated(c, u_all, late[c], cross)
+        recv = lax.ppermute(give, "cols", [(i, i ^ 1) for i in range(cols) if i % 2 != c])
+        sent = (keep + recv.astype(F32)).astype(BF16)
+        parts += [keep, recv, *(shifted(sent, shift, c) for shift in range(1, pairs))]
+    (cross,) = cross
     qt, given, basis = run(
-        orthonormal_kernel, [info], [start, *parts],
+        functools.partial(orthonormal_kernel, len(parts) // pivots), [info], [start, *parts],
         [((width, order), BF16), ((share, width), F32), ((pivots, share, width), F32)],
         [tall, matrix, pltpu.VMEM((share, width), F32), pltpu.SemaphoreType.DMA((1,))], 16,
         128 * square * order, "orthonormal", away=1
     )
     qt_other = lax.ppermute(qt, "cols", swap)
-    give_a, keep_a, left_a = projected(True, qt, cross_own)
+    give_a, keep_a, left_a = projected(True, qt)
     qt_other, give_a, keep_a = lax.optimization_barrier((qt_other, give_a, keep_a))
-    give_b, keep_b, left_b = projected(False, qt_other, cross_other)
+    give_b, keep_b, left_b = projected(False, qt_other)
     give_a, give_b = lax.ppermute(give_a, "cols", swap), lax.ppermute(give_b, "cols", swap)
     sent = run(
         halve_kernel, [info], [keep_b, keep_a, give_a, give_b], [((pivots, share, width), BF16)] * (pairs - 1), [], 8,

time: 133 us -> 138 us (1.038)
  starting transfers between devices: 22.3 us -> 29.1 us
  waiting for transfers between devices: 72.4 us -> 70.4 us
    ppermute x6, waiting for transfers between devices: 6.11 us -> 14.2 us  [step(): lax.ppermute(self.down[t], self.axis, self.behind)]
    ppermute x6, waiting for transfers between devices: 41.6 us -> 34.1 us  [step(): self.up[t] = found[number] = lax.ppermute(self.up[t], self.axis, self.ahead)]
    ppermute x7 -> x9, starting transfers between devices: 7.74 us -> 14.2 us  [the longest x3 5.71 us: shifted(): lax.ppermute(x, 'cols', [(i, (i + 2 * shift) % cols) for i in range(cols)...]
    ppermute x7 -> x9, waiting for transfers between devices: 23.7 us -> 20.8 us  [the longest x3 15.6 us: shifted(): lax.ppermute(x, 'cols', [(i, (i + 2 * shift) % cols) for i in range(cols)...]
    pallas_call x14 -> x13, Pallas kernels: 32.3 us -> 32.6 us  [run(): pl.pallas_call(kernel, out_shape=shapes, in_specs=[smem] * len(scalars) +...]
  transfers between devices with their start and end apart: 23 -> 25, of which waited for: 17 -> 15; matrix products, arithmetic and copies ran while one was open for 1% -> 1% of each run, Pallas kernels for 15% -> 13%
where the time goes in v5:
time: 138 us
  waiting for transfers between devices  70.4 us (51%)
  Pallas kernels  32.6 us (24%)
  starting transfers between devices  29.1 us (21%)
  local copies, waits for them, and re-layouts  3.83 us (3%)
    ppermute x6, waiting for transfers between devices, step(): self.up[t] = found[number] = lax.ppermute(self.up[t], self.axis, self.ahead)  34.1 us
    pallas_call x13, Pallas kernels, run(): pl.pallas_call(kernel, out_shape=shapes, in_specs=[smem] * len(scalars) +...  32.6 us
    ppermute x3, waiting for transfers between devices, shifted(): lax.ppermute(x, 'cols', [(i, (i + 2 * shift) % cols) for i in range(cols)...  15.6 us
    ppermute x6, waiting for transfers between devices, step(): lax.ppermute(self.down[t], self.axis, self.behind)  14.2 us
    ppermute x6, starting transfers between devices, step(): self.up[t] = found[number] = lax.ppermute(self.up[t], self.axis, self.ahead)  12.3 us
    ppermute x3, starting transfers between devices, shifted(): lax.ppermute(x, 'cols', [(i, (i + 2 * shift) % cols) for i in range(cols)...  5.71 us
    ppermute x4, waiting for transfers between devices, step(): lax.ppermute(way[t][c], self.axis, pairs)  5.13 us
    ppermute x2, starting transfers between devices, body(): lax.ppermute(give, 'cols', [(i, i ^ 1) for i in range(cols) if i % 2 != c])  4.38 us
  transfers between devices with their start and end apart: 25, of which 15 were waited for; matrix products, arithmetic and copies ran while one was open for 1% of the time, Pallas kernels for 13%

profile of v5, /device:TPU:0, one launch (start us, length us, event | category | flops | bytes accessed | tf_op | source)
XLA Modules:
  0.0 138.0 jit_solution(13032236923216749964)
XLA Ops:
  0.6 3.0 %collective-permute-start.4 = (bf16[2,4,128,256]{3,2,1,0:T(8,128)(2,1)}, bf16[2,4,128,256]{3,2,1,0:T(8,128)(2,1)S(1)}, u32[]{:S(2)}, u32[]{:S(2)}) collective-permute-start(bf16[2,4,128,256]{3,2,1,0:T(8,128)(2,1)} %refs_0_.1), channel_id=1, source_target_pairs={{8,0},{16,8},{24,16},{28,24},{20,28},{12,20},{4,12},{0,4},{9,1},{1... | collective-permute-start | bytes 1572872 | tf_op jit(solution)/shard_map/ppermute | solution.py:312
  3.8 1.9 %collective-permute-start = (bf16[2,4,128,256]{3,2,1,0:T(8,128)(2,1)}, bf16[2,4,128,256]{3,2,1,0:T(8,128)(2,1)S(1)}, u32[]{:S(2)}, u32[]{:S(2)}) collective-permute-start(bf16[2,4,128,256]{3,2,1,0:T(8,128)(2,1)} %refs_3_.1), channel_id=1, source_target_pairs={{8,0},{16,8},{24,16},{28,24},{20,28},{12,20},{4,12},{0,4},{9,1},{1... | collective-permute-start | bytes 1572872 | tf_op jit(solution)/shard_map/ppermute | solution.py:312
  5.8 10.9 %collective-permute-done.4.refs_1_ = bf16[2,4,128,256]{3,2,1,0:T(8,128)(2,1)S(1)} collective-permute-done((bf16[2,4,128,256]{3,2,1,0:T(8,128)(2,1)}, bf16[2,4,128,256]{3,2,1,0:T(8,128)(2,1)S(1)}, u32[]{:S(2)}, u32[]{:S(2)}) %collective-permute-start.4) | collective-permute-done | bytes 524320 | tf_op jit(solution)/shard_map/ppermute | solution.py:312
  16.7 2.0 %collective-permute-start.6 = (bf16[2,4,128,256]{3,2,1,0:T(8,128)(2,1)S(1)}, bf16[2,4,128,256]{3,2,1,0:T(8,128)(2,1)S(1)}, u32[]{:S(2)}, u32[]{:S(2)}) collective-permute-start(bf16[2,4,128,256]{3,2,1,0:T(8,128)(2,1)S(1)} %collective-permute-done.4.refs_1_), channel_id=1, source_target_pairs={{8,0},{16,8},{24,16},{28,24},{20,28},{12,20},{4,12},{0,4},{9,1},{1... | collective-permute-start | bytes 1572872 | tf_op jit(solution)/shard_map/ppermute | solution.py:312
  19.5 8.4 %collective-permute-done.refs_4_ = bf16[2,4,128,256]{3,2,1,0:T(8,128)(2,1)S(1)} collective-permute-done((bf16[2,4,128,256]{3,2,1,0:T(8,128)(2,1)}, bf16[2,4,128,256]{3,2,1,0:T(8,128)(2,1)S(1)}, u32[]{:S(2)}, u32[]{:S(2)}) %collective-permute-start) | collective-permute-done | bytes 524320 | tf_op jit(solution)/shard_map/ppermute | solution.py:312
  27.9 2.0 %collective-permute-start.1 = (bf16[2,4,128,256]{3,2,1,0:T(8,128)(2,1)S(1)}, bf16[2,4,128,256]{3,2,1,0:T(8,128)(2,1)S(1)}, u32[]{:S(2)}, u32[]{:S(2)}) collective-permute-start(bf16[2,4,128,256]{3,2,1,0:T(8,128)(2,1)S(1)} %collective-permute-done.refs_4_), channel_id=1, source_target_pairs={{8,0},{16,8},{24,16},{28,24},{20,28},{12,20},{4,12},{0,4},{9,1},{1... | collective-permute-start | bytes 1572872 | tf_op jit(solution)/shard_map/ppermute | solution.py:312
  30.1 1.6 %copy-done.7 = bf16[1,4,1024,256]{3,2,1,0:T(8,128)(2,1)S(1)} copy-done((bf16[1,4,1024,256]{3,2,1,0:T(8,128)(2,1)S(1)}, bf16[1,4,1024,256]{3,2,1,0:T(8,128)(2,1)}, u32[]{:S(2)}) %copy-start.7) | copy-done | bytes 2097176
  33.9 1.8 %gather.3 = (f32[2,4,256,256]{3,2,1,0:T(8,128)S(1)}, f32[2,4,256,256]{3,2,1,0:T(8,128)S(1)}, bf16[2,4,1024,256]{3,2,1,0:T(8,128)(2,1)S(1)}) custom-call(s32[10]{0:T(128)S(1)} %pad_add_fusion.info, bf16[4,256,1024]{2,1,0:T(8,128)(2,1)S(1)} %get-tuple-element.46.panel_vt, bf16[256,1024]{1,0:T(8,128)(2,1)S(1)} %get-tuple-element.44.sampler_t, ...), custom_call_target="tpu_custom_call" | custom-call | flops 805306368 | bytes 14155776 | tf_op jit(solution)/shard_map/gather/pallas_call | solution.py:280
  35.8 3.4 %collective-permute-done.6.refs_0_ = bf16[2,4,128,256]{3,2,1,0:T(8,128)(2,1)S(1)} collective-permute-done((bf16[2,4,128,256]{3,2,1,0:T(8,128)(2,1)S(1)}, bf16[2,4,128,256]{3,2,1,0:T(8,128)(2,1)S(1)}, u32[]{:S(2)}, u32[]{:S(2)}) %collective-permute-start.6) | collective-permute-done | bytes 524320 | tf_op jit(solution)/shard_map/ppermute | solution.py:312
  39.1 2.0 %collective-permute-done.7.refs_1_ = bf16[2,4,128,256]{3,2,1,0:T(8,128)(2,1)S(1)} collective-permute-done((bf16[2,4,128,256]{3,2,1,0:T(8,128)(2,1)S(1)}, bf16[2,4,128,256]{3,2,1,0:T(8,128)(2,1)S(1)}, u32[]{:S(2)}, u32[]{:S(2)}) %collective-permute-start.7) | collective-permute-done | bytes 524320 | tf_op jit(solution)/shard_map/ppermute | solution.py:313
  41.1 1.6 %collective-permute-start.8 = (bf16[2,4,128,256]{3,2,1,0:T(8,128)(2,1)S(1)}, bf16[2,4,128,256]{3,2,1,0:T(8,128)(2,1)S(1)}, u32[]{:S(2)}, u32[]{:S(2)}) collective-permute-start(bf16[2,4,128,256]{3,2,1,0:T(8,128)(2,1)S(1)} %collective-permute-done.6.refs_0_), channel_id=1, source_target_pairs={{8,0},{16,8},{24,16},{28,24},{20,28},{12,20},{4,12},{0,4},{9,1},{1... | collective-permute-start | bytes 1572872 | tf_op jit(solution)/shard_map/ppermute | solution.py:312
  44.5 5.9 %collective-permute-done.1.refs_2_ = bf16[2,4,128,256]{3,2,1,0:T(8,128)(2,1)S(1)} collective-permute-done((bf16[2,4,128,256]{3,2,1,0:T(8,128)(2,1)S(1)}, bf16[2,4,128,256]{3,2,1,0:T(8,128)(2,1)S(1)}, u32[]{:S(2)}, u32[]{:S(2)}) %collective-permute-start.1) | collective-permute-done | bytes 524320 | tf_op jit(solution)/shard_map/ppermute | solution.py:312
  50.4 2.0 %collective-permute-done.3.refs_3_ = bf16[2,4,128,256]{3,2,1,0:T(8,128)(2,1)S(1)} collective-permute-done((bf16[2,4,128,256]{3,2,1,0:T(8,128)(2,1)S(1)}, bf16[2,4,128,256]{3,2,1,0:T(8,128)(2,1)S(1)}, u32[]{:S(2)}, u32[]{:S(2)}) %collective-permute-start.3) | collective-permute-done | bytes 524320 | tf_op jit(solution)/shard_map/ppermute | solution.py:313
  52.5 1.9 %collective-permute-start.10 = (bf16[2,4,128,256]{3,2,1,0:T(8,128)(2,1)S(1)}, bf16[2,4,128,256]{3,2,1,0:T(8,128)(2,1)S(1)}, u32[]{:S(2)}, u32[]{:S(2)}) collective-permute-start(bf16[2,4,128,256]{3,2,1,0:T(8,128)(2,1)S(1)} %collective-permute-done.1.refs_2_), channel_id=1, source_target_pairs={{8,0},{16,8},{24,16},{28,24},{20,28},{12,20},{4,12},{0,4},{9,1},{1... | collective-permute-start | bytes 1572872 | tf_op jit(solution)/shard_map/ppermute | solution.py:312
  54.4 1.6 %gather.4 = (f32[2,4,256,256]{3,2,1,0:T(8,128)S(1)}, f32[2,4,256,256]{3,2,1,0:T(8,128)S(1)}, bf16[2,4,1024,256]{3,2,1,0:T(8,128)(2,1)S(1)}) custom-call(s32[10]{0:T(128)S(1)} %pad_add_fusion.info, bf16[4,256,1024]{2,1,0:T(8,128)(2,1)S(1)} %get-tuple-element.46.panel_vt, ...), custom_call_target="tpu_custom_call", output_to_operand_aliasing={{0}: (7, {}), {1}: (8, {}), {2}: (9, {})} | custom-call | flops 536870912 | bytes 21495808 | tf_op jit(solution)/shard_map/gather/pallas_call | solution.py:280
  56.1 5.6 %collective-permute-done.8.refs_0_ = bf16[2,4,128,256]{3,2,1,0:T(8,128)(2,1)S(1)} collective-permute-done((bf16[2,4,128,256]{3,2,1,0:T(8,128)(2,1)S(1)}, bf16[2,4,128,256]{3,2,1,0:T(8,128)(2,1)S(1)}, u32[]{:S(2)}, u32[]{:S(2)}) %collective-permute-start.8) | collective-permute-done | bytes 524320 | tf_op jit(solution)/shard_map/ppermute | solution.py:312
  61.6 2.0 %collective-permute-done.9.refs_1_ = bf16[2,4,128,256]{3,2,1,0:T(8,128)(2,1)S(1)} collective-permute-done((bf16[2,4,128,256]{3,2,1,0:T(8,128)(2,1)S(1)}, bf16[2,4,128,256]{3,2,1,0:T(8,128)(2,1)S(1)}, u32[]{:S(2)}, u32[]{:S(2)}) %collective-permute-start.9) | collective-permute-done | bytes 524320 | tf_op jit(solution)/shard_map/ppermute | solution.py:313
  63.7 1.6 %collective-permute-start.12 = (bf16[4,128,256]{2,1,0:T(8,128)(2,1)S(1)}, bf16[4,128,256]{2,1,0:T(8,128)(2,1)S(1)}, u32[]{:S(2)}, u32[]{:S(2)}) collective-permute-start(bf16[4,128,256]{2,1,0:T(8,128)(2,1)S(1)} %get-tuple-element.91), channel_id=1, source_target_pairs={{8,0},{16,8},{24,16},{28,24},{20,28},{12,20},{4,12},{0,4},{9,1},{1... | collective-permute-start | bytes 786440 | tf_op jit(solution)/shard_map/ppermute | solution.py:316
  65.3 8.1 %collective-permute-done.11.refs_3_ = bf16[2,4,128,256]{3,2,1,0:T(8,128)(2,1)S(1)} collective-permute-done((bf16[2,4,128,256]{3,2,1,0:T(8,128)(2,1)S(1)}, bf16[2,4,128,256]{3,2,1,0:T(8,128)(2,1)S(1)}, u32[]{:S(2)}, u32[]{:S(2)}) %collective-permute-start.11) | collective-permute-done | bytes 524320 | tf_op jit(solution)/shard_map/ppermute | solution.py:313
  73.9 1.6 %collective-permute-start.16 = (bf16[4,128,256]{2,1,0:T(8,128)(2,1)S(1)}, bf16[4,128,256]{2,1,0:T(8,128)(2,1)S(1)}, u32[]{:S(2)}, u32[]{:S(2)}) collective-permute-start(bf16[4,128,256]{2,1,0:T(8,128)(2,1)S(1)} %get-tuple-element.90), channel_id=1, source_target_pairs={{8,0},{16,8},{24,16},{28,24},{20,28},{12,20},{4,12},{0,4},{9,1},{1... | collective-permute-start | bytes 786440 | tf_op jit(solution)/shard_map/ppermute | solution.py:316
  76.0 1.6 %gather.5 = (f32[2,4,256,256]{3,2,1,0:T(8,128)S(1)}, f32[2,4,256,256]{3,2,1,0:T(8,128)S(1)}, bf16[2,4,1024,256]{3,2,1,0:T(8,128)(2,1)S(1)}) custom-call(s32[10]{0:T(128)S(1)} %pad_add_fusion.info, bf16[4,256,1024]{2,1,0:T(8,128)(2,1)S(1)} %get-tuple-element.46.panel_vt, ...), custom_call_target="tpu_custom_call", output_to_operand_aliasing={{0}: (7, {}), {1}: (8, {}), {2}: (9, {})} | custom-call | flops 536870912 | bytes 21495808 | tf_op jit(solution)/shard_map/gather/pallas_call | solution.py:280
  78.5 4.3 %collective-permute-done.13.refs_1_ = bf16[4,128,256]{2,1,0:T(8,128)(2,1)S(1)} collective-permute-done((bf16[4,128,256]{2,1,0:T(8,128)(2,1)S(1)}, bf16[4,128,256]{2,1,0:T(8,128)(2,1)S(1)}, u32[]{:S(2)}, u32[]{:S(2)}) %collective-permute-start.13) | collective-permute-done | bytes 262176 | tf_op jit(solution)/shard_map/ppermute | solution.py:316
  82.7 2.3 %update.2 = (bf16[2,4,256,256]{3,2,1,0:T(8,128)(2,1)S(1)}, bf16[2,4,1024,256]{3,2,1,0:T(8,128)(2,1)S(1)}, bf16[256,1024]{1,0:T(8,128)(2,1)S(1)}, f32[256,1024]{1,0:T(8,128)S(1)}) custom-call(s32[10]{0:T(128)S(1)} %pad_add_fusion.info, s32[1,4]{1,0:T(1,128)S(1)} %copy-done.6, s32[2,4]{1,0:T(2,128)S(1)} %copy-done.5, ...), custom_call_target="tpu_custom_call", output_to_operand_aliasing={{1}: (8, {})} | custom-call | flops 1342177280 | bytes 20447232 | tf_op jit(solution)/shard_map/update/pallas_call | solution.py:280
  86.4 2.3 %update.3 = (bf16[2,4,256,256]{3,2,1,0:T(8,128)(2,1)S(1)}, bf16[2,4,1024,256]{3,2,1,0:T(8,128)(2,1)S(1)}, bf16[256,1024]{1,0:T(8,128)(2,1)S(1)}, f32[256,1024]{1,0:T(8,128)S(1)}) custom-call(s32[10]{0:T(128)S(1)} %pad_add_fusion.info, s32[1,4]{1,0:T(1,128)S(1)} %copy-done.6, s32[2,4]{1,0:T(2,128)S(1)} %copy-done.5, ...), custom_call_target="tpu_custom_call", output_to_operand_aliasing={{1}: (8, {}), {0}: (11, {})} | custom-call | flops 1342177280 | bytes 21495808 | tf_op jit(solution)/shard_map/update/pallas_call | solution.py:280
  88.7 3.1 %collective-permute-start.18 = (bf16[256,1024]{1,0:T(8,128)(2,1)S(1)}, bf16[256,1024]{1,0:T(8,128)(2,1)S(1)}, u32[]{:S(2)}, u32[]{:S(2)}) collective-permute-start(bf16[256,1024]{1,0:T(8,128)(2,1)S(1)} %get-tuple-element.69), channel_id=1, source_target_pairs={{0,1},{2,3},{4,5},{6,7},{8,9},{10,11},{12,13},{14,15},{16,17},{18,... | collective-permute-start | bytes 1572872 | tf_op jit(solution)/shard_map/ppermute | solution.py:429
  91.9 3.4 %collective-permute-start.15 = (bf16[256,1024]{1,0:T(8,128)(2,1)S(1)}, bf16[256,1024]{1,0:T(8,128)(2,1)S(1)}, u32[]{:S(2)}, u32[]{:S(2)}) collective-permute-start(bf16[256,1024]{1,0:T(8,128)(2,1)S(1)} %add_convert_fusion.1), channel_id=1, source_target_pairs={{0,2},{2,0},{4,6},{6,4},{8,10},{10,8},{12,14},{14,12},{16,18},{18,... | collective-permute-start | bytes 1572872 | tf_op jit(solution)/shard_map/ppermute | solution.py:361
  96.3 11.5 %collective-permute-done.15.refs_2_ = bf16[256,1024]{1,0:T(8,128)(2,1)S(1)} collective-permute-done((bf16[256,1024]{1,0:T(8,128)(2,1)S(1)}, bf16[256,1024]{1,0:T(8,128)(2,1)S(1)}, u32[]{:S(2)}, u32[]{:S(2)}) %collective-permute-start.15) | collective-permute-done | bytes 524320 | tf_op jit(solution)/shard_map/ppermute | solution.py:361
  107.8 10.8 %orthonormal.1 = (bf16[256,1024]{1,0:T(8,128)(2,1)S(1)}, f32[256,256]{1,0:T(8,128)S(1)}, f32[2,256,256]{2,1,0:T(8,128)}) custom-call(s32[10]{0:T(128)S(1)} %pad_add_fusion.info, f32[256,1024]{1,0:T(8,128)S(1)} %start.1, f32[256,1024]{1,0:T(8,128)S(1)} %get-tuple-element.64.refs_0_, bf16[256,1024]{1,0:T(8,128)(2,1)S(1)} %collective-permute-done.14.refs_1_, ...), custom_call_target="tpu_custom_call" | custom-call | flops 17179869184 | bytes 6553600 | tf_op jit(solution)/shard_map/orthonormal/pallas_call | solution.py:280
  119.4 3.4 %project.2 = (bf16[2,256,256]{2,1,0:T(8,128)(2,1)S(1)}, f32[2,256,256]{2,1,0:T(8,128)S(1)}, bf16[256,256]{1,0:T(8,128)(2,1)S(1)}) custom-call(s32[10]{0:T(128)S(1)} %pad_add_fusion.info, bf16[256,1024]{1,0:T(8,128)(2,1)S(1)} %get-tuple-element.72.qt, bf16[4,1024,256]{2,1,0:T(8,128)(2,1)S(1)} %bitcast.25, ...), custom_call_target="tpu_custom_call" | custom-call | flops 3623878656 | bytes 8781824 | tf_op jit(solution)/shard_map/project/pallas_call | solution.py:280
  122.8 3.4 %project.3 = (bf16[2,256,256]{2,1,0:T(8,128)(2,1)S(1)}, f32[2,256,256]{2,1,0:T(8,128)S(1)}, bf16[256,256]{1,0:T(8,128)(2,1)S(1)}) custom-call(s32[10]{0:T(128)S(1)} %pad_add_fusion.info, bf16[256,1024]{1,0:T(8,128)(2,1)S(1)} %collective-permute-done.21.qt, bf16[4,1024,256]{2,1,0:T(8,128)(2,1)S(1)} %bitcast.26, ...), custom_call_target="tpu_custom_call" | custom-call | flops 3623878656 | bytes 8781824 | tf_op jit(solution)/shard_map/project/pallas_call | solution.py:280
  128.7 1.6 %collective-permute-start.24 = (bf16[2,256,256]{2,1,0:T(8,128)(2,1)S(1)}, bf16[2,256,256]{2,1,0:T(8,128)(2,1)S(1)}, u32[]{:S(2)}, u32[]{:S(2)}) collective-permute-start(bf16[2,256,256]{2,1,0:T(8,128)(2,1)S(1)} %halve.1), channel_id=1, source_target_pairs={{0,2},{1,3},{2,0},{3,1},{4,6},{5,7},{6,4},{7,5},{8,10},{9,11},{10,... | collective-permute-start | bytes 786440 | tf_op jit(solution)/shard_map/ppermute | solution.py:361
  133.0 4.1 %collective-permute-done.24 = bf16[2,256,256]{2,1,0:T(8,128)(2,1)S(1)} collective-permute-done((bf16[2,256,256]{2,1,0:T(8,128)(2,1)S(1)}, bf16[2,256,256]{2,1,0:T(8,128)(2,1)S(1)}, u32[]{:S(2)}, u32[]{:S(2)}) %collective-permute-start.24) | collective-permute-done | bytes 262176 | tf_op jit(solution)/shard_map/ppermute | solution.py:361
  (56 shorter events, 16.5 us)
Async XLA Ops:
  0.6 16.0 %collective-permute-start.4 = (bf16[2,4,128,256]{3,2,1,0:T(8,128)(2,1)}, bf16[2,4,128,256]{3,2,1,0:T(8,128)(2,1)S(1)}, u32[]{:S(2)}, u32[]{:S(2)}) collective-permute-start(bf16[2,4,128,256]{3,2,1,0:T(8,128)(2,1)} %refs_0_.1), channel_id=1, source_target_pairs={{8,0},{16,8},{24,16},{28,24},{20,28},{12,20},{4,12},{0,4},{9,1},{1... | collective-permute-start | bytes 1572872 | tf_op jit(solution)/shard_map/ppermute | solution.py:312
  3.6 15.1 %collective-permute-start.5 = (bf16[2,4,128,256]{3,2,1,0:T(8,128)(2,1)}, bf16[2,4,128,256]{3,2,1,0:T(8,128)(2,1)S(1)}, u32[]{:S(2)}, u32[]{:S(2)}) collective-permute-start(bf16[2,4,128,256]{3,2,1,0:T(8,128)(2,1)} %refs_0_.1), channel_id=1, source_target_pairs={{0,8},{8,16},{16,24},{24,28},{28,20},{20,12},{12,4},{4,0},{1,9},{9... | collective-permute-start | bytes 1572872 | tf_op jit(solution)/shard_map/ppermute | solution.py:313
  3.8 24.1 %collective-permute-start = (bf16[2,4,128,256]{3,2,1,0:T(8,128)(2,1)}, bf16[2,4,128,256]{3,2,1,0:T(8,128)(2,1)S(1)}, u32[]{:S(2)}, u32[]{:S(2)}) collective-permute-start(bf16[2,4,128,256]{3,2,1,0:T(8,128)(2,1)} %refs_3_.1), channel_id=1, source_target_pairs={{8,0},{16,8},{24,16},{28,24},{20,28},{12,20},{4,12},{0,4},{9,1},{1... | collective-permute-start | bytes 1572872 | tf_op jit(solution)/shard_map/ppermute | solution.py:312
  5.6 24.3 %collective-permute-start.2 = (bf16[2,4,128,256]{3,2,1,0:T(8,128)(2,1)}, bf16[2,4,128,256]{3,2,1,0:T(8,128)(2,1)S(1)}, u32[]{:S(2)}, u32[]{:S(2)}) collective-permute-start(bf16[2,4,128,256]{3,2,1,0:T(8,128)(2,1)} %refs_3_.1), channel_id=1, source_target_pairs={{0,8},{8,16},{16,24},{24,28},{28,20},{20,12},{12,4},{4,0},{1,9},{9... | collective-permute-start | bytes 1572872 | tf_op jit(solution)/shard_map/ppermute | solution.py:313
  16.7 22.5 %collective-permute-start.6 = (bf16[2,4,128,256]{3,2,1,0:T(8,128)(2,1)S(1)}, bf16[2,4,128,256]{3,2,1,0:T(8,128)(2,1)S(1)}, u32[]{:S(2)}, u32[]{:S(2)}) collective-permute-start(bf16[2,4,128,256]{3,2,1,0:T(8,128)(2,1)S(1)} %collective-permute-done.4.refs_1_), channel_id=1, source_target_pairs={{8,0},{16,8},{24,16},{28,24},{20,28},{12,20},{4,12},{0,4},{9,1},{1... | collective-permute-start | bytes 1572872 | tf_op jit(solution)/shard_map/ppermute | solution.py:312
  18.7 22.5 %collective-permute-start.7 = (bf16[2,4,128,256]{3,2,1,0:T(8,128)(2,1)S(1)}, bf16[2,4,128,256]{3,2,1,0:T(8,128)(2,1)S(1)}, u32[]{:S(2)}, u32[]{:S(2)}) collective-permute-start(bf16[2,4,128,256]{3,2,1,0:T(8,128)(2,1)S(1)} %collective-permute-done.5.refs_2_), channel_id=1, source_target_pairs={{0,8},{8,16},{16,24},{24,28},{28,20},{20,12},{12,4},{4,0},{1,9},{9... | collective-permute-start | bytes 1572872 | tf_op jit(solution)/shard_map/ppermute | solution.py:313
  27.9 22.5 %collective-permute-start.1 = (bf16[2,4,128,256]{3,2,1,0:T(8,128)(2,1)S(1)}, bf16[2,4,128,256]{3,2,1,0:T(8,128)(2,1)S(1)}, u32[]{:S(2)}, u32[]{:S(2)}) collective-permute-start(bf16[2,4,128,256]{3,2,1,0:T(8,128)(2,1)S(1)} %collective-permute-done.refs_4_), channel_id=1, source_target_pairs={{8,0},{16,8},{24,16},{28,24},{20,28},{12,20},{4,12},{0,4},{9,1},{1... | collective-permute-start | bytes 1572872 | tf_op jit(solution)/shard_map/ppermute | solution.py:312
  29.9 22.5 %collective-permute-start.3 = (bf16[2,4,128,256]{3,2,1,0:T(8,128)(2,1)S(1)}, bf16[2,4,128,256]{3,2,1,0:T(8,128)(2,1)S(1)}, u32[]{:S(2)}, u32[]{:S(2)}) collective-permute-start(bf16[2,4,128,256]{3,2,1,0:T(8,128)(2,1)S(1)} %collective-permute-done.2.refs_5_), channel_id=1, source_target_pairs={{0,8},{8,16},{16,24},{24,28},{28,20},{20,12},{12,4},{4,0},{1,9},{9... | collective-permute-start | bytes 1572872 | tf_op jit(solution)/shard_map/ppermute | solution.py:313
  30.1 1.6 %copy-start.7 = (bf16[1,4,1024,256]{3,2,1,0:T(8,128)(2,1)S(1)}, bf16[1,4,1024,256]{3,2,1,0:T(8,128)(2,1)}, u32[]{:S(2)}) copy-start(bf16[1,4,1024,256]{3,2,1,0:T(8,128)(2,1)} %param.11) | copy-start | bytes 6291460
  32.7 1.2 copy-start.4
  33.9 9.2 %copy-start.1 = (bf16[2,1,1024,256]{3,2,1,0:T(8,128)(2,1)S(1)}, bf16[2,1,1024,256]{3,2,1,0:T(8,128)(2,1)}, u32[]{:S(2)}) copy-start(bf16[2,1,1024,256]{3,2,1,0:T(8,128)(2,1)} %param.17) | copy-start | bytes 3145732
  33.9 9.2 %copy-start.2 = (bf16[2,1,1024,256]{3,2,1,0:T(8,128)(2,1)S(1)}, bf16[2,1,1024,256]{3,2,1,0:T(8,128)(2,1)}, u32[]{:S(2)}) copy-start(bf16[2,1,1024,256]{3,2,1,0:T(8,128)(2,1)} %param.16) | copy-start | bytes 3145732
  41.1 20.5 %collective-permute-start.8 = (bf16[2,4,128,256]{3,2,1,0:T(8,128)(2,1)S(1)}, bf16[2,4,128,256]{3,2,1,0:T(8,128)(2,1)S(1)}, u32[]{:S(2)}, u32[]{:S(2)}) collective-permute-start(bf16[2,4,128,256]{3,2,1,0:T(8,128)(2,1)S(1)} %collective-permute-done.6.refs_0_), channel_id=1, source_target_pairs={{8,0},{16,8},{24,16},{28,24},{20,28},{12,20},{4,12},{0,4},{9,1},{1... | collective-permute-start | bytes 1572872 | tf_op jit(solution)/shard_map/ppermute | solution.py:312
  42.7 20.9 %collective-permute-start.9 = (bf16[2,4,128,256]{3,2,1,0:T(8,128)(2,1)S(1)}, bf16[2,4,128,256]{3,2,1,0:T(8,128)(2,1)S(1)}, u32[]{:S(2)}, u32[]{:S(2)}) collective-permute-start(bf16[2,4,128,256]{3,2,1,0:T(8,128)(2,1)S(1)} %collective-permute-done.7.refs_1_), channel_id=1, source_target_pairs={{0,8},{8,16},{16,24},{24,28},{28,20},{20,12},{12,4},{4,0},{1,9},{9... | collective-permute-start | bytes 1572872 | tf_op jit(solution)/shard_map/ppermute | solution.py:313
  52.4 21.0 %collective-permute-start.11 = (bf16[2,4,128,256]{3,2,1,0:T(8,128)(2,1)S(1)}, bf16[2,4,128,256]{3,2,1,0:T(8,128)(2,1)S(1)}, u32[]{:S(2)}, u32[]{:S(2)}) collective-permute-start(bf16[2,4,128,256]{3,2,1,0:T(8,128)(2,1)S(1)} %collective-permute-done.3.refs_3_), channel_id=1, source_target_pairs={{0,8},{8,16},{16,24},{24,28},{28,20},{20,12},{12,4},{4,0},{1,9},{9... | collective-permute-start | bytes 1572872 | tf_op jit(solution)/shard_map/ppermute | solution.py:313
  52.5 23.4 %collective-permute-start.10 = (bf16[2,4,128,256]{3,2,1,0:T(8,128)(2,1)S(1)}, bf16[2,4,128,256]{3,2,1,0:T(8,128)(2,1)S(1)}, u32[]{:S(2)}, u32[]{:S(2)}) collective-permute-start(bf16[2,4,128,256]{3,2,1,0:T(8,128)(2,1)S(1)} %collective-permute-done.1.refs_2_), channel_id=1, source_target_pairs={{8,0},{16,8},{24,16},{28,24},{20,28},{12,20},{4,12},{0,4},{9,1},{1... | collective-permute-start | bytes 1572872 | tf_op jit(solution)/shard_map/ppermute | solution.py:312
  63.7 14.8 %collective-permute-start.12 = (bf16[4,128,256]{2,1,0:T(8,128)(2,1)S(1)}, bf16[4,128,256]{2,1,0:T(8,128)(2,1)S(1)}, u32[]{:S(2)}, u32[]{:S(2)}) collective-permute-start(bf16[4,128,256]{2,1,0:T(8,128)(2,1)S(1)} %get-tuple-element.91), channel_id=1, source_target_pairs={{8,0},{16,8},{24,16},{28,24},{20,28},{12,20},{4,12},{0,4},{9,1},{1... | collective-permute-start | bytes 786440 | tf_op jit(solution)/shard_map/ppermute | solution.py:316
  73.4 9.3 %collective-permute-start.13 = (bf16[4,128,256]{2,1,0:T(8,128)(2,1)S(1)}, bf16[4,128,256]{2,1,0:T(8,128)(2,1)S(1)}, u32[]{:S(2)}, u32[]{:S(2)}) collective-permute-start(bf16[4,128,256]{2,1,0:T(8,128)(2,1)S(1)} %get-tuple-element.89), channel_id=1, source_target_pairs={{0,8},{8,16},{16,24},{24,28},{28,20},{20,12},{12,4},{4,0},{1,9},{9... | collective-permute-start | bytes 786440 | tf_op jit(solution)/shard_map/ppermute | solution.py:316
  73.9 12.4 %collective-permute-start.16 = (bf16[4,128,256]{2,1,0:T(8,128)(2,1)S(1)}, bf16[4,128,256]{2,1,0:T(8,128)(2,1)S(1)}, u32[]{:S(2)}, u32[]{:S(2)}) collective-permute-start(bf16[4,128,256]{2,1,0:T(8,128)(2,1)S(1)} %get-tuple-element.90), channel_id=1, source_target_pairs={{8,0},{16,8},{24,16},{28,24},{20,28},{12,20},{4,12},{0,4},{9,1},{1... | collective-permute-start | bytes 786440 | tf_op jit(solution)/shard_map/ppermute | solution.py:316
  75.5 10.9 %collective-permute-start.17 = (bf16[4,128,256]{2,1,0:T(8,128)(2,1)S(1)}, bf16[4,128,256]{2,1,0:T(8,128)(2,1)S(1)}, u32[]{:S(2)}, u32[]{:S(2)}) collective-permute-start(bf16[4,128,256]{2,1,0:T(8,128)(2,1)S(1)} %get-tuple-element.88), channel_id=1, source_target_pairs={{0,8},{8,16},{16,24},{24,28},{28,20},{20,12},{12,4},{4,0},{1,9},{9... | collective-permute-start | bytes 786440 | tf_op jit(solution)/shard_map/ppermute | solution.py:316
  75.9 6.8 %copy-start = (bf16[1,4,1024,256]{3,2,1,0:T(8,128)(2,1)S(1)}, bf16[1,4,1024,256]{3,2,1,0:T(8,128)(2,1)}, u32[]{:S(2)}) copy-start(bf16[1,4,1024,256]{3,2,1,0:T(8,128)(2,1)} %param.10) | copy-start | bytes 6291460
  75.9 6.8 %copy-start.5 = (s32[2,4]{1,0:T(2,128)S(1)}, s32[2,4]{1,0:T(2,128)}, u32[]{:S(2)}) copy-start(s32[2,4]{1,0:T(2,128)} %pivot_rank.3) | copy-start | bytes 100
  75.9 6.8 %copy-start.6 = (s32[1,4]{1,0:T(1,128)S(1)}, s32[1,4]{1,0:T(1,128)}, u32[]{:S(2)}) copy-start(s32[1,4]{1,0:T(1,128)} %panel_rank.3) | copy-start | bytes 52
  85.0 6.7 %collective-permute-start.14 = (bf16[256,1024]{1,0:T(8,128)(2,1)S(1)}, bf16[256,1024]{1,0:T(8,128)(2,1)S(1)}, u32[]{:S(2)}, u32[]{:S(2)}) collective-permute-start(bf16[256,1024]{1,0:T(8,128)(2,1)S(1)} %get-tuple-element.65), channel_id=1, source_target_pairs={{1,0},{3,2},{5,4},{7,6},{9,8},{11,10},{13,12},{15,14},{17,16},{19,... | collective-permute-start | bytes 1572872 | tf_op jit(solution)/shard_map/ppermute | solution.py:429
  88.7 6.7 %collective-permute-start.18 = (bf16[256,1024]{1,0:T(8,128)(2,1)S(1)}, bf16[256,1024]{1,0:T(8,128)(2,1)S(1)}, u32[]{:S(2)}, u32[]{:S(2)}) collective-permute-start(bf16[256,1024]{1,0:T(8,128)(2,1)S(1)} %get-tuple-element.69), channel_id=1, source_target_pairs={{0,1},{2,3},{4,5},{6,7},{8,9},{10,11},{12,13},{14,15},{16,17},{18,... | collective-permute-start | bytes 1572872 | tf_op jit(solution)/shard_map/ppermute | solution.py:429
  91.9 15.8 %collective-permute-start.15 = (bf16[256,1024]{1,0:T(8,128)(2,1)S(1)}, bf16[256,1024]{1,0:T(8,128)(2,1)S(1)}, u32[]{:S(2)}, u32[]{:S(2)}) collective-permute-start(bf16[256,1024]{1,0:T(8,128)(2,1)S(1)} %add_convert_fusion.1), channel_id=1, source_target_pairs={{0,2},{2,0},{4,6},{6,4},{8,10},{10,8},{12,14},{14,12},{16,18},{18,... | collective-permute-start | bytes 1572872 | tf_op jit(solution)/shard_map/ppermute | solution.py:361
  95.6 12.2 %collective-permute-start.19 = (bf16[256,1024]{1,0:T(8,128)(2,1)S(1)}, bf16[256,1024]{1,0:T(8,128)(2,1)S(1)}, u32[]{:S(2)}, u32[]{:S(2)}) collective-permute-start(bf16[256,1024]{1,0:T(8,128)(2,1)S(1)} %add_convert_fusion), channel_id=1, source_target_pairs={{1,3},{3,1},{5,7},{7,5},{9,11},{11,9},{13,15},{15,13},{17,19},{19,... | collective-permute-start | bytes 1572872 | tf_op jit(solution)/shard_map/ppermute | solution.py:361
  118.6 4.2 %collective-permute-start.21 = (bf16[256,1024]{1,0:T(8,128)(2,1)S(1)}, bf16[256,1024]{1,0:T(8,128)(2,1)S(1)}, u32[]{:S(2)}, u32[]{:S(2)}) collective-permute-start(bf16[256,1024]{1,0:T(8,128)(2,1)S(1)} %get-tuple-element.72.qt), channel_id=1, source_target_pairs={{0,1},{1,0},{2,3},{3,2},{4,5},{5,4},{6,7},{7,6},{8,9},{9,8},{10,11... | collective-permute-start | bytes 1572872 | tf_op jit(solution)/shard_map/ppermute | solution.py:439
  126.2 1.6 %collective-permute-start.22 = (bf16[2,256,256]{2,1,0:T(8,128)(2,1)S(1)}, bf16[2,256,256]{2,1,0:T(8,128)(2,1)S(1)}, u32[]{:S(2)}, u32[]{:S(2)}) collective-permute-start(bf16[2,256,256]{2,1,0:T(8,128)(2,1)S(1)} %get-tuple-element.81), channel_id=1, source_target_pairs={{0,1},{1,0},{2,3},{3,2},{4,5},{5,4},{6,7},{7,6},{8,9},{9,8},{10,11... | collective-permute-start | bytes 786440 | tf_op jit(solution)/shard_map/ppermute | solution.py:443
  126.2 1.9 %collective-permute-start.23 = (bf16[2,256,256]{2,1,0:T(8,128)(2,1)S(1)}, bf16[2,256,256]{2,1,0:T(8,128)(2,1)S(1)}, u32[]{:S(2)}, u32[]{:S(2)}) collective-permute-start(bf16[2,256,256]{2,1,0:T(8,128)(2,1)S(1)} %get-tuple-element.82), channel_id=1, source_target_pairs={{0,1},{1,0},{2,3},{3,2},{4,5},{5,4},{6,7},{7,6},{8,9},{9,8},{10,11... | collective-permute-start | bytes 786440 | tf_op jit(solution)/shard_map/ppermute | solution.py:443
  126.7 3.6 %collective-permute-start.20 = (f32[256,256]{1,0:T(8,128)S(1)}, f32[256,256]{1,0:T(8,128)S(1)}, u32[]{:S(2)}, u32[]{:S(2)}) collective-permute-start(f32[256,256]{1,0:T(8,128)S(1)} %get-tuple-element.70), channel_id=1, source_target_pairs={{0,1},{1,0},{2,3},{3,2},{4,5},{5,4},{6,7},{7,6},{8,9},{9,8},{10,11... | collective-permute-start | bytes 786440 | tf_op jit(solution)/shard_map/ppermute | solution.py:455
  128.7 8.4 %collective-permute-start.24 = (bf16[2,256,256]{2,1,0:T(8,128)(2,1)S(1)}, bf16[2,256,256]{2,1,0:T(8,128)(2,1)S(1)}, u32[]{:S(2)}, u32[]{:S(2)}) collective-permute-start(bf16[2,256,256]{2,1,0:T(8,128)(2,1)S(1)} %halve.1), channel_id=1, source_target_pairs={{0,2},{1,3},{2,0},{3,1},{4,6},{5,7},{6,4},{7,5},{8,10},{9,11},{10,... | collective-permute-start | bytes 786440 | tf_op jit(solution)/shard_map/ppermute | solution.py:361
  (2 other events, 2.1 us)

commit v6 on v4

--- a/solution.py
+++ b/solution.py
@@ -37,7 +37,7 @@
     return high, mid, low
 
 
-def eliminate(panel, first):
+def eliminate(panel, first, store):
     rows, width = panel.shape
     lanes = 128
     tile = (SUB, lanes)
@@ -58,12 +58,16 @@
             [jnp.broadcast_to(part[v][mine][:, at + m : at + m + 1], tile) for v in range(top, high)]
             for m in range(SUB)
         ]
-        small = [
-            [jnp.broadcast_to(column[b][0][a : a + 1, :], tile) for b in range(a + 1)] for a in range(SUB)
-        ]
+        for n, value in enumerate([c[0] for c in column] + part[top]):
+            store[top, n * SUB : (n + 1) * SUB, :] = value
+
+        def spread(n, a):
+            return jnp.broadcast_to(store[top, n * SUB + a : n * SUB + a + 1, :], tile)
+
+        small = [[spread(b, a) for b in range(a + 1)] for a in range(SUB)]
         row = []
         for a in range(SUB):
-            row.append([jnp.broadcast_to(part[top][h][a : a + 1, :], tile) for h in range(halves)])
+            row.append([spread(SUB + h, a) for h in range(halves)])
             row[a][mine] = jnp.where(inside, jnp.where(lane == at + a, 1.0, 0.0), row[a][mine])
         pivots = small[0][0]
         factor = []
@@ -103,12 +107,12 @@
     return jnp.concatenate(done, 0)
 
 
-def invert_blocks(work, begin, end):
+def invert_blocks(work, store, begin, end):
     width = work.shape[0]
     lane = lax.broadcasted_iota(jnp.int32, (1, width), 1)
     for first in range(begin, end, BLOCK):
         last = first + BLOCK
-        panel = eliminate(work[first:last, :], first)
+        panel = eliminate(work[first:last, :], first, store)
         work[first:last, :] = panel
         if last < width:
             base = last // 128 * 128
@@ -121,7 +125,7 @@
 
 
 def orthonormal_kernel(info, start, *refs):
-    parts, (qt, given, basis, yt, work, rows, sem) = refs[:-7], refs[-7:]
+    parts, (qt, given, basis, yt, work, store, rows, sem) = refs[:-8], refs[-8:]
     width, order = yt.shape
     core = info[0]
     total = start[...]
@@ -131,7 +135,7 @@
     high, mid, low = split3(yt[...])
     cross = dot11(high, mid) + dot11(high, low)
     work[...] = dot11(high, high) + (cross + cross.T + dot11(mid, mid))
-    invert_blocks(work, 0, width)
+    invert_blocks(work, store, 0, width)
     row = lax.broadcasted_iota(jnp.int32, (width, width), 0)
     col = lax.broadcasted_iota(jnp.int32, (width, width), 1)
     m_high, m_low, _ = split3(jnp.where(col <= row, work[...], 0.0))
@@ -437,7 +441,11 @@
     qt, given, basis = run(
         orthonormal_kernel, [info], [start, *parts],
         [((width, order), BF16), ((share, width), F32), ((pivots, share, width), F32)],
-        [tall, matrix, pltpu.VMEM((share, width), F32), pltpu.SemaphoreType.DMA((1,))], 16,
+        [
+            tall, matrix, pltpu.VMEM((BLOCK // SUB, (SUB + width // 128) * SUB, 128), F32), pltpu.VMEM((share, width), F32),
+            pltpu.SemaphoreType.DMA((1,))
+        ],
+        16,
         128 * square * order, "orthonormal", away=1
     )
     qt_other = lax.ppermute(qt, "cols", swap)

time: 133 us -> 131 us (0.985)
  no operation moved by 1% of the time
where the time goes in v6:
time: 131 us
  waiting for transfers between devices  72.4 us (55%)
  Pallas kernels  31.2 us (24%)
  starting transfers between devices  22.3 us (17%)
  local copies, waits for them, and re-layouts  3.42 us (3%)
    ppermute x6, waiting for transfers between devices, step(): self.up[t] = found[number] = lax.ppermute(self.up[t], self.axis, self.ahead)  41.6 us
    pallas_call x14, Pallas kernels, run(): pl.pallas_call(kernel, out_shape=shapes, in_specs=[smem] * len(scalars) +...  31.2 us
    ppermute x2, waiting for transfers between devices, shifted(): lax.ppermute(x, 'cols', [(i, (i + 2 * shift) % cols) for i in range(cols)])  16.8 us
    ppermute x6, starting transfers between devices, step(): self.up[t] = found[number] = lax.ppermute(self.up[t], self.axis, self.ahead)  12 us
    ppermute x6, waiting for transfers between devices, step(): lax.ppermute(self.down[t], self.axis, self.behind)  6.11 us
    ppermute x2, starting transfers between devices, step(): lax.ppermute(self.up[t][0], self.axis, self.ahead)  3.65 us
    ppermute x2, waiting for transfers between devices, step(): lax.ppermute(self.down[t][1], self.axis, self.behind)  3.38 us
    ppermute x2, waiting for transfers between devices, step(): lax.ppermute(self.up[t][0], self.axis, self.ahead)  3.36 us
  transfers between devices with their start and end apart: 23, of which 17 were waited for; matrix products, arithmetic and copies ran while one was open for 1% of the time, Pallas kernels for 15%

profile of v6, /device:TPU:0, one launch (start us, length us, event | category | flops | bytes accessed | tf_op | source)
XLA Modules:
  0.0 131.3 jit_solution(5788812741496987747)
XLA Ops:
  0.6 3.0 %collective-permute-start.4 = (bf16[2,4,128,256]{3,2,1,0:T(8,128)(2,1)}, bf16[2,4,128,256]{3,2,1,0:T(8,128)(2,1)S(1)}, u32[]{:S(2)}, u32[]{:S(2)}) collective-permute-start(bf16[2,4,128,256]{3,2,1,0:T(8,128)(2,1)} %refs_0_.1), channel_id=1, source_target_pairs={{8,0},{16,8},{24,16},{28,24},{20,28},{12,20},{4,12},{0,4},{9,1},{1... | collective-permute-start | bytes 1572872 | tf_op jit(solution)/shard_map/ppermute | solution.py:324
  3.8 1.9 %collective-permute-start = (bf16[2,4,128,256]{3,2,1,0:T(8,128)(2,1)}, bf16[2,4,128,256]{3,2,1,0:T(8,128)(2,1)S(1)}, u32[]{:S(2)}, u32[]{:S(2)}) collective-permute-start(bf16[2,4,128,256]{3,2,1,0:T(8,128)(2,1)} %refs_3_.1), channel_id=1, source_target_pairs={{8,0},{16,8},{24,16},{28,24},{20,28},{12,20},{4,12},{0,4},{9,1},{1... | collective-permute-start | bytes 1572872 | tf_op jit(solution)/shard_map/ppermute | solution.py:324
  5.8 10.9 %collective-permute-done.4.refs_1_ = bf16[2,4,128,256]{3,2,1,0:T(8,128)(2,1)S(1)} collective-permute-done((bf16[2,4,128,256]{3,2,1,0:T(8,128)(2,1)}, bf16[2,4,128,256]{3,2,1,0:T(8,128)(2,1)S(1)}, u32[]{:S(2)}, u32[]{:S(2)}) %collective-permute-start.4) | collective-permute-done | bytes 524320 | tf_op jit(solution)/shard_map/ppermute | solution.py:324
  16.7 2.0 %collective-permute-start.6 = (bf16[2,4,128,256]{3,2,1,0:T(8,128)(2,1)S(1)}, bf16[2,4,128,256]{3,2,1,0:T(8,128)(2,1)S(1)}, u32[]{:S(2)}, u32[]{:S(2)}) collective-permute-start(bf16[2,4,128,256]{3,2,1,0:T(8,128)(2,1)S(1)} %collective-permute-done.4.refs_1_), channel_id=1, source_target_pairs={{8,0},{16,8},{24,16},{28,24},{20,28},{12,20},{4,12},{0,4},{9,1},{1... | collective-permute-start | bytes 1572872 | tf_op jit(solution)/shard_map/ppermute | solution.py:324
  19.6 1.6 %copy-done.7 = bf16[1,4,1024,256]{3,2,1,0:T(8,128)(2,1)S(1)} copy-done((bf16[1,4,1024,256]{3,2,1,0:T(8,128)(2,1)S(1)}, bf16[1,4,1024,256]{3,2,1,0:T(8,128)(2,1)}, u32[]{:S(2)}) %copy-start.7) | copy-done | bytes 2097176
  23.0 4.9 %collective-permute-done.refs_4_ = bf16[2,4,128,256]{3,2,1,0:T(8,128)(2,1)S(1)} collective-permute-done((bf16[2,4,128,256]{3,2,1,0:T(8,128)(2,1)}, bf16[2,4,128,256]{3,2,1,0:T(8,128)(2,1)S(1)}, u32[]{:S(2)}, u32[]{:S(2)}) %collective-permute-start) | collective-permute-done | bytes 524320 | tf_op jit(solution)/shard_map/ppermute | solution.py:324
  27.9 2.0 %collective-permute-start.1 = (bf16[2,4,128,256]{3,2,1,0:T(8,128)(2,1)S(1)}, bf16[2,4,128,256]{3,2,1,0:T(8,128)(2,1)S(1)}, u32[]{:S(2)}, u32[]{:S(2)}) collective-permute-start(bf16[2,4,128,256]{3,2,1,0:T(8,128)(2,1)S(1)} %collective-permute-done.refs_4_), channel_id=1, source_target_pairs={{8,0},{16,8},{24,16},{28,24},{20,28},{12,20},{4,12},{0,4},{9,1},{1... | collective-permute-start | bytes 1572872 | tf_op jit(solution)/shard_map/ppermute | solution.py:324
  30.0 1.8 %gather.3 = (f32[2,4,256,256]{3,2,1,0:T(8,128)S(1)}, f32[2,4,256,256]{3,2,1,0:T(8,128)S(1)}, bf16[2,4,1024,256]{3,2,1,0:T(8,128)(2,1)S(1)}) custom-call(s32[10]{0:T(128)S(1)} %pad_add_fusion.info, bf16[4,256,1024]{2,1,0:T(8,128)(2,1)S(1)} %get-tuple-element.44.panel_vt, bf16[256,1024]{1,0:T(8,128)(2,1)S(1)} %get-tuple-element.42.sampler_t, ...), custom_call_target="tpu_custom_call" | custom-call | flops 805306368 | bytes 14155776 | tf_op jit(solution)/shard_map/gather/pallas_call | solution.py:292
  31.9 7.3 %collective-permute-done.6.refs_0_ = bf16[2,4,128,256]{3,2,1,0:T(8,128)(2,1)S(1)} collective-permute-done((bf16[2,4,128,256]{3,2,1,0:T(8,128)(2,1)S(1)}, bf16[2,4,128,256]{3,2,1,0:T(8,128)(2,1)S(1)}, u32[]{:S(2)}, u32[]{:S(2)}) %collective-permute-start.6) | collective-permute-done | bytes 524320 | tf_op jit(solution)/shard_map/ppermute | solution.py:324
  39.1 2.0 %collective-permute-done.7.refs_1_ = bf16[2,4,128,256]{3,2,1,0:T(8,128)(2,1)S(1)} collective-permute-done((bf16[2,4,128,256]{3,2,1,0:T(8,128)(2,1)S(1)}, bf16[2,4,128,256]{3,2,1,0:T(8,128)(2,1)S(1)}, u32[]{:S(2)}, u32[]{:S(2)}) %collective-permute-start.7) | collective-permute-done | bytes 524320 | tf_op jit(solution)/shard_map/ppermute | solution.py:325
  41.1 1.6 %collective-permute-start.8 = (bf16[2,4,128,256]{3,2,1,0:T(8,128)(2,1)S(1)}, bf16[2,4,128,256]{3,2,1,0:T(8,128)(2,1)S(1)}, u32[]{:S(2)}, u32[]{:S(2)}) collective-permute-start(bf16[2,4,128,256]{3,2,1,0:T(8,128)(2,1)S(1)} %collective-permute-done.6.refs_0_), channel_id=1, source_target_pairs={{8,0},{16,8},{24,16},{28,24},{20,28},{12,20},{4,12},{0,4},{9,1},{1... | collective-permute-start | bytes 1572872 | tf_op jit(solution)/shard_map/ppermute | solution.py:324
  44.5 5.9 %collective-permute-done.1.refs_2_ = bf16[2,4,128,256]{3,2,1,0:T(8,128)(2,1)S(1)} collective-permute-done((bf16[2,4,128,256]{3,2,1,0:T(8,128)(2,1)S(1)}, bf16[2,4,128,256]{3,2,1,0:T(8,128)(2,1)S(1)}, u32[]{:S(2)}, u32[]{:S(2)}) %collective-permute-start.1) | collective-permute-done | bytes 524320 | tf_op jit(solution)/shard_map/ppermute | solution.py:324
  50.4 2.0 %collective-permute-done.3.refs_3_ = bf16[2,4,128,256]{3,2,1,0:T(8,128)(2,1)S(1)} collective-permute-done((bf16[2,4,128,256]{3,2,1,0:T(8,128)(2,1)S(1)}, bf16[2,4,128,256]{3,2,1,0:T(8,128)(2,1)S(1)}, u32[]{:S(2)}, u32[]{:S(2)}) %collective-permute-start.3) | collective-permute-done | bytes 524320 | tf_op jit(solution)/shard_map/ppermute | solution.py:325
  52.4 1.6 %collective-permute-start.10 = (bf16[2,4,128,256]{3,2,1,0:T(8,128)(2,1)S(1)}, bf16[2,4,128,256]{3,2,1,0:T(8,128)(2,1)S(1)}, u32[]{:S(2)}, u32[]{:S(2)}) collective-permute-start(bf16[2,4,128,256]{3,2,1,0:T(8,128)(2,1)S(1)} %collective-permute-done.1.refs_2_), channel_id=1, source_target_pairs={{8,0},{16,8},{24,16},{28,24},{20,28},{12,20},{4,12},{0,4},{9,1},{1... | collective-permute-start | bytes 1572872 | tf_op jit(solution)/shard_map/ppermute | solution.py:324
  54.4 1.6 %gather.4 = (f32[2,4,256,256]{3,2,1,0:T(8,128)S(1)}, f32[2,4,256,256]{3,2,1,0:T(8,128)S(1)}, bf16[2,4,1024,256]{3,2,1,0:T(8,128)(2,1)S(1)}) custom-call(s32[10]{0:T(128)S(1)} %pad_add_fusion.info, bf16[4,256,1024]{2,1,0:T(8,128)(2,1)S(1)} %get-tuple-element.44.panel_vt, ...), custom_call_target="tpu_custom_call", output_to_operand_aliasing={{0}: (7, {}), {1}: (8, {}), {2}: (9, {})} | custom-call | flops 536870912 | bytes 21495808 | tf_op jit(solution)/shard_map/gather/pallas_call | solution.py:292
  56.1 5.5 %collective-permute-done.8.refs_0_ = bf16[2,4,128,256]{3,2,1,0:T(8,128)(2,1)S(1)} collective-permute-done((bf16[2,4,128,256]{3,2,1,0:T(8,128)(2,1)S(1)}, bf16[2,4,128,256]{3,2,1,0:T(8,128)(2,1)S(1)}, u32[]{:S(2)}, u32[]{:S(2)}) %collective-permute-start.8) | collective-permute-done | bytes 524320 | tf_op jit(solution)/shard_map/ppermute | solution.py:324
  61.6 2.0 %collective-permute-done.9.refs_1_ = bf16[2,4,128,256]{3,2,1,0:T(8,128)(2,1)S(1)} collective-permute-done((bf16[2,4,128,256]{3,2,1,0:T(8,128)(2,1)S(1)}, bf16[2,4,128,256]{3,2,1,0:T(8,128)(2,1)S(1)}, u32[]{:S(2)}, u32[]{:S(2)}) %collective-permute-start.9) | collective-permute-done | bytes 524320 | tf_op jit(solution)/shard_map/ppermute | solution.py:325
  63.6 1.6 %collective-permute-start.12 = (bf16[4,128,256]{2,1,0:T(8,128)(2,1)S(1)}, bf16[4,128,256]{2,1,0:T(8,128)(2,1)S(1)}, u32[]{:S(2)}, u32[]{:S(2)}) collective-permute-start(bf16[4,128,256]{2,1,0:T(8,128)(2,1)S(1)} %slice_bitcast_fusion.3), channel_id=1, source_target_pairs={{8,0},{16,8},{24,16},{28,24},{20,28},{12,20},{4,12},{0,4},{9,1},{1... | collective-permute-start | bytes 786440 | tf_op jit(solution)/shard_map/ppermute | solution.py:328
  65.8 7.1 %collective-permute-done.10.refs_2_ = bf16[2,4,128,256]{3,2,1,0:T(8,128)(2,1)S(1)} collective-permute-done((bf16[2,4,128,256]{3,2,1,0:T(8,128)(2,1)S(1)}, bf16[2,4,128,256]{3,2,1,0:T(8,128)(2,1)S(1)}, u32[]{:S(2)}, u32[]{:S(2)}) %collective-permute-start.10) | collective-permute-done | bytes 524320 | tf_op jit(solution)/shard_map/ppermute | solution.py:324
  72.9 2.0 %collective-permute-start.14 = (bf16[4,128,256]{2,1,0:T(8,128)(2,1)S(1)}, bf16[4,128,256]{2,1,0:T(8,128)(2,1)S(1)}, u32[]{:S(2)}, u32[]{:S(2)}) collective-permute-start(bf16[4,128,256]{2,1,0:T(8,128)(2,1)S(1)} %slice_bitcast_fusion.1), channel_id=1, source_target_pairs={{8,0},{16,8},{24,16},{28,24},{20,28},{12,20},{4,12},{0,4},{9,1},{1... | collective-permute-start | bytes 786440 | tf_op jit(solution)/shard_map/ppermute | solution.py:328
  75.3 1.6 %gather.5 = (f32[2,4,256,256]{3,2,1,0:T(8,128)S(1)}, f32[2,4,256,256]{3,2,1,0:T(8,128)S(1)}, bf16[2,4,1024,256]{3,2,1,0:T(8,128)(2,1)S(1)}) custom-call(s32[10]{0:T(128)S(1)} %pad_add_fusion.info, bf16[4,256,1024]{2,1,0:T(8,128)(2,1)S(1)} %get-tuple-element.44.panel_vt, ...), custom_call_target="tpu_custom_call", output_to_operand_aliasing={{0}: (7, {}), {1}: (8, {}), {2}: (9, {})} | custom-call | flops 536870912 | bytes 21495808 | tf_op jit(solution)/shard_map/gather/pallas_call | solution.py:292
  78.5 2.0 %collective-permute-done.13.refs_1_ = bf16[4,128,256]{2,1,0:T(8,128)(2,1)S(1)} collective-permute-done((bf16[4,128,256]{2,1,0:T(8,128)(2,1)S(1)}, bf16[4,128,256]{2,1,0:T(8,128)(2,1)S(1)}, u32[]{:S(2)}, u32[]{:S(2)}) %collective-permute-start.13) | collective-permute-done | bytes 262176 | tf_op jit(solution)/shard_map/ppermute | solution.py:329
  81.5 1.8 %collective-permute-done.14.refs_0_ = bf16[4,128,256]{2,1,0:T(8,128)(2,1)S(1)} collective-permute-done((bf16[4,128,256]{2,1,0:T(8,128)(2,1)S(1)}, bf16[4,128,256]{2,1,0:T(8,128)(2,1)S(1)}, u32[]{:S(2)}, u32[]{:S(2)}) %collective-permute-start.14) | collective-permute-done | bytes 262176 | tf_op jit(solution)/shard_map/ppermute | solution.py:328
  84.6 1.7 %update.3 = (bf16[4,256,256]{2,1,0:T(8,128)(2,1)S(1)}, bf16[256,1024]{1,0:T(8,128)(2,1)S(1)}) custom-call(s32[10]{0:T(128)S(1)} %pad_add_fusion.info, s32[1,4]{1,0:T(1,128)S(1)} %copy-done.6, s32[2,4]{1,0:T(2,128)S(1)} %copy-done.5, bf16[2,4,256,256]{3,2,1,0:T(8,128)(2,1)S(1)} %get-tuple-element.61.sampled, f32[2,4,256,256]{3,2,1,0:T(8,128)S(1)} %get-tuple-element.62.met, ...), custom_call_target="tpu_custom_call" | custom-call | flops 1342177280 | bytes 8912896 | tf_op jit(solution)/shard_map/update/pallas_call | solution.py:292
  86.4 1.7 %update.2 = (bf16[4,256,256]{2,1,0:T(8,128)(2,1)S(1)}, f32[256,1024]{1,0:T(8,128)S(1)}) custom-call(s32[10]{0:T(128)S(1)} %pad_add_fusion.info, s32[1,4]{1,0:T(1,128)S(1)} %copy-done.6, s32[2,4]{1,0:T(2,128)S(1)} %copy-done.5, bf16[2,4,256,256]{3,2,1,0:T(8,128)(2,1)S(1)} %get-tuple-element.61.sampled, f32[2,4,256,256]{3,2,1,0:T(8,128)S(1)} %get-tuple-element.62.met, ...), custom_call_target="tpu_custom_call" | custom-call | flops 1342177280 | bytes 9437184 | tf_op jit(solution)/shard_map/update/pallas_call | solution.py:292
  88.5 1.6 %collective-permute-start.17 = (bf16[256,1024]{1,0:T(8,128)(2,1)S(1)}, bf16[256,1024]{1,0:T(8,128)(2,1)S(1)}, u32[]{:S(2)}, u32[]{:S(2)}) collective-permute-start(bf16[256,1024]{1,0:T(8,128)(2,1)S(1)} %add_convert_fusion), channel_id=1, source_target_pairs={{0,2},{1,3},{2,0},{3,1},{4,6},{5,7},{6,4},{7,5},{8,10},{9,11},{10,... | collective-permute-start | bytes 1572872 | tf_op jit(solution)/shard_map/ppermute | solution.py:375
  90.1 12.6 %collective-permute-done.17.refs_2_ = bf16[256,1024]{1,0:T(8,128)(2,1)S(1)} collective-permute-done((bf16[256,1024]{1,0:T(8,128)(2,1)S(1)}, bf16[256,1024]{1,0:T(8,128)(2,1)S(1)}, u32[]{:S(2)}, u32[]{:S(2)}) %collective-permute-start.17) | collective-permute-done | bytes 524320 | tf_op jit(solution)/shard_map/ppermute | solution.py:375
  102.7 9.5 %orthonormal.1 = (bf16[256,1024]{1,0:T(8,128)(2,1)S(1)}, f32[256,256]{1,0:T(8,128)S(1)}, f32[2,256,256]{2,1,0:T(8,128)}) custom-call(s32[10]{0:T(128)S(1)} %pad_add_fusion.info, f32[256,1024]{1,0:T(8,128)S(1)} %start.1, f32[256,1024]{1,0:T(8,128)S(1)} %get-tuple-element.63.refs_0_, bf16[256,1024]{1,0:T(8,128)(2,1)S(1)} %collective-permute-done.16.refs_1_, ...), custom_call_target="tpu_custom_call" | custom-call | flops 17179869184 | bytes 4456448 | tf_op jit(solution)/shard_map/orthonormal/pallas_call | solution.py:292
  112.3 3.6 %project.2 = (bf16[2,256,256]{2,1,0:T(8,128)(2,1)S(1)}, f32[2,256,256]{2,1,0:T(8,128)S(1)}, bf16[256,256]{1,0:T(8,128)(2,1)S(1)}) custom-call(s32[10]{0:T(128)S(1)} %pad_add_fusion.info, bf16[256,1024]{1,0:T(8,128)(2,1)S(1)} %get-tuple-element.67.qt, bf16[4,1024,256]{2,1,0:T(8,128)(2,1)S(1)} %bitcast.25, bf16[4,256,256]{2,1,0:T(8,128)(2,1)S(1)} %get-tuple-element.68.cross, ...), custom_call_target="tpu_custom_call" | custom-call | flops 3623878656 | bytes 8257536 | tf_op jit(solution)/shard_map/project/pallas_call | solution.py:292
  116.4 3.4 %project.3 = (bf16[2,256,256]{2,1,0:T(8,128)(2,1)S(1)}, f32[2,256,256]{2,1,0:T(8,128)S(1)}, bf16[256,256]{1,0:T(8,128)(2,1)S(1)}) custom-call(s32[10]{0:T(128)S(1)} %pad_add_fusion.info, bf16[256,1024]{1,0:T(8,128)(2,1)S(1)} %collective-permute-done.19.qt, bf16[4,1024,256]{2,1,0:T(8,128)(2,1)S(1)} %bitcast.26, ...), custom_call_target="tpu_custom_call" | custom-call | flops 3623878656 | bytes 8257536 | tf_op jit(solution)/shard_map/project/pallas_call | solution.py:292
  122.0 1.6 %collective-permute-start.22 = (bf16[2,256,256]{2,1,0:T(8,128)(2,1)S(1)}, bf16[2,256,256]{2,1,0:T(8,128)(2,1)S(1)}, u32[]{:S(2)}, u32[]{:S(2)}) collective-permute-start(bf16[2,256,256]{2,1,0:T(8,128)(2,1)S(1)} %halve.1), channel_id=1, source_target_pairs={{0,2},{1,3},{2,0},{3,1},{4,6},{5,7},{6,4},{7,5},{8,10},{9,11},{10,... | collective-permute-start | bytes 786440 | tf_op jit(solution)/shard_map/ppermute | solution.py:375
  126.3 4.1 %collective-permute-done.22 = bf16[2,256,256]{2,1,0:T(8,128)(2,1)S(1)} collective-permute-done((bf16[2,256,256]{2,1,0:T(8,128)(2,1)S(1)}, bf16[2,256,256]{2,1,0:T(8,128)(2,1)S(1)}, u32[]{:S(2)}, u32[]{:S(2)}) %collective-permute-start.22) | collective-permute-done | bytes 262176 | tf_op jit(solution)/shard_map/ppermute | solution.py:375
  (54 shorter events, 17.0 us)
Async XLA Ops:
  0.6 16.0 %collective-permute-start.4 = (bf16[2,4,128,256]{3,2,1,0:T(8,128)(2,1)}, bf16[2,4,128,256]{3,2,1,0:T(8,128)(2,1)S(1)}, u32[]{:S(2)}, u32[]{:S(2)}) collective-permute-start(bf16[2,4,128,256]{3,2,1,0:T(8,128)(2,1)} %refs_0_.1), channel_id=1, source_target_pairs={{8,0},{16,8},{24,16},{28,24},{20,28},{12,20},{4,12},{0,4},{9,1},{1... | collective-permute-start | bytes 1572872 | tf_op jit(solution)/shard_map/ppermute | solution.py:324
  3.6 15.1 %collective-permute-start.5 = (bf16[2,4,128,256]{3,2,1,0:T(8,128)(2,1)}, bf16[2,4,128,256]{3,2,1,0:T(8,128)(2,1)S(1)}, u32[]{:S(2)}, u32[]{:S(2)}) collective-permute-start(bf16[2,4,128,256]{3,2,1,0:T(8,128)(2,1)} %refs_0_.1), channel_id=1, source_target_pairs={{0,8},{8,16},{16,24},{24,28},{28,20},{20,12},{12,4},{4,0},{1,9},{9... | collective-permute-start | bytes 1572872 | tf_op jit(solution)/shard_map/ppermute | solution.py:325
  3.8 24.1 %collective-permute-start = (bf16[2,4,128,256]{3,2,1,0:T(8,128)(2,1)}, bf16[2,4,128,256]{3,2,1,0:T(8,128)(2,1)S(1)}, u32[]{:S(2)}, u32[]{:S(2)}) collective-permute-start(bf16[2,4,128,256]{3,2,1,0:T(8,128)(2,1)} %refs_3_.1), channel_id=1, source_target_pairs={{8,0},{16,8},{24,16},{28,24},{20,28},{12,20},{4,12},{0,4},{9,1},{1... | collective-permute-start | bytes 1572872 | tf_op jit(solution)/shard_map/ppermute | solution.py:324
  5.6 24.3 %collective-permute-start.2 = (bf16[2,4,128,256]{3,2,1,0:T(8,128)(2,1)}, bf16[2,4,128,256]{3,2,1,0:T(8,128)(2,1)S(1)}, u32[]{:S(2)}, u32[]{:S(2)}) collective-permute-start(bf16[2,4,128,256]{3,2,1,0:T(8,128)(2,1)} %refs_3_.1), channel_id=1, source_target_pairs={{0,8},{8,16},{16,24},{24,28},{28,20},{20,12},{12,4},{4,0},{1,9},{9... | collective-permute-start | bytes 1572872 | tf_op jit(solution)/shard_map/ppermute | solution.py:325
  16.7 22.5 %collective-permute-start.6 = (bf16[2,4,128,256]{3,2,1,0:T(8,128)(2,1)S(1)}, bf16[2,4,128,256]{3,2,1,0:T(8,128)(2,1)S(1)}, u32[]{:S(2)}, u32[]{:S(2)}) collective-permute-start(bf16[2,4,128,256]{3,2,1,0:T(8,128)(2,1)S(1)} %collective-permute-done.4.refs_1_), channel_id=1, source_target_pairs={{8,0},{16,8},{24,16},{28,24},{20,28},{12,20},{4,12},{0,4},{9,1},{1... | collective-permute-start | bytes 1572872 | tf_op jit(solution)/shard_map/ppermute | solution.py:324
  18.7 22.5 %collective-permute-start.7 = (bf16[2,4,128,256]{3,2,1,0:T(8,128)(2,1)S(1)}, bf16[2,4,128,256]{3,2,1,0:T(8,128)(2,1)S(1)}, u32[]{:S(2)}, u32[]{:S(2)}) collective-permute-start(bf16[2,4,128,256]{3,2,1,0:T(8,128)(2,1)S(1)} %collective-permute-done.5.refs_2_), channel_id=1, source_target_pairs={{0,8},{8,16},{16,24},{24,28},{28,20},{20,12},{12,4},{4,0},{1,9},{9... | collective-permute-start | bytes 1572872 | tf_op jit(solution)/shard_map/ppermute | solution.py:325
  19.6 1.6 %copy-start.7 = (bf16[1,4,1024,256]{3,2,1,0:T(8,128)(2,1)S(1)}, bf16[1,4,1024,256]{3,2,1,0:T(8,128)(2,1)}, u32[]{:S(2)}) copy-start(bf16[1,4,1024,256]{3,2,1,0:T(8,128)(2,1)} %param.11) | copy-start | bytes 6291460
  21.2 1.0 copy-start.8
  22.2 7.8 %copy-start.3 = (bf16[2,4,128,256]{3,2,1,0:T(8,128)(2,1)S(1)}, bf16[2,4,128,256]{3,2,1,0:T(8,128)(2,1)}, u32[]{:S(2)}) copy-start(bf16[2,4,128,256]{3,2,1,0:T(8,128)(2,1)} %refs_0_.1) | copy-start | bytes 1572868
  22.2 7.8 %copy-start.4 = (bf16[2,4,128,256]{3,2,1,0:T(8,128)(2,1)S(1)}, bf16[2,4,128,256]{3,2,1,0:T(8,128)(2,1)}, u32[]{:S(2)}) copy-start(bf16[2,4,128,256]{3,2,1,0:T(8,128)(2,1)} %refs_3_.1) | copy-start | bytes 1572868
  27.9 22.5 %collective-permute-start.1 = (bf16[2,4,128,256]{3,2,1,0:T(8,128)(2,1)S(1)}, bf16[2,4,128,256]{3,2,1,0:T(8,128)(2,1)S(1)}, u32[]{:S(2)}, u32[]{:S(2)}) collective-permute-start(bf16[2,4,128,256]{3,2,1,0:T(8,128)(2,1)S(1)} %collective-permute-done.refs_4_), channel_id=1, source_target_pairs={{8,0},{16,8},{24,16},{28,24},{20,28},{12,20},{4,12},{0,4},{9,1},{1... | collective-permute-start | bytes 1572872 | tf_op jit(solution)/shard_map/ppermute | solution.py:324
  29.9 22.5 %collective-permute-start.3 = (bf16[2,4,128,256]{3,2,1,0:T(8,128)(2,1)S(1)}, bf16[2,4,128,256]{3,2,1,0:T(8,128)(2,1)S(1)}, u32[]{:S(2)}, u32[]{:S(2)}) collective-permute-start(bf16[2,4,128,256]{3,2,1,0:T(8,128)(2,1)S(1)} %collective-permute-done.2.refs_5_), channel_id=1, source_target_pairs={{0,8},{8,16},{16,24},{24,28},{28,20},{20,12},{12,4},{4,0},{1,9},{9... | collective-permute-start | bytes 1572872 | tf_op jit(solution)/shard_map/ppermute | solution.py:325
  30.0 13.1 %copy-start.1 = (bf16[2,1,1024,256]{3,2,1,0:T(8,128)(2,1)S(1)}, bf16[2,1,1024,256]{3,2,1,0:T(8,128)(2,1)}, u32[]{:S(2)}) copy-start(bf16[2,1,1024,256]{3,2,1,0:T(8,128)(2,1)} %param.17) | copy-start | bytes 3145732
  30.0 13.1 %copy-start.2 = (bf16[2,1,1024,256]{3,2,1,0:T(8,128)(2,1)S(1)}, bf16[2,1,1024,256]{3,2,1,0:T(8,128)(2,1)}, u32[]{:S(2)}) copy-start(bf16[2,1,1024,256]{3,2,1,0:T(8,128)(2,1)} %param.16) | copy-start | bytes 3145732
  41.1 20.5 %collective-permute-start.8 = (bf16[2,4,128,256]{3,2,1,0:T(8,128)(2,1)S(1)}, bf16[2,4,128,256]{3,2,1,0:T(8,128)(2,1)S(1)}, u32[]{:S(2)}, u32[]{:S(2)}) collective-permute-start(bf16[2,4,128,256]{3,2,1,0:T(8,128)(2,1)S(1)} %collective-permute-done.6.refs_0_), channel_id=1, source_target_pairs={{8,0},{16,8},{24,16},{28,24},{20,28},{12,20},{4,12},{0,4},{9,1},{1... | collective-permute-start | bytes 1572872 | tf_op jit(solution)/shard_map/ppermute | solution.py:324
  42.7 20.9 %collective-permute-start.9 = (bf16[2,4,128,256]{3,2,1,0:T(8,128)(2,1)S(1)}, bf16[2,4,128,256]{3,2,1,0:T(8,128)(2,1)S(1)}, u32[]{:S(2)}, u32[]{:S(2)}) collective-permute-start(bf16[2,4,128,256]{3,2,1,0:T(8,128)(2,1)S(1)} %collective-permute-done.7.refs_1_), channel_id=1, source_target_pairs={{0,8},{8,16},{16,24},{24,28},{28,20},{20,12},{12,4},{4,0},{1,9},{9... | collective-permute-start | bytes 1572872 | tf_op jit(solution)/shard_map/ppermute | solution.py:325
  52.4 20.5 %collective-permute-start.10 = (bf16[2,4,128,256]{3,2,1,0:T(8,128)(2,1)S(1)}, bf16[2,4,128,256]{3,2,1,0:T(8,128)(2,1)S(1)}, u32[]{:S(2)}, u32[]{:S(2)}) collective-permute-start(bf16[2,4,128,256]{3,2,1,0:T(8,128)(2,1)S(1)} %collective-permute-done.1.refs_2_), channel_id=1, source_target_pairs={{8,0},{16,8},{24,16},{28,24},{20,28},{12,20},{4,12},{0,4},{9,1},{1... | collective-permute-start | bytes 1572872 | tf_op jit(solution)/shard_map/ppermute | solution.py:324
  54.0 20.9 %collective-permute-start.11 = (bf16[2,4,128,256]{3,2,1,0:T(8,128)(2,1)S(1)}, bf16[2,4,128,256]{3,2,1,0:T(8,128)(2,1)S(1)}, u32[]{:S(2)}, u32[]{:S(2)}) collective-permute-start(bf16[2,4,128,256]{3,2,1,0:T(8,128)(2,1)S(1)} %collective-permute-done.3.refs_3_), channel_id=1, source_target_pairs={{0,8},{8,16},{16,24},{24,28},{28,20},{20,12},{12,4},{4,0},{1,9},{9... | collective-permute-start | bytes 1572872 | tf_op jit(solution)/shard_map/ppermute | solution.py:325
  63.6 14.8 %collective-permute-start.12 = (bf16[4,128,256]{2,1,0:T(8,128)(2,1)S(1)}, bf16[4,128,256]{2,1,0:T(8,128)(2,1)S(1)}, u32[]{:S(2)}, u32[]{:S(2)}) collective-permute-start(bf16[4,128,256]{2,1,0:T(8,128)(2,1)S(1)} %slice_bitcast_fusion.3), channel_id=1, source_target_pairs={{8,0},{16,8},{24,16},{28,24},{20,28},{12,20},{4,12},{0,4},{9,1},{1... | collective-permute-start | bytes 786440 | tf_op jit(solution)/shard_map/ppermute | solution.py:328
  65.3 15.2 %collective-permute-start.13 = (bf16[4,128,256]{2,1,0:T(8,128)(2,1)S(1)}, bf16[4,128,256]{2,1,0:T(8,128)(2,1)S(1)}, u32[]{:S(2)}, u32[]{:S(2)}) collective-permute-start(bf16[4,128,256]{2,1,0:T(8,128)(2,1)S(1)} %slice_bitcast_fusion.2), channel_id=1, source_target_pairs={{0,8},{8,16},{16,24},{24,28},{28,20},{20,12},{12,4},{4,0},{1,9},{9... | collective-permute-start | bytes 786440 | tf_op jit(solution)/shard_map/ppermute | solution.py:329
  72.9 10.4 %collective-permute-start.14 = (bf16[4,128,256]{2,1,0:T(8,128)(2,1)S(1)}, bf16[4,128,256]{2,1,0:T(8,128)(2,1)S(1)}, u32[]{:S(2)}, u32[]{:S(2)}) collective-permute-start(bf16[4,128,256]{2,1,0:T(8,128)(2,1)S(1)} %slice_bitcast_fusion.1), channel_id=1, source_target_pairs={{8,0},{16,8},{24,16},{28,24},{20,28},{12,20},{4,12},{0,4},{9,1},{1... | collective-permute-start | bytes 786440 | tf_op jit(solution)/shard_map/ppermute | solution.py:328
  74.9 9.7 %collective-permute-start.15 = (bf16[4,128,256]{2,1,0:T(8,128)(2,1)S(1)}, bf16[4,128,256]{2,1,0:T(8,128)(2,1)S(1)}, u32[]{:S(2)}, u32[]{:S(2)}) collective-permute-start(bf16[4,128,256]{2,1,0:T(8,128)(2,1)S(1)} %slice_bitcast_fusion), channel_id=1, source_target_pairs={{0,8},{8,16},{16,24},{24,28},{28,20},{20,12},{12,4},{4,0},{1,9},{9... | collective-permute-start | bytes 786440 | tf_op jit(solution)/shard_map/ppermute | solution.py:329
  80.5 4.2 %copy-start = (bf16[1,4,1024,256]{3,2,1,0:T(8,128)(2,1)S(1)}, bf16[1,4,1024,256]{3,2,1,0:T(8,128)(2,1)}, u32[]{:S(2)}) copy-start(bf16[1,4,1024,256]{3,2,1,0:T(8,128)(2,1)} %param.10) | copy-start | bytes 6291460
  80.5 4.2 %copy-start.5 = (s32[2,4]{1,0:T(2,128)S(1)}, s32[2,4]{1,0:T(2,128)}, u32[]{:S(2)}) copy-start(s32[2,4]{1,0:T(2,128)} %pivot_rank.3) | copy-start | bytes 100
  80.5 4.2 %copy-start.6 = (s32[1,4]{1,0:T(1,128)S(1)}, s32[1,4]{1,0:T(1,128)}, u32[]{:S(2)}) copy-start(s32[1,4]{1,0:T(1,128)} %panel_rank.3) | copy-start | bytes 52
  86.3 2.0 %collective-permute-start.16 = (bf16[256,1024]{1,0:T(8,128)(2,1)S(1)}, bf16[256,1024]{1,0:T(8,128)(2,1)S(1)}, u32[]{:S(2)}, u32[]{:S(2)}) collective-permute-start(bf16[256,1024]{1,0:T(8,128)(2,1)S(1)} %get-tuple-element.64), channel_id=1, source_target_pairs={{0,1},{1,0},{2,3},{3,2},{4,5},{5,4},{6,7},{7,6},{8,9},{9,8},{10,11... | collective-permute-start | bytes 1572872 | tf_op jit(solution)/shard_map/ppermute | solution.py:437
  88.5 14.2 %collective-permute-start.17 = (bf16[256,1024]{1,0:T(8,128)(2,1)S(1)}, bf16[256,1024]{1,0:T(8,128)(2,1)S(1)}, u32[]{:S(2)}, u32[]{:S(2)}) collective-permute-start(bf16[256,1024]{1,0:T(8,128)(2,1)S(1)} %add_convert_fusion), channel_id=1, source_target_pairs={{0,2},{1,3},{2,0},{3,1},{4,6},{5,7},{6,4},{7,5},{8,10},{9,11},{10,... | collective-permute-start | bytes 1572872 | tf_op jit(solution)/shard_map/ppermute | solution.py:375
  112.2 3.7 %collective-permute-start.19 = (bf16[256,1024]{1,0:T(8,128)(2,1)S(1)}, bf16[256,1024]{1,0:T(8,128)(2,1)S(1)}, u32[]{:S(2)}, u32[]{:S(2)}) collective-permute-start(bf16[256,1024]{1,0:T(8,128)(2,1)S(1)} %get-tuple-element.67.qt), channel_id=1, source_target_pairs={{0,1},{1,0},{2,3},{3,2},{4,5},{5,4},{6,7},{7,6},{8,9},{9,8},{10,11... | collective-permute-start | bytes 1572872 | tf_op jit(solution)/shard_map/ppermute | solution.py:451
  115.9 4.5 %collective-permute-start.20 = (bf16[2,256,256]{2,1,0:T(8,128)(2,1)S(1)}, bf16[2,256,256]{2,1,0:T(8,128)(2,1)S(1)}, u32[]{:S(2)}, u32[]{:S(2)}) collective-permute-start(bf16[2,256,256]{2,1,0:T(8,128)(2,1)S(1)} %get-tuple-element.77), channel_id=1, source_target_pairs={{0,1},{1,0},{2,3},{3,2},{4,5},{5,4},{6,7},{7,6},{8,9},{9,8},{10,11... | collective-permute-start | bytes 786440 | tf_op jit(solution)/shard_map/ppermute | solution.py:455
  119.8 1.6 %collective-permute-start.21 = (bf16[2,256,256]{2,1,0:T(8,128)(2,1)S(1)}, bf16[2,256,256]{2,1,0:T(8,128)(2,1)S(1)}, u32[]{:S(2)}, u32[]{:S(2)}) collective-permute-start(bf16[2,256,256]{2,1,0:T(8,128)(2,1)S(1)} %get-tuple-element.78), channel_id=1, source_target_pairs={{0,1},{1,0},{2,3},{3,2},{4,5},{5,4},{6,7},{7,6},{8,9},{9,8},{10,11... | collective-permute-start | bytes 786440 | tf_op jit(solution)/shard_map/ppermute | solution.py:455
  119.9 3.7 %collective-permute-start.18 = (f32[256,256]{1,0:T(8,128)S(1)}, f32[256,256]{1,0:T(8,128)S(1)}, u32[]{:S(2)}, u32[]{:S(2)}) collective-permute-start(f32[256,256]{1,0:T(8,128)S(1)} %get-tuple-element.65), channel_id=1, source_target_pairs={{0,1},{1,0},{2,3},{3,2},{4,5},{5,4},{6,7},{7,6},{8,9},{9,8},{10,11... | collective-permute-start | bytes 786440 | tf_op jit(solution)/shard_map/ppermute | solution.py:467
  122.0 8.4 %collective-permute-start.22 = (bf16[2,256,256]{2,1,0:T(8,128)(2,1)S(1)}, bf16[2,256,256]{2,1,0:T(8,128)(2,1)S(1)}, u32[]{:S(2)}, u32[]{:S(2)}) collective-permute-start(bf16[2,256,256]{2,1,0:T(8,128)(2,1)S(1)} %halve.1), channel_id=1, source_target_pairs={{0,2},{1,3},{2,0},{3,1},{4,6},{5,7},{6,4},{7,5},{8,10},{9,11},{10,... | collective-permute-start | bytes 786440 | tf_op jit(solution)/shard_map/ppermute | solution.py:375

commit v7 on v6

--- a/solution.py
+++ b/solution.py
@@ -11,7 +11,7 @@
 
 F32 = jnp.float32
 BF16 = jnp.bfloat16
-BLOCK = 32
+BLOCK = 64
 SUB = 8
 RING_MOST = 16
 MIB = 1 << 20

time: 131 us -> 132 us (level)
  no operation moved by 1% of the time
where the time goes in v7:
time: 132 us; the launch traced here: 131 us
  waiting for transfers between devices  72.4 us (55%)
  Pallas kernels  31.3 us (24%)
  starting transfers between devices  22.3 us (17%)
  local copies, waits for them, and re-layouts  3.42 us (3%)
    ppermute x6, waiting for transfers between devices, step(): self.up[t] = found[number] = lax.ppermute(self.up[t], self.axis, self.ahead)  41.6 us
    pallas_call x14, Pallas kernels, run(): pl.pallas_call(kernel, out_shape=shapes, in_specs=[smem] * len(scalars) +...  31.3 us
    ppermute x2, waiting for transfers between devices, shifted(): lax.ppermute(x, 'cols', [(i, (i + 2 * shift) % cols) for i in range(cols)])  16.8 us
    ppermute x6, starting transfers between devices, step(): self.up[t] = found[number] = lax.ppermute(self.up[t], self.axis, self.ahead)  12 us
    ppermute x6, waiting for transfers between devices, step(): lax.ppermute(self.down[t], self.axis, self.behind)  6.11 us
    ppermute x2, starting transfers between devices, step(): lax.ppermute(self.up[t][0], self.axis, self.ahead)  3.65 us
    ppermute x2, waiting for transfers between devices, step(): lax.ppermute(self.down[t][1], self.axis, self.behind)  3.38 us
    ppermute x2, waiting for transfers between devices, step(): lax.ppermute(self.up[t][0], self.axis, self.ahead)  3.36 us
  transfers between devices with their start and end apart: 23, of which 17 were waited for; matrix products, arithmetic and copies ran while one was open for 1% of the time, Pallas kernels for 15%

profile of v7, /device:TPU:0, one launch (start us, length us, event | category | flops | bytes accessed | tf_op | source)
XLA Modules:
  0.0 131.3 jit_solution(8286895354542472035)
XLA Ops:
  0.6 3.0 %collective-permute-start.4 = (bf16[2,4,128,256]{3,2,1,0:T(8,128)(2,1)}, bf16[2,4,128,256]{3,2,1,0:T(8,128)(2,1)S(1)}, u32[]{:S(2)}, u32[]{:S(2)}) collective-permute-start(bf16[2,4,128,256]{3,2,1,0:T(8,128)(2,1)} %refs_0_.1), channel_id=1, source_target_pairs={{8,0},{16,8},{24,16},{28,24},{20,28},{12,20},{4,12},{0,4},{9,1},{1... | collective-permute-start | bytes 1572872 | tf_op jit(solution)/shard_map/ppermute | solution.py:324
  3.8 1.9 %collective-permute-start = (bf16[2,4,128,256]{3,2,1,0:T(8,128)(2,1)}, bf16[2,4,128,256]{3,2,1,0:T(8,128)(2,1)S(1)}, u32[]{:S(2)}, u32[]{:S(2)}) collective-permute-start(bf16[2,4,128,256]{3,2,1,0:T(8,128)(2,1)} %refs_3_.1), channel_id=1, source_target_pairs={{8,0},{16,8},{24,16},{28,24},{20,28},{12,20},{4,12},{0,4},{9,1},{1... | collective-permute-start | bytes 1572872 | tf_op jit(solution)/shard_map/ppermute | solution.py:324
  5.8 10.9 %collective-permute-done.4.refs_1_ = bf16[2,4,128,256]{3,2,1,0:T(8,128)(2,1)S(1)} collective-permute-done((bf16[2,4,128,256]{3,2,1,0:T(8,128)(2,1)}, bf16[2,4,128,256]{3,2,1,0:T(8,128)(2,1)S(1)}, u32[]{:S(2)}, u32[]{:S(2)}) %collective-permute-start.4) | collective-permute-done | bytes 524320 | tf_op jit(solution)/shard_map/ppermute | solution.py:324
  16.7 2.0 %collective-permute-start.6 = (bf16[2,4,128,256]{3,2,1,0:T(8,128)(2,1)S(1)}, bf16[2,4,128,256]{3,2,1,0:T(8,128)(2,1)S(1)}, u32[]{:S(2)}, u32[]{:S(2)}) collective-permute-start(bf16[2,4,128,256]{3,2,1,0:T(8,128)(2,1)S(1)} %collective-permute-done.4.refs_1_), channel_id=1, source_target_pairs={{8,0},{16,8},{24,16},{28,24},{20,28},{12,20},{4,12},{0,4},{9,1},{1... | collective-permute-start | bytes 1572872 | tf_op jit(solution)/shard_map/ppermute | solution.py:324
  19.6 1.6 %copy-done.7 = bf16[1,4,1024,256]{3,2,1,0:T(8,128)(2,1)S(1)} copy-done((bf16[1,4,1024,256]{3,2,1,0:T(8,128)(2,1)S(1)}, bf16[1,4,1024,256]{3,2,1,0:T(8,128)(2,1)}, u32[]{:S(2)}) %copy-start.7) | copy-done | bytes 2097176
  23.0 4.9 %collective-permute-done.refs_4_ = bf16[2,4,128,256]{3,2,1,0:T(8,128)(2,1)S(1)} collective-permute-done((bf16[2,4,128,256]{3,2,1,0:T(8,128)(2,1)}, bf16[2,4,128,256]{3,2,1,0:T(8,128)(2,1)S(1)}, u32[]{:S(2)}, u32[]{:S(2)}) %collective-permute-start) | collective-permute-done | bytes 524320 | tf_op jit(solution)/shard_map/ppermute | solution.py:324
  27.9 2.0 %collective-permute-start.1 = (bf16[2,4,128,256]{3,2,1,0:T(8,128)(2,1)S(1)}, bf16[2,4,128,256]{3,2,1,0:T(8,128)(2,1)S(1)}, u32[]{:S(2)}, u32[]{:S(2)}) collective-permute-start(bf16[2,4,128,256]{3,2,1,0:T(8,128)(2,1)S(1)} %collective-permute-done.refs_4_), channel_id=1, source_target_pairs={{8,0},{16,8},{24,16},{28,24},{20,28},{12,20},{4,12},{0,4},{9,1},{1... | collective-permute-start | bytes 1572872 | tf_op jit(solution)/shard_map/ppermute | solution.py:324
  30.0 1.8 %gather.3 = (f32[2,4,256,256]{3,2,1,0:T(8,128)S(1)}, f32[2,4,256,256]{3,2,1,0:T(8,128)S(1)}, bf16[2,4,1024,256]{3,2,1,0:T(8,128)(2,1)S(1)}) custom-call(s32[10]{0:T(128)S(1)} %pad_add_fusion.info, bf16[4,256,1024]{2,1,0:T(8,128)(2,1)S(1)} %get-tuple-element.44.panel_vt, bf16[256,1024]{1,0:T(8,128)(2,1)S(1)} %get-tuple-element.42.sampler_t, ...), custom_call_target="tpu_custom_call" | custom-call | flops 805306368 | bytes 14155776 | tf_op jit(solution)/shard_map/gather/pallas_call | solution.py:292
  31.9 7.3 %collective-permute-done.6.refs_0_ = bf16[2,4,128,256]{3,2,1,0:T(8,128)(2,1)S(1)} collective-permute-done((bf16[2,4,128,256]{3,2,1,0:T(8,128)(2,1)S(1)}, bf16[2,4,128,256]{3,2,1,0:T(8,128)(2,1)S(1)}, u32[]{:S(2)}, u32[]{:S(2)}) %collective-permute-start.6) | collective-permute-done | bytes 524320 | tf_op jit(solution)/shard_map/ppermute | solution.py:324
  39.1 2.0 %collective-permute-done.7.refs_1_ = bf16[2,4,128,256]{3,2,1,0:T(8,128)(2,1)S(1)} collective-permute-done((bf16[2,4,128,256]{3,2,1,0:T(8,128)(2,1)S(1)}, bf16[2,4,128,256]{3,2,1,0:T(8,128)(2,1)S(1)}, u32[]{:S(2)}, u32[]{:S(2)}) %collective-permute-start.7) | collective-permute-done | bytes 524320 | tf_op jit(solution)/shard_map/ppermute | solution.py:325
  41.1 1.6 %collective-permute-start.8 = (bf16[2,4,128,256]{3,2,1,0:T(8,128)(2,1)S(1)}, bf16[2,4,128,256]{3,2,1,0:T(8,128)(2,1)S(1)}, u32[]{:S(2)}, u32[]{:S(2)}) collective-permute-start(bf16[2,4,128,256]{3,2,1,0:T(8,128)(2,1)S(1)} %collective-permute-done.6.refs_0_), channel_id=1, source_target_pairs={{8,0},{16,8},{24,16},{28,24},{20,28},{12,20},{4,12},{0,4},{9,1},{1... | collective-permute-start | bytes 1572872 | tf_op jit(solution)/shard_map/ppermute | solution.py:324
  44.5 5.9 %collective-permute-done.1.refs_2_ = bf16[2,4,128,256]{3,2,1,0:T(8,128)(2,1)S(1)} collective-permute-done((bf16[2,4,128,256]{3,2,1,0:T(8,128)(2,1)S(1)}, bf16[2,4,128,256]{3,2,1,0:T(8,128)(2,1)S(1)}, u32[]{:S(2)}, u32[]{:S(2)}) %collective-permute-start.1) | collective-permute-done | bytes 524320 | tf_op jit(solution)/shard_map/ppermute | solution.py:324
  50.4 2.0 %collective-permute-done.3.refs_3_ = bf16[2,4,128,256]{3,2,1,0:T(8,128)(2,1)S(1)} collective-permute-done((bf16[2,4,128,256]{3,2,1,0:T(8,128)(2,1)S(1)}, bf16[2,4,128,256]{3,2,1,0:T(8,128)(2,1)S(1)}, u32[]{:S(2)}, u32[]{:S(2)}) %collective-permute-start.3) | collective-permute-done | bytes 524320 | tf_op jit(solution)/shard_map/ppermute | solution.py:325
  52.4 1.6 %collective-permute-start.10 = (bf16[2,4,128,256]{3,2,1,0:T(8,128)(2,1)S(1)}, bf16[2,4,128,256]{3,2,1,0:T(8,128)(2,1)S(1)}, u32[]{:S(2)}, u32[]{:S(2)}) collective-permute-start(bf16[2,4,128,256]{3,2,1,0:T(8,128)(2,1)S(1)} %collective-permute-done.1.refs_2_), channel_id=1, source_target_pairs={{8,0},{16,8},{24,16},{28,24},{20,28},{12,20},{4,12},{0,4},{9,1},{1... | collective-permute-start | bytes 1572872 | tf_op jit(solution)/shard_map/ppermute | solution.py:324
  54.4 1.6 %gather.4 = (f32[2,4,256,256]{3,2,1,0:T(8,128)S(1)}, f32[2,4,256,256]{3,2,1,0:T(8,128)S(1)}, bf16[2,4,1024,256]{3,2,1,0:T(8,128)(2,1)S(1)}) custom-call(s32[10]{0:T(128)S(1)} %pad_add_fusion.info, bf16[4,256,1024]{2,1,0:T(8,128)(2,1)S(1)} %get-tuple-element.44.panel_vt, ...), custom_call_target="tpu_custom_call", output_to_operand_aliasing={{0}: (7, {}), {1}: (8, {}), {2}: (9, {})} | custom-call | flops 536870912 | bytes 21495808 | tf_op jit(solution)/shard_map/gather/pallas_call | solution.py:292
  56.1 5.5 %collective-permute-done.8.refs_0_ = bf16[2,4,128,256]{3,2,1,0:T(8,128)(2,1)S(1)} collective-permute-done((bf16[2,4,128,256]{3,2,1,0:T(8,128)(2,1)S(1)}, bf16[2,4,128,256]{3,2,1,0:T(8,128)(2,1)S(1)}, u32[]{:S(2)}, u32[]{:S(2)}) %collective-permute-start.8) | collective-permute-done | bytes 524320 | tf_op jit(solution)/shard_map/ppermute | solution.py:324
  61.6 2.0 %collective-permute-done.9.refs_1_ = bf16[2,4,128,256]{3,2,1,0:T(8,128)(2,1)S(1)} collective-permute-done((bf16[2,4,128,256]{3,2,1,0:T(8,128)(2,1)S(1)}, bf16[2,4,128,256]{3,2,1,0:T(8,128)(2,1)S(1)}, u32[]{:S(2)}, u32[]{:S(2)}) %collective-permute-start.9) | collective-permute-done | bytes 524320 | tf_op jit(solution)/shard_map/ppermute | solution.py:325
  63.6 1.6 %collective-permute-start.12 = (bf16[4,128,256]{2,1,0:T(8,128)(2,1)S(1)}, bf16[4,128,256]{2,1,0:T(8,128)(2,1)S(1)}, u32[]{:S(2)}, u32[]{:S(2)}) collective-permute-start(bf16[4,128,256]{2,1,0:T(8,128)(2,1)S(1)} %slice_bitcast_fusion.3), channel_id=1, source_target_pairs={{8,0},{16,8},{24,16},{28,24},{20,28},{12,20},{4,12},{0,4},{9,1},{1... | collective-permute-start | bytes 786440 | tf_op jit(solution)/shard_map/ppermute | solution.py:328
  65.8 7.1 %collective-permute-done.10.refs_2_ = bf16[2,4,128,256]{3,2,1,0:T(8,128)(2,1)S(1)} collective-permute-done((bf16[2,4,128,256]{3,2,1,0:T(8,128)(2,1)S(1)}, bf16[2,4,128,256]{3,2,1,0:T(8,128)(2,1)S(1)}, u32[]{:S(2)}, u32[]{:S(2)}) %collective-permute-start.10) | collective-permute-done | bytes 524320 | tf_op jit(solution)/shard_map/ppermute | solution.py:324
  72.9 2.0 %collective-permute-start.14 = (bf16[4,128,256]{2,1,0:T(8,128)(2,1)S(1)}, bf16[4,128,256]{2,1,0:T(8,128)(2,1)S(1)}, u32[]{:S(2)}, u32[]{:S(2)}) collective-permute-start(bf16[4,128,256]{2,1,0:T(8,128)(2,1)S(1)} %slice_bitcast_fusion.1), channel_id=1, source_target_pairs={{8,0},{16,8},{24,16},{28,24},{20,28},{12,20},{4,12},{0,4},{9,1},{1... | collective-permute-start | bytes 786440 | tf_op jit(solution)/shard_map/ppermute | solution.py:328
  75.3 1.6 %gather.5 = (f32[2,4,256,256]{3,2,1,0:T(8,128)S(1)}, f32[2,4,256,256]{3,2,1,0:T(8,128)S(1)}, bf16[2,4,1024,256]{3,2,1,0:T(8,128)(2,1)S(1)}) custom-call(s32[10]{0:T(128)S(1)} %pad_add_fusion.info, bf16[4,256,1024]{2,1,0:T(8,128)(2,1)S(1)} %get-tuple-element.44.panel_vt, ...), custom_call_target="tpu_custom_call", output_to_operand_aliasing={{0}: (7, {}), {1}: (8, {}), {2}: (9, {})} | custom-call | flops 536870912 | bytes 21495808 | tf_op jit(solution)/shard_map/gather/pallas_call | solution.py:292
  78.5 2.0 %collective-permute-done.13.refs_1_ = bf16[4,128,256]{2,1,0:T(8,128)(2,1)S(1)} collective-permute-done((bf16[4,128,256]{2,1,0:T(8,128)(2,1)S(1)}, bf16[4,128,256]{2,1,0:T(8,128)(2,1)S(1)}, u32[]{:S(2)}, u32[]{:S(2)}) %collective-permute-start.13) | collective-permute-done | bytes 262176 | tf_op jit(solution)/shard_map/ppermute | solution.py:329
  81.5 1.8 %collective-permute-done.14.refs_0_ = bf16[4,128,256]{2,1,0:T(8,128)(2,1)S(1)} collective-permute-done((bf16[4,128,256]{2,1,0:T(8,128)(2,1)S(1)}, bf16[4,128,256]{2,1,0:T(8,128)(2,1)S(1)}, u32[]{:S(2)}, u32[]{:S(2)}) %collective-permute-start.14) | collective-permute-done | bytes 262176 | tf_op jit(solution)/shard_map/ppermute | solution.py:328
  84.6 1.7 %update.3 = (bf16[4,256,256]{2,1,0:T(8,128)(2,1)S(1)}, bf16[256,1024]{1,0:T(8,128)(2,1)S(1)}) custom-call(s32[10]{0:T(128)S(1)} %pad_add_fusion.info, s32[1,4]{1,0:T(1,128)S(1)} %copy-done.6, s32[2,4]{1,0:T(2,128)S(1)} %copy-done.5, bf16[2,4,256,256]{3,2,1,0:T(8,128)(2,1)S(1)} %get-tuple-element.61.sampled, f32[2,4,256,256]{3,2,1,0:T(8,128)S(1)} %get-tuple-element.62.met, ...), custom_call_target="tpu_custom_call" | custom-call | flops 1342177280 | bytes 8912896 | tf_op jit(solution)/shard_map/update/pallas_call | solution.py:292
  86.4 1.7 %update.2 = (bf16[4,256,256]{2,1,0:T(8,128)(2,1)S(1)}, f32[256,1024]{1,0:T(8,128)S(1)}) custom-call(s32[10]{0:T(128)S(1)} %pad_add_fusion.info, s32[1,4]{1,0:T(1,128)S(1)} %copy-done.6, s32[2,4]{1,0:T(2,128)S(1)} %copy-done.5, bf16[2,4,256,256]{3,2,1,0:T(8,128)(2,1)S(1)} %get-tuple-element.61.sampled, f32[2,4,256,256]{3,2,1,0:T(8,128)S(1)} %get-tuple-element.62.met, ...), custom_call_target="tpu_custom_call" | custom-call | flops 1342177280 | bytes 9437184 | tf_op jit(solution)/shard_map/update/pallas_call | solution.py:292
  88.5 1.6 %collective-permute-start.17 = (bf16[256,1024]{1,0:T(8,128)(2,1)S(1)}, bf16[256,1024]{1,0:T(8,128)(2,1)S(1)}, u32[]{:S(2)}, u32[]{:S(2)}) collective-permute-start(bf16[256,1024]{1,0:T(8,128)(2,1)S(1)} %add_convert_fusion), channel_id=1, source_target_pairs={{0,2},{1,3},{2,0},{3,1},{4,6},{5,7},{6,4},{7,5},{8,10},{9,11},{10,... | collective-permute-start | bytes 1572872 | tf_op jit(solution)/shard_map/ppermute | solution.py:375
  90.1 12.6 %collective-permute-done.17.refs_2_ = bf16[256,1024]{1,0:T(8,128)(2,1)S(1)} collective-permute-done((bf16[256,1024]{1,0:T(8,128)(2,1)S(1)}, bf16[256,1024]{1,0:T(8,128)(2,1)S(1)}, u32[]{:S(2)}, u32[]{:S(2)}) %collective-permute-start.17) | collective-permute-done | bytes 524320 | tf_op jit(solution)/shard_map/ppermute | solution.py:375
  102.7 9.6 %orthonormal.1 = (bf16[256,1024]{1,0:T(8,128)(2,1)S(1)}, f32[256,256]{1,0:T(8,128)S(1)}, f32[2,256,256]{2,1,0:T(8,128)}) custom-call(s32[10]{0:T(128)S(1)} %pad_add_fusion.info, f32[256,1024]{1,0:T(8,128)S(1)} %start.1, f32[256,1024]{1,0:T(8,128)S(1)} %get-tuple-element.63.refs_0_, bf16[256,1024]{1,0:T(8,128)(2,1)S(1)} %collective-permute-done.16.refs_1_, ...), custom_call_target="tpu_custom_call" | custom-call | flops 17179869184 | bytes 4456448 | tf_op jit(solution)/shard_map/orthonormal/pallas_call | solution.py:292
  112.3 3.6 %project.2 = (bf16[2,256,256]{2,1,0:T(8,128)(2,1)S(1)}, f32[2,256,256]{2,1,0:T(8,128)S(1)}, bf16[256,256]{1,0:T(8,128)(2,1)S(1)}) custom-call(s32[10]{0:T(128)S(1)} %pad_add_fusion.info, bf16[256,1024]{1,0:T(8,128)(2,1)S(1)} %get-tuple-element.67.qt, bf16[4,1024,256]{2,1,0:T(8,128)(2,1)S(1)} %bitcast.25, bf16[4,256,256]{2,1,0:T(8,128)(2,1)S(1)} %get-tuple-element.68.cross, ...), custom_call_target="tpu_custom_call" | custom-call | flops 3623878656 | bytes 8257536 | tf_op jit(solution)/shard_map/project/pallas_call | solution.py:292
  116.5 3.4 %project.3 = (bf16[2,256,256]{2,1,0:T(8,128)(2,1)S(1)}, f32[2,256,256]{2,1,0:T(8,128)S(1)}, bf16[256,256]{1,0:T(8,128)(2,1)S(1)}) custom-call(s32[10]{0:T(128)S(1)} %pad_add_fusion.info, bf16[256,1024]{1,0:T(8,128)(2,1)S(1)} %collective-permute-done.19.qt, bf16[4,1024,256]{2,1,0:T(8,128)(2,1)S(1)} %bitcast.26, ...), custom_call_target="tpu_custom_call" | custom-call | flops 3623878656 | bytes 8257536 | tf_op jit(solution)/shard_map/project/pallas_call | solution.py:292
  122.0 1.6 %collective-permute-start.22 = (bf16[2,256,256]{2,1,0:T(8,128)(2,1)S(1)}, bf16[2,256,256]{2,1,0:T(8,128)(2,1)S(1)}, u32[]{:S(2)}, u32[]{:S(2)}) collective-permute-start(bf16[2,256,256]{2,1,0:T(8,128)(2,1)S(1)} %halve.1), channel_id=1, source_target_pairs={{0,2},{1,3},{2,0},{3,1},{4,6},{5,7},{6,4},{7,5},{8,10},{9,11},{10,... | collective-permute-start | bytes 786440 | tf_op jit(solution)/shard_map/ppermute | solution.py:375
  126.3 4.1 %collective-permute-done.22 = bf16[2,256,256]{2,1,0:T(8,128)(2,1)S(1)} collective-permute-done((bf16[2,256,256]{2,1,0:T(8,128)(2,1)S(1)}, bf16[2,256,256]{2,1,0:T(8,128)(2,1)S(1)}, u32[]{:S(2)}, u32[]{:S(2)}) %collective-permute-start.22) | collective-permute-done | bytes 262176 | tf_op jit(solution)/shard_map/ppermute | solution.py:375
  (54 shorter events, 17.0 us)
Async XLA Ops:
  0.6 16.0 %collective-permute-start.4 = (bf16[2,4,128,256]{3,2,1,0:T(8,128)(2,1)}, bf16[2,4,128,256]{3,2,1,0:T(8,128)(2,1)S(1)}, u32[]{:S(2)}, u32[]{:S(2)}) collective-permute-start(bf16[2,4,128,256]{3,2,1,0:T(8,128)(2,1)} %refs_0_.1), channel_id=1, source_target_pairs={{8,0},{16,8},{24,16},{28,24},{20,28},{12,20},{4,12},{0,4},{9,1},{1... | collective-permute-start | bytes 1572872 | tf_op jit(solution)/shard_map/ppermute | solution.py:324
  3.6 15.1 %collective-permute-start.5 = (bf16[2,4,128,256]{3,2,1,0:T(8,128)(2,1)}, bf16[2,4,128,256]{3,2,1,0:T(8,128)(2,1)S(1)}, u32[]{:S(2)}, u32[]{:S(2)}) collective-permute-start(bf16[2,4,128,256]{3,2,1,0:T(8,128)(2,1)} %refs_0_.1), channel_id=1, source_target_pairs={{0,8},{8,16},{16,24},{24,28},{28,20},{20,12},{12,4},{4,0},{1,9},{9... | collective-permute-start | bytes 1572872 | tf_op jit(solution)/shard_map/ppermute | solution.py:325
  3.8 24.1 %collective-permute-start = (bf16[2,4,128,256]{3,2,1,0:T(8,128)(2,1)}, bf16[2,4,128,256]{3,2,1,0:T(8,128)(2,1)S(1)}, u32[]{:S(2)}, u32[]{:S(2)}) collective-permute-start(bf16[2,4,128,256]{3,2,1,0:T(8,128)(2,1)} %refs_3_.1), channel_id=1, source_target_pairs={{8,0},{16,8},{24,16},{28,24},{20,28},{12,20},{4,12},{0,4},{9,1},{1... | collective-permute-start | bytes 1572872 | tf_op jit(solution)/shard_map/ppermute | solution.py:324
  5.6 24.3 %collective-permute-start.2 = (bf16[2,4,128,256]{3,2,1,0:T(8,128)(2,1)}, bf16[2,4,128,256]{3,2,1,0:T(8,128)(2,1)S(1)}, u32[]{:S(2)}, u32[]{:S(2)}) collective-permute-start(bf16[2,4,128,256]{3,2,1,0:T(8,128)(2,1)} %refs_3_.1), channel_id=1, source_target_pairs={{0,8},{8,16},{16,24},{24,28},{28,20},{20,12},{12,4},{4,0},{1,9},{9... | collective-permute-start | bytes 1572872 | tf_op jit(solution)/shard_map/ppermute | solution.py:325
  16.7 22.5 %collective-permute-start.6 = (bf16[2,4,128,256]{3,2,1,0:T(8,128)(2,1)S(1)}, bf16[2,4,128,256]{3,2,1,0:T(8,128)(2,1)S(1)}, u32[]{:S(2)}, u32[]{:S(2)}) collective-permute-start(bf16[2,4,128,256]{3,2,1,0:T(8,128)(2,1)S(1)} %collective-permute-done.4.refs_1_), channel_id=1, source_target_pairs={{8,0},{16,8},{24,16},{28,24},{20,28},{12,20},{4,12},{0,4},{9,1},{1... | collective-permute-start | bytes 1572872 | tf_op jit(solution)/shard_map/ppermute | solution.py:324
  18.7 22.5 %collective-permute-start.7 = (bf16[2,4,128,256]{3,2,1,0:T(8,128)(2,1)S(1)}, bf16[2,4,128,256]{3,2,1,0:T(8,128)(2,1)S(1)}, u32[]{:S(2)}, u32[]{:S(2)}) collective-permute-start(bf16[2,4,128,256]{3,2,1,0:T(8,128)(2,1)S(1)} %collective-permute-done.5.refs_2_), channel_id=1, source_target_pairs={{0,8},{8,16},{16,24},{24,28},{28,20},{20,12},{12,4},{4,0},{1,9},{9... | collective-permute-start | bytes 1572872 | tf_op jit(solution)/shard_map/ppermute | solution.py:325
  19.6 1.6 %copy-start.7 = (bf16[1,4,1024,256]{3,2,1,0:T(8,128)(2,1)S(1)}, bf16[1,4,1024,256]{3,2,1,0:T(8,128)(2,1)}, u32[]{:S(2)}) copy-start(bf16[1,4,1024,256]{3,2,1,0:T(8,128)(2,1)} %param.11) | copy-start | bytes 6291460
  21.2 1.0 copy-start.8
  22.2 7.8 %copy-start.3 = (bf16[2,4,128,256]{3,2,1,0:T(8,128)(2,1)S(1)}, bf16[2,4,128,256]{3,2,1,0:T(8,128)(2,1)}, u32[]{:S(2)}) copy-start(bf16[2,4,128,256]{3,2,1,0:T(8,128)(2,1)} %refs_0_.1) | copy-start | bytes 1572868
  22.2 7.8 %copy-start.4 = (bf16[2,4,128,256]{3,2,1,0:T(8,128)(2,1)S(1)}, bf16[2,4,128,256]{3,2,1,0:T(8,128)(2,1)}, u32[]{:S(2)}) copy-start(bf16[2,4,128,256]{3,2,1,0:T(8,128)(2,1)} %refs_3_.1) | copy-start | bytes 1572868
  27.9 22.5 %collective-permute-start.1 = (bf16[2,4,128,256]{3,2,1,0:T(8,128)(2,1)S(1)}, bf16[2,4,128,256]{3,2,1,0:T(8,128)(2,1)S(1)}, u32[]{:S(2)}, u32[]{:S(2)}) collective-permute-start(bf16[2,4,128,256]{3,2,1,0:T(8,128)(2,1)S(1)} %collective-permute-done.refs_4_), channel_id=1, source_target_pairs={{8,0},{16,8},{24,16},{28,24},{20,28},{12,20},{4,12},{0,4},{9,1},{1... | collective-permute-start | bytes 1572872 | tf_op jit(solution)/shard_map/ppermute | solution.py:324
  29.9 22.5 %collective-permute-start.3 = (bf16[2,4,128,256]{3,2,1,0:T(8,128)(2,1)S(1)}, bf16[2,4,128,256]{3,2,1,0:T(8,128)(2,1)S(1)}, u32[]{:S(2)}, u32[]{:S(2)}) collective-permute-start(bf16[2,4,128,256]{3,2,1,0:T(8,128)(2,1)S(1)} %collective-permute-done.2.refs_5_), channel_id=1, source_target_pairs={{0,8},{8,16},{16,24},{24,28},{28,20},{20,12},{12,4},{4,0},{1,9},{9... | collective-permute-start | bytes 1572872 | tf_op jit(solution)/shard_map/ppermute | solution.py:325
  30.0 13.1 %copy-start.1 = (bf16[2,1,1024,256]{3,2,1,0:T(8,128)(2,1)S(1)}, bf16[2,1,1024,256]{3,2,1,0:T(8,128)(2,1)}, u32[]{:S(2)}) copy-start(bf16[2,1,1024,256]{3,2,1,0:T(8,128)(2,1)} %param.17) | copy-start | bytes 3145732
  30.0 13.1 %copy-start.2 = (bf16[2,1,1024,256]{3,2,1,0:T(8,128)(2,1)S(1)}, bf16[2,1,1024,256]{3,2,1,0:T(8,128)(2,1)}, u32[]{:S(2)}) copy-start(bf16[2,1,1024,256]{3,2,1,0:T(8,128)(2,1)} %param.16) | copy-start | bytes 3145732
  41.1 20.5 %collective-permute-start.8 = (bf16[2,4,128,256]{3,2,1,0:T(8,128)(2,1)S(1)}, bf16[2,4,128,256]{3,2,1,0:T(8,128)(2,1)S(1)}, u32[]{:S(2)}, u32[]{:S(2)}) collective-permute-start(bf16[2,4,128,256]{3,2,1,0:T(8,128)(2,1)S(1)} %collective-permute-done.6.refs_0_), channel_id=1, source_target_pairs={{8,0},{16,8},{24,16},{28,24},{20,28},{12,20},{4,12},{0,4},{9,1},{1... | collective-permute-start | bytes 1572872 | tf_op jit(solution)/shard_map/ppermute | solution.py:324
  42.7 20.9 %collective-permute-start.9 = (bf16[2,4,128,256]{3,2,1,0:T(8,128)(2,1)S(1)}, bf16[2,4,128,256]{3,2,1,0:T(8,128)(2,1)S(1)}, u32[]{:S(2)}, u32[]{:S(2)}) collective-permute-start(bf16[2,4,128,256]{3,2,1,0:T(8,128)(2,1)S(1)} %collective-permute-done.7.refs_1_), channel_id=1, source_target_pairs={{0,8},{8,16},{16,24},{24,28},{28,20},{20,12},{12,4},{4,0},{1,9},{9... | collective-permute-start | bytes 1572872 | tf_op jit(solution)/shard_map/ppermute | solution.py:325
  52.4 20.5 %collective-permute-start.10 = (bf16[2,4,128,256]{3,2,1,0:T(8,128)(2,1)S(1)}, bf16[2,4,128,256]{3,2,1,0:T(8,128)(2,1)S(1)}, u32[]{:S(2)}, u32[]{:S(2)}) collective-permute-start(bf16[2,4,128,256]{3,2,1,0:T(8,128)(2,1)S(1)} %collective-permute-done.1.refs_2_), channel_id=1, source_target_pairs={{8,0},{16,8},{24,16},{28,24},{20,28},{12,20},{4,12},{0,4},{9,1},{1... | collective-permute-start | bytes 1572872 | tf_op jit(solution)/shard_map/ppermute | solution.py:324
  54.0 20.9 %collective-permute-start.11 = (bf16[2,4,128,256]{3,2,1,0:T(8,128)(2,1)S(1)}, bf16[2,4,128,256]{3,2,1,0:T(8,128)(2,1)S(1)}, u32[]{:S(2)}, u32[]{:S(2)}) collective-permute-start(bf16[2,4,128,256]{3,2,1,0:T(8,128)(2,1)S(1)} %collective-permute-done.3.refs_3_), channel_id=1, source_target_pairs={{0,8},{8,16},{16,24},{24,28},{28,20},{20,12},{12,4},{4,0},{1,9},{9... | collective-permute-start | bytes 1572872 | tf_op jit(solution)/shard_map/ppermute | solution.py:325
  63.6 14.8 %collective-permute-start.12 = (bf16[4,128,256]{2,1,0:T(8,128)(2,1)S(1)}, bf16[4,128,256]{2,1,0:T(8,128)(2,1)S(1)}, u32[]{:S(2)}, u32[]{:S(2)}) collective-permute-start(bf16[4,128,256]{2,1,0:T(8,128)(2,1)S(1)} %slice_bitcast_fusion.3), channel_id=1, source_target_pairs={{8,0},{16,8},{24,16},{28,24},{20,28},{12,20},{4,12},{0,4},{9,1},{1... | collective-permute-start | bytes 786440 | tf_op jit(solution)/shard_map/ppermute | solution.py:328
  65.3 15.2 %collective-permute-start.13 = (bf16[4,128,256]{2,1,0:T(8,128)(2,1)S(1)}, bf16[4,128,256]{2,1,0:T(8,128)(2,1)S(1)}, u32[]{:S(2)}, u32[]{:S(2)}) collective-permute-start(bf16[4,128,256]{2,1,0:T(8,128)(2,1)S(1)} %slice_bitcast_fusion.2), channel_id=1, source_target_pairs={{0,8},{8,16},{16,24},{24,28},{28,20},{20,12},{12,4},{4,0},{1,9},{9... | collective-permute-start | bytes 786440 | tf_op jit(solution)/shard_map/ppermute | solution.py:329
  72.9 10.4 %collective-permute-start.14 = (bf16[4,128,256]{2,1,0:T(8,128)(2,1)S(1)}, bf16[4,128,256]{2,1,0:T(8,128)(2,1)S(1)}, u32[]{:S(2)}, u32[]{:S(2)}) collective-permute-start(bf16[4,128,256]{2,1,0:T(8,128)(2,1)S(1)} %slice_bitcast_fusion.1), channel_id=1, source_target_pairs={{8,0},{16,8},{24,16},{28,24},{20,28},{12,20},{4,12},{0,4},{9,1},{1... | collective-permute-start | bytes 786440 | tf_op jit(solution)/shard_map/ppermute | solution.py:328
  74.9 9.7 %collective-permute-start.15 = (bf16[4,128,256]{2,1,0:T(8,128)(2,1)S(1)}, bf16[4,128,256]{2,1,0:T(8,128)(2,1)S(1)}, u32[]{:S(2)}, u32[]{:S(2)}) collective-permute-start(bf16[4,128,256]{2,1,0:T(8,128)(2,1)S(1)} %slice_bitcast_fusion), channel_id=1, source_target_pairs={{0,8},{8,16},{16,24},{24,28},{28,20},{20,12},{12,4},{4,0},{1,9},{9... | collective-permute-start | bytes 786440 | tf_op jit(solution)/shard_map/ppermute | solution.py:329
  80.5 4.2 %copy-start = (bf16[1,4,1024,256]{3,2,1,0:T(8,128)(2,1)S(1)}, bf16[1,4,1024,256]{3,2,1,0:T(8,128)(2,1)}, u32[]{:S(2)}) copy-start(bf16[1,4,1024,256]{3,2,1,0:T(8,128)(2,1)} %param.10) | copy-start | bytes 6291460
  80.5 4.2 %copy-start.5 = (s32[2,4]{1,0:T(2,128)S(1)}, s32[2,4]{1,0:T(2,128)}, u32[]{:S(2)}) copy-start(s32[2,4]{1,0:T(2,128)} %pivot_rank.3) | copy-start | bytes 100
  80.5 4.2 %copy-start.6 = (s32[1,4]{1,0:T(1,128)S(1)}, s32[1,4]{1,0:T(1,128)}, u32[]{:S(2)}) copy-start(s32[1,4]{1,0:T(1,128)} %panel_rank.3) | copy-start | bytes 52
  86.3 2.0 %collective-permute-start.16 = (bf16[256,1024]{1,0:T(8,128)(2,1)S(1)}, bf16[256,1024]{1,0:T(8,128)(2,1)S(1)}, u32[]{:S(2)}, u32[]{:S(2)}) collective-permute-start(bf16[256,1024]{1,0:T(8,128)(2,1)S(1)} %get-tuple-element.64), channel_id=1, source_target_pairs={{0,1},{1,0},{2,3},{3,2},{4,5},{5,4},{6,7},{7,6},{8,9},{9,8},{10,11... | collective-permute-start | bytes 1572872 | tf_op jit(solution)/shard_map/ppermute | solution.py:437
  88.5 14.2 %collective-permute-start.17 = (bf16[256,1024]{1,0:T(8,128)(2,1)S(1)}, bf16[256,1024]{1,0:T(8,128)(2,1)S(1)}, u32[]{:S(2)}, u32[]{:S(2)}) collective-permute-start(bf16[256,1024]{1,0:T(8,128)(2,1)S(1)} %add_convert_fusion), channel_id=1, source_target_pairs={{0,2},{1,3},{2,0},{3,1},{4,6},{5,7},{6,4},{7,5},{8,10},{9,11},{10,... | collective-permute-start | bytes 1572872 | tf_op jit(solution)/shard_map/ppermute | solution.py:375
  112.2 3.7 %collective-permute-start.19 = (bf16[256,1024]{1,0:T(8,128)(2,1)S(1)}, bf16[256,1024]{1,0:T(8,128)(2,1)S(1)}, u32[]{:S(2)}, u32[]{:S(2)}) collective-permute-start(bf16[256,1024]{1,0:T(8,128)(2,1)S(1)} %get-tuple-element.67.qt), channel_id=1, source_target_pairs={{0,1},{1,0},{2,3},{3,2},{4,5},{5,4},{6,7},{7,6},{8,9},{9,8},{10,11... | collective-permute-start | bytes 1572872 | tf_op jit(solution)/shard_map/ppermute | solution.py:451
  115.9 4.5 %collective-permute-start.20 = (bf16[2,256,256]{2,1,0:T(8,128)(2,1)S(1)}, bf16[2,256,256]{2,1,0:T(8,128)(2,1)S(1)}, u32[]{:S(2)}, u32[]{:S(2)}) collective-permute-start(bf16[2,256,256]{2,1,0:T(8,128)(2,1)S(1)} %get-tuple-element.77), channel_id=1, source_target_pairs={{0,1},{1,0},{2,3},{3,2},{4,5},{5,4},{6,7},{7,6},{8,9},{9,8},{10,11... | collective-permute-start | bytes 786440 | tf_op jit(solution)/shard_map/ppermute | solution.py:455
  119.8 1.6 %collective-permute-start.21 = (bf16[2,256,256]{2,1,0:T(8,128)(2,1)S(1)}, bf16[2,256,256]{2,1,0:T(8,128)(2,1)S(1)}, u32[]{:S(2)}, u32[]{:S(2)}) collective-permute-start(bf16[2,256,256]{2,1,0:T(8,128)(2,1)S(1)} %get-tuple-element.78), channel_id=1, source_target_pairs={{0,1},{1,0},{2,3},{3,2},{4,5},{5,4},{6,7},{7,6},{8,9},{9,8},{10,11... | collective-permute-start | bytes 786440 | tf_op jit(solution)/shard_map/ppermute | solution.py:455
  119.9 3.7 %collective-permute-start.18 = (f32[256,256]{1,0:T(8,128)S(1)}, f32[256,256]{1,0:T(8,128)S(1)}, u32[]{:S(2)}, u32[]{:S(2)}) collective-permute-start(f32[256,256]{1,0:T(8,128)S(1)} %get-tuple-element.65), channel_id=1, source_target_pairs={{0,1},{1,0},{2,3},{3,2},{4,5},{5,4},{6,7},{7,6},{8,9},{9,8},{10,11... | collective-permute-start | bytes 786440 | tf_op jit(solution)/shard_map/ppermute | solution.py:467
  122.0 8.4 %collective-permute-start.22 = (bf16[2,256,256]{2,1,0:T(8,128)(2,1)S(1)}, bf16[2,256,256]{2,1,0:T(8,128)(2,1)S(1)}, u32[]{:S(2)}, u32[]{:S(2)}) collective-permute-start(bf16[2,256,256]{2,1,0:T(8,128)(2,1)S(1)} %halve.1), channel_id=1, source_target_pairs={{0,2},{1,3},{2,0},{3,1},{4,6},{5,7},{6,4},{7,5},{8,10},{9,11},{10,... | collective-permute-start | bytes 786440 | tf_op jit(solution)/shard_map/ppermute | solution.py:375

commit v8 on v6

--- a/solution.py
+++ b/solution.py
@@ -221,14 +221,12 @@
         out[:, at : at + half] = total.astype(out.dtype)
 
 
-def project_kernel(blocks, own_column, info, qt, panel_u, cross, u_all, orig_u, give, keep, left, work, u_buf, sem):
+def project_kernel(blocks, own_column, info, qt, panel_u, cross, u_all, give, keep, work):
     _, priors, order, width = u_all.shape
     slab = order // blocks
     pairs, share, _ = keep.shape
     core = info[0]
     column = core if own_column else 1 - core
-    copy = pltpu.make_async_copy(orig_u.at[column], u_buf, sem.at[0])
-    copy.start()
     mids = []
     for j in range(priors):
         inner = dot(qt[...], panel_u[j]).astype(BF16)
@@ -245,8 +243,6 @@
         for out, which in ((give, 1 - core), (keep, core)):
             place = pl.ds(pl.multiple_of((2 * a + which) * share, SUB), share)
             out[a] = work[place, :].astype(out.dtype)
-    copy.wait()
-    left[...] = dot(qt[...], u_buf[...]).astype(BF16)
 
 
 def halve_kernel(info, keep_b, keep_a, give_a, give_b, *sent):
@@ -257,19 +253,22 @@
             sent[shift - 1][column] = (keep[a] + recv[a].astype(F32)).astype(BF16)
 
 
-def own_kernel(info, left_b, left_a, keep_b, keep_a, give_a, give_b, orig_v, out, v_buf, sems):
+def own_kernel(info, qt_b, qt_a, keep_b, keep_a, give_a, give_b, orig_u, orig_v, out, u_buf, v_buf, sems):
     share = out.shape[1]
     pair = info[1] // 2
     rows = pl.ds(pl.multiple_of(info[1] * share, 16), share)
-    work = ((1 - info[0], left_b, keep_b, give_a), (info[0], left_a, keep_a, give_b))
-    copies = [
-        pltpu.make_async_copy(orig_v.at[column, rows], v_buf.at[n], sems.at[n]) for n, (column, *_) in enumerate(work)
-    ]
+    work = ((1 - info[0], qt_b, keep_b, give_a), (info[0], qt_a, keep_a, give_b))
+    copies = []
+    for n, (column, *_) in enumerate(work):
+        copies.append(pltpu.make_async_copy(orig_u.at[column], u_buf.at[n], sems.at[2 * n]))
+        copies.append(pltpu.make_async_copy(orig_v.at[column, rows], v_buf.at[n], sems.at[2 * n + 1]))
     for copy in copies:
         copy.start()
-    for n, (column, left, keep, recv) in enumerate(work):
-        copies[n].wait()
-        out[column] = dot11(v_buf[n], left[...]) - (keep[pair] + recv[pair].astype(F32))
+    for n, (column, qt, keep, recv) in enumerate(work):
+        copies[2 * n].wait()
+        copies[2 * n + 1].wait()
+        left = dot(qt[...], u_buf[n]).astype(BF16)
+        out[column] = dot11(v_buf[n], left) - (keep[pair] + recv[pair].astype(F32))
 
 
 def turn_kernel(panel_v, sampler, panel_vt, sampler_t):
@@ -401,9 +400,8 @@
     def projected(own_column, qt, cross):
         return run(
             functools.partial(project_kernel, blocks, own_column), [info], [qt, panel_u, cross, u_all],
-            [((pairs, share, width), BF16), ((pairs, share, width), F32), ((width, width), BF16)],
-            [pltpu.VMEM((order, width), F32), pltpu.VMEM((order, width), BF16), pltpu.SemaphoreType.DMA((1,))],
-            20, 3 * priors * square * (2 * order + width), "project", apart=[orig_u]
+            [((pairs, share, width), BF16), ((pairs, share, width), F32)], [pltpu.VMEM((order, width), F32)],
+            20, 3 * priors * square * (2 * order + width), "project"
         )
 
     if whole:
@@ -449,19 +447,20 @@
         128 * square * order, "orthonormal", away=1
     )
     qt_other = lax.ppermute(qt, "cols", swap)
-    give_a, keep_a, left_a = projected(True, qt, cross_own)
+    give_a, keep_a = projected(True, qt, cross_own)
     qt_other, give_a, keep_a = lax.optimization_barrier((qt_other, give_a, keep_a))
-    give_b, keep_b, left_b = projected(False, qt_other, cross_other)
+    give_b, keep_b = projected(False, qt_other, cross_other)
     give_a, give_b = lax.ppermute(give_a, "cols", swap), lax.ppermute(give_b, "cols", swap)
     sent = run(
         halve_kernel, [info], [keep_b, keep_a, give_a, give_b], [((pivots, share, width), BF16)] * (pairs - 1), [], 8,
         square, "halve"
     )
-    left_b, *sent = lax.optimization_barrier((left_b, *sent))
+    qt, *sent = lax.optimization_barrier((qt, *sent))
     recv = [shifted(each, shift) for shift, each in enumerate(sent, 1)]
     (coeff,) = run(
-        own_kernel, [info], [left_b, left_a, keep_b, keep_a, give_a, give_b], [((pivots, share, width), F32)],
-        [pltpu.VMEM((pivots, share, width), BF16), pltpu.SemaphoreType.DMA((2,))], 8, square * width, "own", apart=[orig_v]
+        own_kernel, [info], [qt_other, qt, keep_b, keep_a, give_a, give_b], [((pivots, share, width), F32)],
+        [pltpu.VMEM((pivots, order, width), BF16), pltpu.VMEM((pivots, share, width), BF16), pltpu.SemaphoreType.DMA((4,))],
+        12, square * width, "own", apart=[orig_u, orig_v]
     )
     (basis,) = run(
         place_kernel, [info], [lax.ppermute(given, "cols", swap)], [((pivots, share, width), F32)],

time: 131 us -> 130 us (level)
  no operation moved by 1% of the time
where the time goes in v8:
time: 130 us
  waiting for transfers between devices  71.6 us (55%)
  Pallas kernels  30.9 us (24%)
  starting transfers between devices  22.3 us (17%)
  local copies, waits for them, and re-layouts  3.42 us (3%)
    ppermute x6, waiting for transfers between devices, step(): self.up[t] = found[number] = lax.ppermute(self.up[t], self.axis, self.ahead)  41.6 us
    pallas_call x14, Pallas kernels, run(): pl.pallas_call(kernel, out_shape=shapes, in_specs=[smem] * len(scalars) +...  30.9 us
    ppermute x2, waiting for transfers between devices, shifted(): lax.ppermute(x, 'cols', [(i, (i + 2 * shift) % cols) for i in range(cols)])  16 us
    ppermute x6, starting transfers between devices, step(): self.up[t] = found[number] = lax.ppermute(self.up[t], self.axis, self.ahead)  12 us
    ppermute x6, waiting for transfers between devices, step(): lax.ppermute(self.down[t], self.axis, self.behind)  6.11 us
    ppermute x2, starting transfers between devices, step(): lax.ppermute(self.up[t][0], self.axis, self.ahead)  3.65 us
    ppermute x2, waiting for transfers between devices, step(): lax.ppermute(self.down[t][1], self.axis, self.behind)  3.38 us
    ppermute x2, waiting for transfers between devices, step(): lax.ppermute(self.up[t][0], self.axis, self.ahead)  3.36 us
  transfers between devices with their start and end apart: 23, of which 17 were waited for; matrix products, arithmetic and copies ran while one was open for 1% of the time, Pallas kernels for 15%

profile of v8, /device:TPU:0, one launch (start us, length us, event | category | flops | bytes accessed | tf_op | source)
XLA Modules:
  0.0 130.1 jit_solution(8228669051750745976)
XLA Ops:
  0.6 3.0 %collective-permute-start.4 = (bf16[2,4,128,256]{3,2,1,0:T(8,128)(2,1)}, bf16[2,4,128,256]{3,2,1,0:T(8,128)(2,1)S(1)}, u32[]{:S(2)}, u32[]{:S(2)}) collective-permute-start(bf16[2,4,128,256]{3,2,1,0:T(8,128)(2,1)} %refs_0_.1), channel_id=1, source_target_pairs={{8,0},{16,8},{24,16},{28,24},{20,28},{12,20},{4,12},{0,4},{9,1},{1... | collective-permute-start | bytes 1572872 | tf_op jit(solution)/shard_map/ppermute | solution.py:323
  3.8 1.9 %collective-permute-start = (bf16[2,4,128,256]{3,2,1,0:T(8,128)(2,1)}, bf16[2,4,128,256]{3,2,1,0:T(8,128)(2,1)S(1)}, u32[]{:S(2)}, u32[]{:S(2)}) collective-permute-start(bf16[2,4,128,256]{3,2,1,0:T(8,128)(2,1)} %refs_3_.1), channel_id=1, source_target_pairs={{8,0},{16,8},{24,16},{28,24},{20,28},{12,20},{4,12},{0,4},{9,1},{1... | collective-permute-start | bytes 1572872 | tf_op jit(solution)/shard_map/ppermute | solution.py:323
  5.8 10.9 %collective-permute-done.4.refs_1_ = bf16[2,4,128,256]{3,2,1,0:T(8,128)(2,1)S(1)} collective-permute-done((bf16[2,4,128,256]{3,2,1,0:T(8,128)(2,1)}, bf16[2,4,128,256]{3,2,1,0:T(8,128)(2,1)S(1)}, u32[]{:S(2)}, u32[]{:S(2)}) %collective-permute-start.4) | collective-permute-done | bytes 524320 | tf_op jit(solution)/shard_map/ppermute | solution.py:323
  16.7 2.0 %collective-permute-start.6 = (bf16[2,4,128,256]{3,2,1,0:T(8,128)(2,1)S(1)}, bf16[2,4,128,256]{3,2,1,0:T(8,128)(2,1)S(1)}, u32[]{:S(2)}, u32[]{:S(2)}) collective-permute-start(bf16[2,4,128,256]{3,2,1,0:T(8,128)(2,1)S(1)} %collective-permute-done.4.refs_1_), channel_id=1, source_target_pairs={{8,0},{16,8},{24,16},{28,24},{20,28},{12,20},{4,12},{0,4},{9,1},{1... | collective-permute-start | bytes 1572872 | tf_op jit(solution)/shard_map/ppermute | solution.py:323
  19.6 1.6 %copy-done.7 = bf16[1,4,1024,256]{3,2,1,0:T(8,128)(2,1)S(1)} copy-done((bf16[1,4,1024,256]{3,2,1,0:T(8,128)(2,1)S(1)}, bf16[1,4,1024,256]{3,2,1,0:T(8,128)(2,1)}, u32[]{:S(2)}) %copy-start.7) | copy-done | bytes 2097176
  23.0 4.9 %collective-permute-done.refs_4_ = bf16[2,4,128,256]{3,2,1,0:T(8,128)(2,1)S(1)} collective-permute-done((bf16[2,4,128,256]{3,2,1,0:T(8,128)(2,1)}, bf16[2,4,128,256]{3,2,1,0:T(8,128)(2,1)S(1)}, u32[]{:S(2)}, u32[]{:S(2)}) %collective-permute-start) | collective-permute-done | bytes 524320 | tf_op jit(solution)/shard_map/ppermute | solution.py:323
  27.9 2.0 %collective-permute-start.1 = (bf16[2,4,128,256]{3,2,1,0:T(8,128)(2,1)S(1)}, bf16[2,4,128,256]{3,2,1,0:T(8,128)(2,1)S(1)}, u32[]{:S(2)}, u32[]{:S(2)}) collective-permute-start(bf16[2,4,128,256]{3,2,1,0:T(8,128)(2,1)S(1)} %collective-permute-done.refs_4_), channel_id=1, source_target_pairs={{8,0},{16,8},{24,16},{28,24},{20,28},{12,20},{4,12},{0,4},{9,1},{1... | collective-permute-start | bytes 1572872 | tf_op jit(solution)/shard_map/ppermute | solution.py:323
  30.0 1.8 %gather.3 = (f32[2,4,256,256]{3,2,1,0:T(8,128)S(1)}, f32[2,4,256,256]{3,2,1,0:T(8,128)S(1)}, bf16[2,4,1024,256]{3,2,1,0:T(8,128)(2,1)S(1)}) custom-call(s32[10]{0:T(128)S(1)} %pad_add_fusion.info, bf16[4,256,1024]{2,1,0:T(8,128)(2,1)S(1)} %get-tuple-element.42.panel_vt, bf16[256,1024]{1,0:T(8,128)(2,1)S(1)} %get-tuple-element.40.sampler_t, ...), custom_call_target="tpu_custom_call" | custom-call | flops 805306368 | bytes 14155776 | tf_op jit(solution)/shard_map/gather/pallas_call | solution.py:291
  31.9 7.3 %collective-permute-done.6.refs_0_ = bf16[2,4,128,256]{3,2,1,0:T(8,128)(2,1)S(1)} collective-permute-done((bf16[2,4,128,256]{3,2,1,0:T(8,128)(2,1)S(1)}, bf16[2,4,128,256]{3,2,1,0:T(8,128)(2,1)S(1)}, u32[]{:S(2)}, u32[]{:S(2)}) %collective-permute-start.6) | collective-permute-done | bytes 524320 | tf_op jit(solution)/shard_map/ppermute | solution.py:323
  39.1 2.0 %collective-permute-done.7.refs_1_ = bf16[2,4,128,256]{3,2,1,0:T(8,128)(2,1)S(1)} collective-permute-done((bf16[2,4,128,256]{3,2,1,0:T(8,128)(2,1)S(1)}, bf16[2,4,128,256]{3,2,1,0:T(8,128)(2,1)S(1)}, u32[]{:S(2)}, u32[]{:S(2)}) %collective-permute-start.7) | collective-permute-done | bytes 524320 | tf_op jit(solution)/shard_map/ppermute | solution.py:324
  41.1 1.6 %collective-permute-start.8 = (bf16[2,4,128,256]{3,2,1,0:T(8,128)(2,1)S(1)}, bf16[2,4,128,256]{3,2,1,0:T(8,128)(2,1)S(1)}, u32[]{:S(2)}, u32[]{:S(2)}) collective-permute-start(bf16[2,4,128,256]{3,2,1,0:T(8,128)(2,1)S(1)} %collective-permute-done.6.refs_0_), channel_id=1, source_target_pairs={{8,0},{16,8},{24,16},{28,24},{20,28},{12,20},{4,12},{0,4},{9,1},{1... | collective-permute-start | bytes 1572872 | tf_op jit(solution)/shard_map/ppermute | solution.py:323
  44.5 5.9 %collective-permute-done.1.refs_2_ = bf16[2,4,128,256]{3,2,1,0:T(8,128)(2,1)S(1)} collective-permute-done((bf16[2,4,128,256]{3,2,1,0:T(8,128)(2,1)S(1)}, bf16[2,4,128,256]{3,2,1,0:T(8,128)(2,1)S(1)}, u32[]{:S(2)}, u32[]{:S(2)}) %collective-permute-start.1) | collective-permute-done | bytes 524320 | tf_op jit(solution)/shard_map/ppermute | solution.py:323
  50.4 2.0 %collective-permute-done.3.refs_3_ = bf16[2,4,128,256]{3,2,1,0:T(8,128)(2,1)S(1)} collective-permute-done((bf16[2,4,128,256]{3,2,1,0:T(8,128)(2,1)S(1)}, bf16[2,4,128,256]{3,2,1,0:T(8,128)(2,1)S(1)}, u32[]{:S(2)}, u32[]{:S(2)}) %collective-permute-start.3) | collective-permute-done | bytes 524320 | tf_op jit(solution)/shard_map/ppermute | solution.py:324
  54.4 1.6 %gather.4 = (f32[2,4,256,256]{3,2,1,0:T(8,128)S(1)}, f32[2,4,256,256]{3,2,1,0:T(8,128)S(1)}, bf16[2,4,1024,256]{3,2,1,0:T(8,128)(2,1)S(1)}) custom-call(s32[10]{0:T(128)S(1)} %pad_add_fusion.info, bf16[4,256,1024]{2,1,0:T(8,128)(2,1)S(1)} %get-tuple-element.42.panel_vt, ...), custom_call_target="tpu_custom_call", output_to_operand_aliasing={{0}: (7, {}), {1}: (8, {}), {2}: (9, {})} | custom-call | flops 536870912 | bytes 21495808 | tf_op jit(solution)/shard_map/gather/pallas_call | solution.py:291
  56.1 5.5 %collective-permute-done.8.refs_0_ = bf16[2,4,128,256]{3,2,1,0:T(8,128)(2,1)S(1)} collective-permute-done((bf16[2,4,128,256]{3,2,1,0:T(8,128)(2,1)S(1)}, bf16[2,4,128,256]{3,2,1,0:T(8,128)(2,1)S(1)}, u32[]{:S(2)}, u32[]{:S(2)}) %collective-permute-start.8) | collective-permute-done | bytes 524320 | tf_op jit(solution)/shard_map/ppermute | solution.py:323
  61.6 2.0 %collective-permute-done.9.refs_1_ = bf16[2,4,128,256]{3,2,1,0:T(8,128)(2,1)S(1)} collective-permute-done((bf16[2,4,128,256]{3,2,1,0:T(8,128)(2,1)S(1)}, bf16[2,4,128,256]{3,2,1,0:T(8,128)(2,1)S(1)}, u32[]{:S(2)}, u32[]{:S(2)}) %collective-permute-start.9) | collective-permute-done | bytes 524320 | tf_op jit(solution)/shard_map/ppermute | solution.py:324
  63.6 1.6 %collective-permute-start.12 = (bf16[4,128,256]{2,1,0:T(8,128)(2,1)S(1)}, bf16[4,128,256]{2,1,0:T(8,128)(2,1)S(1)}, u32[]{:S(2)}, u32[]{:S(2)}) collective-permute-start(bf16[4,128,256]{2,1,0:T(8,128)(2,1)S(1)} %slice_bitcast_fusion.3), channel_id=1, source_target_pairs={{8,0},{16,8},{24,16},{28,24},{20,28},{12,20},{4,12},{0,4},{9,1},{1... | collective-permute-start | bytes 786440 | tf_op jit(solution)/shard_map/ppermute | solution.py:327
  65.8 7.1 %collective-permute-done.10.refs_2_ = bf16[2,4,128,256]{3,2,1,0:T(8,128)(2,1)S(1)} collective-permute-done((bf16[2,4,128,256]{3,2,1,0:T(8,128)(2,1)S(1)}, bf16[2,4,128,256]{3,2,1,0:T(8,128)(2,1)S(1)}, u32[]{:S(2)}, u32[]{:S(2)}) %collective-permute-start.10) | collective-permute-done | bytes 524320 | tf_op jit(solution)/shard_map/ppermute | solution.py:323
  72.9 2.0 %collective-permute-start.14 = (bf16[4,128,256]{2,1,0:T(8,128)(2,1)S(1)}, bf16[4,128,256]{2,1,0:T(8,128)(2,1)S(1)}, u32[]{:S(2)}, u32[]{:S(2)}) collective-permute-start(bf16[4,128,256]{2,1,0:T(8,128)(2,1)S(1)} %slice_bitcast_fusion.1), channel_id=1, source_target_pairs={{8,0},{16,8},{24,16},{28,24},{20,28},{12,20},{4,12},{0,4},{9,1},{1... | collective-permute-start | bytes 786440 | tf_op jit(solution)/shard_map/ppermute | solution.py:327
  75.3 1.6 %gather.5 = (f32[2,4,256,256]{3,2,1,0:T(8,128)S(1)}, f32[2,4,256,256]{3,2,1,0:T(8,128)S(1)}, bf16[2,4,1024,256]{3,2,1,0:T(8,128)(2,1)S(1)}) custom-call(s32[10]{0:T(128)S(1)} %pad_add_fusion.info, bf16[4,256,1024]{2,1,0:T(8,128)(2,1)S(1)} %get-tuple-element.42.panel_vt, ...), custom_call_target="tpu_custom_call", output_to_operand_aliasing={{0}: (7, {}), {1}: (8, {}), {2}: (9, {})} | custom-call | flops 536870912 | bytes 21495808 | tf_op jit(solution)/shard_map/gather/pallas_call | solution.py:291
  78.5 2.0 %collective-permute-done.13.refs_1_ = bf16[4,128,256]{2,1,0:T(8,128)(2,1)S(1)} collective-permute-done((bf16[4,128,256]{2,1,0:T(8,128)(2,1)S(1)}, bf16[4,128,256]{2,1,0:T(8,128)(2,1)S(1)}, u32[]{:S(2)}, u32[]{:S(2)}) %collective-permute-start.13) | collective-permute-done | bytes 262176 | tf_op jit(solution)/shard_map/ppermute | solution.py:328
  81.5 1.8 %collective-permute-done.14.refs_0_ = bf16[4,128,256]{2,1,0:T(8,128)(2,1)S(1)} collective-permute-done((bf16[4,128,256]{2,1,0:T(8,128)(2,1)S(1)}, bf16[4,128,256]{2,1,0:T(8,128)(2,1)S(1)}, u32[]{:S(2)}, u32[]{:S(2)}) %collective-permute-start.14) | collective-permute-done | bytes 262176 | tf_op jit(solution)/shard_map/ppermute | solution.py:327
  84.6 1.7 %update.3 = (bf16[4,256,256]{2,1,0:T(8,128)(2,1)S(1)}, bf16[256,1024]{1,0:T(8,128)(2,1)S(1)}) custom-call(s32[10]{0:T(128)S(1)} %pad_add_fusion.info, s32[1,4]{1,0:T(1,128)S(1)} %copy-done.6, s32[2,4]{1,0:T(2,128)S(1)} %copy-done.5, bf16[2,4,256,256]{3,2,1,0:T(8,128)(2,1)S(1)} %get-tuple-element.59.sampled, f32[2,4,256,256]{3,2,1,0:T(8,128)S(1)} %get-tuple-element.60.met, ...), custom_call_target="tpu_custom_call" | custom-call | flops 1342177280 | bytes 8912896 | tf_op jit(solution)/shard_map/update/pallas_call | solution.py:291
  86.4 1.7 %update.2 = (bf16[4,256,256]{2,1,0:T(8,128)(2,1)S(1)}, f32[256,1024]{1,0:T(8,128)S(1)}) custom-call(s32[10]{0:T(128)S(1)} %pad_add_fusion.info, s32[1,4]{1,0:T(1,128)S(1)} %copy-done.6, s32[2,4]{1,0:T(2,128)S(1)} %copy-done.5, bf16[2,4,256,256]{3,2,1,0:T(8,128)(2,1)S(1)} %get-tuple-element.59.sampled, f32[2,4,256,256]{3,2,1,0:T(8,128)S(1)} %get-tuple-element.60.met, ...), custom_call_target="tpu_custom_call" | custom-call | flops 1342177280 | bytes 9437184 | tf_op jit(solution)/shard_map/update/pallas_call | solution.py:291
  88.5 1.6 %collective-permute-start.17 = (bf16[256,1024]{1,0:T(8,128)(2,1)S(1)}, bf16[256,1024]{1,0:T(8,128)(2,1)S(1)}, u32[]{:S(2)}, u32[]{:S(2)}) collective-permute-start(bf16[256,1024]{1,0:T(8,128)(2,1)S(1)} %add_convert_fusion), channel_id=1, source_target_pairs={{0,2},{1,3},{2,0},{3,1},{4,6},{5,7},{6,4},{7,5},{8,10},{9,11},{10,... | collective-permute-start | bytes 1572872 | tf_op jit(solution)/shard_map/ppermute | solution.py:374
  90.1 12.6 %collective-permute-done.17.refs_2_ = bf16[256,1024]{1,0:T(8,128)(2,1)S(1)} collective-permute-done((bf16[256,1024]{1,0:T(8,128)(2,1)S(1)}, bf16[256,1024]{1,0:T(8,128)(2,1)S(1)}, u32[]{:S(2)}, u32[]{:S(2)}) %collective-permute-start.17) | collective-permute-done | bytes 524320 | tf_op jit(solution)/shard_map/ppermute | solution.py:374
  102.7 9.5 %orthonormal.1 = (bf16[256,1024]{1,0:T(8,128)(2,1)S(1)}, f32[256,256]{1,0:T(8,128)S(1)}, f32[2,256,256]{2,1,0:T(8,128)}) custom-call(s32[10]{0:T(128)S(1)} %pad_add_fusion.info, f32[256,1024]{1,0:T(8,128)S(1)} %start.1, f32[256,1024]{1,0:T(8,128)S(1)} %get-tuple-element.61.refs_0_, bf16[256,1024]{1,0:T(8,128)(2,1)S(1)} %collective-permute-done.16.refs_1_, ...), custom_call_target="tpu_custom_call" | custom-call | flops 17179869184 | bytes 4456448 | tf_op jit(solution)/shard_map/orthonormal/pallas_call | solution.py:291
  112.3 2.9 %project.2 = (bf16[2,256,256]{2,1,0:T(8,128)(2,1)S(1)}, f32[2,256,256]{2,1,0:T(8,128)S(1)}) custom-call(s32[10]{0:T(128)S(1)} %pad_add_fusion.info, bf16[256,1024]{1,0:T(8,128)(2,1)S(1)} %get-tuple-element.76.qt.qt_a, bf16[4,1024,256]{2,1,0:T(8,128)(2,1)S(1)} %bitcast.25, bf16[4,256,256]{2,1,0:T(8,128)(2,1)S(1)} %get-tuple-element.66.cross, ...), custom_call_target="tpu_custom_call" | custom-call | flops 3623878656 | bytes 8126464 | tf_op jit(solution)/shard_map/project/pallas_call | solution.py:291
  115.7 2.9 %project.3 = (bf16[2,256,256]{2,1,0:T(8,128)(2,1)S(1)}, f32[2,256,256]{2,1,0:T(8,128)S(1)}) custom-call(s32[10]{0:T(128)S(1)} %pad_add_fusion.info, bf16[256,1024]{1,0:T(8,128)(2,1)S(1)} %collective-permute-done.19.qt.qt_b, bf16[4,1024,256]{2,1,0:T(8,128)(2,1)S(1)} %bitcast.26, bf16[4,256,256]{2,1,0:T(8,128)(2,1)S(1)} %get-tuple-element.71.cross, ...), custom_call_target="tpu_custom_call" | custom-call | flops 3623878656 | bytes 8126464 | tf_op jit(solution)/shard_map/project/pallas_call | solution.py:291
  120.8 1.6 %collective-permute-start.22 = (bf16[2,256,256]{2,1,0:T(8,128)(2,1)S(1)}, bf16[2,256,256]{2,1,0:T(8,128)(2,1)S(1)}, u32[]{:S(2)}, u32[]{:S(2)}) collective-permute-start(bf16[2,256,256]{2,1,0:T(8,128)(2,1)S(1)} %halve.1), channel_id=1, source_target_pairs={{0,2},{1,3},{2,0},{3,1},{4,6},{5,7},{6,4},{7,5},{8,10},{9,11},{10,... | collective-permute-start | bytes 786440 | tf_op jit(solution)/shard_map/ppermute | solution.py:374
  123.7 2.2 %own.1 = f32[2,256,256]{2,1,0:T(8,128)S(1)} custom-call(s32[10]{0:T(128)S(1)} %pad_add_fusion.info, bf16[256,1024]{1,0:T(8,128)(2,1)S(1)} %collective-permute-done.19.qt.qt_b, bf16[256,1024]{1,0:T(8,128)(2,1)S(1)} %get-tuple-element.76.qt.qt_a, f32[2,256,256]{2,1,0:T(8,128)S(1)} %get-tuple-element.72.keep_b, f32[2,256,256]{2,1,0:T(8,128)S(1)} %get-tuple-element.73.keep_a, ...), custom_call_target="tpu_custom_call" | custom-call | flops 33554432 | bytes 3145728 | tf_op jit(solution)/shard_map/own/pallas_call | solution.py:291
  125.9 3.3 %collective-permute-done.22 = bf16[2,256,256]{2,1,0:T(8,128)(2,1)S(1)} collective-permute-done((bf16[2,256,256]{2,1,0:T(8,128)(2,1)S(1)}, bf16[2,256,256]{2,1,0:T(8,128)(2,1)S(1)}, u32[]{:S(2)}, u32[]{:S(2)}) %collective-permute-start.22) | collective-permute-done | bytes 262176 | tf_op jit(solution)/shard_map/ppermute | solution.py:374
  (54 shorter events, 17.1 us)
Async XLA Ops:
  0.6 16.0 %collective-permute-start.4 = (bf16[2,4,128,256]{3,2,1,0:T(8,128)(2,1)}, bf16[2,4,128,256]{3,2,1,0:T(8,128)(2,1)S(1)}, u32[]{:S(2)}, u32[]{:S(2)}) collective-permute-start(bf16[2,4,128,256]{3,2,1,0:T(8,128)(2,1)} %refs_0_.1), channel_id=1, source_target_pairs={{8,0},{16,8},{24,16},{28,24},{20,28},{12,20},{4,12},{0,4},{9,1},{1... | collective-permute-start | bytes 1572872 | tf_op jit(solution)/shard_map/ppermute | solution.py:323
  3.6 15.1 %collective-permute-start.5 = (bf16[2,4,128,256]{3,2,1,0:T(8,128)(2,1)}, bf16[2,4,128,256]{3,2,1,0:T(8,128)(2,1)S(1)}, u32[]{:S(2)}, u32[]{:S(2)}) collective-permute-start(bf16[2,4,128,256]{3,2,1,0:T(8,128)(2,1)} %refs_0_.1), channel_id=1, source_target_pairs={{0,8},{8,16},{16,24},{24,28},{28,20},{20,12},{12,4},{4,0},{1,9},{9... | collective-permute-start | bytes 1572872 | tf_op jit(solution)/shard_map/ppermute | solution.py:324
  3.8 24.1 %collective-permute-start = (bf16[2,4,128,256]{3,2,1,0:T(8,128)(2,1)}, bf16[2,4,128,256]{3,2,1,0:T(8,128)(2,1)S(1)}, u32[]{:S(2)}, u32[]{:S(2)}) collective-permute-start(bf16[2,4,128,256]{3,2,1,0:T(8,128)(2,1)} %refs_3_.1), channel_id=1, source_target_pairs={{8,0},{16,8},{24,16},{28,24},{20,28},{12,20},{4,12},{0,4},{9,1},{1... | collective-permute-start | bytes 1572872 | tf_op jit(solution)/shard_map/ppermute | solution.py:323
  5.6 24.3 %collective-permute-start.2 = (bf16[2,4,128,256]{3,2,1,0:T(8,128)(2,1)}, bf16[2,4,128,256]{3,2,1,0:T(8,128)(2,1)S(1)}, u32[]{:S(2)}, u32[]{:S(2)}) collective-permute-start(bf16[2,4,128,256]{3,2,1,0:T(8,128)(2,1)} %refs_3_.1), channel_id=1, source_target_pairs={{0,8},{8,16},{16,24},{24,28},{28,20},{20,12},{12,4},{4,0},{1,9},{9... | collective-permute-start | bytes 1572872 | tf_op jit(solution)/shard_map/ppermute | solution.py:324
  16.7 22.5 %collective-permute-start.6 = (bf16[2,4,128,256]{3,2,1,0:T(8,128)(2,1)S(1)}, bf16[2,4,128,256]{3,2,1,0:T(8,128)(2,1)S(1)}, u32[]{:S(2)}, u32[]{:S(2)}) collective-permute-start(bf16[2,4,128,256]{3,2,1,0:T(8,128)(2,1)S(1)} %collective-permute-done.4.refs_1_), channel_id=1, source_target_pairs={{8,0},{16,8},{24,16},{28,24},{20,28},{12,20},{4,12},{0,4},{9,1},{1... | collective-permute-start | bytes 1572872 | tf_op jit(solution)/shard_map/ppermute | solution.py:323
  18.7 22.5 %collective-permute-start.7 = (bf16[2,4,128,256]{3,2,1,0:T(8,128)(2,1)S(1)}, bf16[2,4,128,256]{3,2,1,0:T(8,128)(2,1)S(1)}, u32[]{:S(2)}, u32[]{:S(2)}) collective-permute-start(bf16[2,4,128,256]{3,2,1,0:T(8,128)(2,1)S(1)} %collective-permute-done.5.refs_2_), channel_id=1, source_target_pairs={{0,8},{8,16},{16,24},{24,28},{28,20},{20,12},{12,4},{4,0},{1,9},{9... | collective-permute-start | bytes 1572872 | tf_op jit(solution)/shard_map/ppermute | solution.py:324
  19.6 1.6 %copy-start.7 = (bf16[1,4,1024,256]{3,2,1,0:T(8,128)(2,1)S(1)}, bf16[1,4,1024,256]{3,2,1,0:T(8,128)(2,1)}, u32[]{:S(2)}) copy-start(bf16[1,4,1024,256]{3,2,1,0:T(8,128)(2,1)} %param.11) | copy-start | bytes 6291460
  21.2 1.0 copy-start.8
  22.2 7.8 %copy-start.3 = (bf16[2,4,128,256]{3,2,1,0:T(8,128)(2,1)S(1)}, bf16[2,4,128,256]{3,2,1,0:T(8,128)(2,1)}, u32[]{:S(2)}) copy-start(bf16[2,4,128,256]{3,2,1,0:T(8,128)(2,1)} %refs_0_.1) | copy-start | bytes 1572868
  22.2 7.8 %copy-start.4 = (bf16[2,4,128,256]{3,2,1,0:T(8,128)(2,1)S(1)}, bf16[2,4,128,256]{3,2,1,0:T(8,128)(2,1)}, u32[]{:S(2)}) copy-start(bf16[2,4,128,256]{3,2,1,0:T(8,128)(2,1)} %refs_3_.1) | copy-start | bytes 1572868
  27.9 22.5 %collective-permute-start.1 = (bf16[2,4,128,256]{3,2,1,0:T(8,128)(2,1)S(1)}, bf16[2,4,128,256]{3,2,1,0:T(8,128)(2,1)S(1)}, u32[]{:S(2)}, u32[]{:S(2)}) collective-permute-start(bf16[2,4,128,256]{3,2,1,0:T(8,128)(2,1)S(1)} %collective-permute-done.refs_4_), channel_id=1, source_target_pairs={{8,0},{16,8},{24,16},{28,24},{20,28},{12,20},{4,12},{0,4},{9,1},{1... | collective-permute-start | bytes 1572872 | tf_op jit(solution)/shard_map/ppermute | solution.py:323
  29.9 22.5 %collective-permute-start.3 = (bf16[2,4,128,256]{3,2,1,0:T(8,128)(2,1)S(1)}, bf16[2,4,128,256]{3,2,1,0:T(8,128)(2,1)S(1)}, u32[]{:S(2)}, u32[]{:S(2)}) collective-permute-start(bf16[2,4,128,256]{3,2,1,0:T(8,128)(2,1)S(1)} %collective-permute-done.2.refs_5_), channel_id=1, source_target_pairs={{0,8},{8,16},{16,24},{24,28},{28,20},{20,12},{12,4},{4,0},{1,9},{9... | collective-permute-start | bytes 1572872 | tf_op jit(solution)/shard_map/ppermute | solution.py:324
  30.0 13.1 %copy-start.1 = (bf16[2,1,1024,256]{3,2,1,0:T(8,128)(2,1)S(1)}, bf16[2,1,1024,256]{3,2,1,0:T(8,128)(2,1)}, u32[]{:S(2)}) copy-start(bf16[2,1,1024,256]{3,2,1,0:T(8,128)(2,1)} %param.16) | copy-start | bytes 3145732
  30.0 13.1 %copy-start.2 = (bf16[2,1,1024,256]{3,2,1,0:T(8,128)(2,1)S(1)}, bf16[2,1,1024,256]{3,2,1,0:T(8,128)(2,1)}, u32[]{:S(2)}) copy-start(bf16[2,1,1024,256]{3,2,1,0:T(8,128)(2,1)} %param.17) | copy-start | bytes 3145732
  41.1 20.5 %collective-permute-start.8 = (bf16[2,4,128,256]{3,2,1,0:T(8,128)(2,1)S(1)}, bf16[2,4,128,256]{3,2,1,0:T(8,128)(2,1)S(1)}, u32[]{:S(2)}, u32[]{:S(2)}) collective-permute-start(bf16[2,4,128,256]{3,2,1,0:T(8,128)(2,1)S(1)} %collective-permute-done.6.refs_0_), channel_id=1, source_target_pairs={{8,0},{16,8},{24,16},{28,24},{20,28},{12,20},{4,12},{0,4},{9,1},{1... | collective-permute-start | bytes 1572872 | tf_op jit(solution)/shard_map/ppermute | solution.py:323
  42.7 20.9 %collective-permute-start.9 = (bf16[2,4,128,256]{3,2,1,0:T(8,128)(2,1)S(1)}, bf16[2,4,128,256]{3,2,1,0:T(8,128)(2,1)S(1)}, u32[]{:S(2)}, u32[]{:S(2)}) collective-permute-start(bf16[2,4,128,256]{3,2,1,0:T(8,128)(2,1)S(1)} %collective-permute-done.7.refs_1_), channel_id=1, source_target_pairs={{0,8},{8,16},{16,24},{24,28},{28,20},{20,12},{12,4},{4,0},{1,9},{9... | collective-permute-start | bytes 1572872 | tf_op jit(solution)/shard_map/ppermute | solution.py:324
  52.4 20.5 %collective-permute-start.10 = (bf16[2,4,128,256]{3,2,1,0:T(8,128)(2,1)S(1)}, bf16[2,4,128,256]{3,2,1,0:T(8,128)(2,1)S(1)}, u32[]{:S(2)}, u32[]{:S(2)}) collective-permute-start(bf16[2,4,128,256]{3,2,1,0:T(8,128)(2,1)S(1)} %collective-permute-done.1.refs_2_), channel_id=1, source_target_pairs={{8,0},{16,8},{24,16},{28,24},{20,28},{12,20},{4,12},{0,4},{9,1},{1... | collective-permute-start | bytes 1572872 | tf_op jit(solution)/shard_map/ppermute | solution.py:323
  54.0 20.9 %collective-permute-start.11 = (bf16[2,4,128,256]{3,2,1,0:T(8,128)(2,1)S(1)}, bf16[2,4,128,256]{3,2,1,0:T(8,128)(2,1)S(1)}, u32[]{:S(2)}, u32[]{:S(2)}) collective-permute-start(bf16[2,4,128,256]{3,2,1,0:T(8,128)(2,1)S(1)} %collective-permute-done.3.refs_3_), channel_id=1, source_target_pairs={{0,8},{8,16},{16,24},{24,28},{28,20},{20,12},{12,4},{4,0},{1,9},{9... | collective-permute-start | bytes 1572872 | tf_op jit(solution)/shard_map/ppermute | solution.py:324
  63.6 14.8 %collective-permute-start.12 = (bf16[4,128,256]{2,1,0:T(8,128)(2,1)S(1)}, bf16[4,128,256]{2,1,0:T(8,128)(2,1)S(1)}, u32[]{:S(2)}, u32[]{:S(2)}) collective-permute-start(bf16[4,128,256]{2,1,0:T(8,128)(2,1)S(1)} %slice_bitcast_fusion.3), channel_id=1, source_target_pairs={{8,0},{16,8},{24,16},{28,24},{20,28},{12,20},{4,12},{0,4},{9,1},{1... | collective-permute-start | bytes 786440 | tf_op jit(solution)/shard_map/ppermute | solution.py:327
  65.3 15.2 %collective-permute-start.13 = (bf16[4,128,256]{2,1,0:T(8,128)(2,1)S(1)}, bf16[4,128,256]{2,1,0:T(8,128)(2,1)S(1)}, u32[]{:S(2)}, u32[]{:S(2)}) collective-permute-start(bf16[4,128,256]{2,1,0:T(8,128)(2,1)S(1)} %slice_bitcast_fusion.2), channel_id=1, source_target_pairs={{0,8},{8,16},{16,24},{24,28},{28,20},{20,12},{12,4},{4,0},{1,9},{9... | collective-permute-start | bytes 786440 | tf_op jit(solution)/shard_map/ppermute | solution.py:328
  72.9 10.4 %collective-permute-start.14 = (bf16[4,128,256]{2,1,0:T(8,128)(2,1)S(1)}, bf16[4,128,256]{2,1,0:T(8,128)(2,1)S(1)}, u32[]{:S(2)}, u32[]{:S(2)}) collective-permute-start(bf16[4,128,256]{2,1,0:T(8,128)(2,1)S(1)} %slice_bitcast_fusion.1), channel_id=1, source_target_pairs={{8,0},{16,8},{24,16},{28,24},{20,28},{12,20},{4,12},{0,4},{9,1},{1... | collective-permute-start | bytes 786440 | tf_op jit(solution)/shard_map/ppermute | solution.py:327
  74.9 9.7 %collective-permute-start.15 = (bf16[4,128,256]{2,1,0:T(8,128)(2,1)S(1)}, bf16[4,128,256]{2,1,0:T(8,128)(2,1)S(1)}, u32[]{:S(2)}, u32[]{:S(2)}) collective-permute-start(bf16[4,128,256]{2,1,0:T(8,128)(2,1)S(1)} %slice_bitcast_fusion), channel_id=1, source_target_pairs={{0,8},{8,16},{16,24},{24,28},{28,20},{20,12},{12,4},{4,0},{1,9},{9... | collective-permute-start | bytes 786440 | tf_op jit(solution)/shard_map/ppermute | solution.py:328
  80.5 4.2 %copy-start = (bf16[1,4,1024,256]{3,2,1,0:T(8,128)(2,1)S(1)}, bf16[1,4,1024,256]{3,2,1,0:T(8,128)(2,1)}, u32[]{:S(2)}) copy-start(bf16[1,4,1024,256]{3,2,1,0:T(8,128)(2,1)} %param.10) | copy-start | bytes 6291460
  80.5 4.2 %copy-start.5 = (s32[2,4]{1,0:T(2,128)S(1)}, s32[2,4]{1,0:T(2,128)}, u32[]{:S(2)}) copy-start(s32[2,4]{1,0:T(2,128)} %pivot_rank.3) | copy-start | bytes 100
  80.5 4.2 %copy-start.6 = (s32[1,4]{1,0:T(1,128)S(1)}, s32[1,4]{1,0:T(1,128)}, u32[]{:S(2)}) copy-start(s32[1,4]{1,0:T(1,128)} %panel_rank.3) | copy-start | bytes 52
  86.3 2.0 %collective-permute-start.16 = (bf16[256,1024]{1,0:T(8,128)(2,1)S(1)}, bf16[256,1024]{1,0:T(8,128)(2,1)S(1)}, u32[]{:S(2)}, u32[]{:S(2)}) collective-permute-start(bf16[256,1024]{1,0:T(8,128)(2,1)S(1)} %get-tuple-element.62), channel_id=1, source_target_pairs={{0,1},{1,0},{2,3},{3,2},{4,5},{5,4},{6,7},{7,6},{8,9},{9,8},{10,11... | collective-permute-start | bytes 1572872 | tf_op jit(solution)/shard_map/ppermute | solution.py:435
  88.5 14.2 %collective-permute-start.17 = (bf16[256,1024]{1,0:T(8,128)(2,1)S(1)}, bf16[256,1024]{1,0:T(8,128)(2,1)S(1)}, u32[]{:S(2)}, u32[]{:S(2)}) collective-permute-start(bf16[256,1024]{1,0:T(8,128)(2,1)S(1)} %add_convert_fusion), channel_id=1, source_target_pairs={{0,2},{1,3},{2,0},{3,1},{4,6},{5,7},{6,4},{7,5},{8,10},{9,11},{10,... | collective-permute-start | bytes 1572872 | tf_op jit(solution)/shard_map/ppermute | solution.py:374
  112.2 3.0 %collective-permute-start.19 = (bf16[256,1024]{1,0:T(8,128)(2,1)S(1)}, bf16[256,1024]{1,0:T(8,128)(2,1)S(1)}, u32[]{:S(2)}, u32[]{:S(2)}) collective-permute-start(bf16[256,1024]{1,0:T(8,128)(2,1)S(1)} %get-tuple-element.76.qt.qt_a), channel_id=1, source_target_pairs={{0,1},{1,0},{2,3},{3,2},{4,5},{5,4},{6,7},{7,6},{8,9},{9,8},{10,11... | collective-permute-start | bytes 1572872 | tf_op jit(solution)/shard_map/ppermute | solution.py:449
  115.2 4.0 %collective-permute-start.20 = (bf16[2,256,256]{2,1,0:T(8,128)(2,1)S(1)}, bf16[2,256,256]{2,1,0:T(8,128)(2,1)S(1)}, u32[]{:S(2)}, u32[]{:S(2)}) collective-permute-start(bf16[2,256,256]{2,1,0:T(8,128)(2,1)S(1)} %get-tuple-element.74), channel_id=1, source_target_pairs={{0,1},{1,0},{2,3},{3,2},{4,5},{5,4},{6,7},{7,6},{8,9},{9,8},{10,11... | collective-permute-start | bytes 786440 | tf_op jit(solution)/shard_map/ppermute | solution.py:453
  118.6 1.6 %collective-permute-start.21 = (bf16[2,256,256]{2,1,0:T(8,128)(2,1)S(1)}, bf16[2,256,256]{2,1,0:T(8,128)(2,1)S(1)}, u32[]{:S(2)}, u32[]{:S(2)}) collective-permute-start(bf16[2,256,256]{2,1,0:T(8,128)(2,1)S(1)} %get-tuple-element.75), channel_id=1, source_target_pairs={{0,1},{1,0},{2,3},{3,2},{4,5},{5,4},{6,7},{7,6},{8,9},{9,8},{10,11... | collective-permute-start | bytes 786440 | tf_op jit(solution)/shard_map/ppermute | solution.py:453
  118.7 3.7 %collective-permute-start.18 = (f32[256,256]{1,0:T(8,128)S(1)}, f32[256,256]{1,0:T(8,128)S(1)}, u32[]{:S(2)}, u32[]{:S(2)}) collective-permute-start(f32[256,256]{1,0:T(8,128)S(1)} %get-tuple-element.63), channel_id=1, source_target_pairs={{0,1},{1,0},{2,3},{3,2},{4,5},{5,4},{6,7},{7,6},{8,9},{9,8},{10,11... | collective-permute-start | bytes 786440 | tf_op jit(solution)/shard_map/ppermute | solution.py:466
  120.8 8.4 %collective-permute-start.22 = (bf16[2,256,256]{2,1,0:T(8,128)(2,1)S(1)}, bf16[2,256,256]{2,1,0:T(8,128)(2,1)S(1)}, u32[]{:S(2)}, u32[]{:S(2)}) collective-permute-start(bf16[2,256,256]{2,1,0:T(8,128)(2,1)S(1)} %halve.1), channel_id=1, source_target_pairs={{0,2},{1,3},{2,0},{3,1},{4,6},{5,7},{6,4},{7,5},{8,10},{9,11},{10,... | collective-permute-start | bytes 786440 | tf_op jit(solution)/shard_map/ppermute | solution.py:374

commit v9 on v8

--- a/solution.py
+++ b/solution.py
@@ -435,9 +435,10 @@
     recv = lax.ppermute(give, "cols", swap)
     cross_own, keep = updated(True, sampled, met)
     sent = (keep + recv.astype(F32)).astype(BF16)
-    parts = [keep, recv, *(shifted(sent, shift) for shift in range(1, pairs))]
+    parts = [shifted(sent, shift) for shift in range(1, pairs)]
+    begun = start - keep - recv.astype(F32)
     qt, given, basis = run(
-        orthonormal_kernel, [info], [start, *parts],
+        orthonormal_kernel, [info], [begun, *parts],
         [((width, order), BF16), ((share, width), F32), ((pivots, share, width), F32)],
         [
             tall, matrix, pltpu.VMEM((BLOCK // SUB, (SUB + width // 128) * SUB, 128), F32), pltpu.VMEM((share, width), F32),

time: 130 us -> 131 us (level)
  transfers between devices with their start and end apart: 23 -> 23, of which waited for: 17 -> 18; matrix products, arithmetic and copies ran while one was open for 1% -> 1% of each run, Pallas kernels for 15% -> 13%
where the time goes in v9:
time: 131 us; the launch traced here: 130 us
  waiting for transfers between devices  71.8 us (55%)
  Pallas kernels  30.7 us (23%)
  starting transfers between devices  22.3 us (17%)
  local copies, waits for them, and re-layouts  3.42 us (3%)
    ppermute x6, waiting for transfers between devices, step(): self.up[t] = found[number] = lax.ppermute(self.up[t], self.axis, self.ahead)  41.6 us
    pallas_call x14, Pallas kernels, run(): pl.pallas_call(kernel, out_shape=shapes, in_specs=[smem] * len(scalars) +...  30.7 us
    ppermute x2, waiting for transfers between devices, shifted(): lax.ppermute(x, 'cols', [(i, (i + 2 * shift) % cols) for i in range(cols)])  16.2 us
    ppermute x6, starting transfers between devices, step(): self.up[t] = found[number] = lax.ppermute(self.up[t], self.axis, self.ahead)  12 us
    ppermute x6, waiting for transfers between devices, step(): lax.ppermute(self.down[t], self.axis, self.behind)  6.11 us
    ppermute x2, starting transfers between devices, step(): lax.ppermute(self.up[t][0], self.axis, self.ahead)  3.65 us
    ppermute x2, waiting for transfers between devices, step(): lax.ppermute(self.down[t][1], self.axis, self.behind)  3.38 us
    ppermute x2, waiting for transfers between devices, step(): lax.ppermute(self.up[t][0], self.axis, self.ahead)  3.36 us
  transfers between devices with their start and end apart: 23, of which 18 were waited for; matrix products, arithmetic and copies ran while one was open for 1% of the time, Pallas kernels for 13%

profile of v9, /device:TPU:0, one launch (start us, length us, event | category | flops | bytes accessed | tf_op | source)
XLA Modules:
  0.0 130.4 jit_solution(6230721786869406878)
XLA Ops:
  0.6 3.0 %collective-permute-start.4 = (bf16[2,4,128,256]{3,2,1,0:T(8,128)(2,1)}, bf16[2,4,128,256]{3,2,1,0:T(8,128)(2,1)S(1)}, u32[]{:S(2)}, u32[]{:S(2)}) collective-permute-start(bf16[2,4,128,256]{3,2,1,0:T(8,128)(2,1)} %refs_0_.1), channel_id=1, source_target_pairs={{8,0},{16,8},{24,16},{28,24},{20,28},{12,20},{4,12},{0,4},{9,1},{1... | collective-permute-start | bytes 1572872 | tf_op jit(solution)/shard_map/ppermute | solution.py:323
  3.8 1.9 %collective-permute-start = (bf16[2,4,128,256]{3,2,1,0:T(8,128)(2,1)}, bf16[2,4,128,256]{3,2,1,0:T(8,128)(2,1)S(1)}, u32[]{:S(2)}, u32[]{:S(2)}) collective-permute-start(bf16[2,4,128,256]{3,2,1,0:T(8,128)(2,1)} %refs_3_.1), channel_id=1, source_target_pairs={{8,0},{16,8},{24,16},{28,24},{20,28},{12,20},{4,12},{0,4},{9,1},{1... | collective-permute-start | bytes 1572872 | tf_op jit(solution)/shard_map/ppermute | solution.py:323
  5.8 10.9 %collective-permute-done.4.refs_1_ = bf16[2,4,128,256]{3,2,1,0:T(8,128)(2,1)S(1)} collective-permute-done((bf16[2,4,128,256]{3,2,1,0:T(8,128)(2,1)}, bf16[2,4,128,256]{3,2,1,0:T(8,128)(2,1)S(1)}, u32[]{:S(2)}, u32[]{:S(2)}) %collective-permute-start.4) | collective-permute-done | bytes 524320 | tf_op jit(solution)/shard_map/ppermute | solution.py:323
  16.7 2.0 %collective-permute-start.6 = (bf16[2,4,128,256]{3,2,1,0:T(8,128)(2,1)S(1)}, bf16[2,4,128,256]{3,2,1,0:T(8,128)(2,1)S(1)}, u32[]{:S(2)}, u32[]{:S(2)}) collective-permute-start(bf16[2,4,128,256]{3,2,1,0:T(8,128)(2,1)S(1)} %collective-permute-done.4.refs_1_), channel_id=1, source_target_pairs={{8,0},{16,8},{24,16},{28,24},{20,28},{12,20},{4,12},{0,4},{9,1},{1... | collective-permute-start | bytes 1572872 | tf_op jit(solution)/shard_map/ppermute | solution.py:323
  19.6 1.6 %copy-done.7 = bf16[1,4,1024,256]{3,2,1,0:T(8,128)(2,1)S(1)} copy-done((bf16[1,4,1024,256]{3,2,1,0:T(8,128)(2,1)S(1)}, bf16[1,4,1024,256]{3,2,1,0:T(8,128)(2,1)}, u32[]{:S(2)}) %copy-start.7) | copy-done | bytes 2097176
  23.0 4.9 %collective-permute-done.refs_4_ = bf16[2,4,128,256]{3,2,1,0:T(8,128)(2,1)S(1)} collective-permute-done((bf16[2,4,128,256]{3,2,1,0:T(8,128)(2,1)}, bf16[2,4,128,256]{3,2,1,0:T(8,128)(2,1)S(1)}, u32[]{:S(2)}, u32[]{:S(2)}) %collective-permute-start) | collective-permute-done | bytes 524320 | tf_op jit(solution)/shard_map/ppermute | solution.py:323
  27.9 2.0 %collective-permute-start.1 = (bf16[2,4,128,256]{3,2,1,0:T(8,128)(2,1)S(1)}, bf16[2,4,128,256]{3,2,1,0:T(8,128)(2,1)S(1)}, u32[]{:S(2)}, u32[]{:S(2)}) collective-permute-start(bf16[2,4,128,256]{3,2,1,0:T(8,128)(2,1)S(1)} %collective-permute-done.refs_4_), channel_id=1, source_target_pairs={{8,0},{16,8},{24,16},{28,24},{20,28},{12,20},{4,12},{0,4},{9,1},{1... | collective-permute-start | bytes 1572872 | tf_op jit(solution)/shard_map/ppermute | solution.py:323
  30.0 1.8 %gather.3 = (f32[2,4,256,256]{3,2,1,0:T(8,128)S(1)}, f32[2,4,256,256]{3,2,1,0:T(8,128)S(1)}, bf16[2,4,1024,256]{3,2,1,0:T(8,128)(2,1)S(1)}) custom-call(s32[10]{0:T(128)S(1)} %pad_add_fusion.info, bf16[4,256,1024]{2,1,0:T(8,128)(2,1)S(1)} %get-tuple-element.42.panel_vt, bf16[256,1024]{1,0:T(8,128)(2,1)S(1)} %get-tuple-element.40.sampler_t, ...), custom_call_target="tpu_custom_call" | custom-call | flops 805306368 | bytes 14155776 | tf_op jit(solution)/shard_map/gather/pallas_call | solution.py:291
  31.9 7.3 %collective-permute-done.6.refs_0_ = bf16[2,4,128,256]{3,2,1,0:T(8,128)(2,1)S(1)} collective-permute-done((bf16[2,4,128,256]{3,2,1,0:T(8,128)(2,1)S(1)}, bf16[2,4,128,256]{3,2,1,0:T(8,128)(2,1)S(1)}, u32[]{:S(2)}, u32[]{:S(2)}) %collective-permute-start.6) | collective-permute-done | bytes 524320 | tf_op jit(solution)/shard_map/ppermute | solution.py:323
  39.1 2.0 %collective-permute-done.7.refs_1_ = bf16[2,4,128,256]{3,2,1,0:T(8,128)(2,1)S(1)} collective-permute-done((bf16[2,4,128,256]{3,2,1,0:T(8,128)(2,1)S(1)}, bf16[2,4,128,256]{3,2,1,0:T(8,128)(2,1)S(1)}, u32[]{:S(2)}, u32[]{:S(2)}) %collective-permute-start.7) | collective-permute-done | bytes 524320 | tf_op jit(solution)/shard_map/ppermute | solution.py:324
  41.1 1.6 %collective-permute-start.8 = (bf16[2,4,128,256]{3,2,1,0:T(8,128)(2,1)S(1)}, bf16[2,4,128,256]{3,2,1,0:T(8,128)(2,1)S(1)}, u32[]{:S(2)}, u32[]{:S(2)}) collective-permute-start(bf16[2,4,128,256]{3,2,1,0:T(8,128)(2,1)S(1)} %collective-permute-done.6.refs_0_), channel_id=1, source_target_pairs={{8,0},{16,8},{24,16},{28,24},{20,28},{12,20},{4,12},{0,4},{9,1},{1... | collective-permute-start | bytes 1572872 | tf_op jit(solution)/shard_map/ppermute | solution.py:323
  44.5 5.9 %collective-permute-done.1.refs_2_ = bf16[2,4,128,256]{3,2,1,0:T(8,128)(2,1)S(1)} collective-permute-done((bf16[2,4,128,256]{3,2,1,0:T(8,128)(2,1)S(1)}, bf16[2,4,128,256]{3,2,1,0:T(8,128)(2,1)S(1)}, u32[]{:S(2)}, u32[]{:S(2)}) %collective-permute-start.1) | collective-permute-done | bytes 524320 | tf_op jit(solution)/shard_map/ppermute | solution.py:323
  50.4 2.0 %collective-permute-done.3.refs_3_ = bf16[2,4,128,256]{3,2,1,0:T(8,128)(2,1)S(1)} collective-permute-done((bf16[2,4,128,256]{3,2,1,0:T(8,128)(2,1)S(1)}, bf16[2,4,128,256]{3,2,1,0:T(8,128)(2,1)S(1)}, u32[]{:S(2)}, u32[]{:S(2)}) %collective-permute-start.3) | collective-permute-done | bytes 524320 | tf_op jit(solution)/shard_map/ppermute | solution.py:324
  54.4 1.6 %gather.4 = (f32[2,4,256,256]{3,2,1,0:T(8,128)S(1)}, f32[2,4,256,256]{3,2,1,0:T(8,128)S(1)}, bf16[2,4,1024,256]{3,2,1,0:T(8,128)(2,1)S(1)}) custom-call(s32[10]{0:T(128)S(1)} %pad_add_fusion.info, bf16[4,256,1024]{2,1,0:T(8,128)(2,1)S(1)} %get-tuple-element.42.panel_vt, ...), custom_call_target="tpu_custom_call", output_to_operand_aliasing={{0}: (7, {}), {1}: (8, {}), {2}: (9, {})} | custom-call | flops 536870912 | bytes 21495808 | tf_op jit(solution)/shard_map/gather/pallas_call | solution.py:291
  56.1 5.5 %collective-permute-done.8.refs_0_ = bf16[2,4,128,256]{3,2,1,0:T(8,128)(2,1)S(1)} collective-permute-done((bf16[2,4,128,256]{3,2,1,0:T(8,128)(2,1)S(1)}, bf16[2,4,128,256]{3,2,1,0:T(8,128)(2,1)S(1)}, u32[]{:S(2)}, u32[]{:S(2)}) %collective-permute-start.8) | collective-permute-done | bytes 524320 | tf_op jit(solution)/shard_map/ppermute | solution.py:323
  61.6 2.0 %collective-permute-done.9.refs_1_ = bf16[2,4,128,256]{3,2,1,0:T(8,128)(2,1)S(1)} collective-permute-done((bf16[2,4,128,256]{3,2,1,0:T(8,128)(2,1)S(1)}, bf16[2,4,128,256]{3,2,1,0:T(8,128)(2,1)S(1)}, u32[]{:S(2)}, u32[]{:S(2)}) %collective-permute-start.9) | collective-permute-done | bytes 524320 | tf_op jit(solution)/shard_map/ppermute | solution.py:324
  63.6 1.6 %collective-permute-start.12 = (bf16[4,128,256]{2,1,0:T(8,128)(2,1)S(1)}, bf16[4,128,256]{2,1,0:T(8,128)(2,1)S(1)}, u32[]{:S(2)}, u32[]{:S(2)}) collective-permute-start(bf16[4,128,256]{2,1,0:T(8,128)(2,1)S(1)} %slice_bitcast_fusion.3), channel_id=1, source_target_pairs={{8,0},{16,8},{24,16},{28,24},{20,28},{12,20},{4,12},{0,4},{9,1},{1... | collective-permute-start | bytes 786440 | tf_op jit(solution)/shard_map/ppermute | solution.py:327
  65.8 7.1 %collective-permute-done.10.refs_2_ = bf16[2,4,128,256]{3,2,1,0:T(8,128)(2,1)S(1)} collective-permute-done((bf16[2,4,128,256]{3,2,1,0:T(8,128)(2,1)S(1)}, bf16[2,4,128,256]{3,2,1,0:T(8,128)(2,1)S(1)}, u32[]{:S(2)}, u32[]{:S(2)}) %collective-permute-start.10) | collective-permute-done | bytes 524320 | tf_op jit(solution)/shard_map/ppermute | solution.py:323
  72.9 2.0 %collective-permute-start.14 = (bf16[4,128,256]{2,1,0:T(8,128)(2,1)S(1)}, bf16[4,128,256]{2,1,0:T(8,128)(2,1)S(1)}, u32[]{:S(2)}, u32[]{:S(2)}) collective-permute-start(bf16[4,128,256]{2,1,0:T(8,128)(2,1)S(1)} %slice_bitcast_fusion.1), channel_id=1, source_target_pairs={{8,0},{16,8},{24,16},{28,24},{20,28},{12,20},{4,12},{0,4},{9,1},{1... | collective-permute-start | bytes 786440 | tf_op jit(solution)/shard_map/ppermute | solution.py:327
  75.3 1.6 %gather.5 = (f32[2,4,256,256]{3,2,1,0:T(8,128)S(1)}, f32[2,4,256,256]{3,2,1,0:T(8,128)S(1)}, bf16[2,4,1024,256]{3,2,1,0:T(8,128)(2,1)S(1)}) custom-call(s32[10]{0:T(128)S(1)} %pad_add_fusion.info, bf16[4,256,1024]{2,1,0:T(8,128)(2,1)S(1)} %get-tuple-element.42.panel_vt, ...), custom_call_target="tpu_custom_call", output_to_operand_aliasing={{0}: (7, {}), {1}: (8, {}), {2}: (9, {})} | custom-call | flops 536870912 | bytes 21495808 | tf_op jit(solution)/shard_map/gather/pallas_call | solution.py:291
  78.5 2.0 %collective-permute-done.13.refs_1_ = bf16[4,128,256]{2,1,0:T(8,128)(2,1)S(1)} collective-permute-done((bf16[4,128,256]{2,1,0:T(8,128)(2,1)S(1)}, bf16[4,128,256]{2,1,0:T(8,128)(2,1)S(1)}, u32[]{:S(2)}, u32[]{:S(2)}) %collective-permute-start.13) | collective-permute-done | bytes 262176 | tf_op jit(solution)/shard_map/ppermute | solution.py:328
  81.5 1.8 %collective-permute-done.14.refs_0_ = bf16[4,128,256]{2,1,0:T(8,128)(2,1)S(1)} collective-permute-done((bf16[4,128,256]{2,1,0:T(8,128)(2,1)S(1)}, bf16[4,128,256]{2,1,0:T(8,128)(2,1)S(1)}, u32[]{:S(2)}, u32[]{:S(2)}) %collective-permute-start.14) | collective-permute-done | bytes 262176 | tf_op jit(solution)/shard_map/ppermute | solution.py:327
  84.6 1.7 %update.3 = (bf16[4,256,256]{2,1,0:T(8,128)(2,1)S(1)}, bf16[256,1024]{1,0:T(8,128)(2,1)S(1)}) custom-call(s32[10]{0:T(128)S(1)} %pad_add_fusion.info, s32[1,4]{1,0:T(1,128)S(1)} %copy-done.6, s32[2,4]{1,0:T(2,128)S(1)} %copy-done.5, bf16[2,4,256,256]{3,2,1,0:T(8,128)(2,1)S(1)} %get-tuple-element.59.sampled, f32[2,4,256,256]{3,2,1,0:T(8,128)S(1)} %get-tuple-element.60.met, ...), custom_call_target="tpu_custom_call" | custom-call | flops 1342177280 | bytes 8912896 | tf_op jit(solution)/shard_map/update/pallas_call | solution.py:291
  86.4 1.7 %update.2 = (bf16[4,256,256]{2,1,0:T(8,128)(2,1)S(1)}, f32[256,1024]{1,0:T(8,128)S(1)}) custom-call(s32[10]{0:T(128)S(1)} %pad_add_fusion.info, s32[1,4]{1,0:T(1,128)S(1)} %copy-done.6, s32[2,4]{1,0:T(2,128)S(1)} %copy-done.5, bf16[2,4,256,256]{3,2,1,0:T(8,128)(2,1)S(1)} %get-tuple-element.59.sampled, f32[2,4,256,256]{3,2,1,0:T(8,128)S(1)} %get-tuple-element.60.met, ...), custom_call_target="tpu_custom_call" | custom-call | flops 1342177280 | bytes 9437184 | tf_op jit(solution)/shard_map/update/pallas_call | solution.py:291
  88.7 1.6 %collective-permute-start.17 = (bf16[256,1024]{1,0:T(8,128)(2,1)S(1)}, bf16[256,1024]{1,0:T(8,128)(2,1)S(1)}, u32[]{:S(2)}, u32[]{:S(2)}) collective-permute-start(bf16[256,1024]{1,0:T(8,128)(2,1)S(1)} %get-tuple-element.80), channel_id=1, source_target_pairs={{0,2},{1,3},{2,0},{3,1},{4,6},{5,7},{6,4},{7,5},{8,10},{9,11},{10,... | collective-permute-start | bytes 1572872 | tf_op jit(solution)/shard_map/ppermute | solution.py:374
  90.3 12.6 %collective-permute-done.17.refs_0_ = bf16[256,1024]{1,0:T(8,128)(2,1)S(1)} collective-permute-done((bf16[256,1024]{1,0:T(8,128)(2,1)S(1)}, bf16[256,1024]{1,0:T(8,128)(2,1)S(1)}, u32[]{:S(2)}, u32[]{:S(2)}) %collective-permute-start.17) | collective-permute-done | bytes 524320 | tf_op jit(solution)/shard_map/ppermute | solution.py:374
  102.9 9.4 %orthonormal.1 = (bf16[256,1024]{1,0:T(8,128)(2,1)S(1)}, f32[256,256]{1,0:T(8,128)S(1)}, f32[2,256,256]{2,1,0:T(8,128)}) custom-call(s32[10]{0:T(128)S(1)} %pad_add_fusion.info, f32[256,1024]{1,0:T(8,128)S(1)} %get-tuple-element.81.start, bf16[256,1024]{1,0:T(8,128)(2,1)S(1)} %collective-permute-done.17.refs_0_), custom_call_target="tpu_custom_call" | custom-call | flops 17179869184 | bytes 2883584 | tf_op jit(solution)/shard_map/orthonormal/pallas_call | solution.py:291
  112.3 2.9 %project.2 = (bf16[2,256,256]{2,1,0:T(8,128)(2,1)S(1)}, f32[2,256,256]{2,1,0:T(8,128)S(1)}) custom-call(s32[10]{0:T(128)S(1)} %pad_add_fusion.info, bf16[256,1024]{1,0:T(8,128)(2,1)S(1)} %get-tuple-element.76.qt.qt_a, bf16[4,1024,256]{2,1,0:T(8,128)(2,1)S(1)} %bitcast.25, bf16[4,256,256]{2,1,0:T(8,128)(2,1)S(1)} %get-tuple-element.66.cross, ...), custom_call_target="tpu_custom_call" | custom-call | flops 3623878656 | bytes 8126464 | tf_op jit(solution)/shard_map/project/pallas_call | solution.py:291
  115.2 2.9 %project.3 = (bf16[2,256,256]{2,1,0:T(8,128)(2,1)S(1)}, f32[2,256,256]{2,1,0:T(8,128)S(1)}) custom-call(s32[10]{0:T(128)S(1)} %pad_add_fusion.info, bf16[256,1024]{1,0:T(8,128)(2,1)S(1)} %collective-permute-done.19.qt.qt_b, bf16[4,1024,256]{2,1,0:T(8,128)(2,1)S(1)} %bitcast.26, bf16[4,256,256]{2,1,0:T(8,128)(2,1)S(1)} %get-tuple-element.71.cross, ...), custom_call_target="tpu_custom_call" | custom-call | flops 3623878656 | bytes 8126464 | tf_op jit(solution)/shard_map/project/pallas_call | solution.py:291
  120.9 1.6 %collective-permute-start.22 = (bf16[2,256,256]{2,1,0:T(8,128)(2,1)S(1)}, bf16[2,256,256]{2,1,0:T(8,128)(2,1)S(1)}, u32[]{:S(2)}, u32[]{:S(2)}) collective-permute-start(bf16[2,256,256]{2,1,0:T(8,128)(2,1)S(1)} %halve.1), channel_id=1, source_target_pairs={{0,2},{1,3},{2,0},{3,1},{4,6},{5,7},{6,4},{7,5},{8,10},{9,11},{10,... | collective-permute-start | bytes 786440 | tf_op jit(solution)/shard_map/ppermute | solution.py:374
  123.7 2.2 %own.1 = f32[2,256,256]{2,1,0:T(8,128)S(1)} custom-call(s32[10]{0:T(128)S(1)} %pad_add_fusion.info, bf16[256,1024]{1,0:T(8,128)(2,1)S(1)} %collective-permute-done.19.qt.qt_b, bf16[256,1024]{1,0:T(8,128)(2,1)S(1)} %get-tuple-element.76.qt.qt_a, f32[2,256,256]{2,1,0:T(8,128)S(1)} %get-tuple-element.72.keep_b, f32[2,256,256]{2,1,0:T(8,128)S(1)} %get-tuple-element.73.keep_a, ...), custom_call_target="tpu_custom_call" | custom-call | flops 33554432 | bytes 3145728 | tf_op jit(solution)/shard_map/own/pallas_call | solution.py:291
  125.9 3.6 %collective-permute-done.22 = bf16[2,256,256]{2,1,0:T(8,128)(2,1)S(1)} collective-permute-done((bf16[2,256,256]{2,1,0:T(8,128)(2,1)S(1)}, bf16[2,256,256]{2,1,0:T(8,128)(2,1)S(1)}, u32[]{:S(2)}, u32[]{:S(2)}) %collective-permute-start.22) | collective-permute-done | bytes 262176 | tf_op jit(solution)/shard_map/ppermute | solution.py:374
  (54 shorter events, 17.3 us)
Async XLA Ops:
  0.6 16.0 %collective-permute-start.4 = (bf16[2,4,128,256]{3,2,1,0:T(8,128)(2,1)}, bf16[2,4,128,256]{3,2,1,0:T(8,128)(2,1)S(1)}, u32[]{:S(2)}, u32[]{:S(2)}) collective-permute-start(bf16[2,4,128,256]{3,2,1,0:T(8,128)(2,1)} %refs_0_.1), channel_id=1, source_target_pairs={{8,0},{16,8},{24,16},{28,24},{20,28},{12,20},{4,12},{0,4},{9,1},{1... | collective-permute-start | bytes 1572872 | tf_op jit(solution)/shard_map/ppermute | solution.py:323
  3.6 15.1 %collective-permute-start.5 = (bf16[2,4,128,256]{3,2,1,0:T(8,128)(2,1)}, bf16[2,4,128,256]{3,2,1,0:T(8,128)(2,1)S(1)}, u32[]{:S(2)}, u32[]{:S(2)}) collective-permute-start(bf16[2,4,128,256]{3,2,1,0:T(8,128)(2,1)} %refs_0_.1), channel_id=1, source_target_pairs={{0,8},{8,16},{16,24},{24,28},{28,20},{20,12},{12,4},{4,0},{1,9},{9... | collective-permute-start | bytes 1572872 | tf_op jit(solution)/shard_map/ppermute | solution.py:324
  3.8 24.1 %collective-permute-start = (bf16[2,4,128,256]{3,2,1,0:T(8,128)(2,1)}, bf16[2,4,128,256]{3,2,1,0:T(8,128)(2,1)S(1)}, u32[]{:S(2)}, u32[]{:S(2)}) collective-permute-start(bf16[2,4,128,256]{3,2,1,0:T(8,128)(2,1)} %refs_3_.1), channel_id=1, source_target_pairs={{8,0},{16,8},{24,16},{28,24},{20,28},{12,20},{4,12},{0,4},{9,1},{1... | collective-permute-start | bytes 1572872 | tf_op jit(solution)/shard_map/ppermute | solution.py:323
  5.6 24.3 %collective-permute-start.2 = (bf16[2,4,128,256]{3,2,1,0:T(8,128)(2,1)}, bf16[2,4,128,256]{3,2,1,0:T(8,128)(2,1)S(1)}, u32[]{:S(2)}, u32[]{:S(2)}) collective-permute-start(bf16[2,4,128,256]{3,2,1,0:T(8,128)(2,1)} %refs_3_.1), channel_id=1, source_target_pairs={{0,8},{8,16},{16,24},{24,28},{28,20},{20,12},{12,4},{4,0},{1,9},{9... | collective-permute-start | bytes 1572872 | tf_op jit(solution)/shard_map/ppermute | solution.py:324
  16.7 22.5 %collective-permute-start.6 = (bf16[2,4,128,256]{3,2,1,0:T(8,128)(2,1)S(1)}, bf16[2,4,128,256]{3,2,1,0:T(8,128)(2,1)S(1)}, u32[]{:S(2)}, u32[]{:S(2)}) collective-permute-start(bf16[2,4,128,256]{3,2,1,0:T(8,128)(2,1)S(1)} %collective-permute-done.4.refs_1_), channel_id=1, source_target_pairs={{8,0},{16,8},{24,16},{28,24},{20,28},{12,20},{4,12},{0,4},{9,1},{1... | collective-permute-start | bytes 1572872 | tf_op jit(solution)/shard_map/ppermute | solution.py:323
  18.7 22.5 %collective-permute-start.7 = (bf16[2,4,128,256]{3,2,1,0:T(8,128)(2,1)S(1)}, bf16[2,4,128,256]{3,2,1,0:T(8,128)(2,1)S(1)}, u32[]{:S(2)}, u32[]{:S(2)}) collective-permute-start(bf16[2,4,128,256]{3,2,1,0:T(8,128)(2,1)S(1)} %collective-permute-done.5.refs_2_), channel_id=1, source_target_pairs={{0,8},{8,16},{16,24},{24,28},{28,20},{20,12},{12,4},{4,0},{1,9},{9... | collective-permute-start | bytes 1572872 | tf_op jit(solution)/shard_map/ppermute | solution.py:324
  19.6 1.6 %copy-start.7 = (bf16[1,4,1024,256]{3,2,1,0:T(8,128)(2,1)S(1)}, bf16[1,4,1024,256]{3,2,1,0:T(8,128)(2,1)}, u32[]{:S(2)}) copy-start(bf16[1,4,1024,256]{3,2,1,0:T(8,128)(2,1)} %param.11) | copy-start | bytes 6291460
  21.2 1.0 copy-start.8
  22.2 7.8 %copy-start.3 = (bf16[2,4,128,256]{3,2,1,0:T(8,128)(2,1)S(1)}, bf16[2,4,128,256]{3,2,1,0:T(8,128)(2,1)}, u32[]{:S(2)}) copy-start(bf16[2,4,128,256]{3,2,1,0:T(8,128)(2,1)} %refs_0_.1) | copy-start | bytes 1572868
  22.2 7.8 %copy-start.4 = (bf16[2,4,128,256]{3,2,1,0:T(8,128)(2,1)S(1)}, bf16[2,4,128,256]{3,2,1,0:T(8,128)(2,1)}, u32[]{:S(2)}) copy-start(bf16[2,4,128,256]{3,2,1,0:T(8,128)(2,1)} %refs_3_.1) | copy-start | bytes 1572868
  27.9 22.5 %collective-permute-start.1 = (bf16[2,4,128,256]{3,2,1,0:T(8,128)(2,1)S(1)}, bf16[2,4,128,256]{3,2,1,0:T(8,128)(2,1)S(1)}, u32[]{:S(2)}, u32[]{:S(2)}) collective-permute-start(bf16[2,4,128,256]{3,2,1,0:T(8,128)(2,1)S(1)} %collective-permute-done.refs_4_), channel_id=1, source_target_pairs={{8,0},{16,8},{24,16},{28,24},{20,28},{12,20},{4,12},{0,4},{9,1},{1... | collective-permute-start | bytes 1572872 | tf_op jit(solution)/shard_map/ppermute | solution.py:323
  29.9 22.5 %collective-permute-start.3 = (bf16[2,4,128,256]{3,2,1,0:T(8,128)(2,1)S(1)}, bf16[2,4,128,256]{3,2,1,0:T(8,128)(2,1)S(1)}, u32[]{:S(2)}, u32[]{:S(2)}) collective-permute-start(bf16[2,4,128,256]{3,2,1,0:T(8,128)(2,1)S(1)} %collective-permute-done.2.refs_5_), channel_id=1, source_target_pairs={{0,8},{8,16},{16,24},{24,28},{28,20},{20,12},{12,4},{4,0},{1,9},{9... | collective-permute-start | bytes 1572872 | tf_op jit(solution)/shard_map/ppermute | solution.py:324
  30.0 13.1 %copy-start.1 = (bf16[2,1,1024,256]{3,2,1,0:T(8,128)(2,1)S(1)}, bf16[2,1,1024,256]{3,2,1,0:T(8,128)(2,1)}, u32[]{:S(2)}) copy-start(bf16[2,1,1024,256]{3,2,1,0:T(8,128)(2,1)} %param.16) | copy-start | bytes 3145732
  30.0 13.1 %copy-start.2 = (bf16[2,1,1024,256]{3,2,1,0:T(8,128)(2,1)S(1)}, bf16[2,1,1024,256]{3,2,1,0:T(8,128)(2,1)}, u32[]{:S(2)}) copy-start(bf16[2,1,1024,256]{3,2,1,0:T(8,128)(2,1)} %param.17) | copy-start | bytes 3145732
  41.1 20.5 %collective-permute-start.8 = (bf16[2,4,128,256]{3,2,1,0:T(8,128)(2,1)S(1)}, bf16[2,4,128,256]{3,2,1,0:T(8,128)(2,1)S(1)}, u32[]{:S(2)}, u32[]{:S(2)}) collective-permute-start(bf16[2,4,128,256]{3,2,1,0:T(8,128)(2,1)S(1)} %collective-permute-done.6.refs_0_), channel_id=1, source_target_pairs={{8,0},{16,8},{24,16},{28,24},{20,28},{12,20},{4,12},{0,4},{9,1},{1... | collective-permute-start | bytes 1572872 | tf_op jit(solution)/shard_map/ppermute | solution.py:323
  42.7 20.9 %collective-permute-start.9 = (bf16[2,4,128,256]{3,2,1,0:T(8,128)(2,1)S(1)}, bf16[2,4,128,256]{3,2,1,0:T(8,128)(2,1)S(1)}, u32[]{:S(2)}, u32[]{:S(2)}) collective-permute-start(bf16[2,4,128,256]{3,2,1,0:T(8,128)(2,1)S(1)} %collective-permute-done.7.refs_1_), channel_id=1, source_target_pairs={{0,8},{8,16},{16,24},{24,28},{28,20},{20,12},{12,4},{4,0},{1,9},{9... | collective-permute-start | bytes 1572872 | tf_op jit(solution)/shard_map/ppermute | solution.py:324
  52.4 20.5 %collective-permute-start.10 = (bf16[2,4,128,256]{3,2,1,0:T(8,128)(2,1)S(1)}, bf16[2,4,128,256]{3,2,1,0:T(8,128)(2,1)S(1)}, u32[]{:S(2)}, u32[]{:S(2)}) collective-permute-start(bf16[2,4,128,256]{3,2,1,0:T(8,128)(2,1)S(1)} %collective-permute-done.1.refs_2_), channel_id=1, source_target_pairs={{8,0},{16,8},{24,16},{28,24},{20,28},{12,20},{4,12},{0,4},{9,1},{1... | collective-permute-start | bytes 1572872 | tf_op jit(solution)/shard_map/ppermute | solution.py:323
  54.0 20.9 %collective-permute-start.11 = (bf16[2,4,128,256]{3,2,1,0:T(8,128)(2,1)S(1)}, bf16[2,4,128,256]{3,2,1,0:T(8,128)(2,1)S(1)}, u32[]{:S(2)}, u32[]{:S(2)}) collective-permute-start(bf16[2,4,128,256]{3,2,1,0:T(8,128)(2,1)S(1)} %collective-permute-done.3.refs_3_), channel_id=1, source_target_pairs={{0,8},{8,16},{16,24},{24,28},{28,20},{20,12},{12,4},{4,0},{1,9},{9... | collective-permute-start | bytes 1572872 | tf_op jit(solution)/shard_map/ppermute | solution.py:324
  63.6 14.8 %collective-permute-start.12 = (bf16[4,128,256]{2,1,0:T(8,128)(2,1)S(1)}, bf16[4,128,256]{2,1,0:T(8,128)(2,1)S(1)}, u32[]{:S(2)}, u32[]{:S(2)}) collective-permute-start(bf16[4,128,256]{2,1,0:T(8,128)(2,1)S(1)} %slice_bitcast_fusion.3), channel_id=1, source_target_pairs={{8,0},{16,8},{24,16},{28,24},{20,28},{12,20},{4,12},{0,4},{9,1},{1... | collective-permute-start | bytes 786440 | tf_op jit(solution)/shard_map/ppermute | solution.py:327
  65.3 15.2 %collective-permute-start.13 = (bf16[4,128,256]{2,1,0:T(8,128)(2,1)S(1)}, bf16[4,128,256]{2,1,0:T(8,128)(2,1)S(1)}, u32[]{:S(2)}, u32[]{:S(2)}) collective-permute-start(bf16[4,128,256]{2,1,0:T(8,128)(2,1)S(1)} %slice_bitcast_fusion.2), channel_id=1, source_target_pairs={{0,8},{8,16},{16,24},{24,28},{28,20},{20,12},{12,4},{4,0},{1,9},{9... | collective-permute-start | bytes 786440 | tf_op jit(solution)/shard_map/ppermute | solution.py:328
  72.9 10.4 %collective-permute-start.14 = (bf16[4,128,256]{2,1,0:T(8,128)(2,1)S(1)}, bf16[4,128,256]{2,1,0:T(8,128)(2,1)S(1)}, u32[]{:S(2)}, u32[]{:S(2)}) collective-permute-start(bf16[4,128,256]{2,1,0:T(8,128)(2,1)S(1)} %slice_bitcast_fusion.1), channel_id=1, source_target_pairs={{8,0},{16,8},{24,16},{28,24},{20,28},{12,20},{4,12},{0,4},{9,1},{1... | collective-permute-start | bytes 786440 | tf_op jit(solution)/shard_map/ppermute | solution.py:327
  74.9 9.7 %collective-permute-start.15 = (bf16[4,128,256]{2,1,0:T(8,128)(2,1)S(1)}, bf16[4,128,256]{2,1,0:T(8,128)(2,1)S(1)}, u32[]{:S(2)}, u32[]{:S(2)}) collective-permute-start(bf16[4,128,256]{2,1,0:T(8,128)(2,1)S(1)} %slice_bitcast_fusion), channel_id=1, source_target_pairs={{0,8},{8,16},{16,24},{24,28},{28,20},{20,12},{12,4},{4,0},{1,9},{9... | collective-permute-start | bytes 786440 | tf_op jit(solution)/shard_map/ppermute | solution.py:328
  80.5 4.2 %copy-start = (bf16[1,4,1024,256]{3,2,1,0:T(8,128)(2,1)S(1)}, bf16[1,4,1024,256]{3,2,1,0:T(8,128)(2,1)}, u32[]{:S(2)}) copy-start(bf16[1,4,1024,256]{3,2,1,0:T(8,128)(2,1)} %param.10) | copy-start | bytes 6291460
  80.5 4.2 %copy-start.5 = (s32[2,4]{1,0:T(2,128)S(1)}, s32[2,4]{1,0:T(2,128)}, u32[]{:S(2)}) copy-start(s32[2,4]{1,0:T(2,128)} %pivot_rank.3) | copy-start | bytes 100
  80.5 4.2 %copy-start.6 = (s32[1,4]{1,0:T(1,128)S(1)}, s32[1,4]{1,0:T(1,128)}, u32[]{:S(2)}) copy-start(s32[1,4]{1,0:T(1,128)} %panel_rank.3) | copy-start | bytes 52
  86.3 2.0 %collective-permute-start.16 = (bf16[256,1024]{1,0:T(8,128)(2,1)S(1)}, bf16[256,1024]{1,0:T(8,128)(2,1)S(1)}, u32[]{:S(2)}, u32[]{:S(2)}) collective-permute-start(bf16[256,1024]{1,0:T(8,128)(2,1)S(1)} %get-tuple-element.62), channel_id=1, source_target_pairs={{0,1},{1,0},{2,3},{3,2},{4,5},{5,4},{6,7},{7,6},{8,9},{9,8},{10,11... | collective-permute-start | bytes 1572872 | tf_op jit(solution)/shard_map/ppermute | solution.py:435
  88.7 14.2 %collective-permute-start.17 = (bf16[256,1024]{1,0:T(8,128)(2,1)S(1)}, bf16[256,1024]{1,0:T(8,128)(2,1)S(1)}, u32[]{:S(2)}, u32[]{:S(2)}) collective-permute-start(bf16[256,1024]{1,0:T(8,128)(2,1)S(1)} %get-tuple-element.80), channel_id=1, source_target_pairs={{0,2},{1,3},{2,0},{3,1},{4,6},{5,7},{6,4},{7,5},{8,10},{9,11},{10,... | collective-permute-start | bytes 1572872 | tf_op jit(solution)/shard_map/ppermute | solution.py:374
  112.3 3.0 %collective-permute-start.19 = (bf16[256,1024]{1,0:T(8,128)(2,1)S(1)}, bf16[256,1024]{1,0:T(8,128)(2,1)S(1)}, u32[]{:S(2)}, u32[]{:S(2)}) collective-permute-start(bf16[256,1024]{1,0:T(8,128)(2,1)S(1)} %get-tuple-element.76.qt.qt_a), channel_id=1, source_target_pairs={{0,1},{1,0},{2,3},{3,2},{4,5},{5,4},{6,7},{7,6},{8,9},{9,8},{10,11... | collective-permute-start | bytes 1572872 | tf_op jit(solution)/shard_map/ppermute | solution.py:450
  118.1 1.7 %collective-permute-start.21 = (bf16[2,256,256]{2,1,0:T(8,128)(2,1)S(1)}, bf16[2,256,256]{2,1,0:T(8,128)(2,1)S(1)}, u32[]{:S(2)}, u32[]{:S(2)}) collective-permute-start(bf16[2,256,256]{2,1,0:T(8,128)(2,1)S(1)} %get-tuple-element.75), channel_id=1, source_target_pairs={{0,1},{1,0},{2,3},{3,2},{4,5},{5,4},{6,7},{7,6},{8,9},{9,8},{10,11... | collective-permute-start | bytes 786440 | tf_op jit(solution)/shard_map/ppermute | solution.py:454
  118.7 1.5 %collective-permute-start.20 = (bf16[2,256,256]{2,1,0:T(8,128)(2,1)S(1)}, bf16[2,256,256]{2,1,0:T(8,128)(2,1)S(1)}, u32[]{:S(2)}, u32[]{:S(2)}) collective-permute-start(bf16[2,256,256]{2,1,0:T(8,128)(2,1)S(1)} %get-tuple-element.74), channel_id=1, source_target_pairs={{0,1},{1,0},{2,3},{3,2},{4,5},{5,4},{6,7},{7,6},{8,9},{9,8},{10,11... | collective-permute-start | bytes 786440 | tf_op jit(solution)/shard_map/ppermute | solution.py:454
  118.8 3.7 %collective-permute-start.18 = (f32[256,256]{1,0:T(8,128)S(1)}, f32[256,256]{1,0:T(8,128)S(1)}, u32[]{:S(2)}, u32[]{:S(2)}) collective-permute-start(f32[256,256]{1,0:T(8,128)S(1)} %get-tuple-element.63), channel_id=1, source_target_pairs={{0,1},{1,0},{2,3},{3,2},{4,5},{5,4},{6,7},{7,6},{8,9},{9,8},{10,11... | collective-permute-start | bytes 786440 | tf_op jit(solution)/shard_map/ppermute | solution.py:467
  120.9 8.7 %collective-permute-start.22 = (bf16[2,256,256]{2,1,0:T(8,128)(2,1)S(1)}, bf16[2,256,256]{2,1,0:T(8,128)(2,1)S(1)}, u32[]{:S(2)}, u32[]{:S(2)}) collective-permute-start(bf16[2,256,256]{2,1,0:T(8,128)(2,1)S(1)} %halve.1), channel_id=1, source_target_pairs={{0,2},{1,3},{2,0},{3,1},{4,6},{5,7},{6,4},{7,5},{8,10},{9,11},{10,... | collective-permute-start | bytes 786440 | tf_op jit(solution)/shard_map/ppermute | solution.py:374
